TPU v7x, 32 devices: a whole 2x2x4 slice. The times are simulated.
32 devices in a mesh: replica: 2 (over x), node: 2 (over core), local: 8 (over z, y).
Axes of the slice: x: 2, y: 2, z: 4, core: 2. Of those that a mesh axis runs over, the one named last changes fastest.
Arguments:
- tokens: bfloat16 [2048, 3584], P(('replica', 'node', 'local')), parts along dimension 0, may hold values from -6 to 6
- expert_ids: int32 [2048, 4], P(('replica', 'node', 'local')), parts along dimension 0, may hold values from 0 to 7, all different within a row; in each aligned block of 64 rows (0 to 63, 64 to 127, ...) at most 48 rows name the same one
- combine_weights: bfloat16 [2048, 4], P(('replica', 'node', 'local')), parts along dimension 0, may hold values from 0.099609375 to 1
- w_gate: bfloat16 [16, 3584, 512], P(('node', 'local')), may hold values from -0.09375 to 0.09375
- w_up: bfloat16 [16, 3584, 512], P(('node', 'local')), may hold values from -0.09375 to 0.09375
- w_down: bfloat16 [16, 512, 3584], P(('node', 'local')), may hold values from -0.1875 to 0.1875
- queries: bfloat16 [2048, 64, 576], P(('replica', 'node', 'local')), parts along dimension 0, may hold values from -400 to 400
- latent_cache: bfloat16 [2048, 64, 576], P(('replica', 'node', 'local')), parts along dimension 0, may hold values from -6 to 6
- cache_lengths: int32 [2048], P(('replica', 'node', 'local')), parts along dimension 0, may hold values from 2 to 64, as said below
Outputs:
- moe_out: bfloat16 [2048, 3584], P(('replica', 'node', 'local')), parts along dimension 0
- attn_latent: bfloat16 [2048, 64, 512], P(('replica', 'node', 'local')), parts along dimension 0
There are 2 independent parts, one for each index of `replica`. A program takes and returns all parts, laid end to end along the dimension named above; an argument that names none is the same for every part. Nothing has to cross between parts.
Inputs may be any that keep to these rules, and one draw needn't show every extreme that they name: `expert_ids`: each row names 4 different experts; among the rows of one device no expert is named more than 48 times, and some device names some expert exactly 48 times. `cache_lengths`: some sequence has exactly 64 live positions.
All inputs are finite; a program needn't handle non-finite values.
Results may differ from a plain program's by a relative error of at most 0.0085.
Values may be sent and summed in bfloat16 or wider, within the bound.
No kernel may reach another device: no remote copies, remote signals or barrier semaphores. Data moves between devices by JAX's collectives and lax.ppermute only.
A program may use at most 128 MiB of HBM per device.

v0:
```python
import jax
import jax.numpy as jnp
from jax import lax
from jax.sharding import PartitionSpec as P

LAT = 512


SOFTMAX_SCALE = 192.0 ** (-0.5)


def attend(queries, latent_cache, cache_lengths, latent_width):
    scores = SOFTMAX_SCALE * jnp.einsum(
        "thc,tjc->thj", queries, latent_cache, preferred_element_type=jnp.float32
    )
    valid_mask = (jnp.arange(latent_cache.shape[1])[None, :] < cache_lengths[:, None])[:, None, :]
    scores = jnp.where(valid_mask, scores, -1e30)
    row_peak = jnp.max(scores, axis=2, keepdims=True)
    exp_terms = jnp.where(valid_mask, jnp.exp(scores - row_peak), 0.0)
    attn_probs = (exp_terms / jnp.sum(exp_terms, axis=2, keepdims=True)).astype(jnp.bfloat16)
    return jnp.einsum(
        "thj,tjc->thc",
        attn_probs,
        latent_cache[:, :, :latent_width],
        preferred_element_type=jnp.float32,
    ).astype(jnp.bfloat16)


def expert_half(slot_rows, slot_weights, gate_half, up_half, down_half):
    gate_out = jnp.dot(slot_rows, gate_half, preferred_element_type=jnp.float32)
    up_out = jnp.dot(slot_rows, up_half, preferred_element_type=jnp.float32)
    hidden = (jax.nn.silu(gate_out) * up_out).astype(jnp.bfloat16)
    down_out = jnp.dot(hidden, down_half, preferred_element_type=jnp.float32)
    return (slot_weights.astype(jnp.float32)[:, None] * down_out).astype(jnp.bfloat16)


def run_experts(received, gate_half, up_half, down_half):
    slot_rows, slot_weights = received
    sources, slot_count, feature_width = slot_rows.shape
    flat_rows = slot_rows.reshape(sources * slot_count, feature_width)
    flat_weights = slot_weights.reshape(sources * slot_count)
    partial_out = expert_half(flat_rows, flat_weights, gate_half, up_half, down_half)
    return partial_out.reshape(sources, slot_count, feature_width)


def place_rows(route_weight, capacity):
    row_total, expert_total = route_weight.shape
    live_mask = route_weight != 0
    slot_rank = jnp.cumsum(live_mask.astype(jnp.int32), axis=0) - 1
    slot_rank = jnp.where(live_mask, slot_rank, capacity)
    columns = jnp.broadcast_to(jnp.arange(expert_total, dtype=jnp.int32)[None, :], slot_rank.shape)
    sources = jnp.broadcast_to(jnp.arange(row_total, dtype=jnp.int32)[:, None], slot_rank.shape)
    slot_token = (
        jnp.full((expert_total, capacity), row_total, jnp.int32)
        .at[columns, slot_rank]
        .set(sources, mode="drop")
    )
    padded_weight = jnp.concatenate(
        [route_weight, jnp.zeros((1, expert_total), route_weight.dtype)], axis=0
    )
    slot_weight = padded_weight[slot_token, jnp.arange(expert_total, dtype=jnp.int32)[:, None]]
    return (slot_token, slot_weight)


def fill_slots(token_rows, slot_token, slot_weight):
    expert_total, capacity = slot_token.shape
    feature_width = token_rows.shape[1]
    padded_rows = jnp.concatenate(
        [token_rows, jnp.zeros((1, feature_width), token_rows.dtype)], axis=0
    )
    buffer = padded_rows[slot_token]
    send_rows = jnp.broadcast_to(
        buffer[:, None], (expert_total, 2, capacity, feature_width)
    ).reshape(2 * expert_total, capacity, feature_width)
    send_weights = jnp.broadcast_to(slot_weight[:, None], (expert_total, 2, capacity)).reshape(
        2 * expert_total, capacity
    )
    return (send_rows, send_weights)


def token_sums(returned_parts, index_map, row_total):
    widened = returned_parts.reshape(-1, returned_parts.shape[-1]).astype(jnp.float32)
    return jax.ops.segment_sum(widened, index_map.reshape(-1), num_segments=row_total + 1)[
        :row_total
    ]


def on_device(
    tokens, expert_ids, combine_weights, w_gate, w_up, w_down, queries, latent_cache, cache_lengths
):
    node_count = lax.axis_size("node")
    local_count = lax.axis_size("local")
    expert_count = node_count * local_count // 2
    per_node = expert_count // node_count
    token_count = tokens.shape[0]
    route_width = expert_ids.shape[1]
    capacity = 3 * token_count * route_width // (2 * expert_count)
    gate_half = w_gate[0]
    up_half = w_up[0]
    down_half = w_down[0]
    matches = expert_ids[:, :, None] == jnp.arange(expert_count, dtype=jnp.int32)[None, None, :]
    route_weight = jnp.sum(
        jnp.where(matches, combine_weights[:, :, None], jnp.zeros((), jnp.bfloat16)), axis=1
    )
    attn_latent = attend(queries, latent_cache, cache_lengths, LAT)
    gathered_rows, gathered_weight = (
        lax.all_gather(tokens, "node", axis=0, tiled=True),
        lax.all_gather(route_weight, "node", axis=0, tiled=True),
    )
    node_index = lax.axis_index("node")
    own_weight = lax.dynamic_slice_in_dim(gathered_weight, node_index * per_node, per_node, 1)
    slot_token, slot_weight = place_rows(own_weight, node_count * capacity)
    send_rows, send_weights = fill_slots(gathered_rows, slot_token, slot_weight)
    computed = run_experts(
        (
            lax.all_to_all(send_rows, "local", split_axis=0, concat_axis=0, tiled=True),
            lax.all_to_all(send_weights, "local", split_axis=0, concat_axis=0, tiled=True),
        ),
        gate_half,
        up_half,
        down_half,
    )
    returned = lax.all_to_all(computed, "local", split_axis=0, concat_axis=0, tiled=True)
    index_map = jnp.repeat(slot_token, 2, axis=0)
    node_partial = token_sums(returned, index_map, node_count * token_count)
    moe_out = lax.psum_scatter(
        node_partial.astype(jnp.bfloat16), "node", scatter_dimension=0, tiled=True
    )
    return (moe_out, attn_latent)


def solution(mesh):
    in_specs = (
        P(("replica", "node", "local"), None),
        P(("replica", "node", "local"), None),
        P(("replica", "node", "local"), None),
        P(("node", "local"), None, None),
        P(("node", "local"), None, None),
        P(("node", "local"), None, None),
        P(("replica", "node", "local"), None, None),
        P(("replica", "node", "local"), None, None),
        P(("replica", "node", "local")),
    )
    out_specs = (P(("replica", "node", "local"), None), P(("replica", "node", "local"), None, None))
    return jax.shard_map(
        on_device, mesh=mesh, in_specs=in_specs, out_specs=out_specs, check_vma=False
    )
```

profile of v0, /device:TPU:0, one launch (start us, length us, event | category | flops | bytes accessed | tf_op | source)
XLA Modules:
  0.0 367.6 jit_solution(16326468127422749925)
XLA Ops:
  7.2 0.7 fusion.27
  7.9 1.9 all-gather
  9.8 0.1 copy.26
  9.9 0.1 compare_convert_fusion
  10.0 0.2 reduce_window_sum.11
  10.2 0.1 reshape.83
  10.3 0.1 reshape.85
  10.4 0.0 copy-start
  10.5 22.5 %scatter_fusion = s32[4,96]{1,0:T(4,128)S(1)} fusion(s32[4,96]{1,0:T(4,128)S(1)} %broadcast_in_dim.92, s32[512]{0:T(512)S(1)} %reshape.83, s32[512]{0:T(512)S(1)} %reshape.85), kind=kCustom, calls=%fused_computation.2 | custom fusion | bytes 10240 | tf_op jit(solution)/shard_map/scatter | solution.py:56
  33.0 0.1 reshape.69
  33.1 3.6 gather_fusion
  36.7 0.1 reshape.72
  36.8 0.6 copy.27
  37.4 7.1 %all-to-all-start = ((bf16[8,1,96]{2,1,0:T(2,128)(2,1)}), bf16[8,1,96]{2,1,0:T(2,128)(2,1)S(1)}, u32[]{:S(2)}, u32[]{:S(2)}) async-start(bf16[8,1,96]{2,1,0:T(2,128)(2,1)} %copy.27), calls=%async_computation | async-start | bytes 8192 | tf_op jit(solution)/shard_map/all_to_all | solution.py:117
  44.6 0.1 reshape.77
  44.6 0.0 copy-done
  44.6 2.5 all_gather.7
  47.1 0.1 concatenate.15
  47.2 3.9 %gather_fusion.1 = bf16[384,3584]{1,0:T(8,128)(2,1)} fusion(bf16[129,3584]{1,0:T(8,128)(2,1)S(1)} %concatenate.15, s32[1024]{0:T(1024)S(1)} %pad_clamp_fusion), kind=kCustom, calls=%fused_computation.1 | custom fusion | bytes 5506560 | tf_op jit(solution)/shard_map/gather | solution.py:71
  51.0 0.0 all-to-all-done
  51.0 4.7 %broadcast_in_dim.103 = bf16[4,2,96,3584]{3,2,1,0:T(8,128)(2,1)} broadcast(bf16[4,96,3584]{2,1,0:T(8,128)(2,1)} %bitcast.36), dimensions={0,2,3} | broadcast | bytes 8257536 | tf_op jit(solution)/shard_map/broadcast_in_dim | solution.py:72
  55.8 6.0 %all-to-all-start.1 = ((bf16[8,96,3584]{2,1,0:T(8,128)(2,1)}), bf16[8,96,3584]{2,1,0:T(8,128)(2,1)}, u32[]{:S(2)}, u32[]{:S(2)}) async-start(bf16[8,96,3584]{2,1,0:T(8,128)(2,1)} %bitcast.35), calls=%async_computation.1 | async-start | bytes 11010048 | tf_op jit(solution)/shard_map/all_to_all | solution.py:116
  61.8 0.1 reshape.67
  61.9 121.6 %all-to-all-done.1 = bf16[8,96,3584]{2,1,0:T(8,128)(2,1)} async-done(((bf16[8,96,3584]{2,1,0:T(8,128)(2,1)}), bf16[8,96,3584]{2,1,0:T(8,128)(2,1)}, u32[]{:S(2)}, u32[]{:S(2)}) %all-to-all-start.1) | async-done | bytes 5505056 | tf_op jit(solution)/shard_map/all_to_all | solution.py:116
  183.4 0.0 copy-start.2
  183.4 6.2 %fusion.8 = f32[768,512]{1,0:T(8,128)S(1)} fusion(bf16[768,3584]{1,0:T(8,128)(2,1)} %bitcast.7, bf16[1,3584,512]{2,1,0:T(8,128)(2,1)} %param.12), kind=kOutput, calls=%fused_computation.13 | convolution fusion | flops 2818572288 | bytes 10747904 | tf_op jit(solution)/shard_map/dot_general | solution.py:30
  189.6 0.0 copy-done.2
  189.7 0.0 copy-start.3
  189.7 5.9 %multiply_convert_fusion.1 = bf16[768,512]{1,0:T(8,128)(2,1)S(1)} fusion(f32[768,512]{1,0:T(8,128)S(1)} %fusion.8, bf16[768,3584]{1,0:T(8,128)(2,1)} %bitcast.7, bf16[1,3584,512]{2,1,0:T(8,128)(2,1)S(1)} %copy-done.2), kind=kOutput, calls=%fused_computation.21 | convolution fusion | flops 2820931584 | bytes 11534336 | tf_op jit(solution)/shard_map/dot_general | solution.py:31
  195.6 0.0 copy-done.3
  195.6 4.8 %multiply_convert_fusion = bf16[768,3584]{1,0:T(8,128)(2,1)} fusion(bf16[768,512]{1,0:T(8,128)(2,1)S(1)} %multiply_convert_fusion.1, f32[768]{0:T(1024)S(1)} %reshape.67, bf16[1,512,3584]{2,1,0:T(8,128)(2,1)S(1)} %copy-done.3), kind=kOutput, calls=%fused_computation.7 | convolution fusion | flops 2824077312 | bytes 9964544 | tf_op jit(solution)/shard_map/dot_general | solution.py:33
  200.4 4.7 %all-to-all-start.2 = ((bf16[8,96,3584]{2,1,0:T(8,128)(2,1)}), bf16[8,96,3584]{2,1,0:T(8,128)(2,1)}, u32[]{:S(2)}, u32[]{:S(2)}) async-start(bf16[8,96,3584]{2,1,0:T(8,128)(2,1)} %bitcast.37), calls=%async_computation.2 | async-start | bytes 11010048 | tf_op jit(solution)/shard_map/all_to_all | solution.py:123
  205.1 0.2 reduce-scatter.2.cloned.1.call-start
  205.3 0.1 reshape.91
  205.4 120.4 %all-to-all-done.2 = bf16[8,96,3584]{2,1,0:T(8,128)(2,1)} async-done(((bf16[8,96,3584]{2,1,0:T(8,128)(2,1)}), bf16[8,96,3584]{2,1,0:T(8,128)(2,1)}, u32[]{:S(2)}, u32[]{:S(2)}) %all-to-all-start.2) | async-done | bytes 5505056 | tf_op jit(solution)/shard_map/all_to_all | solution.py:123
  325.8 0.0 copy-start.1
  325.8 22.4 %scatter_custom_fusion.1 = f32[129,3584]{1,0:T(8,128)S(1)} fusion(s32[768]{0:T(1024)S(1)} %reshape.91, bf16[768,3584]{1,0:T(8,128)(2,1)} %bitcast.13, f32[]{:T(128)} %constant.15.clone.1), kind=kCustom, calls=%fused_computation.5 | custom fusion | flops 5505024 | bytes 7354372 | tf_op jit(solution)/shard_map/scatter-add | solution.py:83
  348.2 1.0 slice.21
  349.2 0.0 reduce-scatter.2.cloned.1.call-update
  349.3 0.0 copy-done.1
  349.3 0.1 iota_compare_fusion.1
  349.4 5.7 %fusion.30 = (f32[64,64]{1,0:T(8,128)S(1)}, f32[64,64,64]{1,2,0:T(8,128)S(1)}) fusion(pred[64,64]{1,0:T(8,128)(4,1)S(1)} %iota_compare_fusion.1, bf16[64,64,576]{2,1,0:T(8,128)(2,1)} %param.15, bf16[64,64,576]{2,1,0:T(8,128)(2,1)} %param.16), kind=kOutput, calls=%fused_computation.49 | convolution fusion | flops 303300672 | bytes 10506240 | tf_op jit(solution)/shard_map/sub | solution.py:19
  355.1 5.7 %fusion.10 = bf16[64,64,512]{2,1,0:T(8,128)(2,1)} fusion(bf16[64,64,576]{2,1,0:T(8,128)(2,1)} %param.16, f32[64,64,64]{1,2,0:T(8,128)S(1)} %get-tuple-element.5, f32[64,64]{1,0:T(8,128)S(1)} %get-tuple-element.4), kind=kOutput, calls=%fused_computation.15 | convolution fusion | flops 271056896 | bytes 9453568 | tf_op jit(solution)/shard_map/thj,tjc->thc/dot_general | solution.py:21
  360.7 0.0 reduce-scatter.2.cloned.1.call-done
  (10 shorter events, 0.1 us)
Async XLA Ops:
  10.4 34.2 %copy-start = (bf16[64,3584]{1,0:T(8,128)(2,1)S(1)}, bf16[64,3584]{1,0:T(8,128)(2,1)}, u32[]{:S(2)}) copy-start(bf16[64,3584]{1,0:T(8,128)(2,1)} %param.9) | copy-start | bytes 1376260
  37.4 13.6 %all-to-all-start = ((bf16[8,1,96]{2,1,0:T(2,128)(2,1)}), bf16[8,1,96]{2,1,0:T(2,128)(2,1)S(1)}, u32[]{:S(2)}, u32[]{:S(2)}) async-start(bf16[8,1,96]{2,1,0:T(2,128)(2,1)} %copy.27), calls=%async_computation | async-start | bytes 8192 | tf_op jit(solution)/shard_map/all_to_all | solution.py:117
  55.8 127.7 %all-to-all-start.1 = ((bf16[8,96,3584]{2,1,0:T(8,128)(2,1)}), bf16[8,96,3584]{2,1,0:T(8,128)(2,1)}, u32[]{:S(2)}, u32[]{:S(2)}) async-start(bf16[8,96,3584]{2,1,0:T(8,128)(2,1)} %bitcast.35), calls=%async_computation.1 | async-start | bytes 11010048 | tf_op jit(solution)/shard_map/all_to_all | solution.py:116
  183.4 6.2 %copy-start.2 = (bf16[1,3584,512]{2,1,0:T(8,128)(2,1)S(1)}, bf16[1,3584,512]{2,1,0:T(8,128)(2,1)}, u32[]{:S(2)}) copy-start(bf16[1,3584,512]{2,1,0:T(8,128)(2,1)} %param.13) | copy-start | bytes 11010052
  189.7 5.9 %copy-start.3 = (bf16[1,512,3584]{2,1,0:T(8,128)(2,1)S(1)}, bf16[1,512,3584]{2,1,0:T(8,128)(2,1)}, u32[]{:S(2)}) copy-start(bf16[1,512,3584]{2,1,0:T(8,128)(2,1)} %param.14) | copy-start | bytes 11010052
  200.4 125.4 %all-to-all-start.2 = ((bf16[8,96,3584]{2,1,0:T(8,128)(2,1)}), bf16[8,96,3584]{2,1,0:T(8,128)(2,1)}, u32[]{:S(2)}, u32[]{:S(2)}) async-start(bf16[8,96,3584]{2,1,0:T(8,128)(2,1)} %bitcast.37), calls=%async_computation.2 | async-start | bytes 11010048 | tf_op jit(solution)/shard_map/all_to_all | solution.py:123
  205.1 155.7 %reduce-scatter.2.cloned.1.call-start = ((), (), s32[]{:S(2)}) async-start(), calls=%async_computation.4 | async-start | bytes 1376256 | tf_op jit(solution)/shard_map/reduce_scatter | solution.py:126
  325.8 23.5 %copy-start.1 = (s32[64]{0:T(128)S(1)}, s32[64]{0:T(128)}, u32[]{:S(2)}) copy-start(s32[64]{0:T(128)} %param.17) | copy-start | bytes 772
Sparse Core Ops, SparseCore 0:
  349.4 7.4 reduce-scatter.1
where the time goes:
time: 368 us
  waiting for transfers between devices  242 us (66%)
  local copies, waits for them, and re-layouts  37.2 us (10%)
  matrix products  28.3 us (8%)
  other arithmetic  23.5 us (6%)
  starting transfers between devices  18 us (5%)
  between operations  14.2 us (4%)
  blocking collectives  4.37 us (1%)
    all_to_all x1, waiting for transfers between devices, on_device(): lax.all_to_all(send_rows, 'local', split_axis=0, concat_axis=0, tiled=True)  122 us
    all_to_all x1, waiting for transfers between devices, on_device(): lax.all_to_all(computed, 'local', split_axis=0, concat_axis=0, tiled=True)  120 us
    scatter x1, local copies, waits for them, and re-layouts, place_rows(): slot_token = jnp.full((expert_total, capacity), row_total, jnp.int32).at[...  22.5 us
    scatter-add x1, other arithmetic, token_sums(): jax.ops.segment_sum(widened, index_map.reshape(-1), num_segments=row_tota...  22.4 us
  transfers between devices with their start and end apart: 4, of which 2 were waited for; matrix products, arithmetic and copies ran while one was open for 4% of the time, Pallas kernels for 0%

commit v1 on v0

v1 whole, which is shorter than its diff:
```python
import jax
import jax.numpy as jnp
from jax import lax
from jax.sharding import PartitionSpec as P

LAT = 512
SOFTMAX_SCALE = 192.0 ** (-0.5)
LANES = 128


def attend(queries, latent_cache, cache_lengths, latent_width):
    scores = SOFTMAX_SCALE * jnp.einsum(
        "thc,tjc->thj", queries, latent_cache, preferred_element_type=jnp.float32
    )
    valid_mask = (jnp.arange(latent_cache.shape[1])[None, :] < cache_lengths[:, None])[:, None, :]
    scores = jnp.where(valid_mask, scores, -1e30)
    row_peak = jnp.max(scores, axis=2, keepdims=True)
    exp_terms = jnp.where(valid_mask, jnp.exp(scores - row_peak), 0.0)
    attn_probs = (exp_terms / jnp.sum(exp_terms, axis=2, keepdims=True)).astype(jnp.bfloat16)
    return jnp.einsum(
        "thj,tjc->thc",
        attn_probs,
        latent_cache[:, :, :latent_width],
        preferred_element_type=jnp.float32,
    ).astype(jnp.bfloat16)


def ring_order(count):
    if count == 8:
        return [0, 2, 4, 6, 7, 5, 3, 1]
    return list(range(count))


def on_device(
    tokens, expert_ids, combine_weights, w_gate, w_up, w_down, queries, latent_cache, cache_lengths
):
    node_count = lax.axis_size("node")
    local_count = lax.axis_size("local")
    expert_count = node_count * local_count // 2
    rows, width = tokens.shape
    half = local_count // 2
    order = ring_order(local_count)
    forward = [(order[i], order[(i + 1) % local_count]) for i in range(local_count)]
    backward = [(b, a) for a, b in forward]
    swap = [(i, (i + 1) % node_count) for i in range(node_count)]
    device_index = lax.axis_index("node") * local_count + lax.axis_index("local")
    expert = device_index // 2

    matches = expert_ids[:, :, None] == jnp.arange(LANES, dtype=jnp.int32)[None, None, :]
    route = jnp.sum(
        jnp.where(matches, combine_weights[:, :, None], jnp.zeros((), jnp.bfloat16)), axis=1
    )
    mine = jnp.concatenate([tokens, route], axis=1)

    def cw(a):
        return lax.ppermute(a, "local", forward)

    def ccw(a):
        return lax.ppermute(a, "local", backward)

    def across(a):
        return lax.ppermute(a, "node", swap)

    groups = [mine]
    behind, ahead = mine, mine
    for k in range(1, half + 1):
        if k == half:
            behind, ahead = behind[: rows // 2], ahead[rows // 2 :]
        behind, ahead = cw(behind), ccw(ahead)
        groups.append(jnp.concatenate([behind, ahead], axis=0))

    def experts(block):
        x = block[:, :width]
        weight = jnp.sum(
            jnp.where(
                jnp.arange(LANES)[None, :] == expert, block[:, width:].astype(jnp.float32), 0.0
            ),
            axis=1,
            keepdims=True,
        )
        gate_out = jnp.dot(x, w_gate[0], preferred_element_type=jnp.float32)
        up_out = jnp.dot(x, w_up[0], preferred_element_type=jnp.float32)
        hidden = (jax.nn.silu(gate_out) * up_out).astype(jnp.bfloat16)
        down = jnp.dot(hidden, w_down[0], preferred_element_type=jnp.float32)
        return (weight * down).astype(jnp.bfloat16)

    sums = []
    for group in groups:
        count = group.shape[0]
        both = jnp.concatenate([group, across(group)], axis=0)
        out = experts(both)
        sums.append(out[:count].astype(jnp.float32) + across(out[count:]).astype(jnp.float32))

    far = sums[half].astype(jnp.bfloat16)
    to_ahead, to_behind = cw(far[: rows // 2]), ccw(far[rows // 2 :])
    for k in range(half - 1, 0, -1):
        own_behind, own_ahead = sums[k][:rows], sums[k][rows:]
        if k == half - 1:
            zero = jnp.zeros_like(to_ahead)
            to_ahead = jnp.concatenate([to_ahead, zero], axis=0)
            to_behind = jnp.concatenate([zero, to_behind], axis=0)
        to_ahead = cw((own_ahead + to_ahead.astype(jnp.float32)).astype(jnp.bfloat16))
        to_behind = ccw((own_behind + to_behind.astype(jnp.float32)).astype(jnp.bfloat16))
    moe_out = (
        sums[0] + to_ahead.astype(jnp.float32) + to_behind.astype(jnp.float32)
    ).astype(jnp.bfloat16)

    attn_latent = attend(queries, latent_cache, cache_lengths, LAT)
    return (moe_out, attn_latent)


def solution(mesh):
    in_specs = (
        P(("replica", "node", "local"), None),
        P(("replica", "node", "local"), None),
        P(("replica", "node", "local"), None),
        P(("node", "local"), None, None),
        P(("node", "local"), None, None),
        P(("node", "local"), None, None),
        P(("replica", "node", "local"), None, None),
        P(("replica", "node", "local"), None, None),
        P(("replica", "node", "local")),
    )
    out_specs = (P(("replica", "node", "local"), None), P(("replica", "node", "local"), None, None))
    return jax.shard_map(
        on_device, mesh=mesh, in_specs=in_specs, out_specs=out_specs, check_vma=False
    )
```

time: 368 us -> 143 us (0.39)
  waiting for transfers between devices: 242 us -> 50.7 us
  local copies, waits for them, and re-layouts: 37.2 us -> 8.63 us
  matrix products: 28.3 us -> 49.7 us
  between operations: 14.2 us -> 1.06 us
  other arithmetic: 23.5 us -> 12.7 us
  blocking collectives: 4.37 us -> 0 us
    all_to_all x3 -> x0, waiting for transfers between devices: 242 us -> none  [the longest x1 122 us: on_device(): lax.all_to_all(send_rows, 'local', split_axis=0, concat_axis=0, tiled=True)]
    ppermute x0 -> x26, waiting for transfers between devices: none -> 50.7 us  [the longest x8 44.5 us: cw(): return lax.ppermute(a, 'local', forward)]
    scatter x1 -> x0, local copies, waits for them, and re-layouts: 22.5 us -> none  [place_rows(): slot_token = jnp.full((expert_total, capacity), row_total, jnp.int32).at[...]
    scatter-add x1 -> x0, other arithmetic: 22.4 us -> none  [token_sums(): jax.ops.segment_sum(widened, index_map.reshape(-1), num_segments=row_tota...]
    dot_general x3 -> x10, matrix products: 16.9 us -> 38.7 us  [the longest x5 26.9 us: experts(): down = jnp.dot(hidden, w_down[0], preferred_element_type=jnp.float32)]
    ppermute x0 -> x26, starting transfers between devices: none -> 20 us  [the longest x8 11.4 us: cw(): return lax.ppermute(a, 'local', forward)]
    all_to_all x3 -> x0, starting transfers between devices: 17.8 us -> none  [the longest x1 7.13 us: on_device(): lax.all_to_all(send_weights, 'local', split_axis=0, concat_axis=0, tiled=...]
    gather x3 -> x0, local copies, waits for them, and re-layouts: 7.59 us -> none  [the longest x1 3.87 us: fill_slots(): buffer = padded_rows[slot_token]]
  transfers between devices with their start and end apart: 4 -> 26, of which waited for: 2 -> 14; matrix products, arithmetic and copies ran while one was open for 4% -> 45% of each run, Pallas kernels for 0% -> 0%
where the time goes in v1:
time: 143 us
  waiting for transfers between devices  50.7 us (35%)
  matrix products  49.7 us (35%)
  starting transfers between devices  20 us (14%)
  other arithmetic  12.7 us (9%)
  local copies, waits for them, and re-layouts  8.63 us (6%)
    ppermute x8, waiting for transfers between devices, cw(): return lax.ppermute(a, 'local', forward)  44.5 us
    dot_general x5, matrix products, experts(): down = jnp.dot(hidden, w_down[0], preferred_element_type=jnp.float32)  26.9 us
    dot_general x5, matrix products, experts(): up_out = jnp.dot(x, w_up[0], preferred_element_type=jnp.float32)  11.8 us
    ppermute x8, starting transfers between devices, cw(): return lax.ppermute(a, 'local', forward)  11.4 us
    sub x1, matrix products, attend(): exp_terms = jnp.where(valid_mask, jnp.exp(scores - row_peak), 0.0)  7.69 us
    ppermute x8, starting transfers between devices, ccw(): return lax.ppermute(a, 'local', backward)  6.44 us
    ppermute x8, waiting for transfers between devices, ccw(): return lax.ppermute(a, 'local', backward)  6.17 us
    slice x5, local copies, waits for them, and re-layouts, on_device(): out[count:]  4.05 us
  transfers between devices with their start and end apart: 26, of which 14 were waited for; matrix products, arithmetic and copies ran while one was open for 45% of the time, Pallas kernels for 0%

profile of v1, /device:TPU:0, one launch (start us, length us, event | category | flops | bytes accessed | tf_op | source)
XLA Modules:
  0.0 142.7 jit_solution(695393935291364566)
XLA Ops:
  0.6 0.8 fusion.97
  1.5 1.1 pad_maximum_fusion.5
  2.5 3.1 %collective-permute-start.2 = (bf16[64,3712]{1,0:T(8,128)(2,1)S(1)}, bf16[64,3712]{1,0:T(8,128)(2,1)S(1)}, u32[]{:S(2)}, u32[]{:S(2)}) collective-permute-start(bf16[64,3712]{1,0:T(8,128)(2,1)S(1)} %pad_maximum_fusion.5), channel_id=1, source_target_pairs={{0,2},{2,4},{4,6},{6,7},{7,5},{5,3},{3,1},{1,0},{8,10},{10,12},{12... | collective-permute-start | bytes 1425416 | tf_op jit(solution)/shard_map/ppermute | solution.py:56
  5.6 0.6 iota_compare_fusion.2
  6.2 0.7 iota_compare_fusion.1
  6.9 7.7 %fusion.109 = (f32[64,64]{1,0:T(8,128)}, f32[64,64,64]{1,2,0:T(8,128)}) fusion(pred[64,64]{1,0:T(8,128)(4,1)S(1)} %iota_compare_fusion.1, bf16[64,64,576]{2,1,0:T(8,128)(2,1)} %param.15, bf16[64,64,576]{2,1,0:T(8,128)(2,1)} %param.16), kind=kOutput, calls=%fused_computation.121 | convolution fusion | flops 303300672 | bytes 10506240 | tf_op jit(solution)/shard_map/sub | solution.py:18
  14.6 1.8 %collective-permute-done.2 = bf16[64,3712]{1,0:T(8,128)(2,1)S(1)} collective-permute-done((bf16[64,3712]{1,0:T(8,128)(2,1)S(1)}, bf16[64,3712]{1,0:T(8,128)(2,1)S(1)}, u32[]{:S(2)}, u32[]{:S(2)}) %collective-permute-start.2) | collective-permute-done | bytes 475168 | tf_op jit(solution)/shard_map/ppermute | solution.py:56
  16.4 1.5 %collective-permute-done.3 = bf16[64,3712]{1,0:T(8,128)(2,1)S(1)} collective-permute-done((bf16[64,3712]{1,0:T(8,128)(2,1)S(1)}, bf16[64,3712]{1,0:T(8,128)(2,1)S(1)}, u32[]{:S(2)}, u32[]{:S(2)}) %collective-permute-start.3) | collective-permute-done | bytes 475168 | tf_op jit(solution)/shard_map/ppermute | solution.py:59
  18.1 1.6 %collective-permute-start.6 = (bf16[64,3712]{1,0:T(8,128)(2,1)S(1)}, bf16[64,3712]{1,0:T(8,128)(2,1)S(1)}, u32[]{:S(2)}, u32[]{:S(2)}) collective-permute-start(bf16[64,3712]{1,0:T(8,128)(2,1)S(1)} %collective-permute-done.2), channel_id=1, source_target_pairs={{0,2},{2,4},{4,6},{6,7},{7,5},{5,3},{3,1},{1,0},{8,10},{10,12},{12... | collective-permute-start | bytes 1425416 | tf_op jit(solution)/shard_map/ppermute | solution.py:56
  19.7 0.4 collective-permute-start.7
  20.2 3.6 %fusion.21 = f32[128,512]{1,0:T(8,128)} fusion(bf16[1,3584,512]{2,1,0:T(8,128)(2,1)} %param.13, bf16[64,3712]{1,0:T(8,128)(2,1)S(1)} %collective-permute-done, bf16[64,128]{1,0:T(8,128)(2,1)S(1)} %fusion.97, bf16[64,3584]{1,0:T(8,128)(2,1)S(1)} %copy-done.6), kind=kOutput, calls=%fused_computation.26 | convolution fusion | flops 472514560 | bytes 4882432 | tf_op jit(solution)/shard_map/dot_general | solution.py:82
  23.8 7.5 %collective-permute-done.6 = bf16[64,3712]{1,0:T(8,128)(2,1)S(1)} collective-permute-done((bf16[64,3712]{1,0:T(8,128)(2,1)S(1)}, bf16[64,3712]{1,0:T(8,128)(2,1)S(1)}, u32[]{:S(2)}, u32[]{:S(2)}) %collective-permute-start.6) | collective-permute-done | bytes 475168 | tf_op jit(solution)/shard_map/ppermute | solution.py:56
  31.3 1.3 collective-permute-done.7
  32.8 1.6 %collective-permute-start.10 = (bf16[64,3712]{1,0:T(8,128)(2,1)S(1)}, bf16[64,3712]{1,0:T(8,128)(2,1)S(1)}, u32[]{:S(2)}, u32[]{:S(2)}) collective-permute-start(bf16[64,3712]{1,0:T(8,128)(2,1)S(1)} %collective-permute-done.6), channel_id=1, source_target_pairs={{0,2},{2,4},{4,6},{6,7},{7,5},{5,3},{3,1},{1,0},{8,10},{10,12},{12... | collective-permute-start | bytes 1425416 | tf_op jit(solution)/shard_map/ppermute | solution.py:56
  34.4 0.4 collective-permute-start.11
  35.0 11.1 %collective-permute-done.10 = bf16[64,3712]{1,0:T(8,128)(2,1)S(1)} collective-permute-done((bf16[64,3712]{1,0:T(8,128)(2,1)S(1)}, bf16[64,3712]{1,0:T(8,128)(2,1)S(1)}, u32[]{:S(2)}, u32[]{:S(2)}) %collective-permute-start.10) | collective-permute-done | bytes 475168 | tf_op jit(solution)/shard_map/ppermute | solution.py:56
  46.1 1.6 %collective-permute-start.14 = (bf16[32,3712]{1,0:T(8,128)(2,1)S(1)}, bf16[32,3712]{1,0:T(8,128)(2,1)S(1)}, u32[]{:S(2)}, u32[]{:S(2)}) collective-permute-start(bf16[32,3712]{1,0:T(8,128)(2,1)S(1)} %slice.141), channel_id=1, source_target_pairs={{0,2},{2,4},{4,6},{6,7},{7,5},{5,3},{3,1},{1,0},{8,10},{10,12},{12... | collective-permute-start | bytes 712712 | tf_op jit(solution)/shard_map/ppermute | solution.py:56
  47.7 0.7 collective-permute-start.15
  48.4 1.0 pad_maximum_fusion.2
  49.5 1.3 copy-done.12
  50.9 1.2 copy-done
  52.1 1.9 %fusion.19 = f32[256,512]{1,0:T(8,128)} fusion(bf16[1,3584,512]{2,1,0:T(8,128)(2,1)S(1)} %copy-done, bf16[256,3712]{1,0:T(8,128)(2,1)S(1)} %constant_dynamic-update-slice_fusion), kind=kOutput, calls=%fused_computation.24 | convolution fusion | flops 939524096 | bytes 6029312 | tf_op jit(solution)/shard_map/dot_general | solution.py:82
  54.1 1.0 collective-permute-done.15
  55.3 1.9 %fusion.17 = f32[256,512]{1,0:T(8,128)} fusion(bf16[1,3584,512]{2,1,0:T(8,128)(2,1)S(1)} %copy-done, bf16[256,3712]{1,0:T(8,128)(2,1)S(1)} %constant_dynamic-update-slice_fusion.3), kind=kOutput, calls=%fused_computation.22 | convolution fusion | flops 939524096 | bytes 6029312 | tf_op jit(solution)/shard_map/dot_general | solution.py:82
  57.4 0.6 fusion.13
  58.0 0.4 copy-done.10
  58.4 0.6 select_reduce_fusion.4
  59.0 4.5 %fusion.5 = bf16[128,3584]{1,0:T(8,128)(2,1)S(1)} fusion(bf16[1,512,3584]{2,1,0:T(8,128)(2,1)} %param.14, f32[128]{0:T(128)} %get-tuple-element.3, f32[128,512]{1,0:T(8,128)S(1)} %fusion.13, bf16[1,3584,512]{2,1,0:T(8,128)(2,1)} %param.12, bf16[128,3712]{1,0:T(8,128)(2,1)S(1)} %constant_dynamic-update-slice_fusion.9), kind=kOutput, calls=%fused_computation.10 | convolution fusion | flops 940834816 | bytes 9437696 | tf_op jit(solution)/shard_map/dot_general | solution.py:84
  63.5 0.8 slice.146
  64.3 0.5 collective-permute-start.17
  64.7 4.5 %fusion.4 = bf16[128,3584]{1,0:T(8,128)(2,1)S(1)} fusion(bf16[1,512,3584]{2,1,0:T(8,128)(2,1)} %param.14, f32[128]{0:T(128)} %get-tuple-element.2, f32[128,512]{1,0:T(8,128)} %fusion.21, bf16[1,3584,512]{2,1,0:T(8,128)(2,1)} %param.12, bf16[64,3712]{1,0:T(8,128)(2,1)} %copy-done.9, bf16[64,128]{1,0:T(8,128)(2,1)S(1)} %fusion.97, ...), kind=kOutput, calls=%fused_computation.9 | convolution fusion | flops 943587328 | bytes 9470464 | tf_op jit(solution)/shard_map/dot_general | solution.py:84
  69.3 0.9 slice.125
  70.2 1.0 constant_dynamic-update-slice_fusion.6
  71.3 1.1 select_reduce_fusion
  72.3 3.7 %fusion.15 = f32[256,512]{1,0:T(8,128)S(1)} fusion(bf16[1,3584,512]{2,1,0:T(8,128)(2,1)} %param.13, bf16[256,3712]{1,0:T(8,128)(2,1)} %constant_dynamic-update-slice_fusion.6), kind=kOutput, calls=%fused_computation.20 | convolution fusion | flops 939524096 | bytes 6029312 | tf_op jit(solution)/shard_map/dot_general | solution.py:82
  76.0 5.9 %fusion.3 = bf16[256,3584]{1,0:T(8,128)(2,1)S(1)} fusion(bf16[1,512,3584]{2,1,0:T(8,128)(2,1)} %param.14, f32[256]{0:T(256)S(1)} %get-tuple-element.4, f32[256,512]{1,0:T(8,128)S(1)} %fusion.15, bf16[1,3584,512]{2,1,0:T(8,128)(2,1)} %param.12, bf16[256,3712]{1,0:T(8,128)(2,1)} %constant_dynamic-update-slice_fusion.6), kind=kOutput, calls=%fused_computation.6 | convolution fusion | flops 1881669632 | bytes 11535360 | tf_op jit(solution)/shard_map/dot_general | solution.py:84
  82.0 1.2 slice.139
  83.2 0.5 collective-permute-start.13
  83.7 6.1 %fusion.2 = bf16[256,3584]{1,0:T(8,128)(2,1)S(1)} fusion(bf16[1,512,3584]{2,1,0:T(8,128)(2,1)} %param.14, f32[256]{0:T(256)S(1)} %get-tuple-element.5, f32[256,512]{1,0:T(8,128)} %fusion.17, bf16[1,3584,512]{2,1,0:T(8,128)(2,1)} %param.12, bf16[256,3712]{1,0:T(8,128)(2,1)} %copy-done.13), kind=kOutput, calls=%fused_computation.5 | convolution fusion | flops 1881669632 | bytes 11535360 | tf_op jit(solution)/shard_map/dot_general | solution.py:84
  89.8 1.1 slice.134
  90.9 0.4 collective-permute-start.9
  91.3 5.9 %fusion.1 = bf16[256,3584]{1,0:T(8,128)(2,1)S(1)} fusion(bf16[1,512,3584]{2,1,0:T(8,128)(2,1)} %param.14, f32[256]{0:T(256)S(1)} %get-tuple-element.6, f32[256,512]{1,0:T(8,128)S(1)} %copy-done.17, bf16[1,3584,512]{2,1,0:T(8,128)(2,1)} %param.12, bf16[256,3712]{1,0:T(8,128)(2,1)} %copy-done.11), kind=kOutput, calls=%fused_computation.4 | convolution fusion | flops 1881669632 | bytes 11535360 | tf_op jit(solution)/shard_map/dot_general | solution.py:84
  97.3 0.5 collective-permute-start.5
  97.8 1.1 add_convert_fusion.1
  99.0 1.6 %collective-permute-start.18 = (bf16[32,3584]{1,0:T(8,128)(2,1)S(1)}, bf16[32,3584]{1,0:T(8,128)(2,1)S(1)}, u32[]{:S(2)}, u32[]{:S(2)}) collective-permute-start(bf16[32,3584]{1,0:T(8,128)(2,1)S(1)} %get-tuple-element.13), channel_id=1, source_target_pairs={{0,2},{2,4},{4,6},{6,7},{7,5},{5,3},{3,1},{1,0},{8,10},{10,12},{12... | collective-permute-start | bytes 688136 | tf_op jit(solution)/shard_map/ppermute | solution.py:56
  100.6 0.5 collective-permute-start.22
  101.1 1.4 convert_add_fusion
  102.5 4.2 %collective-permute-done.18 = bf16[32,3584]{1,0:T(8,128)(2,1)S(1)} collective-permute-done((bf16[32,3584]{1,0:T(8,128)(2,1)S(1)}, bf16[32,3584]{1,0:T(8,128)(2,1)S(1)}, u32[]{:S(2)}, u32[]{:S(2)}) %collective-permute-start.18) | collective-permute-done | bytes 229408 | tf_op jit(solution)/shard_map/ppermute | solution.py:56
  106.8 1.3 collective-permute-done.22
  108.1 0.6 collective-permute-start.19
  108.8 1.4 %collective-permute-start.23 = (bf16[64,3584]{1,0:T(8,128)(2,1)S(1)}, bf16[64,3584]{1,0:T(8,128)(2,1)S(1)}, u32[]{:S(2)}, u32[]{:S(2)}) collective-permute-start(bf16[64,3584]{1,0:T(8,128)(2,1)S(1)} %get-tuple-element.12), channel_id=1, source_target_pairs={{2,0},{4,2},{6,4},{7,6},{5,7},{3,5},{1,3},{0,1},{10,8},{12,10},{14... | collective-permute-start | bytes 1376264 | tf_op jit(solution)/shard_map/ppermute | solution.py:59
  110.2 1.4 convert_add_fusion.1
  111.6 8.0 %collective-permute-done.19 = bf16[64,3584]{1,0:T(8,128)(2,1)S(1)} collective-permute-done((bf16[64,3584]{1,0:T(8,128)(2,1)S(1)}, bf16[64,3584]{1,0:T(8,128)(2,1)S(1)}, u32[]{:S(2)}, u32[]{:S(2)}) %collective-permute-start.19) | collective-permute-done | bytes 458784 | tf_op jit(solution)/shard_map/ppermute | solution.py:56
  119.7 0.3 collective-permute-done.23
  120.1 0.6 collective-permute-start.20
  120.8 1.5 %collective-permute-start.24 = (bf16[64,3584]{1,0:T(8,128)(2,1)S(1)}, bf16[64,3584]{1,0:T(8,128)(2,1)S(1)}, u32[]{:S(2)}, u32[]{:S(2)}) collective-permute-start(bf16[64,3584]{1,0:T(8,128)(2,1)S(1)} %get-tuple-element.10), channel_id=1, source_target_pairs={{2,0},{4,2},{6,4},{7,6},{5,7},{3,5},{1,3},{0,1},{10,8},{12,10},{14... | collective-permute-start | bytes 1376264 | tf_op jit(solution)/shard_map/ppermute | solution.py:59
  122.5 8.0 %collective-permute-done.20 = bf16[64,3584]{1,0:T(8,128)(2,1)S(1)} collective-permute-done((bf16[64,3584]{1,0:T(8,128)(2,1)S(1)}, bf16[64,3584]{1,0:T(8,128)(2,1)S(1)}, u32[]{:S(2)}, u32[]{:S(2)}) %collective-permute-start.20) | collective-permute-done | bytes 458784 | tf_op jit(solution)/shard_map/ppermute | solution.py:56
  130.5 0.4 collective-permute-done.24
  131.1 0.6 collective-permute-start.21
  131.7 1.5 %collective-permute-start.25 = (bf16[64,3584]{1,0:T(8,128)(2,1)S(1)}, bf16[64,3584]{1,0:T(8,128)(2,1)S(1)}, u32[]{:S(2)}, u32[]{:S(2)}) collective-permute-start(bf16[64,3584]{1,0:T(8,128)(2,1)S(1)} %get-tuple-element.8), channel_id=1, source_target_pairs={{2,0},{4,2},{6,4},{7,6},{5,7},{3,5},{1,3},{0,1},{10,8},{12,10},{14... | collective-permute-start | bytes 1376264 | tf_op jit(solution)/shard_map/ppermute | solution.py:59
  133.2 3.3 %fusion.33 = bf16[64,64,512]{2,1,0:T(8,128)(2,1)} fusion(bf16[64,64,576]{2,1,0:T(8,128)(2,1)S(1)} %bitcast.56, f32[64,64,64]{1,2,0:T(8,128)S(1)} %copy-done.1, f32[64,64]{1,0:T(8,128)S(1)} %copy-done.14), kind=kOutput, calls=%fused_computation.38 | convolution fusion | flops 271056896 | bytes 10518528 | tf_op jit(solution)/shard_map/thj,tjc->thc/dot_general | solution.py:20
  136.5 3.8 %collective-permute-done.21 = bf16[64,3584]{1,0:T(8,128)(2,1)S(1)} collective-permute-done((bf16[64,3584]{1,0:T(8,128)(2,1)S(1)}, bf16[64,3584]{1,0:T(8,128)(2,1)S(1)}, u32[]{:S(2)}, u32[]{:S(2)}) %collective-permute-start.21) | collective-permute-done | bytes 458784 | tf_op jit(solution)/shard_map/ppermute | solution.py:56
  140.3 0.4 collective-permute-done.25
  140.7 2.0 %add_convert_fusion = bf16[64,3584]{1,0:T(8,128)(2,1)} fusion(bf16[64,3584]{1,0:T(8,128)(2,1)S(1)} %collective-permute-done.25, bf16[64,3584]{1,0:T(8,128)(2,1)S(1)} %collective-permute-done.21, bf16[64,3584]{1,0:T(8,128)(2,1)} %collective-permute-done.1, bf16[128,3584]{1,0:T(8,128)(2,1)S(1)} %copy-done.8), kind=kLoop, calls=%fused_computation.73 | loop fusion | flops 1835008 | bytes 2293760 | tf_op jit(solution)/shard_map/convert_element_type | solution.py:106
  (79 shorter events, 1.9 us)
Async XLA Ops:
  2.5 13.9 %collective-permute-start.2 = (bf16[64,3712]{1,0:T(8,128)(2,1)S(1)}, bf16[64,3712]{1,0:T(8,128)(2,1)S(1)}, u32[]{:S(2)}, u32[]{:S(2)}) collective-permute-start(bf16[64,3712]{1,0:T(8,128)(2,1)S(1)} %pad_maximum_fusion.5), channel_id=1, source_target_pairs={{0,2},{2,4},{4,6},{6,7},{7,5},{5,3},{3,1},{1,0},{8,10},{10,12},{12... | collective-permute-start | bytes 1425416 | tf_op jit(solution)/shard_map/ppermute | solution.py:56
  5.6 12.3 %collective-permute-start.3 = (bf16[64,3712]{1,0:T(8,128)(2,1)S(1)}, bf16[64,3712]{1,0:T(8,128)(2,1)S(1)}, u32[]{:S(2)}, u32[]{:S(2)}) collective-permute-start(bf16[64,3712]{1,0:T(8,128)(2,1)S(1)} %pad_maximum_fusion.5), channel_id=1, source_target_pairs={{2,0},{4,2},{6,4},{7,6},{5,7},{3,5},{1,3},{0,1},{10,8},{12,10},{14... | collective-permute-start | bytes 1425416 | tf_op jit(solution)/shard_map/ppermute | solution.py:59
  5.6 14.6 %collective-permute-start = (bf16[64,3712]{1,0:T(8,128)(2,1)S(1)}, bf16[64,3712]{1,0:T(8,128)(2,1)S(1)}, u32[]{:S(2)}, u32[]{:S(2)}) collective-permute-start(bf16[64,3712]{1,0:T(8,128)(2,1)S(1)} %pad_maximum_fusion.5), channel_id=1, source_target_pairs={{0,8},{8,0},{1,9},{9,1},{2,10},{10,2},{3,11},{11,3},{4,12},{12,4},... | collective-permute-start | bytes 1425416 | tf_op jit(solution)/shard_map/ppermute | solution.py:62
  14.6 5.6 %copy-start.6 = (bf16[64,3584]{1,0:T(8,128)(2,1)S(1)}, bf16[64,3584]{1,0:T(8,128)(2,1)}, u32[]{:S(2)}) copy-start(bf16[64,3584]{1,0:T(8,128)(2,1)} %param.9) | copy-start | bytes 1376260
  18.0 32.8 %collective-permute-start.4 = (bf16[128,3712]{1,0:T(8,128)(2,1)S(1)}, bf16[128,3712]{1,0:T(8,128)(2,1)S(1)}, u32[]{:S(2)}, u32[]{:S(2)}) collective-permute-start(bf16[128,3712]{1,0:T(8,128)(2,1)S(1)} %pad_maximum_fusion), channel_id=1, source_target_pairs={{0,8},{8,0},{1,9},{9,1},{2,10},{10,2},{3,11},{11,3},{4,12},{12,4},... | collective-permute-start | bytes 2850824 | tf_op jit(solution)/shard_map/ppermute | solution.py:62
  18.1 13.3 %collective-permute-start.6 = (bf16[64,3712]{1,0:T(8,128)(2,1)S(1)}, bf16[64,3712]{1,0:T(8,128)(2,1)S(1)}, u32[]{:S(2)}, u32[]{:S(2)}) collective-permute-start(bf16[64,3712]{1,0:T(8,128)(2,1)S(1)} %collective-permute-done.2), channel_id=1, source_target_pairs={{0,2},{2,4},{4,6},{6,7},{7,5},{5,3},{3,1},{1,0},{8,10},{10,12},{12... | collective-permute-start | bytes 1425416 | tf_op jit(solution)/shard_map/ppermute | solution.py:56
  19.7 12.9 %collective-permute-start.7 = (bf16[64,3712]{1,0:T(8,128)(2,1)S(1)}, bf16[64,3712]{1,0:T(8,128)(2,1)S(1)}, u32[]{:S(2)}, u32[]{:S(2)}) collective-permute-start(bf16[64,3712]{1,0:T(8,128)(2,1)S(1)} %collective-permute-done.3), channel_id=1, source_target_pairs={{2,0},{4,2},{6,4},{7,6},{5,7},{3,5},{1,3},{0,1},{10,8},{12,10},{14... | collective-permute-start | bytes 1425416 | tf_op jit(solution)/shard_map/ppermute | solution.py:59
  20.2 3.6 %copy-start.9 = (bf16[64,3712]{1,0:T(8,128)(2,1)}, bf16[64,3712]{1,0:T(8,128)(2,1)S(1)}, u32[]{:S(2)}) copy-start(bf16[64,3712]{1,0:T(8,128)(2,1)S(1)} %collective-permute-done) | copy-start | bytes 1425412
  32.7 22.5 %collective-permute-start.8 = (bf16[128,3712]{1,0:T(8,128)(2,1)S(1)}, bf16[128,3712]{1,0:T(8,128)(2,1)S(1)}, u32[]{:S(2)}, u32[]{:S(2)}) collective-permute-start(bf16[128,3712]{1,0:T(8,128)(2,1)S(1)} %pad_maximum_fusion.1), channel_id=1, source_target_pairs={{0,8},{8,0},{1,9},{9,1},{2,10},{10,2},{3,11},{11,3},{4,12},{12,4},... | collective-permute-start | bytes 2850824 | tf_op jit(solution)/shard_map/ppermute | solution.py:62
  32.8 13.3 %collective-permute-start.10 = (bf16[64,3712]{1,0:T(8,128)(2,1)S(1)}, bf16[64,3712]{1,0:T(8,128)(2,1)S(1)}, u32[]{:S(2)}, u32[]{:S(2)}) collective-permute-start(bf16[64,3712]{1,0:T(8,128)(2,1)S(1)} %collective-permute-done.6), channel_id=1, source_target_pairs={{0,2},{2,4},{4,6},{6,7},{7,5},{5,3},{3,1},{1,0},{8,10},{10,12},{12... | collective-permute-start | bytes 1425416 | tf_op jit(solution)/shard_map/ppermute | solution.py:56
  34.4 13.3 %collective-permute-start.11 = (bf16[64,3712]{1,0:T(8,128)(2,1)S(1)}, bf16[64,3712]{1,0:T(8,128)(2,1)S(1)}, u32[]{:S(2)}, u32[]{:S(2)}) collective-permute-start(bf16[64,3712]{1,0:T(8,128)(2,1)S(1)} %collective-permute-done.7), channel_id=1, source_target_pairs={{2,0},{4,2},{6,4},{7,6},{5,7},{3,5},{1,3},{0,1},{10,8},{12,10},{14... | collective-permute-start | bytes 1425416 | tf_op jit(solution)/shard_map/ppermute | solution.py:59
  46.1 8.0 %collective-permute-start.14 = (bf16[32,3712]{1,0:T(8,128)(2,1)S(1)}, bf16[32,3712]{1,0:T(8,128)(2,1)S(1)}, u32[]{:S(2)}, u32[]{:S(2)}) collective-permute-start(bf16[32,3712]{1,0:T(8,128)(2,1)S(1)} %slice.141), channel_id=1, source_target_pairs={{0,2},{2,4},{4,6},{6,7},{7,5},{5,3},{3,1},{1,0},{8,10},{10,12},{12... | collective-permute-start | bytes 712712 | tf_op jit(solution)/shard_map/ppermute | solution.py:56
  47.7 7.3 %collective-permute-start.15 = (bf16[32,3712]{1,0:T(8,128)(2,1)S(1)}, bf16[32,3712]{1,0:T(8,128)(2,1)S(1)}, u32[]{:S(2)}, u32[]{:S(2)}) collective-permute-start(bf16[32,3712]{1,0:T(8,128)(2,1)S(1)} %slice.142), channel_id=1, source_target_pairs={{2,0},{4,2},{6,4},{7,6},{5,7},{3,5},{1,3},{0,1},{10,8},{12,10},{14... | collective-permute-start | bytes 712712 | tf_op jit(solution)/shard_map/ppermute | solution.py:59
  49.4 2.7 %copy-start = (bf16[1,3584,512]{2,1,0:T(8,128)(2,1)S(1)}, bf16[1,3584,512]{2,1,0:T(8,128)(2,1)}, u32[]{:S(2)}) copy-start(bf16[1,3584,512]{2,1,0:T(8,128)(2,1)} %param.13) | copy-start | bytes 11010052
  49.4 20.8 %collective-permute-start.12 = (bf16[128,3712]{1,0:T(8,128)(2,1)}, bf16[128,3712]{1,0:T(8,128)(2,1)S(1)}, u32[]{:S(2)}, u32[]{:S(2)}) collective-permute-start(bf16[128,3712]{1,0:T(8,128)(2,1)} %pad_maximum_fusion.2), channel_id=1, source_target_pairs={{0,8},{8,0},{1,9},{9,1},{2,10},{10,2},{3,11},{11,3},{4,12},{12,4},... | collective-permute-start | bytes 2850824 | tf_op jit(solution)/shard_map/ppermute | solution.py:62
  49.5 1.3 copy-start.12
  52.1 1.9 %copy-start.11 = (bf16[256,3712]{1,0:T(8,128)(2,1)}, bf16[256,3712]{1,0:T(8,128)(2,1)S(1)}, u32[]{:S(2)}) copy-start(bf16[256,3712]{1,0:T(8,128)(2,1)S(1)} %constant_dynamic-update-slice_fusion) | copy-start | bytes 5701636
  55.1 2.2 %collective-permute-start.16 = (bf16[64,3712]{1,0:T(8,128)(2,1)S(1)}, bf16[64,3712]{1,0:T(8,128)(2,1)S(1)}, u32[]{:S(2)}, u32[]{:S(2)}) collective-permute-start(bf16[64,3712]{1,0:T(8,128)(2,1)S(1)} %pad_maximum_fusion.6), channel_id=1, source_target_pairs={{0,8},{8,0},{1,9},{9,1},{2,10},{10,2},{3,11},{11,3},{4,12},{12,4},... | collective-permute-start | bytes 1425416 | tf_op jit(solution)/shard_map/ppermute | solution.py:62
  55.3 2.0 %copy-start.13 = (bf16[256,3712]{1,0:T(8,128)(2,1)}, bf16[256,3712]{1,0:T(8,128)(2,1)S(1)}, u32[]{:S(2)}) copy-start(bf16[256,3712]{1,0:T(8,128)(2,1)S(1)} %constant_dynamic-update-slice_fusion.3) | copy-start | bytes 5701636
  57.3 1.0 copy-start.10
  57.4 1.0 copy-start.15
  64.3 33.6 %collective-permute-start.17 = (bf16[64,3584]{1,0:T(8,128)(2,1)}, bf16[64,3584]{1,0:T(8,128)(2,1)}, u32[]{:S(2)}, u32[]{:S(2)}) collective-permute-start(bf16[64,3584]{1,0:T(8,128)(2,1)} %slice.146), channel_id=1, source_target_pairs={{0,8},{8,0},{1,9},{9,1},{2,10},{10,2},{3,11},{11,3},{4,12},{12,4},... | collective-permute-start | bytes 1376264 | tf_op jit(solution)/shard_map/ppermute | solution.py:62
  69.3 6.8 %copy-start.7 = (bf16[128,3584]{1,0:T(8,128)(2,1)}, bf16[128,3584]{1,0:T(8,128)(2,1)S(1)}, u32[]{:S(2)}) copy-start(bf16[128,3584]{1,0:T(8,128)(2,1)S(1)} %fusion.4) | copy-start | bytes 2752516
  69.3 2.0 %copy-start.16 = (pred[128]{0:T(512)(128)(4,1)S(1)}, pred[128]{0:T(512)(128)(4,1)}, u32[]{:S(2)}) copy-start(pred[128]{0:T(512)(128)(4,1)} %iota_compare_fusion.2) | copy-start | bytes 388
  70.2 66.3 %collective-permute-start.1 = (bf16[64,3584]{1,0:T(8,128)(2,1)}, bf16[64,3584]{1,0:T(8,128)(2,1)}, u32[]{:S(2)}, u32[]{:S(2)}) collective-permute-start(bf16[64,3584]{1,0:T(8,128)(2,1)} %slice.125), channel_id=1, source_target_pairs={{0,8},{8,0},{1,9},{9,1},{2,10},{10,2},{3,11},{11,3},{4,12},{12,4},... | collective-permute-start | bytes 1376264 | tf_op jit(solution)/shard_map/ppermute | solution.py:62
  82.0 1.7 %copy-start.4 = (bf16[256,3584]{1,0:T(8,128)(2,1)}, bf16[256,3584]{1,0:T(8,128)(2,1)S(1)}, u32[]{:S(2)}) copy-start(bf16[256,3584]{1,0:T(8,128)(2,1)S(1)} %fusion.3) | copy-start | bytes 5505028
  83.2 17.4 %collective-permute-start.13 = (bf16[128,3584]{1,0:T(8,128)(2,1)}, bf16[128,3584]{1,0:T(8,128)(2,1)}, u32[]{:S(2)}, u32[]{:S(2)}) collective-permute-start(bf16[128,3584]{1,0:T(8,128)(2,1)} %slice.139), channel_id=1, source_target_pairs={{0,8},{8,0},{1,9},{9,1},{2,10},{10,2},{3,11},{11,3},{4,12},{12,4},... | collective-permute-start | bytes 2752520 | tf_op jit(solution)/shard_map/ppermute | solution.py:62
  83.7 7.7 %copy-start.17 = (f32[256,512]{1,0:T(8,128)S(1)}, f32[256,512]{1,0:T(8,128)}, u32[]{:S(2)}) copy-start(f32[256,512]{1,0:T(8,128)} %fusion.19) | copy-start | bytes 1572868
  89.8 1.5 %copy-start.2 = (bf16[256,3584]{1,0:T(8,128)(2,1)}, bf16[256,3584]{1,0:T(8,128)(2,1)S(1)}, u32[]{:S(2)}) copy-start(bf16[256,3584]{1,0:T(8,128)(2,1)S(1)} %fusion.2) | copy-start | bytes 5505028
  90.9 19.3 %collective-permute-start.9 = (bf16[128,3584]{1,0:T(8,128)(2,1)}, bf16[128,3584]{1,0:T(8,128)(2,1)}, u32[]{:S(2)}, u32[]{:S(2)}) collective-permute-start(bf16[128,3584]{1,0:T(8,128)(2,1)} %slice.134), channel_id=1, source_target_pairs={{0,8},{8,0},{1,9},{9,1},{2,10},{10,2},{3,11},{11,3},{4,12},{12,4},... | collective-permute-start | bytes 2752520 | tf_op jit(solution)/shard_map/ppermute | solution.py:62
  97.3 3.8 %copy-start.5 = (bf16[256,3584]{1,0:T(8,128)(2,1)S(1)}, bf16[256,3584]{1,0:T(8,128)(2,1)}, u32[]{:S(2)}) copy-start(bf16[256,3584]{1,0:T(8,128)(2,1)} %copy-done.4) | copy-start | bytes 5505028
  97.3 24.9 %collective-permute-start.5 = (bf16[128,3584]{1,0:T(8,128)(2,1)S(1)}, bf16[128,3584]{1,0:T(8,128)(2,1)S(1)}, u32[]{:S(2)}, u32[]{:S(2)}) collective-permute-start(bf16[128,3584]{1,0:T(8,128)(2,1)S(1)} %slice.129), channel_id=1, source_target_pairs={{0,8},{8,0},{1,9},{9,1},{2,10},{10,2},{3,11},{11,3},{4,12},{12,4},... | collective-permute-start | bytes 2752520 | tf_op jit(solution)/shard_map/ppermute | solution.py:62
  99.0 7.8 %collective-permute-start.18 = (bf16[32,3584]{1,0:T(8,128)(2,1)S(1)}, bf16[32,3584]{1,0:T(8,128)(2,1)S(1)}, u32[]{:S(2)}, u32[]{:S(2)}) collective-permute-start(bf16[32,3584]{1,0:T(8,128)(2,1)S(1)} %get-tuple-element.13), channel_id=1, source_target_pairs={{0,2},{2,4},{4,6},{6,7},{7,5},{5,3},{3,1},{1,0},{8,10},{10,12},{12... | collective-permute-start | bytes 688136 | tf_op jit(solution)/shard_map/ppermute | solution.py:56
  100.6 7.4 %collective-permute-start.22 = (bf16[32,3584]{1,0:T(8,128)(2,1)S(1)}, bf16[32,3584]{1,0:T(8,128)(2,1)S(1)}, u32[]{:S(2)}, u32[]{:S(2)}) collective-permute-start(bf16[32,3584]{1,0:T(8,128)(2,1)S(1)} %get-tuple-element.14), channel_id=1, source_target_pairs={{2,0},{4,2},{6,4},{7,6},{5,7},{3,5},{1,3},{0,1},{10,8},{12,10},{14... | collective-permute-start | bytes 688136 | tf_op jit(solution)/shard_map/ppermute | solution.py:59
  102.5 7.7 %copy-start.3 = (bf16[256,3584]{1,0:T(8,128)(2,1)S(1)}, bf16[256,3584]{1,0:T(8,128)(2,1)}, u32[]{:S(2)}) copy-start(bf16[256,3584]{1,0:T(8,128)(2,1)} %copy-done.2) | copy-start | bytes 5505028
  108.0 25.1 %slice-start = ((s8[5242880]{0:T(1024)(128)(4,1)}), s8[4194304]{0:T(1024)(128)(4,1)S(1)}, s32[]{:S(2)}) async-start(s8[5242880]{0:T(1024)(128)(4,1)} %bitcast.55), calls=%async_computation | async-start | bytes 8388608
  108.1 11.5 %collective-permute-start.19 = (bf16[64,3584]{1,0:T(8,128)(2,1)S(1)}, bf16[64,3584]{1,0:T(8,128)(2,1)S(1)}, u32[]{:S(2)}, u32[]{:S(2)}) collective-permute-start(bf16[64,3584]{1,0:T(8,128)(2,1)S(1)} %get-tuple-element.11), channel_id=1, source_target_pairs={{0,2},{2,4},{4,6},{6,7},{7,5},{5,3},{3,1},{1,0},{8,10},{10,12},{12... | collective-permute-start | bytes 1376264 | tf_op jit(solution)/shard_map/ppermute | solution.py:56
  108.8 11.2 %collective-permute-start.23 = (bf16[64,3584]{1,0:T(8,128)(2,1)S(1)}, bf16[64,3584]{1,0:T(8,128)(2,1)S(1)}, u32[]{:S(2)}, u32[]{:S(2)}) collective-permute-start(bf16[64,3584]{1,0:T(8,128)(2,1)S(1)} %get-tuple-element.12), channel_id=1, source_target_pairs={{2,0},{4,2},{6,4},{7,6},{5,7},{3,5},{1,3},{0,1},{10,8},{12,10},{14... | collective-permute-start | bytes 1376264 | tf_op jit(solution)/shard_map/ppermute | solution.py:59
  111.6 21.5 %slice-start.1 = ((s8[5242880]{0:T(1024)(128)(4,1)}), s8[1048576]{0:T(1024)(128)(4,1)S(1)}, s32[]{:S(2)}) async-start(s8[5242880]{0:T(1024)(128)(4,1)} %bitcast.55), calls=%async_computation.1 | async-start | bytes 2097152
  120.1 10.3 %collective-permute-start.20 = (bf16[64,3584]{1,0:T(8,128)(2,1)S(1)}, bf16[64,3584]{1,0:T(8,128)(2,1)S(1)}, u32[]{:S(2)}, u32[]{:S(2)}) collective-permute-start(bf16[64,3584]{1,0:T(8,128)(2,1)S(1)} %get-tuple-element.9), channel_id=1, source_target_pairs={{0,2},{2,4},{4,6},{6,7},{7,5},{5,3},{3,1},{1,0},{8,10},{10,12},{12... | collective-permute-start | bytes 1376264 | tf_op jit(solution)/shard_map/ppermute | solution.py:56
  120.8 10.1 %collective-permute-start.24 = (bf16[64,3584]{1,0:T(8,128)(2,1)S(1)}, bf16[64,3584]{1,0:T(8,128)(2,1)S(1)}, u32[]{:S(2)}, u32[]{:S(2)}) collective-permute-start(bf16[64,3584]{1,0:T(8,128)(2,1)S(1)} %get-tuple-element.10), channel_id=1, source_target_pairs={{2,0},{4,2},{6,4},{7,6},{5,7},{3,5},{1,3},{0,1},{10,8},{12,10},{14... | collective-permute-start | bytes 1376264 | tf_op jit(solution)/shard_map/ppermute | solution.py:59
  122.4 10.7 %copy-start.1 = (f32[64,64,64]{1,2,0:T(8,128)S(1)}, f32[64,64,64]{1,2,0:T(8,128)}, u32[]{:S(2)}) copy-start(f32[64,64,64]{1,2,0:T(8,128)} %get-tuple-element.16) | copy-start | bytes 3145732
  122.5 10.7 %copy-start.14 = (f32[64,64]{1,0:T(8,128)S(1)}, f32[64,64]{1,0:T(8,128)}, u32[]{:S(2)}) copy-start(f32[64,64]{1,0:T(8,128)} %get-tuple-element.15) | copy-start | bytes 49156
  131.1 9.3 %collective-permute-start.21 = (bf16[64,3584]{1,0:T(8,128)(2,1)S(1)}, bf16[64,3584]{1,0:T(8,128)(2,1)S(1)}, u32[]{:S(2)}, u32[]{:S(2)}) collective-permute-start(bf16[64,3584]{1,0:T(8,128)(2,1)S(1)} %get-tuple-element.7), channel_id=1, source_target_pairs={{0,2},{2,4},{4,6},{6,7},{7,5},{5,3},{3,1},{1,0},{8,10},{10,12},{12... | collective-permute-start | bytes 1376264 | tf_op jit(solution)/shard_map/ppermute | solution.py:56
  131.7 9.0 %collective-permute-start.25 = (bf16[64,3584]{1,0:T(8,128)(2,1)S(1)}, bf16[64,3584]{1,0:T(8,128)(2,1)S(1)}, u32[]{:S(2)}, u32[]{:S(2)}) collective-permute-start(bf16[64,3584]{1,0:T(8,128)(2,1)S(1)} %get-tuple-element.8), channel_id=1, source_target_pairs={{2,0},{4,2},{6,4},{7,6},{5,7},{3,5},{1,3},{0,1},{10,8},{12,10},{14... | collective-permute-start | bytes 1376264 | tf_op jit(solution)/shard_map/ppermute | solution.py:59
  133.2 7.6 %copy-start.8 = (bf16[128,3584]{1,0:T(8,128)(2,1)S(1)}, bf16[128,3584]{1,0:T(8,128)(2,1)}, u32[]{:S(2)}) copy-start(bf16[128,3584]{1,0:T(8,128)(2,1)} %copy-done.7) | copy-start | bytes 2752516

commit v2 on v1

v2 whole, which is shorter than its diff:
```python
import jax
import jax.numpy as jnp
from jax import lax
from jax.experimental import pallas as pl
from jax.experimental.pallas import tpu as pltpu
from jax.sharding import PartitionSpec as P

LAT = 512
SOFTMAX_SCALE = 192.0 ** (-0.5)
LANES = 128


def attend(queries, latent_cache, cache_lengths, latent_width):
    scores = SOFTMAX_SCALE * jnp.einsum(
        "thc,tjc->thj", queries, latent_cache, preferred_element_type=jnp.float32
    )
    valid_mask = (jnp.arange(latent_cache.shape[1])[None, :] < cache_lengths[:, None])[:, None, :]
    scores = jnp.where(valid_mask, scores, -1e30)
    row_peak = jnp.max(scores, axis=2, keepdims=True)
    exp_terms = jnp.where(valid_mask, jnp.exp(scores - row_peak), 0.0)
    attn_probs = (exp_terms / jnp.sum(exp_terms, axis=2, keepdims=True)).astype(jnp.bfloat16)
    return jnp.einsum(
        "thj,tjc->thc",
        attn_probs,
        latent_cache[:, :, :latent_width],
        preferred_element_type=jnp.float32,
    ).astype(jnp.bfloat16)


def expert_kernel(expert_ref, own_ref, other_ref, gate_ref, up_ref, down_ref, own_out, other_out):
    rows, width = own_out.shape
    x = jnp.concatenate([own_ref[:, :width], other_ref[:, :width]], axis=0)
    gate = jnp.dot(x, gate_ref[...], preferred_element_type=jnp.float32)
    up = jnp.dot(x, up_ref[...], preferred_element_type=jnp.float32)
    hidden = (gate / (1.0 + jnp.exp(-gate)) * up).astype(jnp.bfloat16)
    down = jnp.dot(hidden, down_ref[...], preferred_element_type=jnp.float32)
    lane = lax.broadcasted_iota(jnp.int32, (rows, LANES), 1)
    for at, source, out in ((0, own_ref, own_out), (rows, other_ref, other_out)):
        route = source[:, width:].astype(jnp.float32)
        weight = jnp.sum(jnp.where(lane == expert_ref[0], route, 0.0), axis=1, keepdims=True)
        out[...] = (weight * down[at : at + rows]).astype(jnp.bfloat16)


def run_experts(expert, own, other, gate, up, down):
    rows, wide = own.shape
    width, hidden = gate.shape

    def whole(shape):
        return pl.BlockSpec(shape, lambda i, e: (0, 0))

    return pl.pallas_call(
        expert_kernel,
        grid_spec=pltpu.PrefetchScalarGridSpec(
            num_scalar_prefetch=1,
            grid=(1,),
            in_specs=[
                whole((rows, wide)),
                whole((rows, wide)),
                whole((width, hidden)),
                whole((width, hidden)),
                whole((hidden, width)),
            ],
            out_specs=[whole((rows, width)), whole((rows, width))],
        ),
        out_shape=[jax.ShapeDtypeStruct((rows, width), jnp.bfloat16)] * 2,
        compiler_params=pltpu.CompilerParams(vmem_limit_bytes=16 << 20),
        cost_estimate=pl.CostEstimate(
            flops=12 * rows * width * hidden,
            bytes_accessed=6 * width * hidden,
            transcendentals=2 * rows * hidden,
        ),
        name="expert_half",
    )(expert, own, other, gate, up, down)


def ring_order(count):
    if count == 8:
        return [0, 2, 4, 6, 7, 5, 3, 1]
    return list(range(count))


def on_device(
    tokens, expert_ids, combine_weights, w_gate, w_up, w_down, queries, latent_cache, cache_lengths
):
    local_count = lax.axis_size("local")
    rows, width = tokens.shape
    part = rows // 2
    node = lax.axis_index("node")
    order = ring_order(local_count)
    hops = []
    for i in range(local_count):
        here, there = order[i], order[(i + 1) % local_count]
        hops.append((here, there))
        hops.append((local_count + there, local_count + here))
    expert = ((node * local_count + lax.axis_index("local")) // 2).astype(jnp.int32).reshape(1)

    def onward(a):
        return lax.ppermute(a, ("node", "local"), hops)

    def across(a):
        return lax.ppermute(a, "node", [(0, 1), (1, 0)])

    matches = expert_ids[:, :, None] == jnp.arange(LANES, dtype=jnp.int32)[None, None, :]
    route = jnp.sum(
        jnp.where(matches, combine_weights[:, :, None], jnp.zeros((), jnp.bfloat16)), axis=1
    )
    mine = jnp.concatenate([tokens, route], axis=1)
    first = node == 0
    kept = jnp.where(first, mine[:part], mine[part:])
    given = jnp.where(first, mine[part:], mine[:part])
    gate, up, down = [
        pltpu.with_memory_space_constraint(w[0], pltpu.VMEM) for w in (w_gate, w_up, w_down)
    ]

    block = jnp.concatenate([kept, across(given)], axis=0)
    own_sums, other_sums = [], []
    for k in range(local_count):
        if k:
            block = onward(block)
        own, other = run_experts(expert, block, across(block), gate, up, down)
        own_sums.append(own)
        other_sums.append(across(other))

    def chip_sum(k):
        return own_sums[k].astype(jnp.float32) + other_sums[k].astype(jnp.float32)

    running = chip_sum(1).astype(jnp.bfloat16)
    for k in range(2, local_count):
        running = (chip_sum(k) + onward(running).astype(jnp.float32)).astype(jnp.bfloat16)
    total = (chip_sum(0) + onward(running).astype(jnp.float32)).astype(jnp.bfloat16)
    mine_out, back = total[:part], across(total[part:])
    moe_out = jnp.where(
        first,
        jnp.concatenate([mine_out, back], axis=0),
        jnp.concatenate([back, mine_out], axis=0),
    )

    attn_latent = attend(queries, latent_cache, cache_lengths, LAT)
    return (moe_out, attn_latent)


def solution(mesh):
    in_specs = (
        P(("replica", "node", "local"), None),
        P(("replica", "node", "local"), None),
        P(("replica", "node", "local"), None),
        P(("node", "local"), None, None),
        P(("node", "local"), None, None),
        P(("node", "local"), None, None),
        P(("replica", "node", "local"), None, None),
        P(("replica", "node", "local"), None, None),
        P(("replica", "node", "local")),
    )
    out_specs = (P(("replica", "node", "local"), None), P(("replica", "node", "local"), None, None))
    return jax.shard_map(
        on_device, mesh=mesh, in_specs=in_specs, out_specs=out_specs, check_vma=False
    )
```

time: 143 us -> 105 us (0.73)
  matrix products: 49.7 us -> 11.2 us
  waiting for transfers between devices: 50.7 us -> 36.1 us
  Pallas kernels: 0 us -> 13.8 us
  starting transfers between devices: 20 us -> 30 us
  other arithmetic: 12.7 us -> 6.11 us
  local copies, waits for them, and re-layouts: 8.63 us -> 6.16 us
    dot_general x10 -> x0, matrix products: 38.7 us -> none  [the longest x5 26.9 us: experts(): down = jnp.dot(hidden, w_down[0], preferred_element_type=jnp.float32)]
    ppermute x26 -> x32, waiting for transfers between devices: 50.7 us -> 36.1 us  [the longest x14 35 us: onward(): return lax.ppermute(a, ('node', 'local'), hops)]
    pallas_call x0 -> x8, Pallas kernels: none -> 13.8 us  [run_experts(): pl.pallas_call(expert_kernel, grid_spec=pltpu.PrefetchScalarGridSpec(num_...]
    ppermute x26 -> x32, starting transfers between devices: 20 us -> 30 us  [the longest x14 27.3 us: onward(): return lax.ppermute(a, ('node', 'local'), hops)]
    slice x8 -> x1, local copies, waits for them, and re-layouts: 4.11 us -> 0.03 us  [on_device(): mine_out, back = (total[:part], across(total[part:]))]
    add x3 -> x0, other arithmetic: 3.04 us -> none  [on_device(): out[:count].astype(jnp.float32) + across(out[count:]).astype(jnp.float32)]
    unnamed x48 -> x14, local copies, waits for them, and re-layouts: 3.21 us -> 6.13 us
    dot_general x1, matrix products: 3.32 us -> 5.51 us  [attend(): jnp.einsum('thj,tjc->thc', attn_probs, latent_cache[:, :, :latent_width],...]
  transfers between devices with their start and end apart: 26 -> 32, of which waited for: 14 -> 14; matrix products, arithmetic and copies ran while one was open for 45% -> 13% of each run, Pallas kernels for 0% -> 13%
where the time goes in v2:
time: 105 us; the launch traced here: 104 us
  waiting for transfers between devices  36.1 us (34%)
  starting transfers between devices  30 us (29%)
  Pallas kernels  13.8 us (13%)
  matrix products  11.2 us (11%)
  local copies, waits for them, and re-layouts  6.16 us (6%)
  other arithmetic  6.11 us (6%)
    ppermute x14, waiting for transfers between devices, onward(): return lax.ppermute(a, ('node', 'local'), hops)  35 us
    ppermute x14, starting transfers between devices, onward(): return lax.ppermute(a, ('node', 'local'), hops)  27.3 us
    pallas_call x8, Pallas kernels, run_experts(): pl.pallas_call(expert_kernel, grid_spec=pltpu.PrefetchScalarGridSpec(num_...  13.8 us
    unnamed x14, local copies, waits for them, and re-layouts  6.13 us
    sub x1, matrix products, attend(): exp_terms = jnp.where(valid_mask, jnp.exp(scores - row_peak), 0.0)  5.69 us
    dot_general x1, matrix products, attend(): jnp.einsum('thj,tjc->thc', attn_probs, latent_cache[:, :, :latent_width],...  5.51 us
    ppermute x18, starting transfers between devices, across(): return lax.ppermute(a, 'node', [(0, 1), (1, 0)])  2.66 us
  transfers between devices with their start and end apart: 32, of which 14 were waited for; matrix products, arithmetic and copies ran while one was open for 13% of the time, Pallas kernels for 13%

profile of v2, /device:TPU:0, one launch (start us, length us, event | category | flops | bytes accessed | tf_op | source)
XLA Modules:
  0.0 104.2 jit_solution(3351455861875298396)
XLA Ops:
  0.6 0.8 fusion.13
  1.5 1.3 %broadcast_select_fusion.1 = (bf16[32,3712]{1,0:T(8,128)(2,1)S(1)}, bf16[32,3712]{1,0:T(8,128)(2,1)S(1)}) fusion(pred[]{:T(512)S(6)} %eq.16, bf16[64,128]{1,0:T(8,128)(2,1)S(1)} %fusion.13, bf16[64,3584]{1,0:T(8,128)(2,1)} %param.9), kind=kLoop, calls=%fused_computation.27 | loop fusion | flops 1662976 | bytes 950273 | tf_op jit(solution)/shard_map/jit(_where)/select_n | solution.py:109
  2.7 0.5 collective-permute-start
  3.2 1.1 %collective-permute-done = bf16[32,3712]{1,0:T(8,128)(2,1)S(1)} collective-permute-done((bf16[32,3712]{1,0:T(8,128)(2,1)S(1)}, bf16[32,3712]{1,0:T(8,128)(2,1)S(1)}, u32[]{:S(2)}, u32[]{:S(2)}) %collective-permute-start) | collective-permute-done | bytes 237600 | tf_op jit(solution)/shard_map/ppermute | solution.py:101
  4.4 3.0 %collective-permute-start.3 = (bf16[64,3712]{1,0:T(8,128)(2,1)S(1)}, bf16[64,3712]{1,0:T(8,128)(2,1)S(1)}, u32[]{:S(2)}, u32[]{:S(2)}) collective-permute-start(bf16[64,3712]{1,0:T(8,128)(2,1)S(1)} %pad_maximum_fusion.own_ref), channel_id=1, source_target_pairs={{0,2},{10,8},{2,4},{12,10},{4,6},{14,12},{6,7},{15,14},{7,5},{13,1... | collective-permute-start | bytes 1425416 | tf_op jit(solution)/shard_map/ppermute | solution.py:98
  7.4 6.6 %collective-permute-done.3.own_ref = bf16[64,3712]{1,0:T(8,128)(2,1)S(1)} collective-permute-done((bf16[64,3712]{1,0:T(8,128)(2,1)S(1)}, bf16[64,3712]{1,0:T(8,128)(2,1)S(1)}, u32[]{:S(2)}, u32[]{:S(2)}) %collective-permute-start.3) | collective-permute-done | bytes 475168 | tf_op jit(solution)/shard_map/ppermute | solution.py:98
  14.0 2.1 %collective-permute-start.4 = (bf16[64,3712]{1,0:T(8,128)(2,1)S(1)}, bf16[64,3712]{1,0:T(8,128)(2,1)S(1)}, u32[]{:S(2)}, u32[]{:S(2)}) collective-permute-start(bf16[64,3712]{1,0:T(8,128)(2,1)S(1)} %collective-permute-done.3.own_ref), channel_id=1, source_target_pairs={{0,2},{10,8},{2,4},{12,10},{4,6},{14,12},{6,7},{15,14},{7,5},{13,1... | collective-permute-start | bytes 1425416 | tf_op jit(solution)/shard_map/ppermute | solution.py:98
  16.1 2.0 %copy-done = bf16[1,3584,512]{2,1,0:T(8,128)(2,1)S(1)} copy-done((bf16[1,3584,512]{2,1,0:T(8,128)(2,1)S(1)}, bf16[1,3584,512]{2,1,0:T(8,128)(2,1)}, u32[]{:S(2)}) %copy-start) | copy-done | bytes 3670040
  18.1 2.0 %copy-done.2 = bf16[1,3584,512]{2,1,0:T(8,128)(2,1)S(1)} copy-done((bf16[1,3584,512]{2,1,0:T(8,128)(2,1)S(1)}, bf16[1,3584,512]{2,1,0:T(8,128)(2,1)}, u32[]{:S(2)}) %copy-start.2) | copy-done | bytes 3670040
  20.2 2.0 %copy-done.4 = bf16[1,512,3584]{2,1,0:T(8,128)(2,1)S(1)} copy-done((bf16[1,512,3584]{2,1,0:T(8,128)(2,1)S(1)}, bf16[1,512,3584]{2,1,0:T(8,128)(2,1)}, u32[]{:S(2)}) %copy-start.4) | copy-done | bytes 3670040
  22.2 1.8 %expert_half.15 = (bf16[64,3584]{1,0:T(8,128)(2,1)S(1)}, bf16[64,3584]{1,0:T(8,128)(2,1)S(1)}) custom-call(s32[1]{0:T(128)} %bitcast.expert_ref, bf16[64,3712]{1,0:T(8,128)(2,1)S(1)} %collective-permute-done.3.own_ref, bf16[64,3712]{1,0:T(8,128)(2,1)S(1)} %collective-permute-done.22.other_ref, bf16[3584,512]{1,0:T(8,128)(2,1)S(1)} %bitcast.6, ...), custom_call_target="tpu_custom_call" | custom-call | flops 1409286144 | bytes 11010048 | tf_op jit(solution)/shard_map/expert_half/pallas_call | solution.py:51
  24.0 0.2 collective-permute-start.23
  24.2 0.3 collective-permute-start.20
  24.5 1.8 %collective-permute-start.5 = (bf16[64,3712]{1,0:T(8,128)(2,1)S(1)}, bf16[64,3712]{1,0:T(8,128)(2,1)S(1)}, u32[]{:S(2)}, u32[]{:S(2)}) collective-permute-start(bf16[64,3712]{1,0:T(8,128)(2,1)S(1)} %collective-permute-done.4.own_ref), channel_id=1, source_target_pairs={{0,2},{10,8},{2,4},{12,10},{4,6},{14,12},{6,7},{15,14},{7,5},{13,1... | collective-permute-start | bytes 1425416 | tf_op jit(solution)/shard_map/ppermute | solution.py:98
  26.4 0.1 add_convert_fusion.7
  26.5 1.6 %collective-permute-start.24 = (bf16[64,3584]{1,0:T(8,128)(2,1)S(1)}, bf16[64,3584]{1,0:T(8,128)(2,1)S(1)}, u32[]{:S(2)}, u32[]{:S(2)}) collective-permute-start(bf16[64,3584]{1,0:T(8,128)(2,1)S(1)} %add_convert_fusion.7), channel_id=1, source_target_pairs={{0,2},{10,8},{2,4},{12,10},{4,6},{14,12},{6,7},{15,14},{7,5},{13,1... | collective-permute-start | bytes 1376264 | tf_op jit(solution)/shard_map/ppermute | solution.py:98
  28.1 1.7 %expert_half.14 = (bf16[64,3584]{1,0:T(8,128)(2,1)S(1)}, bf16[64,3584]{1,0:T(8,128)(2,1)S(1)}) custom-call(s32[1]{0:T(128)} %bitcast.expert_ref, bf16[64,3712]{1,0:T(8,128)(2,1)S(1)} %collective-permute-done.4.own_ref, bf16[64,3712]{1,0:T(8,128)(2,1)S(1)} %collective-permute-done.20.other_ref, bf16[3584,512]{1,0:T(8,128)(2,1)S(1)} %bitcast.7, ...), custom_call_target="tpu_custom_call" | custom-call | flops 1409286144 | bytes 11010048 | tf_op jit(solution)/shard_map/expert_half/pallas_call | solution.py:51
  29.9 0.1 collective-permute-start.21
  29.9 3.2 %collective-permute-done.5.own_ref = bf16[64,3712]{1,0:T(8,128)(2,1)S(1)} collective-permute-done((bf16[64,3712]{1,0:T(8,128)(2,1)S(1)}, bf16[64,3712]{1,0:T(8,128)(2,1)S(1)}, u32[]{:S(2)}, u32[]{:S(2)}) %collective-permute-start.5) | collective-permute-done | bytes 475168 | tf_op jit(solution)/shard_map/ppermute | solution.py:98
  33.2 1.8 %collective-permute-start.6 = (bf16[64,3712]{1,0:T(8,128)(2,1)S(1)}, bf16[64,3712]{1,0:T(8,128)(2,1)S(1)}, u32[]{:S(2)}, u32[]{:S(2)}) collective-permute-start(bf16[64,3712]{1,0:T(8,128)(2,1)S(1)} %collective-permute-done.5.own_ref), channel_id=1, source_target_pairs={{0,2},{10,8},{2,4},{12,10},{4,6},{14,12},{6,7},{15,14},{7,5},{13,1... | collective-permute-start | bytes 1425416 | tf_op jit(solution)/shard_map/ppermute | solution.py:98
  35.0 3.1 %collective-permute-done.24 = bf16[64,3584]{1,0:T(8,128)(2,1)S(1)} collective-permute-done((bf16[64,3584]{1,0:T(8,128)(2,1)S(1)}, bf16[64,3584]{1,0:T(8,128)(2,1)S(1)}, u32[]{:S(2)}, u32[]{:S(2)}) %collective-permute-start.24) | collective-permute-done | bytes 458784 | tf_op jit(solution)/shard_map/ppermute | solution.py:98
  38.1 0.2 add_convert_fusion.6
  38.3 1.9 %collective-permute-start.25 = (bf16[64,3584]{1,0:T(8,128)(2,1)S(1)}, bf16[64,3584]{1,0:T(8,128)(2,1)S(1)}, u32[]{:S(2)}, u32[]{:S(2)}) collective-permute-start(bf16[64,3584]{1,0:T(8,128)(2,1)S(1)} %add_convert_fusion.6), channel_id=1, source_target_pairs={{0,2},{10,8},{2,4},{12,10},{4,6},{14,12},{6,7},{15,14},{7,5},{13,1... | collective-permute-start | bytes 1376264 | tf_op jit(solution)/shard_map/ppermute | solution.py:98
  40.2 1.7 %expert_half.13 = (bf16[64,3584]{1,0:T(8,128)(2,1)S(1)}, bf16[64,3584]{1,0:T(8,128)(2,1)S(1)}) custom-call(s32[1]{0:T(128)} %bitcast.expert_ref, bf16[64,3712]{1,0:T(8,128)(2,1)S(1)} %collective-permute-done.5.own_ref, bf16[64,3712]{1,0:T(8,128)(2,1)S(1)} %collective-permute-done.18.other_ref, bf16[3584,512]{1,0:T(8,128)(2,1)S(1)} %bitcast.8, ...), custom_call_target="tpu_custom_call" | custom-call | flops 1409286144 | bytes 11010048 | tf_op jit(solution)/shard_map/expert_half/pallas_call | solution.py:51
  41.9 0.1 collective-permute-start.19
  42.0 1.2 %collective-permute-done.6.own_ref = bf16[64,3712]{1,0:T(8,128)(2,1)S(1)} collective-permute-done((bf16[64,3712]{1,0:T(8,128)(2,1)S(1)}, bf16[64,3712]{1,0:T(8,128)(2,1)S(1)}, u32[]{:S(2)}, u32[]{:S(2)}) %collective-permute-start.6) | collective-permute-done | bytes 475168 | tf_op jit(solution)/shard_map/ppermute | solution.py:98
  43.2 1.8 %collective-permute-start.7 = (bf16[64,3712]{1,0:T(8,128)(2,1)S(1)}, bf16[64,3712]{1,0:T(8,128)(2,1)S(1)}, u32[]{:S(2)}, u32[]{:S(2)}) collective-permute-start(bf16[64,3712]{1,0:T(8,128)(2,1)S(1)} %collective-permute-done.6.own_ref), channel_id=1, source_target_pairs={{0,2},{10,8},{2,4},{12,10},{4,6},{14,12},{6,7},{15,14},{7,5},{13,1... | collective-permute-start | bytes 1425416 | tf_op jit(solution)/shard_map/ppermute | solution.py:98
  45.0 3.1 %collective-permute-done.25 = bf16[64,3584]{1,0:T(8,128)(2,1)S(1)} collective-permute-done((bf16[64,3584]{1,0:T(8,128)(2,1)S(1)}, bf16[64,3584]{1,0:T(8,128)(2,1)S(1)}, u32[]{:S(2)}, u32[]{:S(2)}) %collective-permute-start.25) | collective-permute-done | bytes 458784 | tf_op jit(solution)/shard_map/ppermute | solution.py:98
  48.1 0.2 add_convert_fusion.5
  48.3 1.9 %collective-permute-start.26 = (bf16[64,3584]{1,0:T(8,128)(2,1)S(1)}, bf16[64,3584]{1,0:T(8,128)(2,1)S(1)}, u32[]{:S(2)}, u32[]{:S(2)}) collective-permute-start(bf16[64,3584]{1,0:T(8,128)(2,1)S(1)} %add_convert_fusion.5), channel_id=1, source_target_pairs={{0,2},{10,8},{2,4},{12,10},{4,6},{14,12},{6,7},{15,14},{7,5},{13,1... | collective-permute-start | bytes 1376264 | tf_op jit(solution)/shard_map/ppermute | solution.py:98
  50.2 1.7 %expert_half.12 = (bf16[64,3584]{1,0:T(8,128)(2,1)S(1)}, bf16[64,3584]{1,0:T(8,128)(2,1)S(1)}) custom-call(s32[1]{0:T(128)} %bitcast.expert_ref, bf16[64,3712]{1,0:T(8,128)(2,1)S(1)} %collective-permute-done.6.own_ref, bf16[64,3712]{1,0:T(8,128)(2,1)S(1)} %collective-permute-done.16.other_ref, bf16[3584,512]{1,0:T(8,128)(2,1)S(1)} %bitcast.9, ...), custom_call_target="tpu_custom_call" | custom-call | flops 1409286144 | bytes 11010048 | tf_op jit(solution)/shard_map/expert_half/pallas_call | solution.py:51
  52.0 1.2 %collective-permute-done.7.own_ref = bf16[64,3712]{1,0:T(8,128)(2,1)S(1)} collective-permute-done((bf16[64,3712]{1,0:T(8,128)(2,1)S(1)}, bf16[64,3712]{1,0:T(8,128)(2,1)S(1)}, u32[]{:S(2)}, u32[]{:S(2)}) %collective-permute-start.7) | collective-permute-done | bytes 475168 | tf_op jit(solution)/shard_map/ppermute | solution.py:98
  53.2 1.8 %collective-permute-start.8 = (bf16[64,3712]{1,0:T(8,128)(2,1)S(1)}, bf16[64,3712]{1,0:T(8,128)(2,1)S(1)}, u32[]{:S(2)}, u32[]{:S(2)}) collective-permute-start(bf16[64,3712]{1,0:T(8,128)(2,1)S(1)} %collective-permute-done.7.own_ref), channel_id=1, source_target_pairs={{0,2},{10,8},{2,4},{12,10},{4,6},{14,12},{6,7},{15,14},{7,5},{13,1... | collective-permute-start | bytes 1425416 | tf_op jit(solution)/shard_map/ppermute | solution.py:98
  55.0 3.1 %collective-permute-done.26 = bf16[64,3584]{1,0:T(8,128)(2,1)S(1)} collective-permute-done((bf16[64,3584]{1,0:T(8,128)(2,1)S(1)}, bf16[64,3584]{1,0:T(8,128)(2,1)S(1)}, u32[]{:S(2)}, u32[]{:S(2)}) %collective-permute-start.26) | collective-permute-done | bytes 458784 | tf_op jit(solution)/shard_map/ppermute | solution.py:98
  58.1 0.2 add_convert_fusion.4
  58.3 1.9 %collective-permute-start.27 = (bf16[64,3584]{1,0:T(8,128)(2,1)S(1)}, bf16[64,3584]{1,0:T(8,128)(2,1)S(1)}, u32[]{:S(2)}, u32[]{:S(2)}) collective-permute-start(bf16[64,3584]{1,0:T(8,128)(2,1)S(1)} %add_convert_fusion.4), channel_id=1, source_target_pairs={{0,2},{10,8},{2,4},{12,10},{4,6},{14,12},{6,7},{15,14},{7,5},{13,1... | collective-permute-start | bytes 1376264 | tf_op jit(solution)/shard_map/ppermute | solution.py:98
  60.2 1.7 %expert_half.11 = (bf16[64,3584]{1,0:T(8,128)(2,1)S(1)}, bf16[64,3584]{1,0:T(8,128)(2,1)S(1)}) custom-call(s32[1]{0:T(128)} %bitcast.expert_ref, bf16[64,3712]{1,0:T(8,128)(2,1)S(1)} %collective-permute-done.7.own_ref, bf16[64,3712]{1,0:T(8,128)(2,1)S(1)} %collective-permute-done.14.other_ref, bf16[3584,512]{1,0:T(8,128)(2,1)S(1)} %bitcast.10, ...), custom_call_target="tpu_custom_call" | custom-call | flops 1409286144 | bytes 11010048 | tf_op jit(solution)/shard_map/expert_half/pallas_call | solution.py:51
  61.9 0.1 collective-permute-start.15
  62.0 1.2 %collective-permute-done.8.own_ref = bf16[64,3712]{1,0:T(8,128)(2,1)S(1)} collective-permute-done((bf16[64,3712]{1,0:T(8,128)(2,1)S(1)}, bf16[64,3712]{1,0:T(8,128)(2,1)S(1)}, u32[]{:S(2)}, u32[]{:S(2)}) %collective-permute-start.8) | collective-permute-done | bytes 475168 | tf_op jit(solution)/shard_map/ppermute | solution.py:98
  63.2 1.8 %collective-permute-start.9 = (bf16[64,3712]{1,0:T(8,128)(2,1)S(1)}, bf16[64,3712]{1,0:T(8,128)(2,1)S(1)}, u32[]{:S(2)}, u32[]{:S(2)}) collective-permute-start(bf16[64,3712]{1,0:T(8,128)(2,1)S(1)} %collective-permute-done.8.own_ref), channel_id=1, source_target_pairs={{0,2},{10,8},{2,4},{12,10},{4,6},{14,12},{6,7},{15,14},{7,5},{13,1... | collective-permute-start | bytes 1425416 | tf_op jit(solution)/shard_map/ppermute | solution.py:98
  65.1 3.1 %collective-permute-done.27 = bf16[64,3584]{1,0:T(8,128)(2,1)S(1)} collective-permute-done((bf16[64,3584]{1,0:T(8,128)(2,1)S(1)}, bf16[64,3584]{1,0:T(8,128)(2,1)S(1)}, u32[]{:S(2)}, u32[]{:S(2)}) %collective-permute-start.27) | collective-permute-done | bytes 458784 | tf_op jit(solution)/shard_map/ppermute | solution.py:98
  68.1 0.2 add_convert_fusion.3
  68.3 2.1 %collective-permute-start.28 = (bf16[64,3584]{1,0:T(8,128)(2,1)S(1)}, bf16[64,3584]{1,0:T(8,128)(2,1)S(1)}, u32[]{:S(2)}, u32[]{:S(2)}) collective-permute-start(bf16[64,3584]{1,0:T(8,128)(2,1)S(1)} %add_convert_fusion.3), channel_id=1, source_target_pairs={{0,2},{10,8},{2,4},{12,10},{4,6},{14,12},{6,7},{15,14},{7,5},{13,1... | collective-permute-start | bytes 1376264 | tf_op jit(solution)/shard_map/ppermute | solution.py:98
  70.4 1.7 %expert_half.10 = (bf16[64,3584]{1,0:T(8,128)(2,1)S(1)}, bf16[64,3584]{1,0:T(8,128)(2,1)S(1)}) custom-call(s32[1]{0:T(128)} %bitcast.expert_ref, bf16[64,3712]{1,0:T(8,128)(2,1)S(1)} %collective-permute-done.8.own_ref, bf16[64,3712]{1,0:T(8,128)(2,1)S(1)} %collective-permute-done.12.other_ref, bf16[3584,512]{1,0:T(8,128)(2,1)S(1)} %bitcast.11, ...), custom_call_target="tpu_custom_call" | custom-call | flops 1409286144 | bytes 11010048 | tf_op jit(solution)/shard_map/expert_half/pallas_call | solution.py:51
  72.1 0.1 collective-permute-start.13
  72.2 0.5 collective-permute-start.1
  72.7 0.5 collective-permute-done.9.own_ref
  73.2 4.9 %collective-permute-done.28 = bf16[64,3584]{1,0:T(8,128)(2,1)S(1)} collective-permute-done((bf16[64,3584]{1,0:T(8,128)(2,1)S(1)}, bf16[64,3584]{1,0:T(8,128)(2,1)S(1)}, u32[]{:S(2)}, u32[]{:S(2)}) %collective-permute-start.28) | collective-permute-done | bytes 458784 | tf_op jit(solution)/shard_map/ppermute | solution.py:98
  78.1 0.2 add_convert_fusion.2
  78.3 1.9 %collective-permute-start.29 = (bf16[64,3584]{1,0:T(8,128)(2,1)S(1)}, bf16[64,3584]{1,0:T(8,128)(2,1)S(1)}, u32[]{:S(2)}, u32[]{:S(2)}) collective-permute-start(bf16[64,3584]{1,0:T(8,128)(2,1)S(1)} %add_convert_fusion.2), channel_id=1, source_target_pairs={{0,2},{10,8},{2,4},{12,10},{4,6},{14,12},{6,7},{15,14},{7,5},{13,1... | collective-permute-start | bytes 1376264 | tf_op jit(solution)/shard_map/ppermute | solution.py:98
  80.2 1.7 %expert_half.9 = (bf16[64,3584]{1,0:T(8,128)(2,1)S(1)}, bf16[64,3584]{1,0:T(8,128)(2,1)S(1)}) custom-call(s32[1]{0:T(128)} %bitcast.expert_ref, bf16[64,3712]{1,0:T(8,128)(2,1)S(1)} %collective-permute-done.9.own_ref, bf16[64,3712]{1,0:T(8,128)(2,1)S(1)} %collective-permute-done.10.other_ref, bf16[3584,512]{1,0:T(8,128)(2,1)S(1)} %bitcast.12, ...), custom_call_target="tpu_custom_call" | custom-call | flops 1409286144 | bytes 11010048 | tf_op jit(solution)/shard_map/expert_half/pallas_call | solution.py:51
  81.9 0.1 collective-permute-start.11
  82.0 0.1 iota_compare_fusion.1
  82.1 1.7 %expert_half.8 = (bf16[64,3584]{1,0:T(8,128)(2,1)S(1)}, bf16[64,3584]{1,0:T(8,128)(2,1)S(1)}) custom-call(s32[1]{0:T(128)} %bitcast.expert_ref, bf16[64,3712]{1,0:T(8,128)(2,1)S(1)} %pad_maximum_fusion.own_ref, bf16[64,3712]{1,0:T(8,128)(2,1)S(1)} %collective-permute-done.1.other_ref, bf16[3584,512]{1,0:T(8,128)(2,1)S(1)} %bitcast.13, ...), custom_call_target="tpu_custom_call" | custom-call | flops 1409286144 | bytes 11010048 | tf_op jit(solution)/shard_map/expert_half/pallas_call | solution.py:51
  83.8 0.6 collective-permute-start.2
  84.4 2.4 %collective-permute-done.29 = bf16[64,3584]{1,0:T(8,128)(2,1)S(1)} collective-permute-done((bf16[64,3584]{1,0:T(8,128)(2,1)S(1)}, bf16[64,3584]{1,0:T(8,128)(2,1)S(1)}, u32[]{:S(2)}, u32[]{:S(2)}) %collective-permute-start.29) | collective-permute-done | bytes 458784 | tf_op jit(solution)/shard_map/ppermute | solution.py:98
  86.9 0.9 add_convert_fusion.1
  87.8 1.8 %collective-permute-start.30 = (bf16[64,3584]{1,0:T(8,128)(2,1)}, bf16[64,3584]{1,0:T(8,128)(2,1)}, u32[]{:S(2)}, u32[]{:S(2)}) collective-permute-start(bf16[64,3584]{1,0:T(8,128)(2,1)} %add_convert_fusion.1), channel_id=1, source_target_pairs={{0,2},{10,8},{2,4},{12,10},{4,6},{14,12},{6,7},{15,14},{7,5},{13,1... | collective-permute-start | bytes 1376264 | tf_op jit(solution)/shard_map/ppermute | solution.py:98
  89.6 5.7 %fusion.17 = (f32[64,64]{1,0:T(8,128)S(1)}, f32[64,64,64]{1,2,0:T(8,128)S(1)}) fusion(pred[64,64]{1,0:T(8,128)(4,1)S(1)} %iota_compare_fusion.1, bf16[64,64,576]{2,1,0:T(8,128)(2,1)} %param.15, bf16[64,64,576]{2,1,0:T(8,128)(2,1)} %param.16), kind=kOutput, calls=%fused_computation.35 | convolution fusion | flops 303300672 | bytes 10506240 | tf_op jit(solution)/shard_map/sub | solution.py:20
  95.3 1.2 %collective-permute-done.30 = bf16[64,3584]{1,0:T(8,128)(2,1)} collective-permute-done((bf16[64,3584]{1,0:T(8,128)(2,1)}, bf16[64,3584]{1,0:T(8,128)(2,1)}, u32[]{:S(2)}, u32[]{:S(2)}) %collective-permute-start.30) | collective-permute-done | bytes 458784 | tf_op jit(solution)/shard_map/ppermute | solution.py:98
  96.6 1.2 %add_convert_fusion = bf16[64,3584]{1,0:T(8,128)(2,1)S(1)} fusion(bf16[64,3584]{1,0:T(8,128)(2,1)} %collective-permute-done.30, bf16[64,3584]{1,0:T(8,128)(2,1)S(1)} %collective-permute-done.2, bf16[64,3584]{1,0:T(8,128)(2,1)S(1)} %get-tuple-element.18), kind=kLoop, calls=%fused_computation.12 | loop fusion | flops 1376256 | bytes 1835008 | tf_op jit(solution)/shard_map/convert_element_type | solution.py:130
  97.8 0.1 collective-permute-start.31
  97.9 5.5 %fusion.3 = bf16[64,64,512]{2,1,0:T(8,128)(2,1)} fusion(bf16[64,64,576]{2,1,0:T(8,128)(2,1)} %param.16, f32[64,64,64]{1,2,0:T(8,128)S(1)} %get-tuple-element.39, f32[64,64]{1,0:T(8,128)S(1)} %get-tuple-element.38), kind=kOutput, calls=%fused_computation.3 | convolution fusion | flops 271056896 | bytes 9453568 | tf_op jit(solution)/shard_map/thj,tjc->thc/dot_general | solution.py:22
  103.4 0.8 maximum_select_fusion
  (38 shorter events, 0.2 us)
Async XLA Ops:
  2.7 1.6 %collective-permute-start = (bf16[32,3712]{1,0:T(8,128)(2,1)S(1)}, bf16[32,3712]{1,0:T(8,128)(2,1)S(1)}, u32[]{:S(2)}, u32[]{:S(2)}) collective-permute-start(bf16[32,3712]{1,0:T(8,128)(2,1)S(1)} %get-tuple-element.35), channel_id=1, source_target_pairs={{0,8},{8,0},{1,9},{9,1},{2,10},{10,2},{3,11},{11,3},{4,12},{12,4},... | collective-permute-start | bytes 712712 | tf_op jit(solution)/shard_map/ppermute | solution.py:101
  4.4 9.6 %collective-permute-start.3 = (bf16[64,3712]{1,0:T(8,128)(2,1)S(1)}, bf16[64,3712]{1,0:T(8,128)(2,1)S(1)}, u32[]{:S(2)}, u32[]{:S(2)}) collective-permute-start(bf16[64,3712]{1,0:T(8,128)(2,1)S(1)} %pad_maximum_fusion.own_ref), channel_id=1, source_target_pairs={{0,2},{10,8},{2,4},{12,10},{4,6},{14,12},{6,7},{15,14},{7,5},{13,1... | collective-permute-start | bytes 1425416 | tf_op jit(solution)/shard_map/ppermute | solution.py:98
  14.0 2.1 %collective-permute-start.22 = (bf16[64,3712]{1,0:T(8,128)(2,1)S(1)}, bf16[64,3712]{1,0:T(8,128)(2,1)S(1)}, u32[]{:S(2)}, u32[]{:S(2)}) collective-permute-start(bf16[64,3712]{1,0:T(8,128)(2,1)S(1)} %collective-permute-done.3.own_ref), channel_id=1, source_target_pairs={{0,8},{8,0},{1,9},{9,1},{2,10},{10,2},{3,11},{11,3},{4,12},{12,4},... | collective-permute-start | bytes 1425416 | tf_op jit(solution)/shard_map/ppermute | solution.py:101
  14.0 10.2 %collective-permute-start.4 = (bf16[64,3712]{1,0:T(8,128)(2,1)S(1)}, bf16[64,3712]{1,0:T(8,128)(2,1)S(1)}, u32[]{:S(2)}, u32[]{:S(2)}) collective-permute-start(bf16[64,3712]{1,0:T(8,128)(2,1)S(1)} %collective-permute-done.3.own_ref), channel_id=1, source_target_pairs={{0,2},{10,8},{2,4},{12,10},{4,6},{14,12},{6,7},{15,14},{7,5},{13,1... | collective-permute-start | bytes 1425416 | tf_op jit(solution)/shard_map/ppermute | solution.py:98
  16.1 2.0 %copy-start = (bf16[1,3584,512]{2,1,0:T(8,128)(2,1)S(1)}, bf16[1,3584,512]{2,1,0:T(8,128)(2,1)}, u32[]{:S(2)}) copy-start(bf16[1,3584,512]{2,1,0:T(8,128)(2,1)} %param.12) | copy-start | bytes 11010052
  18.1 2.0 %copy-start.2 = (bf16[1,3584,512]{2,1,0:T(8,128)(2,1)S(1)}, bf16[1,3584,512]{2,1,0:T(8,128)(2,1)}, u32[]{:S(2)}) copy-start(bf16[1,3584,512]{2,1,0:T(8,128)(2,1)} %param.13) | copy-start | bytes 11010052
  20.2 2.0 %copy-start.4 = (bf16[1,512,3584]{2,1,0:T(8,128)(2,1)S(1)}, bf16[1,512,3584]{2,1,0:T(8,128)(2,1)}, u32[]{:S(2)}) copy-start(bf16[1,512,3584]{2,1,0:T(8,128)(2,1)} %param.14) | copy-start | bytes 11010052
  22.2 5.9 %copy-start.1 = (bf16[1,3584,512]{2,1,0:T(8,128)(2,1)S(1)}, bf16[1,3584,512]{2,1,0:T(8,128)(2,1)}, u32[]{:S(2)}) copy-start(bf16[1,3584,512]{2,1,0:T(8,128)(2,1)} %param.12) | copy-start | bytes 11010052
  22.2 5.9 %copy-start.3 = (bf16[1,3584,512]{2,1,0:T(8,128)(2,1)S(1)}, bf16[1,3584,512]{2,1,0:T(8,128)(2,1)}, u32[]{:S(2)}) copy-start(bf16[1,3584,512]{2,1,0:T(8,128)(2,1)} %param.13) | copy-start | bytes 11010052
  22.2 5.9 %copy-start.5 = (bf16[1,512,3584]{2,1,0:T(8,128)(2,1)S(1)}, bf16[1,512,3584]{2,1,0:T(8,128)(2,1)}, u32[]{:S(2)}) copy-start(bf16[1,512,3584]{2,1,0:T(8,128)(2,1)} %param.14) | copy-start | bytes 11010052
  24.0 2.4 %collective-permute-start.23 = (bf16[64,3584]{1,0:T(8,128)(2,1)S(1)}, bf16[64,3584]{1,0:T(8,128)(2,1)S(1)}, u32[]{:S(2)}, u32[]{:S(2)}) collective-permute-start(bf16[64,3584]{1,0:T(8,128)(2,1)S(1)} %get-tuple-element.33), channel_id=1, source_target_pairs={{0,8},{8,0},{1,9},{9,1},{2,10},{10,2},{3,11},{11,3},{4,12},{12,4},... | collective-permute-start | bytes 1376264 | tf_op jit(solution)/shard_map/ppermute | solution.py:101
  24.2 3.9 %collective-permute-start.20 = (bf16[64,3712]{1,0:T(8,128)(2,1)S(1)}, bf16[64,3712]{1,0:T(8,128)(2,1)S(1)}, u32[]{:S(2)}, u32[]{:S(2)}) collective-permute-start(bf16[64,3712]{1,0:T(8,128)(2,1)S(1)} %collective-permute-done.4.own_ref), channel_id=1, source_target_pairs={{0,8},{8,0},{1,9},{9,1},{2,10},{10,2},{3,11},{11,3},{4,12},{12,4},... | collective-permute-start | bytes 1425416 | tf_op jit(solution)/shard_map/ppermute | solution.py:101
  24.5 8.7 %collective-permute-start.5 = (bf16[64,3712]{1,0:T(8,128)(2,1)S(1)}, bf16[64,3712]{1,0:T(8,128)(2,1)S(1)}, u32[]{:S(2)}, u32[]{:S(2)}) collective-permute-start(bf16[64,3712]{1,0:T(8,128)(2,1)S(1)} %collective-permute-done.4.own_ref), channel_id=1, source_target_pairs={{0,2},{10,8},{2,4},{12,10},{4,6},{14,12},{6,7},{15,14},{7,5},{13,1... | collective-permute-start | bytes 1425416 | tf_op jit(solution)/shard_map/ppermute | solution.py:98
  26.5 11.6 %collective-permute-start.24 = (bf16[64,3584]{1,0:T(8,128)(2,1)S(1)}, bf16[64,3584]{1,0:T(8,128)(2,1)S(1)}, u32[]{:S(2)}, u32[]{:S(2)}) collective-permute-start(bf16[64,3584]{1,0:T(8,128)(2,1)S(1)} %add_convert_fusion.7), channel_id=1, source_target_pairs={{0,2},{10,8},{2,4},{12,10},{4,6},{14,12},{6,7},{15,14},{7,5},{13,1... | collective-permute-start | bytes 1376264 | tf_op jit(solution)/shard_map/ppermute | solution.py:98
  29.9 8.2 %collective-permute-start.21 = (bf16[64,3584]{1,0:T(8,128)(2,1)S(1)}, bf16[64,3584]{1,0:T(8,128)(2,1)S(1)}, u32[]{:S(2)}, u32[]{:S(2)}) collective-permute-start(bf16[64,3584]{1,0:T(8,128)(2,1)S(1)} %get-tuple-element.31), channel_id=1, source_target_pairs={{0,8},{8,0},{1,9},{9,1},{2,10},{10,2},{3,11},{11,3},{4,12},{12,4},... | collective-permute-start | bytes 1376264 | tf_op jit(solution)/shard_map/ppermute | solution.py:101
  33.2 7.0 %collective-permute-start.18 = (bf16[64,3712]{1,0:T(8,128)(2,1)S(1)}, bf16[64,3712]{1,0:T(8,128)(2,1)S(1)}, u32[]{:S(2)}, u32[]{:S(2)}) collective-permute-start(bf16[64,3712]{1,0:T(8,128)(2,1)S(1)} %collective-permute-done.5.own_ref), channel_id=1, source_target_pairs={{0,8},{8,0},{1,9},{9,1},{2,10},{10,2},{3,11},{11,3},{4,12},{12,4},... | collective-permute-start | bytes 1425416 | tf_op jit(solution)/shard_map/ppermute | solution.py:101
  33.2 10.0 %collective-permute-start.6 = (bf16[64,3712]{1,0:T(8,128)(2,1)S(1)}, bf16[64,3712]{1,0:T(8,128)(2,1)S(1)}, u32[]{:S(2)}, u32[]{:S(2)}) collective-permute-start(bf16[64,3712]{1,0:T(8,128)(2,1)S(1)} %collective-permute-done.5.own_ref), channel_id=1, source_target_pairs={{0,2},{10,8},{2,4},{12,10},{4,6},{14,12},{6,7},{15,14},{7,5},{13,1... | collective-permute-start | bytes 1425416 | tf_op jit(solution)/shard_map/ppermute | solution.py:98
  38.3 9.8 %collective-permute-start.25 = (bf16[64,3584]{1,0:T(8,128)(2,1)S(1)}, bf16[64,3584]{1,0:T(8,128)(2,1)S(1)}, u32[]{:S(2)}, u32[]{:S(2)}) collective-permute-start(bf16[64,3584]{1,0:T(8,128)(2,1)S(1)} %add_convert_fusion.6), channel_id=1, source_target_pairs={{0,2},{10,8},{2,4},{12,10},{4,6},{14,12},{6,7},{15,14},{7,5},{13,1... | collective-permute-start | bytes 1376264 | tf_op jit(solution)/shard_map/ppermute | solution.py:98
  41.9 6.2 %collective-permute-start.19 = (bf16[64,3584]{1,0:T(8,128)(2,1)S(1)}, bf16[64,3584]{1,0:T(8,128)(2,1)S(1)}, u32[]{:S(2)}, u32[]{:S(2)}) collective-permute-start(bf16[64,3584]{1,0:T(8,128)(2,1)S(1)} %get-tuple-element.29), channel_id=1, source_target_pairs={{0,8},{8,0},{1,9},{9,1},{2,10},{10,2},{3,11},{11,3},{4,12},{12,4},... | collective-permute-start | bytes 1376264 | tf_op jit(solution)/shard_map/ppermute | solution.py:101
  43.2 7.0 %collective-permute-start.16 = (bf16[64,3712]{1,0:T(8,128)(2,1)S(1)}, bf16[64,3712]{1,0:T(8,128)(2,1)S(1)}, u32[]{:S(2)}, u32[]{:S(2)}) collective-permute-start(bf16[64,3712]{1,0:T(8,128)(2,1)S(1)} %collective-permute-done.6.own_ref), channel_id=1, source_target_pairs={{0,8},{8,0},{1,9},{9,1},{2,10},{10,2},{3,11},{11,3},{4,12},{12,4},... | collective-permute-start | bytes 1425416 | tf_op jit(solution)/shard_map/ppermute | solution.py:101
  43.2 10.0 %collective-permute-start.7 = (bf16[64,3712]{1,0:T(8,128)(2,1)S(1)}, bf16[64,3712]{1,0:T(8,128)(2,1)S(1)}, u32[]{:S(2)}, u32[]{:S(2)}) collective-permute-start(bf16[64,3712]{1,0:T(8,128)(2,1)S(1)} %collective-permute-done.6.own_ref), channel_id=1, source_target_pairs={{0,2},{10,8},{2,4},{12,10},{4,6},{14,12},{6,7},{15,14},{7,5},{13,1... | collective-permute-start | bytes 1425416 | tf_op jit(solution)/shard_map/ppermute | solution.py:98
  48.3 9.8 %collective-permute-start.26 = (bf16[64,3584]{1,0:T(8,128)(2,1)S(1)}, bf16[64,3584]{1,0:T(8,128)(2,1)S(1)}, u32[]{:S(2)}, u32[]{:S(2)}) collective-permute-start(bf16[64,3584]{1,0:T(8,128)(2,1)S(1)} %add_convert_fusion.5), channel_id=1, source_target_pairs={{0,2},{10,8},{2,4},{12,10},{4,6},{14,12},{6,7},{15,14},{7,5},{13,1... | collective-permute-start | bytes 1376264 | tf_op jit(solution)/shard_map/ppermute | solution.py:98
  51.9 6.2 %collective-permute-start.17 = (bf16[64,3584]{1,0:T(8,128)(2,1)S(1)}, bf16[64,3584]{1,0:T(8,128)(2,1)S(1)}, u32[]{:S(2)}, u32[]{:S(2)}) collective-permute-start(bf16[64,3584]{1,0:T(8,128)(2,1)S(1)} %get-tuple-element.27), channel_id=1, source_target_pairs={{0,8},{8,0},{1,9},{9,1},{2,10},{10,2},{3,11},{11,3},{4,12},{12,4},... | collective-permute-start | bytes 1376264 | tf_op jit(solution)/shard_map/ppermute | solution.py:101
  53.2 7.0 %collective-permute-start.14 = (bf16[64,3712]{1,0:T(8,128)(2,1)S(1)}, bf16[64,3712]{1,0:T(8,128)(2,1)S(1)}, u32[]{:S(2)}, u32[]{:S(2)}) collective-permute-start(bf16[64,3712]{1,0:T(8,128)(2,1)S(1)} %collective-permute-done.7.own_ref), channel_id=1, source_target_pairs={{0,8},{8,0},{1,9},{9,1},{2,10},{10,2},{3,11},{11,3},{4,12},{12,4},... | collective-permute-start | bytes 1425416 | tf_op jit(solution)/shard_map/ppermute | solution.py:101
  53.2 10.0 %collective-permute-start.8 = (bf16[64,3712]{1,0:T(8,128)(2,1)S(1)}, bf16[64,3712]{1,0:T(8,128)(2,1)S(1)}, u32[]{:S(2)}, u32[]{:S(2)}) collective-permute-start(bf16[64,3712]{1,0:T(8,128)(2,1)S(1)} %collective-permute-done.7.own_ref), channel_id=1, source_target_pairs={{0,2},{10,8},{2,4},{12,10},{4,6},{14,12},{6,7},{15,14},{7,5},{13,1... | collective-permute-start | bytes 1425416 | tf_op jit(solution)/shard_map/ppermute | solution.py:98
  58.3 9.8 %collective-permute-start.27 = (bf16[64,3584]{1,0:T(8,128)(2,1)S(1)}, bf16[64,3584]{1,0:T(8,128)(2,1)S(1)}, u32[]{:S(2)}, u32[]{:S(2)}) collective-permute-start(bf16[64,3584]{1,0:T(8,128)(2,1)S(1)} %add_convert_fusion.4), channel_id=1, source_target_pairs={{0,2},{10,8},{2,4},{12,10},{4,6},{14,12},{6,7},{15,14},{7,5},{13,1... | collective-permute-start | bytes 1376264 | tf_op jit(solution)/shard_map/ppermute | solution.py:98
  61.9 6.2 %collective-permute-start.15 = (bf16[64,3584]{1,0:T(8,128)(2,1)S(1)}, bf16[64,3584]{1,0:T(8,128)(2,1)S(1)}, u32[]{:S(2)}, u32[]{:S(2)}) collective-permute-start(bf16[64,3584]{1,0:T(8,128)(2,1)S(1)} %get-tuple-element.25), channel_id=1, source_target_pairs={{0,8},{8,0},{1,9},{9,1},{2,10},{10,2},{3,11},{11,3},{4,12},{12,4},... | collective-permute-start | bytes 1376264 | tf_op jit(solution)/shard_map/ppermute | solution.py:101
  63.2 7.2 %collective-permute-start.12 = (bf16[64,3712]{1,0:T(8,128)(2,1)S(1)}, bf16[64,3712]{1,0:T(8,128)(2,1)S(1)}, u32[]{:S(2)}, u32[]{:S(2)}) collective-permute-start(bf16[64,3712]{1,0:T(8,128)(2,1)S(1)} %collective-permute-done.8.own_ref), channel_id=1, source_target_pairs={{0,8},{8,0},{1,9},{9,1},{2,10},{10,2},{3,11},{11,3},{4,12},{12,4},... | collective-permute-start | bytes 1425416 | tf_op jit(solution)/shard_map/ppermute | solution.py:101
  63.2 10.0 %collective-permute-start.9 = (bf16[64,3712]{1,0:T(8,128)(2,1)S(1)}, bf16[64,3712]{1,0:T(8,128)(2,1)S(1)}, u32[]{:S(2)}, u32[]{:S(2)}) collective-permute-start(bf16[64,3712]{1,0:T(8,128)(2,1)S(1)} %collective-permute-done.8.own_ref), channel_id=1, source_target_pairs={{0,2},{10,8},{2,4},{12,10},{4,6},{14,12},{6,7},{15,14},{7,5},{13,1... | collective-permute-start | bytes 1425416 | tf_op jit(solution)/shard_map/ppermute | solution.py:98
  68.3 9.8 %collective-permute-start.28 = (bf16[64,3584]{1,0:T(8,128)(2,1)S(1)}, bf16[64,3584]{1,0:T(8,128)(2,1)S(1)}, u32[]{:S(2)}, u32[]{:S(2)}) collective-permute-start(bf16[64,3584]{1,0:T(8,128)(2,1)S(1)} %add_convert_fusion.3), channel_id=1, source_target_pairs={{0,2},{10,8},{2,4},{12,10},{4,6},{14,12},{6,7},{15,14},{7,5},{13,1... | collective-permute-start | bytes 1376264 | tf_op jit(solution)/shard_map/ppermute | solution.py:98
  72.1 6.0 %collective-permute-start.13 = (bf16[64,3584]{1,0:T(8,128)(2,1)S(1)}, bf16[64,3584]{1,0:T(8,128)(2,1)S(1)}, u32[]{:S(2)}, u32[]{:S(2)}) collective-permute-start(bf16[64,3584]{1,0:T(8,128)(2,1)S(1)} %get-tuple-element.23), channel_id=1, source_target_pairs={{0,8},{8,0},{1,9},{9,1},{2,10},{10,2},{3,11},{11,3},{4,12},{12,4},... | collective-permute-start | bytes 1376264 | tf_op jit(solution)/shard_map/ppermute | solution.py:101
  72.2 9.9 %collective-permute-start.1 = (bf16[64,3712]{1,0:T(8,128)(2,1)S(1)}, bf16[64,3712]{1,0:T(8,128)(2,1)S(1)}, u32[]{:S(2)}, u32[]{:S(2)}) collective-permute-start(bf16[64,3712]{1,0:T(8,128)(2,1)S(1)} %pad_maximum_fusion.own_ref), channel_id=1, source_target_pairs={{0,8},{8,0},{1,9},{9,1},{2,10},{10,2},{3,11},{11,3},{4,12},{12,4},... | collective-permute-start | bytes 1425416 | tf_op jit(solution)/shard_map/ppermute | solution.py:101
  73.2 7.0 %collective-permute-start.10 = (bf16[64,3712]{1,0:T(8,128)(2,1)S(1)}, bf16[64,3712]{1,0:T(8,128)(2,1)S(1)}, u32[]{:S(2)}, u32[]{:S(2)}) collective-permute-start(bf16[64,3712]{1,0:T(8,128)(2,1)S(1)} %collective-permute-done.9.own_ref), channel_id=1, source_target_pairs={{0,8},{8,0},{1,9},{9,1},{2,10},{10,2},{3,11},{11,3},{4,12},{12,4},... | collective-permute-start | bytes 1425416 | tf_op jit(solution)/shard_map/ppermute | solution.py:101
  78.3 3.7 %copy-start.6 = (s32[64]{0:T(128)S(1)}, s32[64]{0:T(128)}, u32[]{:S(2)}) copy-start(s32[64]{0:T(128)} %param.17) | copy-start | bytes 772
  78.3 8.5 %collective-permute-start.29 = (bf16[64,3584]{1,0:T(8,128)(2,1)S(1)}, bf16[64,3584]{1,0:T(8,128)(2,1)S(1)}, u32[]{:S(2)}, u32[]{:S(2)}) collective-permute-start(bf16[64,3584]{1,0:T(8,128)(2,1)S(1)} %add_convert_fusion.2), channel_id=1, source_target_pairs={{0,2},{10,8},{2,4},{12,10},{4,6},{14,12},{6,7},{15,14},{7,5},{13,1... | collective-permute-start | bytes 1376264 | tf_op jit(solution)/shard_map/ppermute | solution.py:98
  81.9 4.9 %collective-permute-start.11 = (bf16[64,3584]{1,0:T(8,128)(2,1)S(1)}, bf16[64,3584]{1,0:T(8,128)(2,1)S(1)}, u32[]{:S(2)}, u32[]{:S(2)}) collective-permute-start(bf16[64,3584]{1,0:T(8,128)(2,1)S(1)} %get-tuple-element.21), channel_id=1, source_target_pairs={{0,8},{8,0},{1,9},{9,1},{2,10},{10,2},{3,11},{11,3},{4,12},{12,4},... | collective-permute-start | bytes 1376264 | tf_op jit(solution)/shard_map/ppermute | solution.py:101
  83.8 11.5 %collective-permute-start.2 = (bf16[64,3584]{1,0:T(8,128)(2,1)S(1)}, bf16[64,3584]{1,0:T(8,128)(2,1)S(1)}, u32[]{:S(2)}, u32[]{:S(2)}) collective-permute-start(bf16[64,3584]{1,0:T(8,128)(2,1)S(1)} %get-tuple-element.19), channel_id=1, source_target_pairs={{0,8},{8,0},{1,9},{9,1},{2,10},{10,2},{3,11},{11,3},{4,12},{12,4},... | collective-permute-start | bytes 1376264 | tf_op jit(solution)/shard_map/ppermute | solution.py:101
  87.8 8.8 %collective-permute-start.30 = (bf16[64,3584]{1,0:T(8,128)(2,1)}, bf16[64,3584]{1,0:T(8,128)(2,1)}, u32[]{:S(2)}, u32[]{:S(2)}) collective-permute-start(bf16[64,3584]{1,0:T(8,128)(2,1)} %add_convert_fusion.1), channel_id=1, source_target_pairs={{0,2},{10,8},{2,4},{12,10},{4,6},{14,12},{6,7},{15,14},{7,5},{13,1... | collective-permute-start | bytes 1376264 | tf_op jit(solution)/shard_map/ppermute | solution.py:98
  97.8 5.6 %collective-permute-start.31 = (bf16[32,3584]{1,0:T(8,128)(2,1)S(1)}, bf16[32,3584]{1,0:T(8,128)(2,1)S(1)}, u32[]{:S(2)}, u32[]{:S(2)}) collective-permute-start(bf16[32,3584]{1,0:T(8,128)(2,1)S(1)} %get-tuple-element.37), channel_id=1, source_target_pairs={{0,8},{8,0},{1,9},{9,1},{2,10},{10,2},{3,11},{11,3},{4,12},{12,4},... | collective-permute-start | bytes 688136 | tf_op jit(solution)/shard_map/ppermute | solution.py:101

commit v3 on v2

--- a/solution.py
+++ b/solution.py
@@ -10,7 +10,7 @@
 LANES = 128
 
 
-def attend(queries, latent_cache, cache_lengths, latent_width):
+def attention_probs(queries, latent_cache, cache_lengths):
     scores = SOFTMAX_SCALE * jnp.einsum(
         "thc,tjc->thj", queries, latent_cache, preferred_element_type=jnp.float32
     )
@@ -18,16 +18,11 @@
     scores = jnp.where(valid_mask, scores, -1e30)
     row_peak = jnp.max(scores, axis=2, keepdims=True)
     exp_terms = jnp.where(valid_mask, jnp.exp(scores - row_peak), 0.0)
-    attn_probs = (exp_terms / jnp.sum(exp_terms, axis=2, keepdims=True)).astype(jnp.bfloat16)
-    return jnp.einsum(
-        "thj,tjc->thc",
-        attn_probs,
-        latent_cache[:, :, :latent_width],
-        preferred_element_type=jnp.float32,
-    ).astype(jnp.bfloat16)
+    return (exp_terms / jnp.sum(exp_terms, axis=2, keepdims=True)).astype(jnp.bfloat16)
 
 
-def expert_kernel(expert_ref, own_ref, other_ref, gate_ref, up_ref, down_ref, own_out, other_out):
+def expert_kernel(expert_ref, own_ref, other_ref, gate_ref, up_ref, down_ref, *rest):
+    own_out, other_out = rest[-2:]
     rows, width = own_out.shape
     x = jnp.concatenate([own_ref[:, :width], other_ref[:, :width]], axis=0)
     gate = jnp.dot(x, gate_ref[...], preferred_element_type=jnp.float32)
@@ -41,7 +36,7 @@
         out[...] = (weight * down[at : at + rows]).astype(jnp.bfloat16)
 
 
-def run_experts(expert, own, other, gate, up, down):
+def run_experts(expert, own, other, gate, up, down, after=()):
     rows, wide = own.shape
     width, hidden = gate.shape
 
@@ -59,7 +54,8 @@
                 whole((width, hidden)),
                 whole((width, hidden)),
                 whole((hidden, width)),
-            ],
+            ]
+            + [pl.BlockSpec(memory_space=pl.ANY)] * len(after),
             out_specs=[whole((rows, width)), whole((rows, width))],
         ),
         out_shape=[jax.ShapeDtypeStruct((rows, width), jnp.bfloat16)] * 2,
@@ -70,7 +66,7 @@
             transcendentals=2 * rows * hidden,
         ),
         name="expert_half",
-    )(expert, own, other, gate, up, down)
+    )(expert, own, other, gate, up, down, *after)
 
 
 def ring_order(count):
@@ -87,15 +83,16 @@
     part = rows // 2
     node = lax.axis_index("node")
     order = ring_order(local_count)
-    hops = []
+    hops, hops_in, hops_out = [], [], []
     for i in range(local_count):
         here, there = order[i], order[(i + 1) % local_count]
-        hops.append((here, there))
-        hops.append((local_count + there, local_count + here))
+        hops += [(here, there), (local_count + there, local_count + here)]
+        hops_in += [(local_count + here, there), (there, local_count + here)]
+        hops_out += [(here, local_count + there), (local_count + there, here)]
     expert = ((node * local_count + lax.axis_index("local")) // 2).astype(jnp.int32).reshape(1)
 
-    def onward(a):
-        return lax.ppermute(a, ("node", "local"), hops)
+    def onward(a, pairs=hops):
+        return lax.ppermute(a, ("node", "local"), pairs)
 
     def across(a):
         return lax.ppermute(a, "node", [(0, 1), (1, 0)])
@@ -108,18 +105,20 @@
     first = node == 0
     kept = jnp.where(first, mine[:part], mine[part:])
     given = jnp.where(first, mine[part:], mine[:part])
-    gate, up, down = [
-        pltpu.with_memory_space_constraint(w[0], pltpu.VMEM) for w in (w_gate, w_up, w_down)
-    ]
+    gate, up, down = w_gate[0], w_up[0], w_down[0]
 
-    block = jnp.concatenate([kept, across(given)], axis=0)
-    own_sums, other_sums = [], []
-    for k in range(local_count):
-        if k:
+    block = jnp.concatenate([onward(kept), onward(given, hops_in)], axis=0)
+    probs = attention_probs(queries, latent_cache, cache_lengths)
+    own, other = run_experts(expert, mine, across(mine), gate, up, down)
+    own_sums, other_sums = [own], [across(other)]
+    after = (own, probs)
+    for k in range(1, local_count):
+        if k > 1:
             block = onward(block)
-        own, other = run_experts(expert, block, across(block), gate, up, down)
+        own, other = run_experts(expert, block, across(block), gate, up, down, after)
         own_sums.append(own)
         other_sums.append(across(other))
+        after = ()
 
     def chip_sum(k):
         return own_sums[k].astype(jnp.float32) + other_sums[k].astype(jnp.float32)
@@ -127,15 +126,15 @@
     running = chip_sum(1).astype(jnp.bfloat16)
     for k in range(2, local_count):
         running = (chip_sum(k) + onward(running).astype(jnp.float32)).astype(jnp.bfloat16)
-    total = (chip_sum(0) + onward(running).astype(jnp.float32)).astype(jnp.bfloat16)
-    mine_out, back = total[:part], across(total[part:])
-    moe_out = jnp.where(
-        first,
-        jnp.concatenate([mine_out, back], axis=0),
-        jnp.concatenate([back, mine_out], axis=0),
+    same, cross = onward(running[:part]), onward(running[part:], hops_out)
+    arrived = jnp.where(
+        first, jnp.concatenate([same, cross], axis=0), jnp.concatenate([cross, same], axis=0)
     )
+    moe_out = (chip_sum(0) + arrived.astype(jnp.float32)).astype(jnp.bfloat16)
 
-    attn_latent = attend(queries, latent_cache, cache_lengths, LAT)
+    attn_latent = jnp.einsum(
+        "thj,tjc->thc", probs, latent_cache[:, :, :LAT], preferred_element_type=jnp.float32
+    ).astype(jnp.bfloat16)
     return (moe_out, attn_latent)
 
 

time: 105 us -> 101 us (0.962)
  starting transfers between devices: 30 us -> 26.7 us
  matrix products: 11.2 us -> 9.24 us
  other arithmetic: 6.11 us -> 7.38 us
    ppermute x14 -> x16, starting transfers between devices: 27.3 us -> 24.3 us  [onward(): return lax.ppermute(a, ('node', 'local'), pairs)]
    dot_general x1, matrix products: 5.51 us -> 3.24 us  [on_device(): jnp.einsum('thj,tjc->thc', probs, latent_cache[:, :, :LAT], preferred_ele...]
    lt x1, other arithmetic: 0.07 us -> 1.33 us  [attention_probs(): jnp.arange(latent_cache.shape[1])[None, :] < cache_lengths[:, None]]
    ppermute x18 -> x16, waiting for transfers between devices: 1.17 us -> 0.04 us  [across(): return lax.ppermute(a, 'node', [(0, 1), (1, 0)])]
    unnamed x14 -> x11, local copies, waits for them, and re-layouts: 6.13 us -> 5.2 us
    select_n x2 -> x1, other arithmetic: 2.1 us -> 1.39 us  [on_device(): given = jnp.where(first, mine[part:], mine[:part])]
    ppermute x14 -> x16, waiting for transfers between devices: 35 us -> 35.6 us  [onward(): return lax.ppermute(a, ('node', 'local'), pairs)]
    ppermute x18 -> x16, starting transfers between devices: 2.66 us -> 2.44 us  [across(): return lax.ppermute(a, 'node', [(0, 1), (1, 0)])]
  transfers between devices with their start and end apart: 32 -> 32, of which waited for: 14 -> 13; matrix products, arithmetic and copies ran while one was open for 13% -> 16% of each run, Pallas kernels for 13% -> 14%
where the time goes in v3:
time: 101 us; the launch traced here: 99.9 us
  waiting for transfers between devices  35.7 us (35%)
  starting transfers between devices  26.7 us (26%)
  Pallas kernels  13.7 us (14%)
  matrix products  9.24 us (9%)
  other arithmetic  7.38 us (7%)
  local copies, waits for them, and re-layouts  6.28 us (6%)
    ppermute x16, waiting for transfers between devices, onward(): return lax.ppermute(a, ('node', 'local'), pairs)  35.6 us
    ppermute x16, starting transfers between devices, onward(): return lax.ppermute(a, ('node', 'local'), pairs)  24.3 us
    pallas_call x8, Pallas kernels, run_experts(): pl.pallas_call(expert_kernel, grid_spec=pltpu.PrefetchScalarGridSpec(num_...  13.7 us
    sub x1, matrix products, attention_probs(): exp_terms = jnp.where(valid_mask, jnp.exp(scores - row_peak), 0.0)  6 us
    unnamed x11, local copies, waits for them, and re-layouts  5.2 us
    dot_general x1, matrix products, on_device(): jnp.einsum('thj,tjc->thc', probs, latent_cache[:, :, :LAT], preferred_ele...  3.24 us
    ppermute x16, starting transfers between devices, across(): return lax.ppermute(a, 'node', [(0, 1), (1, 0)])  2.44 us
  transfers between devices with their start and end apart: 32, of which 13 were waited for; matrix products, arithmetic and copies ran while one was open for 16% of the time, Pallas kernels for 14%

profile of v3, /device:TPU:0, one launch (start us, length us, event | category | flops | bytes accessed | tf_op | source)
XLA Modules:
  0.0 99.9 jit_solution(13028567322450561428)
XLA Ops:
  0.6 0.8 fusion.13
  1.5 1.1 %pad_maximum_fusion.own_ref = bf16[64,3712]{1,0:T(8,128)(2,1)S(1)} fusion(bf16[64,128]{1,0:T(8,128)(2,1)S(1)} %fusion.13, bf16[64,3584]{1,0:T(8,128)(2,1)} %param.9), kind=kLoop, calls=%fused_computation.21 | loop fusion | flops 950272 | bytes 950272 | tf_op jit(solution)/shard_map/concatenate | solution.py:104
  2.5 0.5 collective-permute-start
  3.0 1.4 %broadcast_select_fusion = (bf16[32,3712]{1,0:T(8,128)(2,1)S(1)}, bf16[32,3712]{1,0:T(8,128)(2,1)S(1)}) fusion(pred[]{:T(512)S(6)} %eq.19, bf16[64,128]{1,0:T(8,128)(2,1)S(1)} %fusion.13, bf16[64,3584]{1,0:T(8,128)(2,1)} %param.9), kind=kLoop, calls=%fused_computation.27 | loop fusion | flops 2138112 | bytes 950273 | tf_op jit(solution)/shard_map/jit(_where)/select_n | solution.py:107
  4.4 2.6 %collective-permute-start.2 = (bf16[32,3712]{1,0:T(8,128)(2,1)S(1)}, bf16[32,3712]{1,0:T(8,128)(2,1)}, u32[]{:S(2)}, u32[]{:S(2)}) collective-permute-start(bf16[32,3712]{1,0:T(8,128)(2,1)S(1)} %get-tuple-element.35), channel_id=1, source_target_pairs={{0,2},{10,8},{2,4},{12,10},{4,6},{14,12},{6,7},{15,14},{7,5},{13,1... | collective-permute-start | bytes 712712 | tf_op jit(solution)/shard_map/ppermute | solution.py:95
  7.1 1.3 %collective-permute-start.3 = (bf16[32,3712]{1,0:T(8,128)(2,1)S(1)}, bf16[32,3712]{1,0:T(8,128)(2,1)}, u32[]{:S(2)}, u32[]{:S(2)}) collective-permute-start(bf16[32,3712]{1,0:T(8,128)(2,1)S(1)} %get-tuple-element.34), channel_id=1, source_target_pairs={{8,2},{2,8},{10,4},{4,10},{12,6},{6,12},{14,7},{7,14},{15,5},{5,15... | collective-permute-start | bytes 712712 | tf_op jit(solution)/shard_map/ppermute | solution.py:95
  8.4 1.3 %iota_compare_fusion.1 = pred[64,64]{1,0:T(8,128)(4,1)} fusion(s32[64]{0:T(128)} %param.17), kind=kLoop, calls=%fused_computation.32 | loop fusion | flops 4096 | bytes 4352 | tf_op jit(solution)/shard_map/lt | solution.py:17
  9.7 6.0 %fusion.17 = (f32[64,64]{1,0:T(8,128)S(1)}, f32[64,64,64]{2,1,0:T(8,128)S(1)}) fusion(pred[64,64]{1,0:T(8,128)(4,1)} %iota_compare_fusion.1, bf16[64,64,576]{2,1,0:T(8,128)(2,1)} %param.15, bf16[64,64,576]{2,1,0:T(8,128)(2,1)} %param.16), kind=kOutput, calls=%fused_computation.38 | convolution fusion | flops 303300672 | bytes 10506240 | tf_op jit(solution)/shard_map/sub | solution.py:20
  15.8 1.1 %constant_dynamic-update-slice_fusion.1 = bf16[64,3712]{1,0:T(8,128)(2,1)S(1)} fusion(bf16[32,3712]{1,0:T(8,128)(2,1)} %collective-permute-done.2), kind=kLoop, calls=%fused_computation.34 | loop fusion | bytes 475136
  16.9 1.0 %constant_dynamic-update-slice_fusion.own_ref = bf16[64,3712]{1,0:T(8,128)(2,1)S(1)} fusion(bf16[64,3712]{1,0:T(8,128)(2,1)S(1)} %constant_dynamic-update-slice_fusion.1, bf16[32,3712]{1,0:T(8,128)(2,1)} %collective-permute-done.3), kind=kLoop, calls=%fused_computation.33 | loop fusion | bytes 475136 | tf_op jit(solution)/shard_map/concatenate | solution.py:110
  17.9 0.4 collective-permute-start.22
  18.4 0.7 divide_convert_fusion.rest_1_
  19.1 1.6 %collective-permute-start.4 = (bf16[64,3712]{1,0:T(8,128)(2,1)S(1)}, bf16[64,3712]{1,0:T(8,128)(2,1)S(1)}, u32[]{:S(2)}, u32[]{:S(2)}) collective-permute-start(bf16[64,3712]{1,0:T(8,128)(2,1)S(1)} %constant_dynamic-update-slice_fusion.own_ref), channel_id=1, source_target_pairs={{0,2},{10,8},{2,4},{12,10},{4,6},{14,12},{6,7},{15,14},{7,5},{13,1... | collective-permute-start | bytes 1425416 | tf_op jit(solution)/shard_map/ppermute | solution.py:95
  20.7 2.0 %copy-done.1 = bf16[1,3584,512]{2,1,0:T(8,128)(2,1)S(1)} copy-done((bf16[1,3584,512]{2,1,0:T(8,128)(2,1)S(1)}, bf16[1,3584,512]{2,1,0:T(8,128)(2,1)}, u32[]{:S(2)}) %copy-start.1) | copy-done | bytes 3670040
  22.8 2.0 %copy-done.2 = bf16[1,512,3584]{2,1,0:T(8,128)(2,1)S(1)} copy-done((bf16[1,512,3584]{2,1,0:T(8,128)(2,1)S(1)}, bf16[1,512,3584]{2,1,0:T(8,128)(2,1)}, u32[]{:S(2)}) %copy-start.2) | copy-done | bytes 3670040
  24.8 1.7 %expert_half.8 = (bf16[64,3584]{1,0:T(8,128)(2,1)S(1)}, bf16[64,3584]{1,0:T(8,128)(2,1)S(1)}) custom-call(s32[1]{0:T(128)} %bitcast.expert_ref, bf16[64,3712]{1,0:T(8,128)(2,1)S(1)} %pad_maximum_fusion.own_ref, bf16[64,3712]{1,0:T(8,128)(2,1)S(1)} %collective-permute-done.other_ref, bf16[3584,512]{1,0:T(8,128)(2,1)S(1)} %bitcast.7, ...), custom_call_target="tpu_custom_call" | custom-call | flops 1409286144 | bytes 11010048 | tf_op jit(solution)/shard_map/expert_half/pallas_call | solution.py:46
  26.6 1.7 %expert_half.15 = (bf16[64,3584]{1,0:T(8,128)(2,1)S(1)}, bf16[64,3584]{1,0:T(8,128)(2,1)S(1)}) custom-call(s32[1]{0:T(128)} %bitcast.expert_ref, bf16[64,3712]{1,0:T(8,128)(2,1)S(1)} %constant_dynamic-update-slice_fusion.own_ref, bf16[64,3712]{1,0:T(8,128)(2,1)S(1)} %collective-permute-done.22.other_ref, bf16[3584,512]{1,0:T(8,128)(2,1)S(1)} %bitcast.8, ...), custom_call_target="tpu_custom_call" | custom-call | flops 1409286144 | bytes 11010048 | tf_op jit(solution)/shard_map/expert_half/pallas_call | solution.py:46
  28.3 0.1 collective-permute-start.23
  28.4 0.5 collective-permute-start.20
  28.9 1.5 %collective-permute-start.5 = (bf16[64,3712]{1,0:T(8,128)(2,1)S(1)}, bf16[64,3712]{1,0:T(8,128)(2,1)S(1)}, u32[]{:S(2)}, u32[]{:S(2)}) collective-permute-start(bf16[64,3712]{1,0:T(8,128)(2,1)S(1)} %collective-permute-done.4.own_ref), channel_id=1, source_target_pairs={{0,2},{10,8},{2,4},{12,10},{4,6},{14,12},{6,7},{15,14},{7,5},{13,1... | collective-permute-start | bytes 1425416 | tf_op jit(solution)/shard_map/ppermute | solution.py:95
  30.4 0.1 add_convert_fusion.7
  30.5 1.4 %collective-permute-start.24 = (bf16[64,3584]{1,0:T(8,128)(2,1)S(1)}, bf16[64,3584]{1,0:T(8,128)(2,1)S(1)}, u32[]{:S(2)}, u32[]{:S(2)}) collective-permute-start(bf16[64,3584]{1,0:T(8,128)(2,1)S(1)} %add_convert_fusion.7), channel_id=1, source_target_pairs={{0,2},{10,8},{2,4},{12,10},{4,6},{14,12},{6,7},{15,14},{7,5},{13,1... | collective-permute-start | bytes 1376264 | tf_op jit(solution)/shard_map/ppermute | solution.py:95
  31.9 1.7 %expert_half.14 = (bf16[64,3584]{1,0:T(8,128)(2,1)S(1)}, bf16[64,3584]{1,0:T(8,128)(2,1)S(1)}) custom-call(s32[1]{0:T(128)} %bitcast.expert_ref, bf16[64,3712]{1,0:T(8,128)(2,1)S(1)} %collective-permute-done.4.own_ref, bf16[64,3712]{1,0:T(8,128)(2,1)S(1)} %collective-permute-done.20.other_ref, bf16[3584,512]{1,0:T(8,128)(2,1)S(1)} %bitcast.9, ...), custom_call_target="tpu_custom_call" | custom-call | flops 1409286144 | bytes 11010048 | tf_op jit(solution)/shard_map/expert_half/pallas_call | solution.py:46
  33.6 0.1 collective-permute-start.21
  33.7 3.9 %collective-permute-done.5.own_ref = bf16[64,3712]{1,0:T(8,128)(2,1)S(1)} collective-permute-done((bf16[64,3712]{1,0:T(8,128)(2,1)S(1)}, bf16[64,3712]{1,0:T(8,128)(2,1)S(1)}, u32[]{:S(2)}, u32[]{:S(2)}) %collective-permute-start.5) | collective-permute-done | bytes 475168 | tf_op jit(solution)/shard_map/ppermute | solution.py:95
  37.5 1.5 %collective-permute-start.6 = (bf16[64,3712]{1,0:T(8,128)(2,1)S(1)}, bf16[64,3712]{1,0:T(8,128)(2,1)S(1)}, u32[]{:S(2)}, u32[]{:S(2)}) collective-permute-start(bf16[64,3712]{1,0:T(8,128)(2,1)S(1)} %collective-permute-done.5.own_ref), channel_id=1, source_target_pairs={{0,2},{10,8},{2,4},{12,10},{4,6},{14,12},{6,7},{15,14},{7,5},{13,1... | collective-permute-start | bytes 1425416 | tf_op jit(solution)/shard_map/ppermute | solution.py:95
  39.1 3.4 %collective-permute-done.24 = bf16[64,3584]{1,0:T(8,128)(2,1)S(1)} collective-permute-done((bf16[64,3584]{1,0:T(8,128)(2,1)S(1)}, bf16[64,3584]{1,0:T(8,128)(2,1)S(1)}, u32[]{:S(2)}, u32[]{:S(2)}) %collective-permute-start.24) | collective-permute-done | bytes 458784 | tf_op jit(solution)/shard_map/ppermute | solution.py:95
  42.4 0.2 add_convert_fusion.6
  42.6 1.6 %collective-permute-start.25 = (bf16[64,3584]{1,0:T(8,128)(2,1)S(1)}, bf16[64,3584]{1,0:T(8,128)(2,1)S(1)}, u32[]{:S(2)}, u32[]{:S(2)}) collective-permute-start(bf16[64,3584]{1,0:T(8,128)(2,1)S(1)} %add_convert_fusion.6), channel_id=1, source_target_pairs={{0,2},{10,8},{2,4},{12,10},{4,6},{14,12},{6,7},{15,14},{7,5},{13,1... | collective-permute-start | bytes 1376264 | tf_op jit(solution)/shard_map/ppermute | solution.py:95
  44.2 1.7 %expert_half.13 = (bf16[64,3584]{1,0:T(8,128)(2,1)S(1)}, bf16[64,3584]{1,0:T(8,128)(2,1)S(1)}) custom-call(s32[1]{0:T(128)} %bitcast.expert_ref, bf16[64,3712]{1,0:T(8,128)(2,1)S(1)} %collective-permute-done.5.own_ref, bf16[64,3712]{1,0:T(8,128)(2,1)S(1)} %collective-permute-done.18.other_ref, bf16[3584,512]{1,0:T(8,128)(2,1)S(1)} %bitcast.10, ...), custom_call_target="tpu_custom_call" | custom-call | flops 1409286144 | bytes 11010048 | tf_op jit(solution)/shard_map/expert_half/pallas_call | solution.py:46
  45.9 0.1 collective-permute-start.19
  46.0 1.5 %collective-permute-done.6.own_ref = bf16[64,3712]{1,0:T(8,128)(2,1)S(1)} collective-permute-done((bf16[64,3712]{1,0:T(8,128)(2,1)S(1)}, bf16[64,3712]{1,0:T(8,128)(2,1)S(1)}, u32[]{:S(2)}, u32[]{:S(2)}) %collective-permute-start.6) | collective-permute-done | bytes 475168 | tf_op jit(solution)/shard_map/ppermute | solution.py:95
  47.5 1.5 %collective-permute-start.7 = (bf16[64,3712]{1,0:T(8,128)(2,1)S(1)}, bf16[64,3712]{1,0:T(8,128)(2,1)S(1)}, u32[]{:S(2)}, u32[]{:S(2)}) collective-permute-start(bf16[64,3712]{1,0:T(8,128)(2,1)S(1)} %collective-permute-done.6.own_ref), channel_id=1, source_target_pairs={{0,2},{10,8},{2,4},{12,10},{4,6},{14,12},{6,7},{15,14},{7,5},{13,1... | collective-permute-start | bytes 1425416 | tf_op jit(solution)/shard_map/ppermute | solution.py:95
  49.1 3.4 %collective-permute-done.25 = bf16[64,3584]{1,0:T(8,128)(2,1)S(1)} collective-permute-done((bf16[64,3584]{1,0:T(8,128)(2,1)S(1)}, bf16[64,3584]{1,0:T(8,128)(2,1)S(1)}, u32[]{:S(2)}, u32[]{:S(2)}) %collective-permute-start.25) | collective-permute-done | bytes 458784 | tf_op jit(solution)/shard_map/ppermute | solution.py:95
  52.4 0.2 add_convert_fusion.5
  52.6 1.8 %collective-permute-start.26 = (bf16[64,3584]{1,0:T(8,128)(2,1)S(1)}, bf16[64,3584]{1,0:T(8,128)(2,1)S(1)}, u32[]{:S(2)}, u32[]{:S(2)}) collective-permute-start(bf16[64,3584]{1,0:T(8,128)(2,1)S(1)} %add_convert_fusion.5), channel_id=1, source_target_pairs={{0,2},{10,8},{2,4},{12,10},{4,6},{14,12},{6,7},{15,14},{7,5},{13,1... | collective-permute-start | bytes 1376264 | tf_op jit(solution)/shard_map/ppermute | solution.py:95
  54.4 1.7 %expert_half.12 = (bf16[64,3584]{1,0:T(8,128)(2,1)S(1)}, bf16[64,3584]{1,0:T(8,128)(2,1)S(1)}) custom-call(s32[1]{0:T(128)} %bitcast.expert_ref, bf16[64,3712]{1,0:T(8,128)(2,1)S(1)} %collective-permute-done.6.own_ref, bf16[64,3712]{1,0:T(8,128)(2,1)S(1)} %collective-permute-done.16.other_ref, bf16[3584,512]{1,0:T(8,128)(2,1)S(1)} %bitcast.11, ...), custom_call_target="tpu_custom_call" | custom-call | flops 1409286144 | bytes 11010048 | tf_op jit(solution)/shard_map/expert_half/pallas_call | solution.py:46
  56.1 0.1 collective-permute-start.17
  56.2 1.4 %collective-permute-done.7.own_ref = bf16[64,3712]{1,0:T(8,128)(2,1)S(1)} collective-permute-done((bf16[64,3712]{1,0:T(8,128)(2,1)S(1)}, bf16[64,3712]{1,0:T(8,128)(2,1)S(1)}, u32[]{:S(2)}, u32[]{:S(2)}) %collective-permute-start.7) | collective-permute-done | bytes 475168 | tf_op jit(solution)/shard_map/ppermute | solution.py:95
  57.5 1.5 %collective-permute-start.8 = (bf16[64,3712]{1,0:T(8,128)(2,1)S(1)}, bf16[64,3712]{1,0:T(8,128)(2,1)S(1)}, u32[]{:S(2)}, u32[]{:S(2)}) collective-permute-start(bf16[64,3712]{1,0:T(8,128)(2,1)S(1)} %collective-permute-done.7.own_ref), channel_id=1, source_target_pairs={{0,2},{10,8},{2,4},{12,10},{4,6},{14,12},{6,7},{15,14},{7,5},{13,1... | collective-permute-start | bytes 1425416 | tf_op jit(solution)/shard_map/ppermute | solution.py:95
  59.1 3.4 %collective-permute-done.26 = bf16[64,3584]{1,0:T(8,128)(2,1)S(1)} collective-permute-done((bf16[64,3584]{1,0:T(8,128)(2,1)S(1)}, bf16[64,3584]{1,0:T(8,128)(2,1)S(1)}, u32[]{:S(2)}, u32[]{:S(2)}) %collective-permute-start.26) | collective-permute-done | bytes 458784 | tf_op jit(solution)/shard_map/ppermute | solution.py:95
  62.5 0.2 add_convert_fusion.4
  62.6 1.6 %collective-permute-start.27 = (bf16[64,3584]{1,0:T(8,128)(2,1)S(1)}, bf16[64,3584]{1,0:T(8,128)(2,1)S(1)}, u32[]{:S(2)}, u32[]{:S(2)}) collective-permute-start(bf16[64,3584]{1,0:T(8,128)(2,1)S(1)} %add_convert_fusion.4), channel_id=1, source_target_pairs={{0,2},{10,8},{2,4},{12,10},{4,6},{14,12},{6,7},{15,14},{7,5},{13,1... | collective-permute-start | bytes 1376264 | tf_op jit(solution)/shard_map/ppermute | solution.py:95
  64.2 1.7 %expert_half.11 = (bf16[64,3584]{1,0:T(8,128)(2,1)S(1)}, bf16[64,3584]{1,0:T(8,128)(2,1)S(1)}) custom-call(s32[1]{0:T(128)} %bitcast.expert_ref, bf16[64,3712]{1,0:T(8,128)(2,1)S(1)} %collective-permute-done.7.own_ref, bf16[64,3712]{1,0:T(8,128)(2,1)S(1)} %collective-permute-done.14.other_ref, bf16[3584,512]{1,0:T(8,128)(2,1)S(1)} %bitcast.12, ...), custom_call_target="tpu_custom_call" | custom-call | flops 1409286144 | bytes 11010048 | tf_op jit(solution)/shard_map/expert_half/pallas_call | solution.py:46
  66.0 1.5 %collective-permute-done.8.own_ref = bf16[64,3712]{1,0:T(8,128)(2,1)S(1)} collective-permute-done((bf16[64,3712]{1,0:T(8,128)(2,1)S(1)}, bf16[64,3712]{1,0:T(8,128)(2,1)S(1)}, u32[]{:S(2)}, u32[]{:S(2)}) %collective-permute-start.8) | collective-permute-done | bytes 475168 | tf_op jit(solution)/shard_map/ppermute | solution.py:95
  67.5 1.5 %collective-permute-start.9 = (bf16[64,3712]{1,0:T(8,128)(2,1)S(1)}, bf16[64,3712]{1,0:T(8,128)(2,1)S(1)}, u32[]{:S(2)}, u32[]{:S(2)}) collective-permute-start(bf16[64,3712]{1,0:T(8,128)(2,1)S(1)} %collective-permute-done.8.own_ref), channel_id=1, source_target_pairs={{0,2},{10,8},{2,4},{12,10},{4,6},{14,12},{6,7},{15,14},{7,5},{13,1... | collective-permute-start | bytes 1425416 | tf_op jit(solution)/shard_map/ppermute | solution.py:95
  69.1 3.4 %collective-permute-done.27 = bf16[64,3584]{1,0:T(8,128)(2,1)S(1)} collective-permute-done((bf16[64,3584]{1,0:T(8,128)(2,1)S(1)}, bf16[64,3584]{1,0:T(8,128)(2,1)S(1)}, u32[]{:S(2)}, u32[]{:S(2)}) %collective-permute-start.27) | collective-permute-done | bytes 458784 | tf_op jit(solution)/shard_map/ppermute | solution.py:95
  72.5 0.2 add_convert_fusion.3
  72.6 1.6 %collective-permute-start.28 = (bf16[64,3584]{1,0:T(8,128)(2,1)S(1)}, bf16[64,3584]{1,0:T(8,128)(2,1)S(1)}, u32[]{:S(2)}, u32[]{:S(2)}) collective-permute-start(bf16[64,3584]{1,0:T(8,128)(2,1)S(1)} %add_convert_fusion.3), channel_id=1, source_target_pairs={{0,2},{10,8},{2,4},{12,10},{4,6},{14,12},{6,7},{15,14},{7,5},{13,1... | collective-permute-start | bytes 1376264 | tf_op jit(solution)/shard_map/ppermute | solution.py:95
  74.2 1.7 %expert_half.10 = (bf16[64,3584]{1,0:T(8,128)(2,1)S(1)}, bf16[64,3584]{1,0:T(8,128)(2,1)S(1)}) custom-call(s32[1]{0:T(128)} %bitcast.expert_ref, bf16[64,3712]{1,0:T(8,128)(2,1)S(1)} %collective-permute-done.8.own_ref, bf16[64,3712]{1,0:T(8,128)(2,1)S(1)} %collective-permute-done.12.other_ref, bf16[3584,512]{1,0:T(8,128)(2,1)S(1)} %bitcast.13, ...), custom_call_target="tpu_custom_call" | custom-call | flops 1409286144 | bytes 11010048 | tf_op jit(solution)/shard_map/expert_half/pallas_call | solution.py:46
  76.0 1.5 %collective-permute-done.9.own_ref = bf16[64,3712]{1,0:T(8,128)(2,1)S(1)} collective-permute-done((bf16[64,3712]{1,0:T(8,128)(2,1)S(1)}, bf16[64,3712]{1,0:T(8,128)(2,1)S(1)}, u32[]{:S(2)}, u32[]{:S(2)}) %collective-permute-start.9) | collective-permute-done | bytes 475168 | tf_op jit(solution)/shard_map/ppermute | solution.py:95
  77.6 4.9 %collective-permute-done.28 = bf16[64,3584]{1,0:T(8,128)(2,1)S(1)} collective-permute-done((bf16[64,3584]{1,0:T(8,128)(2,1)S(1)}, bf16[64,3584]{1,0:T(8,128)(2,1)S(1)}, u32[]{:S(2)}, u32[]{:S(2)}) %collective-permute-start.28) | collective-permute-done | bytes 458784 | tf_op jit(solution)/shard_map/ppermute | solution.py:95
  82.5 0.2 add_convert_fusion.2
  82.7 1.6 %collective-permute-start.29 = (bf16[64,3584]{1,0:T(8,128)(2,1)S(1)}, bf16[64,3584]{1,0:T(8,128)(2,1)S(1)}, u32[]{:S(2)}, u32[]{:S(2)}) collective-permute-start(bf16[64,3584]{1,0:T(8,128)(2,1)S(1)} %add_convert_fusion.2), channel_id=1, source_target_pairs={{0,2},{10,8},{2,4},{12,10},{4,6},{14,12},{6,7},{15,14},{7,5},{13,1... | collective-permute-start | bytes 1376264 | tf_op jit(solution)/shard_map/ppermute | solution.py:95
  84.2 1.7 %expert_half.9 = (bf16[64,3584]{1,0:T(8,128)(2,1)S(1)}, bf16[64,3584]{1,0:T(8,128)(2,1)S(1)}) custom-call(s32[1]{0:T(128)} %bitcast.expert_ref, bf16[64,3712]{1,0:T(8,128)(2,1)S(1)} %collective-permute-done.9.own_ref, bf16[64,3712]{1,0:T(8,128)(2,1)S(1)} %collective-permute-done.10.other_ref, bf16[3584,512]{1,0:T(8,128)(2,1)S(1)} %bitcast.14, ...), custom_call_target="tpu_custom_call" | custom-call | flops 1409286144 | bytes 11010048 | tf_op jit(solution)/shard_map/expert_half/pallas_call | solution.py:46
  86.0 0.1 collective-permute-start.11
  86.0 0.5 collective-permute-start.1
  86.5 4.6 %collective-permute-done.29 = bf16[64,3584]{1,0:T(8,128)(2,1)S(1)} collective-permute-done((bf16[64,3584]{1,0:T(8,128)(2,1)S(1)}, bf16[64,3584]{1,0:T(8,128)(2,1)S(1)}, u32[]{:S(2)}, u32[]{:S(2)}) %collective-permute-start.29) | collective-permute-done | bytes 458784 | tf_op jit(solution)/shard_map/ppermute | solution.py:95
  91.2 0.2 add_convert_fusion.1
  91.4 1.6 %collective-permute-start.30 = (bf16[32,3584]{1,0:T(8,128)(2,1)S(1)}, bf16[32,3584]{1,0:T(8,128)(2,1)S(1)}, u32[]{:S(2)}, u32[]{:S(2)}) collective-permute-start(bf16[32,3584]{1,0:T(8,128)(2,1)S(1)} %get-tuple-element.36), channel_id=1, source_target_pairs={{0,2},{10,8},{2,4},{12,10},{4,6},{14,12},{6,7},{15,14},{7,5},{13,1... | collective-permute-start | bytes 688136 | tf_op jit(solution)/shard_map/ppermute | solution.py:95
  93.0 3.2 %fusion.3 = bf16[64,64,512]{2,1,0:T(8,128)(2,1)} fusion(bf16[64,64,64]{2,1,0:T(8,128)(2,1)S(1)} %divide_convert_fusion.rest_1_, bf16[64,64,576]{2,1,0:T(8,128)(2,1)S(1)} %bitcast.32), kind=kOutput, calls=%fused_computation.3 | convolution fusion | flops 270532608 | bytes 9437184 | tf_op jit(solution)/shard_map/thj,tjc->thc/dot_general | solution.py:135
  96.2 1.2 %collective-permute-done.30 = bf16[32,3584]{1,0:T(8,128)(2,1)S(1)} collective-permute-done((bf16[32,3584]{1,0:T(8,128)(2,1)S(1)}, bf16[32,3584]{1,0:T(8,128)(2,1)S(1)}, u32[]{:S(2)}, u32[]{:S(2)}) %collective-permute-start.30) | collective-permute-done | bytes 229408 | tf_op jit(solution)/shard_map/ppermute | solution.py:95
  97.5 1.5 %collective-permute-done.31 = bf16[32,3584]{1,0:T(8,128)(2,1)S(1)} collective-permute-done((bf16[32,3584]{1,0:T(8,128)(2,1)S(1)}, bf16[32,3584]{1,0:T(8,128)(2,1)S(1)}, u32[]{:S(2)}, u32[]{:S(2)}) %collective-permute-start.31) | collective-permute-done | bytes 229408 | tf_op jit(solution)/shard_map/ppermute | solution.py:95
  99.0 1.0 add_convert_fusion
  (37 shorter events, 0.3 us)
Async XLA Ops:
  2.5 18.2 %collective-permute-start = (bf16[64,3712]{1,0:T(8,128)(2,1)S(1)}, bf16[64,3712]{1,0:T(8,128)(2,1)S(1)}, u32[]{:S(2)}, u32[]{:S(2)}) collective-permute-start(bf16[64,3712]{1,0:T(8,128)(2,1)S(1)} %pad_maximum_fusion.own_ref), channel_id=1, source_target_pairs={{0,8},{8,0},{1,9},{9,1},{2,10},{10,2},{3,11},{11,3},{4,12},{12,4},... | collective-permute-start | bytes 1425416 | tf_op jit(solution)/shard_map/ppermute | solution.py:98
  4.4 11.3 %collective-permute-start.2 = (bf16[32,3712]{1,0:T(8,128)(2,1)S(1)}, bf16[32,3712]{1,0:T(8,128)(2,1)}, u32[]{:S(2)}, u32[]{:S(2)}) collective-permute-start(bf16[32,3712]{1,0:T(8,128)(2,1)S(1)} %get-tuple-element.35), channel_id=1, source_target_pairs={{0,2},{10,8},{2,4},{12,10},{4,6},{14,12},{6,7},{15,14},{7,5},{13,1... | collective-permute-start | bytes 712712 | tf_op jit(solution)/shard_map/ppermute | solution.py:95
  7.1 9.8 %collective-permute-start.3 = (bf16[32,3712]{1,0:T(8,128)(2,1)S(1)}, bf16[32,3712]{1,0:T(8,128)(2,1)}, u32[]{:S(2)}, u32[]{:S(2)}) collective-permute-start(bf16[32,3712]{1,0:T(8,128)(2,1)S(1)} %get-tuple-element.34), channel_id=1, source_target_pairs={{8,2},{2,8},{10,4},{4,10},{12,6},{6,12},{14,7},{7,14},{15,5},{5,15... | collective-permute-start | bytes 712712 | tf_op jit(solution)/shard_map/ppermute | solution.py:95
  15.8 5.0 %copy-start = (bf16[1,3584,512]{2,1,0:T(8,128)(2,1)S(1)}, bf16[1,3584,512]{2,1,0:T(8,128)(2,1)}, u32[]{:S(2)}) copy-start(bf16[1,3584,512]{2,1,0:T(8,128)(2,1)} %param.12) | copy-start | bytes 11010052
  17.9 8.6 %collective-permute-start.22 = (bf16[64,3712]{1,0:T(8,128)(2,1)S(1)}, bf16[64,3712]{1,0:T(8,128)(2,1)S(1)}, u32[]{:S(2)}, u32[]{:S(2)}) collective-permute-start(bf16[64,3712]{1,0:T(8,128)(2,1)S(1)} %constant_dynamic-update-slice_fusion.own_ref), channel_id=1, source_target_pairs={{0,8},{8,0},{1,9},{9,1},{2,10},{10,2},{3,11},{11,3},{4,12},{12,4},... | collective-permute-start | bytes 1425416 | tf_op jit(solution)/shard_map/ppermute | solution.py:98
  19.1 9.3 %collective-permute-start.4 = (bf16[64,3712]{1,0:T(8,128)(2,1)S(1)}, bf16[64,3712]{1,0:T(8,128)(2,1)S(1)}, u32[]{:S(2)}, u32[]{:S(2)}) collective-permute-start(bf16[64,3712]{1,0:T(8,128)(2,1)S(1)} %constant_dynamic-update-slice_fusion.own_ref), channel_id=1, source_target_pairs={{0,2},{10,8},{2,4},{12,10},{4,6},{14,12},{6,7},{15,14},{7,5},{13,1... | collective-permute-start | bytes 1425416 | tf_op jit(solution)/shard_map/ppermute | solution.py:95
  20.7 2.0 %copy-start.1 = (bf16[1,3584,512]{2,1,0:T(8,128)(2,1)S(1)}, bf16[1,3584,512]{2,1,0:T(8,128)(2,1)}, u32[]{:S(2)}) copy-start(bf16[1,3584,512]{2,1,0:T(8,128)(2,1)} %param.13) | copy-start | bytes 11010052
  22.8 2.0 %copy-start.2 = (bf16[1,512,3584]{2,1,0:T(8,128)(2,1)S(1)}, bf16[1,512,3584]{2,1,0:T(8,128)(2,1)}, u32[]{:S(2)}) copy-start(bf16[1,512,3584]{2,1,0:T(8,128)(2,1)} %param.14) | copy-start | bytes 11010052
  28.3 2.1 %collective-permute-start.23 = (bf16[64,3584]{1,0:T(8,128)(2,1)S(1)}, bf16[64,3584]{1,0:T(8,128)(2,1)S(1)}, u32[]{:S(2)}, u32[]{:S(2)}) collective-permute-start(bf16[64,3584]{1,0:T(8,128)(2,1)S(1)} %get-tuple-element.33), channel_id=1, source_target_pairs={{0,8},{8,0},{1,9},{9,1},{2,10},{10,2},{3,11},{11,3},{4,12},{12,4},... | collective-permute-start | bytes 1376264 | tf_op jit(solution)/shard_map/ppermute | solution.py:98
  28.4 3.5 %collective-permute-start.20 = (bf16[64,3712]{1,0:T(8,128)(2,1)S(1)}, bf16[64,3712]{1,0:T(8,128)(2,1)S(1)}, u32[]{:S(2)}, u32[]{:S(2)}) collective-permute-start(bf16[64,3712]{1,0:T(8,128)(2,1)S(1)} %collective-permute-done.4.own_ref), channel_id=1, source_target_pairs={{0,8},{8,0},{1,9},{9,1},{2,10},{10,2},{3,11},{11,3},{4,12},{12,4},... | collective-permute-start | bytes 1425416 | tf_op jit(solution)/shard_map/ppermute | solution.py:98
  28.9 8.7 %collective-permute-start.5 = (bf16[64,3712]{1,0:T(8,128)(2,1)S(1)}, bf16[64,3712]{1,0:T(8,128)(2,1)S(1)}, u32[]{:S(2)}, u32[]{:S(2)}) collective-permute-start(bf16[64,3712]{1,0:T(8,128)(2,1)S(1)} %collective-permute-done.4.own_ref), channel_id=1, source_target_pairs={{0,2},{10,8},{2,4},{12,10},{4,6},{14,12},{6,7},{15,14},{7,5},{13,1... | collective-permute-start | bytes 1425416 | tf_op jit(solution)/shard_map/ppermute | solution.py:95
  30.5 11.9 %collective-permute-start.24 = (bf16[64,3584]{1,0:T(8,128)(2,1)S(1)}, bf16[64,3584]{1,0:T(8,128)(2,1)S(1)}, u32[]{:S(2)}, u32[]{:S(2)}) collective-permute-start(bf16[64,3584]{1,0:T(8,128)(2,1)S(1)} %add_convert_fusion.7), channel_id=1, source_target_pairs={{0,2},{10,8},{2,4},{12,10},{4,6},{14,12},{6,7},{15,14},{7,5},{13,1... | collective-permute-start | bytes 1376264 | tf_op jit(solution)/shard_map/ppermute | solution.py:95
  33.6 8.9 %collective-permute-start.21 = (bf16[64,3584]{1,0:T(8,128)(2,1)S(1)}, bf16[64,3584]{1,0:T(8,128)(2,1)S(1)}, u32[]{:S(2)}, u32[]{:S(2)}) collective-permute-start(bf16[64,3584]{1,0:T(8,128)(2,1)S(1)} %get-tuple-element.31), channel_id=1, source_target_pairs={{0,8},{8,0},{1,9},{9,1},{2,10},{10,2},{3,11},{11,3},{4,12},{12,4},... | collective-permute-start | bytes 1376264 | tf_op jit(solution)/shard_map/ppermute | solution.py:98
  37.5 6.7 %collective-permute-start.18 = (bf16[64,3712]{1,0:T(8,128)(2,1)S(1)}, bf16[64,3712]{1,0:T(8,128)(2,1)S(1)}, u32[]{:S(2)}, u32[]{:S(2)}) collective-permute-start(bf16[64,3712]{1,0:T(8,128)(2,1)S(1)} %collective-permute-done.5.own_ref), channel_id=1, source_target_pairs={{0,8},{8,0},{1,9},{9,1},{2,10},{10,2},{3,11},{11,3},{4,12},{12,4},... | collective-permute-start | bytes 1425416 | tf_op jit(solution)/shard_map/ppermute | solution.py:98
  37.5 10.0 %collective-permute-start.6 = (bf16[64,3712]{1,0:T(8,128)(2,1)S(1)}, bf16[64,3712]{1,0:T(8,128)(2,1)S(1)}, u32[]{:S(2)}, u32[]{:S(2)}) collective-permute-start(bf16[64,3712]{1,0:T(8,128)(2,1)S(1)} %collective-permute-done.5.own_ref), channel_id=1, source_target_pairs={{0,2},{10,8},{2,4},{12,10},{4,6},{14,12},{6,7},{15,14},{7,5},{13,1... | collective-permute-start | bytes 1425416 | tf_op jit(solution)/shard_map/ppermute | solution.py:95
  42.6 9.8 %collective-permute-start.25 = (bf16[64,3584]{1,0:T(8,128)(2,1)S(1)}, bf16[64,3584]{1,0:T(8,128)(2,1)S(1)}, u32[]{:S(2)}, u32[]{:S(2)}) collective-permute-start(bf16[64,3584]{1,0:T(8,128)(2,1)S(1)} %add_convert_fusion.6), channel_id=1, source_target_pairs={{0,2},{10,8},{2,4},{12,10},{4,6},{14,12},{6,7},{15,14},{7,5},{13,1... | collective-permute-start | bytes 1376264 | tf_op jit(solution)/shard_map/ppermute | solution.py:95
  45.9 6.5 %collective-permute-start.19 = (bf16[64,3584]{1,0:T(8,128)(2,1)S(1)}, bf16[64,3584]{1,0:T(8,128)(2,1)S(1)}, u32[]{:S(2)}, u32[]{:S(2)}) collective-permute-start(bf16[64,3584]{1,0:T(8,128)(2,1)S(1)} %get-tuple-element.29), channel_id=1, source_target_pairs={{0,8},{8,0},{1,9},{9,1},{2,10},{10,2},{3,11},{11,3},{4,12},{12,4},... | collective-permute-start | bytes 1376264 | tf_op jit(solution)/shard_map/ppermute | solution.py:98
  47.5 6.9 %collective-permute-start.16 = (bf16[64,3712]{1,0:T(8,128)(2,1)S(1)}, bf16[64,3712]{1,0:T(8,128)(2,1)S(1)}, u32[]{:S(2)}, u32[]{:S(2)}) collective-permute-start(bf16[64,3712]{1,0:T(8,128)(2,1)S(1)} %collective-permute-done.6.own_ref), channel_id=1, source_target_pairs={{0,8},{8,0},{1,9},{9,1},{2,10},{10,2},{3,11},{11,3},{4,12},{12,4},... | collective-permute-start | bytes 1425416 | tf_op jit(solution)/shard_map/ppermute | solution.py:98
  47.5 10.0 %collective-permute-start.7 = (bf16[64,3712]{1,0:T(8,128)(2,1)S(1)}, bf16[64,3712]{1,0:T(8,128)(2,1)S(1)}, u32[]{:S(2)}, u32[]{:S(2)}) collective-permute-start(bf16[64,3712]{1,0:T(8,128)(2,1)S(1)} %collective-permute-done.6.own_ref), channel_id=1, source_target_pairs={{0,2},{10,8},{2,4},{12,10},{4,6},{14,12},{6,7},{15,14},{7,5},{13,1... | collective-permute-start | bytes 1425416 | tf_op jit(solution)/shard_map/ppermute | solution.py:95
  52.6 9.8 %collective-permute-start.26 = (bf16[64,3584]{1,0:T(8,128)(2,1)S(1)}, bf16[64,3584]{1,0:T(8,128)(2,1)S(1)}, u32[]{:S(2)}, u32[]{:S(2)}) collective-permute-start(bf16[64,3584]{1,0:T(8,128)(2,1)S(1)} %add_convert_fusion.5), channel_id=1, source_target_pairs={{0,2},{10,8},{2,4},{12,10},{4,6},{14,12},{6,7},{15,14},{7,5},{13,1... | collective-permute-start | bytes 1376264 | tf_op jit(solution)/shard_map/ppermute | solution.py:95
  56.1 6.3 %collective-permute-start.17 = (bf16[64,3584]{1,0:T(8,128)(2,1)S(1)}, bf16[64,3584]{1,0:T(8,128)(2,1)S(1)}, u32[]{:S(2)}, u32[]{:S(2)}) collective-permute-start(bf16[64,3584]{1,0:T(8,128)(2,1)S(1)} %get-tuple-element.27), channel_id=1, source_target_pairs={{0,8},{8,0},{1,9},{9,1},{2,10},{10,2},{3,11},{11,3},{4,12},{12,4},... | collective-permute-start | bytes 1376264 | tf_op jit(solution)/shard_map/ppermute | solution.py:98
  57.5 6.7 %collective-permute-start.14 = (bf16[64,3712]{1,0:T(8,128)(2,1)S(1)}, bf16[64,3712]{1,0:T(8,128)(2,1)S(1)}, u32[]{:S(2)}, u32[]{:S(2)}) collective-permute-start(bf16[64,3712]{1,0:T(8,128)(2,1)S(1)} %collective-permute-done.7.own_ref), channel_id=1, source_target_pairs={{0,8},{8,0},{1,9},{9,1},{2,10},{10,2},{3,11},{11,3},{4,12},{12,4},... | collective-permute-start | bytes 1425416 | tf_op jit(solution)/shard_map/ppermute | solution.py:98
  57.5 10.0 %collective-permute-start.8 = (bf16[64,3712]{1,0:T(8,128)(2,1)S(1)}, bf16[64,3712]{1,0:T(8,128)(2,1)S(1)}, u32[]{:S(2)}, u32[]{:S(2)}) collective-permute-start(bf16[64,3712]{1,0:T(8,128)(2,1)S(1)} %collective-permute-done.7.own_ref), channel_id=1, source_target_pairs={{0,2},{10,8},{2,4},{12,10},{4,6},{14,12},{6,7},{15,14},{7,5},{13,1... | collective-permute-start | bytes 1425416 | tf_op jit(solution)/shard_map/ppermute | solution.py:95
  62.6 9.8 %collective-permute-start.27 = (bf16[64,3584]{1,0:T(8,128)(2,1)S(1)}, bf16[64,3584]{1,0:T(8,128)(2,1)S(1)}, u32[]{:S(2)}, u32[]{:S(2)}) collective-permute-start(bf16[64,3584]{1,0:T(8,128)(2,1)S(1)} %add_convert_fusion.4), channel_id=1, source_target_pairs={{0,2},{10,8},{2,4},{12,10},{4,6},{14,12},{6,7},{15,14},{7,5},{13,1... | collective-permute-start | bytes 1376264 | tf_op jit(solution)/shard_map/ppermute | solution.py:95
  65.9 6.5 %collective-permute-start.15 = (bf16[64,3584]{1,0:T(8,128)(2,1)S(1)}, bf16[64,3584]{1,0:T(8,128)(2,1)S(1)}, u32[]{:S(2)}, u32[]{:S(2)}) collective-permute-start(bf16[64,3584]{1,0:T(8,128)(2,1)S(1)} %get-tuple-element.25), channel_id=1, source_target_pairs={{0,8},{8,0},{1,9},{9,1},{2,10},{10,2},{3,11},{11,3},{4,12},{12,4},... | collective-permute-start | bytes 1376264 | tf_op jit(solution)/shard_map/ppermute | solution.py:98
  67.5 6.7 %collective-permute-start.12 = (bf16[64,3712]{1,0:T(8,128)(2,1)S(1)}, bf16[64,3712]{1,0:T(8,128)(2,1)S(1)}, u32[]{:S(2)}, u32[]{:S(2)}) collective-permute-start(bf16[64,3712]{1,0:T(8,128)(2,1)S(1)} %collective-permute-done.8.own_ref), channel_id=1, source_target_pairs={{0,8},{8,0},{1,9},{9,1},{2,10},{10,2},{3,11},{11,3},{4,12},{12,4},... | collective-permute-start | bytes 1425416 | tf_op jit(solution)/shard_map/ppermute | solution.py:98
  67.5 10.0 %collective-permute-start.9 = (bf16[64,3712]{1,0:T(8,128)(2,1)S(1)}, bf16[64,3712]{1,0:T(8,128)(2,1)S(1)}, u32[]{:S(2)}, u32[]{:S(2)}) collective-permute-start(bf16[64,3712]{1,0:T(8,128)(2,1)S(1)} %collective-permute-done.8.own_ref), channel_id=1, source_target_pairs={{0,2},{10,8},{2,4},{12,10},{4,6},{14,12},{6,7},{15,14},{7,5},{13,1... | collective-permute-start | bytes 1425416 | tf_op jit(solution)/shard_map/ppermute | solution.py:95
  72.6 9.8 %collective-permute-start.28 = (bf16[64,3584]{1,0:T(8,128)(2,1)S(1)}, bf16[64,3584]{1,0:T(8,128)(2,1)S(1)}, u32[]{:S(2)}, u32[]{:S(2)}) collective-permute-start(bf16[64,3584]{1,0:T(8,128)(2,1)S(1)} %add_convert_fusion.3), channel_id=1, source_target_pairs={{0,2},{10,8},{2,4},{12,10},{4,6},{14,12},{6,7},{15,14},{7,5},{13,1... | collective-permute-start | bytes 1376264 | tf_op jit(solution)/shard_map/ppermute | solution.py:95
  75.9 6.5 %collective-permute-start.13 = (bf16[64,3584]{1,0:T(8,128)(2,1)S(1)}, bf16[64,3584]{1,0:T(8,128)(2,1)S(1)}, u32[]{:S(2)}, u32[]{:S(2)}) collective-permute-start(bf16[64,3584]{1,0:T(8,128)(2,1)S(1)} %get-tuple-element.23), channel_id=1, source_target_pairs={{0,8},{8,0},{1,9},{9,1},{2,10},{10,2},{3,11},{11,3},{4,12},{12,4},... | collective-permute-start | bytes 1376264 | tf_op jit(solution)/shard_map/ppermute | solution.py:98
  77.6 6.7 %collective-permute-start.10 = (bf16[64,3712]{1,0:T(8,128)(2,1)S(1)}, bf16[64,3712]{1,0:T(8,128)(2,1)S(1)}, u32[]{:S(2)}, u32[]{:S(2)}) collective-permute-start(bf16[64,3712]{1,0:T(8,128)(2,1)S(1)} %collective-permute-done.9.own_ref), channel_id=1, source_target_pairs={{0,8},{8,0},{1,9},{9,1},{2,10},{10,2},{3,11},{11,3},{4,12},{12,4},... | collective-permute-start | bytes 1425416 | tf_op jit(solution)/shard_map/ppermute | solution.py:98
  82.5 10.5 %slice-start = ((s8[5242880]{0:T(1024)(128)(4,1)}), s8[4194304]{0:T(1024)(128)(4,1)S(1)}, s32[]{:S(2)}) async-start(s8[5242880]{0:T(1024)(128)(4,1)} %bitcast.31), calls=%async_computation | async-start | bytes 8388608
  82.6 10.4 %slice-start.1 = ((s8[5242880]{0:T(1024)(128)(4,1)}), s8[1048576]{0:T(1024)(128)(4,1)S(1)}, s32[]{:S(2)}) async-start(s8[5242880]{0:T(1024)(128)(4,1)} %bitcast.31), calls=%async_computation.1 | async-start | bytes 2097152
  82.7 8.5 %collective-permute-start.29 = (bf16[64,3584]{1,0:T(8,128)(2,1)S(1)}, bf16[64,3584]{1,0:T(8,128)(2,1)S(1)}, u32[]{:S(2)}, u32[]{:S(2)}) collective-permute-start(bf16[64,3584]{1,0:T(8,128)(2,1)S(1)} %add_convert_fusion.2), channel_id=1, source_target_pairs={{0,2},{10,8},{2,4},{12,10},{4,6},{14,12},{6,7},{15,14},{7,5},{13,1... | collective-permute-start | bytes 1376264 | tf_op jit(solution)/shard_map/ppermute | solution.py:95
  86.0 5.2 %collective-permute-start.11 = (bf16[64,3584]{1,0:T(8,128)(2,1)S(1)}, bf16[64,3584]{1,0:T(8,128)(2,1)S(1)}, u32[]{:S(2)}, u32[]{:S(2)}) collective-permute-start(bf16[64,3584]{1,0:T(8,128)(2,1)S(1)} %get-tuple-element.21), channel_id=1, source_target_pairs={{0,8},{8,0},{1,9},{9,1},{2,10},{10,2},{3,11},{11,3},{4,12},{12,4},... | collective-permute-start | bytes 1376264 | tf_op jit(solution)/shard_map/ppermute | solution.py:98
  86.0 10.2 %collective-permute-start.1 = (bf16[64,3584]{1,0:T(8,128)(2,1)S(1)}, bf16[64,3584]{1,0:T(8,128)(2,1)S(1)}, u32[]{:S(2)}, u32[]{:S(2)}) collective-permute-start(bf16[64,3584]{1,0:T(8,128)(2,1)S(1)} %get-tuple-element.19), channel_id=1, source_target_pairs={{0,8},{8,0},{1,9},{9,1},{2,10},{10,2},{3,11},{11,3},{4,12},{12,4},... | collective-permute-start | bytes 1376264 | tf_op jit(solution)/shard_map/ppermute | solution.py:98
  91.4 6.1 %collective-permute-start.30 = (bf16[32,3584]{1,0:T(8,128)(2,1)S(1)}, bf16[32,3584]{1,0:T(8,128)(2,1)S(1)}, u32[]{:S(2)}, u32[]{:S(2)}) collective-permute-start(bf16[32,3584]{1,0:T(8,128)(2,1)S(1)} %get-tuple-element.36), channel_id=1, source_target_pairs={{0,2},{10,8},{2,4},{12,10},{4,6},{14,12},{6,7},{15,14},{7,5},{13,1... | collective-permute-start | bytes 688136 | tf_op jit(solution)/shard_map/ppermute | solution.py:95
  93.0 6.0 %collective-permute-start.31 = (bf16[32,3584]{1,0:T(8,128)(2,1)S(1)}, bf16[32,3584]{1,0:T(8,128)(2,1)S(1)}, u32[]{:S(2)}, u32[]{:S(2)}) collective-permute-start(bf16[32,3584]{1,0:T(8,128)(2,1)S(1)} %get-tuple-element.37), channel_id=1, source_target_pairs={{0,10},{10,0},{2,12},{12,2},{4,14},{14,4},{6,15},{15,6},{7,13},{13... | collective-permute-start | bytes 688136 | tf_op jit(solution)/shard_map/ppermute | solution.py:95

commit v4 on v3

--- a/solution.py
+++ b/solution.py
@@ -1,3 +1,5 @@
+import functools
+
 import jax
 import jax.numpy as jnp
 from jax import lax
@@ -8,17 +10,74 @@
 LAT = 512
 SOFTMAX_SCALE = 192.0 ** (-0.5)
 LANES = 128
-
-
-def attention_probs(queries, latent_cache, cache_lengths):
-    scores = SOFTMAX_SCALE * jnp.einsum(
-        "thc,tjc->thj", queries, latent_cache, preferred_element_type=jnp.float32
-    )
-    valid_mask = (jnp.arange(latent_cache.shape[1])[None, :] < cache_lengths[:, None])[:, None, :]
-    scores = jnp.where(valid_mask, scores, -1e30)
-    row_peak = jnp.max(scores, axis=2, keepdims=True)
-    exp_terms = jnp.where(valid_mask, jnp.exp(scores - row_peak), 0.0)
-    return (exp_terms / jnp.sum(exp_terms, axis=2, keepdims=True)).astype(jnp.bfloat16)
+PIECES = 4
+
+
+def attend_kernel(len_ref, q_ref, c_ref, *rest, base, pair):
+    done_ref = rest[-1]
+    done_ref[...] = jnp.zeros_like(done_ref)
+    out_ref = rest[-2]
+    step, heads, wide = q_ref.shape
+    slots = c_ref.shape[1]
+    lat = out_ref.shape[2]
+    row = lax.broadcasted_iota(jnp.int32, (pair * heads, pair * slots), 0) // heads
+    col = lax.broadcasted_iota(jnp.int32, (pair * heads, pair * slots), 1)
+    place = jnp.where(col // slots == row, col % slots, slots)
+    which = lax.broadcasted_iota(jnp.int32, (pair * heads, 1), 0) // heads
+    groups = range(0, step, pair)
+    caches = [c_ref[at : at + pair].reshape(pair * slots, wide) for at in groups]
+    scores = [
+        lax.dot_general(
+            q_ref[at : at + pair].reshape(pair * heads, wide),
+            cache,
+            (((1,), (1,)), ((), ())),
+            preferred_element_type=jnp.float32,
+        )
+        for at, cache in zip(groups, caches, strict=True)
+    ]
+    probs = []
+    for at, score in zip(groups, scores, strict=True):
+        live = jnp.full((pair * heads, 1), len_ref[base + at], jnp.int32)
+        for j in range(1, pair):
+            live = jnp.where(which == j, len_ref[base + at + j], live)
+        score = jnp.where(place < live, score * SOFTMAX_SCALE, -1e30)
+        terms = jnp.exp(score - jnp.max(score, axis=1, keepdims=True))
+        probs.append((terms * (1.0 / jnp.sum(terms, axis=1, keepdims=True))).astype(jnp.bfloat16))
+    for at, prob, cache in zip(groups, probs, caches, strict=True):
+        mixed = jnp.dot(prob, cache[:, :lat], preferred_element_type=jnp.float32)
+        out_ref[at : at + pair] = mixed.astype(jnp.bfloat16).reshape(pair, heads, lat)
+
+
+def attend_piece(lengths, queries, latent_cache, lat, piece, count, out, after):
+    total, heads, wide = queries.shape
+    slots = latent_cache.shape[1]
+
+    def rows(middle, last):
+        return pl.BlockSpec((count, middle, last), lambda i, n: (piece, 0, 0))
+
+    extra = ([] if out is None else [out]) + list(after)
+    return pl.pallas_call(
+        functools.partial(attend_kernel, base=piece * count, pair=2),
+        grid_spec=pltpu.PrefetchScalarGridSpec(
+            num_scalar_prefetch=1,
+            grid=(1,),
+            in_specs=[rows(heads, wide), rows(slots, wide)]
+            + [pl.BlockSpec(memory_space=pl.ANY)] * len(extra),
+            out_specs=[rows(heads, lat), pl.BlockSpec((8, LANES), lambda i, n: (0, 0))],
+        ),
+        out_shape=[
+            jax.ShapeDtypeStruct((total, heads, lat), jnp.bfloat16),
+            jax.ShapeDtypeStruct((8, LANES), jnp.float32),
+        ],
+        input_output_aliases={} if out is None else {3: 0},
+        compiler_params=pltpu.CompilerParams(vmem_limit_bytes=16 << 20),
+        cost_estimate=pl.CostEstimate(
+            flops=2 * count * heads * slots * (wide + lat),
+            bytes_accessed=2 * count * (heads * (wide + lat) + slots * wide),
+            transcendentals=count * heads * slots,
+        ),
+        name="attend",
+    )(lengths, queries, latent_cache, *extra)
 
 
 def expert_kernel(expert_ref, own_ref, other_ref, gate_ref, up_ref, down_ref, *rest):
@@ -83,11 +142,10 @@
     part = rows // 2
     node = lax.axis_index("node")
     order = ring_order(local_count)
-    hops, hops_in, hops_out = [], [], []
+    hops, hops_out = [], []
     for i in range(local_count):
         here, there = order[i], order[(i + 1) % local_count]
         hops += [(here, there), (local_count + there, local_count + here)]
-        hops_in += [(local_count + here, there), (there, local_count + here)]
         hops_out += [(here, local_count + there), (local_count + there, here)]
     expert = ((node * local_count + lax.axis_index("local")) // 2).astype(jnp.int32).reshape(1)
 
@@ -101,40 +159,58 @@
     route = jnp.sum(
         jnp.where(matches, combine_weights[:, :, None], jnp.zeros((), jnp.bfloat16)), axis=1
     )
-    mine = jnp.concatenate([tokens, route], axis=1)
     first = node == 0
-    kept = jnp.where(first, mine[:part], mine[part:])
-    given = jnp.where(first, mine[part:], mine[:part])
+
+    def halves(a):
+        return jnp.where(first, a[:part], a[part:]), jnp.where(first, a[part:], a[:part])
+
+    kept, given = [
+        jnp.concatenate(pair, axis=1) for pair in zip(halves(tokens), halves(route), strict=True)
+    ]
+    swapped = across(given)
+    block = jnp.concatenate([kept, swapped], axis=0)
+    mine = jnp.concatenate([tokens, lax.optimization_barrier((route, block))[0]], axis=1)
     gate, up, down = w_gate[0], w_up[0], w_down[0]
-
-    block = jnp.concatenate([onward(kept), onward(given, hops_in)], axis=0)
-    probs = attention_probs(queries, latent_cache, cache_lengths)
     own, other = run_experts(expert, mine, across(mine), gate, up, down)
     own_sums, other_sums = [own], [across(other)]
-    after = (own, probs)
+    after = (own,)
+    attn_latent, done = None, None
     for k in range(1, local_count):
-        if k > 1:
-            block = onward(block)
+        block = onward(block)
+        if k == 1:
+            block = lax.optimization_barrier((block, own))[0]
         own, other = run_experts(expert, block, across(block), gate, up, down, after)
         own_sums.append(own)
         other_sums.append(across(other))
         after = ()
+        if done is not None:
+            after, done = (done,), None
+        if k <= PIECES:
+            attn_latent, done = attend_piece(
+                cache_lengths,
+                queries,
+                latent_cache,
+                LAT,
+                k - 1,
+                queries.shape[0] // PIECES,
+                attn_latent,
+                (own,),
+            )
 
     def chip_sum(k):
         return own_sums[k].astype(jnp.float32) + other_sums[k].astype(jnp.float32)
 
     running = chip_sum(1).astype(jnp.bfloat16)
-    for k in range(2, local_count):
+    for k in range(2, local_count - 1):
         running = (chip_sum(k) + onward(running).astype(jnp.float32)).astype(jnp.bfloat16)
-    same, cross = onward(running[:part]), onward(running[part:], hops_out)
+    total = chip_sum(local_count - 1) + onward(running).astype(jnp.float32)
+    same = onward(total[:part].astype(jnp.bfloat16))
+    cross = onward(total[part:].astype(jnp.bfloat16), hops_out)
     arrived = jnp.where(
         first, jnp.concatenate([same, cross], axis=0), jnp.concatenate([cross, same], axis=0)
     )
     moe_out = (chip_sum(0) + arrived.astype(jnp.float32)).astype(jnp.bfloat16)
 
-    attn_latent = jnp.einsum(
-        "thj,tjc->thc", probs, latent_cache[:, :, :LAT], preferred_element_type=jnp.float32
-    ).astype(jnp.bfloat16)
     return (moe_out, attn_latent)
 
 

time: 101 us -> 96.2 us (0.952)
  Pallas kernels: 13.7 us -> 24.2 us
  matrix products: 9.24 us -> 0 us
  waiting for transfers between devices: 35.7 us -> 30.6 us
  other arithmetic: 7.38 us -> 4.08 us
  starting transfers between devices: 26.7 us -> 28.4 us
  local copies, waits for them, and re-layouts: 6.28 us -> 7.75 us
    pallas_call x0 -> x4, Pallas kernels: none -> 10.3 us  [attend_piece(): pl.pallas_call(functools.partial(attend_kernel, base=piece * count, pair=...]
    sub x1 -> x0, matrix products: 6 us -> none  [attention_probs(): exp_terms = jnp.where(valid_mask, jnp.exp(scores - row_peak), 0.0)]
    ppermute x16 -> x15, waiting for transfers between devices: 35.6 us -> 30.5 us  [onward(): return lax.ppermute(a, ('node', 'local'), pairs)]
    dot_general x1 -> x0, matrix products: 3.24 us -> none  [on_device(): jnp.einsum('thj,tjc->thc', probs, latent_cache[:, :, :LAT], preferred_ele...]
    unnamed x11 -> x23, local copies, waits for them, and re-layouts: 5.2 us -> 7.71 us
    lt x1 -> x0, other arithmetic: 1.33 us -> none  [attention_probs(): jnp.arange(latent_cache.shape[1])[None, :] < cache_lengths[:, None]]
    ppermute x16 -> x17, starting transfers between devices: 2.44 us -> 3.54 us  [across(): return lax.ppermute(a, 'node', [(0, 1), (1, 0)])]
    concatenate x1, local copies, waits for them, and re-layouts: 1.04 us -> 0.01 us  [on_device(): jnp.concatenate([tokens, lax.optimization_barrier((route, block))[0]], ax...]
  transfers between devices with their start and end apart: 32 -> 32, of which waited for: 13 -> 12; matrix products, arithmetic and copies ran while one was open for 16% -> 2% of each run, Pallas kernels for 14% -> 25%
where the time goes in v4:
time: 96.2 us; the launch traced here: 95.9 us
  waiting for transfers between devices  30.6 us (32%)
  starting transfers between devices  28.4 us (30%)
  Pallas kernels  24.2 us (25%)
  local copies, waits for them, and re-layouts  7.75 us (8%)
  other arithmetic  4.08 us (4%)
    ppermute x15, waiting for transfers between devices, onward(): return lax.ppermute(a, ('node', 'local'), pairs)  30.5 us
    ppermute x15, starting transfers between devices, onward(): return lax.ppermute(a, ('node', 'local'), pairs)  24.8 us
    pallas_call x8, Pallas kernels, run_experts(): pl.pallas_call(expert_kernel, grid_spec=pltpu.PrefetchScalarGridSpec(num_...  13.8 us
    pallas_call x4, Pallas kernels, attend_piece(): pl.pallas_call(functools.partial(attend_kernel, base=piece * count, pair=...  10.3 us
    unnamed x23, local copies, waits for them, and re-layouts  7.71 us
    ppermute x17, starting transfers between devices, across(): return lax.ppermute(a, 'node', [(0, 1), (1, 0)])  3.54 us
  transfers between devices with their start and end apart: 32, of which 12 were waited for; matrix products, arithmetic and copies ran while one was open for 2% of the time, Pallas kernels for 25%

profile of v4, /device:TPU:0, one launch (start us, length us, event | category | flops | bytes accessed | tf_op | source)
XLA Modules:
  0.0 95.9 jit_solution(6586537466470755604)
XLA Ops:
  0.6 0.8 fusion.1
  1.5 1.1 %broadcast_select_fusion.1 = (bf16[32,3584]{1,0:T(8,128)(2,1)S(1)}, bf16[32,3584]{1,0:T(8,128)(2,1)S(1)}) fusion(pred[]{:T(512)S(6)} %eq.19, bf16[64,3584]{1,0:T(8,128)(2,1)} %param.9), kind=kLoop, calls=%fused_computation.12 | loop fusion | flops 229376 | bytes 917505 | tf_op jit(solution)/shard_map/jit(_where)/select_n | solution.py:165
  2.6 0.5 collective-permute-start
  3.1 1.0 %constant_dynamic-update-slice_fusion.1 = bf16[64,3712]{1,0:T(8,128)(2,1)S(1)} fusion(bf16[64,3584]{1,0:T(8,128)(2,1)} %param.9), kind=kLoop, calls=%fused_computation.19 | loop fusion | bytes 917504
  4.2 0.1 collective-permute-done
  4.3 0.4 collective-permute-start.1
  4.7 2.7 %collective-permute-start.3 = (bf16[64,3712]{1,0:T(8,128)(2,1)S(1)}, bf16[64,3712]{1,0:T(8,128)(2,1)S(1)}, u32[]{:S(2)}, u32[]{:S(2)}) collective-permute-start(bf16[64,3712]{1,0:T(8,128)(2,1)S(1)} %pad_maximum_fusion), channel_id=1, source_target_pairs={{0,2},{10,8},{2,4},{12,10},{4,6},{14,12},{6,7},{15,14},{7,5},{13,1... | collective-permute-start | bytes 1425416 | tf_op jit(solution)/shard_map/ppermute | solution.py:153
  7.5 2.0 %copy-done = bf16[1,3584,512]{2,1,0:T(8,128)(2,1)S(1)} copy-done((bf16[1,3584,512]{2,1,0:T(8,128)(2,1)S(1)}, bf16[1,3584,512]{2,1,0:T(8,128)(2,1)}, u32[]{:S(2)}) %copy-start) | copy-done | bytes 3670040
  9.5 2.0 %copy-done.2 = bf16[1,3584,512]{2,1,0:T(8,128)(2,1)S(1)} copy-done((bf16[1,3584,512]{2,1,0:T(8,128)(2,1)S(1)}, bf16[1,3584,512]{2,1,0:T(8,128)(2,1)}, u32[]{:S(2)}) %copy-start.2) | copy-done | bytes 3670040
  11.5 2.0 %copy-done.4 = bf16[1,512,3584]{2,1,0:T(8,128)(2,1)S(1)} copy-done((bf16[1,512,3584]{2,1,0:T(8,128)(2,1)S(1)}, bf16[1,512,3584]{2,1,0:T(8,128)(2,1)}, u32[]{:S(2)}) %copy-start.4) | copy-done | bytes 3670040
  13.6 1.7 %expert_half.8 = (bf16[64,3584]{1,0:T(8,128)(2,1)S(1)}, bf16[64,3584]{1,0:T(8,128)(2,1)S(1)}) custom-call(s32[1]{0:T(128)} %bitcast.expert_ref, bf16[64,3712]{1,0:T(8,128)(2,1)S(1)} %constant_dynamic-update-slice_fusion.own_ref, bf16[64,3712]{1,0:T(8,128)(2,1)S(1)} %collective-permute-done.1.other_ref, bf16[3584,512]{1,0:T(8,128)(2,1)S(1)} %bitcast.4, ...), custom_call_target="tpu_custom_call" | custom-call | flops 1409286144 | bytes 11010048 | tf_op jit(solution)/shard_map/expert_half/pallas_call | solution.py:105
  15.3 0.1 collective-permute-start.13
  15.4 1.8 %collective-permute-start.4 = (bf16[64,3712]{1,0:T(8,128)(2,1)S(1)}, bf16[64,3712]{1,0:T(8,128)(2,1)S(1)}, u32[]{:S(2)}, u32[]{:S(2)}) collective-permute-start(bf16[64,3712]{1,0:T(8,128)(2,1)S(1)} %collective-permute-done.3.own_ref), channel_id=1, source_target_pairs={{0,2},{10,8},{2,4},{12,10},{4,6},{14,12},{6,7},{15,14},{7,5},{13,1... | collective-permute-start | bytes 1425416 | tf_op jit(solution)/shard_map/ppermute | solution.py:153
  17.3 0.5 copy-done.5
  17.8 1.7 %expert_half.10 = (bf16[64,3584]{1,0:T(8,128)(2,1)S(1)}, bf16[64,3584]{1,0:T(8,128)(2,1)S(1)}) custom-call(s32[1]{0:T(128)} %bitcast.expert_ref, bf16[64,3712]{1,0:T(8,128)(2,1)S(1)} %collective-permute-done.3.own_ref, bf16[64,3712]{1,0:T(8,128)(2,1)S(1)} %collective-permute-done.13.other_ref, bf16[3584,512]{1,0:T(8,128)(2,1)S(1)} %bitcast.5, ...), custom_call_target="tpu_custom_call" | custom-call | flops 1409286144 | bytes 11010048 | tf_op jit(solution)/shard_map/expert_half/pallas_call | solution.py:105
  19.5 0.1 collective-permute-start.23
  19.6 4.5 %collective-permute-done.4.own_ref = bf16[64,3712]{1,0:T(8,128)(2,1)S(1)} collective-permute-done((bf16[64,3712]{1,0:T(8,128)(2,1)S(1)}, bf16[64,3712]{1,0:T(8,128)(2,1)S(1)}, u32[]{:S(2)}, u32[]{:S(2)}) %collective-permute-start.4) | collective-permute-done | bytes 475168 | tf_op jit(solution)/shard_map/ppermute | solution.py:153
  24.1 1.8 %collective-permute-start.5 = (bf16[64,3712]{1,0:T(8,128)(2,1)S(1)}, bf16[64,3712]{1,0:T(8,128)(2,1)S(1)}, u32[]{:S(2)}, u32[]{:S(2)}) collective-permute-start(bf16[64,3712]{1,0:T(8,128)(2,1)S(1)} %collective-permute-done.4.own_ref), channel_id=1, source_target_pairs={{0,2},{10,8},{2,4},{12,10},{4,6},{14,12},{6,7},{15,14},{7,5},{13,1... | collective-permute-start | bytes 1425416 | tf_op jit(solution)/shard_map/ppermute | solution.py:153
  25.9 0.1 add_convert_fusion.7
  26.0 1.6 %collective-permute-start.24 = (bf16[64,3584]{1,0:T(8,128)(2,1)S(1)}, bf16[64,3584]{1,0:T(8,128)(2,1)S(1)}, u32[]{:S(2)}, u32[]{:S(2)}) collective-permute-start(bf16[64,3584]{1,0:T(8,128)(2,1)S(1)} %add_convert_fusion.7), channel_id=1, source_target_pairs={{0,2},{10,8},{2,4},{12,10},{4,6},{14,12},{6,7},{15,14},{7,5},{13,1... | collective-permute-start | bytes 1376264 | tf_op jit(solution)/shard_map/ppermute | solution.py:153
  27.7 1.7 %expert_half.11 = (bf16[64,3584]{1,0:T(8,128)(2,1)S(1)}, bf16[64,3584]{1,0:T(8,128)(2,1)S(1)}) custom-call(s32[1]{0:T(128)} %bitcast.expert_ref, bf16[64,3712]{1,0:T(8,128)(2,1)S(1)} %collective-permute-done.4.own_ref, bf16[64,3712]{1,0:T(8,128)(2,1)S(1)} %collective-permute-done.14.other_ref, bf16[3584,512]{1,0:T(8,128)(2,1)S(1)} %bitcast.6, ...), custom_call_target="tpu_custom_call" | custom-call | flops 1409286144 | bytes 11010048 | tf_op jit(solution)/shard_map/expert_half/pallas_call | solution.py:105
  29.6 2.6 %attend.4 = (bf16[64,64,512]{2,1,0:T(8,128)(2,1)}, f32[8,128]{1,0:T(8,128)S(1)}) custom-call(s32[64]{0:T(128)S(1)} %copy-done.6, bf16[64,64,576]{2,1,0:T(8,128)(2,1)S(1)} %bitcast.29, bf16[64,64,576]{2,1,0:T(8,128)(2,1)S(1)} %bitcast.31, bf16[64,3584]{1,0:T(8,128)(2,1)S(1)} %get-tuple-element.34.rest_0_), custom_call_target="tpu_custom_call" | custom-call | flops 142606336 | bytes 3407872 | tf_op jit(solution)/shard_map/attend/pallas_call | solution.py:59
  32.1 0.7 collective-permute-done.5.own_ref
  32.8 1.8 %collective-permute-start.6 = (bf16[64,3712]{1,0:T(8,128)(2,1)S(1)}, bf16[64,3712]{1,0:T(8,128)(2,1)S(1)}, u32[]{:S(2)}, u32[]{:S(2)}) collective-permute-start(bf16[64,3712]{1,0:T(8,128)(2,1)S(1)} %collective-permute-done.5.own_ref), channel_id=1, source_target_pairs={{0,2},{10,8},{2,4},{12,10},{4,6},{14,12},{6,7},{15,14},{7,5},{13,1... | collective-permute-start | bytes 1425416 | tf_op jit(solution)/shard_map/ppermute | solution.py:153
  34.6 3.1 %collective-permute-done.24 = bf16[64,3584]{1,0:T(8,128)(2,1)S(1)} collective-permute-done((bf16[64,3584]{1,0:T(8,128)(2,1)S(1)}, bf16[64,3584]{1,0:T(8,128)(2,1)S(1)}, u32[]{:S(2)}, u32[]{:S(2)}) %collective-permute-start.24) | collective-permute-done | bytes 458784 | tf_op jit(solution)/shard_map/ppermute | solution.py:153
  37.7 0.2 add_convert_fusion.6
  37.9 1.8 %collective-permute-start.25 = (bf16[64,3584]{1,0:T(8,128)(2,1)S(1)}, bf16[64,3584]{1,0:T(8,128)(2,1)S(1)}, u32[]{:S(2)}, u32[]{:S(2)}) collective-permute-start(bf16[64,3584]{1,0:T(8,128)(2,1)S(1)} %add_convert_fusion.6), channel_id=1, source_target_pairs={{0,2},{10,8},{2,4},{12,10},{4,6},{14,12},{6,7},{15,14},{7,5},{13,1... | collective-permute-start | bytes 1376264 | tf_op jit(solution)/shard_map/ppermute | solution.py:153
  39.7 1.7 %expert_half.12 = (bf16[64,3584]{1,0:T(8,128)(2,1)S(1)}, bf16[64,3584]{1,0:T(8,128)(2,1)S(1)}) custom-call(s32[1]{0:T(128)} %bitcast.expert_ref, bf16[64,3712]{1,0:T(8,128)(2,1)S(1)} %collective-permute-done.5.own_ref, bf16[64,3712]{1,0:T(8,128)(2,1)S(1)} %collective-permute-done.15.other_ref, bf16[3584,512]{1,0:T(8,128)(2,1)S(1)} %bitcast.7, ...), custom_call_target="tpu_custom_call" | custom-call | flops 1409286144 | bytes 11010048 | tf_op jit(solution)/shard_map/expert_half/pallas_call | solution.py:105
  41.4 0.1 collective-permute-start.21
  41.5 2.6 %attend.5 = (bf16[64,64,512]{2,1,0:T(8,128)(2,1)}, f32[8,128]{1,0:T(8,128)S(1)}) custom-call(s32[64]{0:T(128)S(1)} %copy-done.6, bf16[64,64,576]{2,1,0:T(8,128)(2,1)S(1)} %bitcast.29, bf16[64,64,576]{2,1,0:T(8,128)(2,1)S(1)} %bitcast.31, bf16[64,64,512]{2,1,0:T(8,128)(2,1)} %get-tuple-element.35.rest_0_, ...), custom_call_target="tpu_custom_call", output_to_operand_aliasing={{0}: (3, {})} | custom-call | flops 142606336 | bytes 3407872 | tf_op jit(solution)/shard_map/attend/pallas_call | solution.py:59
  44.1 0.5 collective-permute-start.16
  44.6 1.6 %collective-permute-start.7 = (bf16[64,3712]{1,0:T(8,128)(2,1)S(1)}, bf16[64,3712]{1,0:T(8,128)(2,1)S(1)}, u32[]{:S(2)}, u32[]{:S(2)}) collective-permute-start(bf16[64,3712]{1,0:T(8,128)(2,1)S(1)} %collective-permute-done.6.own_ref), channel_id=1, source_target_pairs={{0,2},{10,8},{2,4},{12,10},{4,6},{14,12},{6,7},{15,14},{7,5},{13,1... | collective-permute-start | bytes 1425416 | tf_op jit(solution)/shard_map/ppermute | solution.py:153
  46.2 1.5 %collective-permute-done.25 = bf16[64,3584]{1,0:T(8,128)(2,1)S(1)} collective-permute-done((bf16[64,3584]{1,0:T(8,128)(2,1)S(1)}, bf16[64,3584]{1,0:T(8,128)(2,1)S(1)}, u32[]{:S(2)}, u32[]{:S(2)}) %collective-permute-start.25) | collective-permute-done | bytes 458784 | tf_op jit(solution)/shard_map/ppermute | solution.py:153
  47.7 0.2 add_convert_fusion.5
  47.9 2.0 %collective-permute-start.26 = (bf16[64,3584]{1,0:T(8,128)(2,1)S(1)}, bf16[64,3584]{1,0:T(8,128)(2,1)S(1)}, u32[]{:S(2)}, u32[]{:S(2)}) collective-permute-start(bf16[64,3584]{1,0:T(8,128)(2,1)S(1)} %add_convert_fusion.5), channel_id=1, source_target_pairs={{0,2},{10,8},{2,4},{12,10},{4,6},{14,12},{6,7},{15,14},{7,5},{13,1... | collective-permute-start | bytes 1376264 | tf_op jit(solution)/shard_map/ppermute | solution.py:153
  49.9 1.7 %expert_half.13 = (bf16[64,3584]{1,0:T(8,128)(2,1)S(1)}, bf16[64,3584]{1,0:T(8,128)(2,1)S(1)}) custom-call(s32[1]{0:T(128)} %bitcast.expert_ref, bf16[64,3712]{1,0:T(8,128)(2,1)S(1)} %collective-permute-done.6.own_ref, bf16[64,3712]{1,0:T(8,128)(2,1)S(1)} %collective-permute-done.16.other_ref, bf16[3584,512]{1,0:T(8,128)(2,1)S(1)} %bitcast.8, ...), custom_call_target="tpu_custom_call" | custom-call | flops 1409286144 | bytes 11010048 | tf_op jit(solution)/shard_map/expert_half/pallas_call | solution.py:105
  51.7 2.6 %attend.6 = (bf16[64,64,512]{2,1,0:T(8,128)(2,1)}, f32[8,128]{1,0:T(8,128)S(1)}) custom-call(s32[64]{0:T(128)S(1)} %copy-done.6, bf16[64,64,576]{2,1,0:T(8,128)(2,1)S(1)} %bitcast.29, bf16[64,64,576]{2,1,0:T(8,128)(2,1)S(1)} %bitcast.31, bf16[64,64,512]{2,1,0:T(8,128)(2,1)} %get-tuple-element.37.rest_0_, ...), custom_call_target="tpu_custom_call", output_to_operand_aliasing={{0}: (3, {})} | custom-call | flops 142606336 | bytes 3407872 | tf_op jit(solution)/shard_map/attend/pallas_call | solution.py:59
  54.3 0.5 collective-permute-start.18
  54.8 1.6 %collective-permute-start.8 = (bf16[64,3712]{1,0:T(8,128)(2,1)S(1)}, bf16[64,3712]{1,0:T(8,128)(2,1)S(1)}, u32[]{:S(2)}, u32[]{:S(2)}) collective-permute-start(bf16[64,3712]{1,0:T(8,128)(2,1)S(1)} %collective-permute-done.7.own_ref), channel_id=1, source_target_pairs={{0,2},{10,8},{2,4},{12,10},{4,6},{14,12},{6,7},{15,14},{7,5},{13,1... | collective-permute-start | bytes 1425416 | tf_op jit(solution)/shard_map/ppermute | solution.py:153
  56.4 1.8 %collective-permute-done.26 = bf16[64,3584]{1,0:T(8,128)(2,1)S(1)} collective-permute-done((bf16[64,3584]{1,0:T(8,128)(2,1)S(1)}, bf16[64,3584]{1,0:T(8,128)(2,1)S(1)}, u32[]{:S(2)}, u32[]{:S(2)}) %collective-permute-start.26) | collective-permute-done | bytes 458784 | tf_op jit(solution)/shard_map/ppermute | solution.py:153
  58.2 0.2 add_convert_fusion.4
  58.3 1.6 %collective-permute-start.27 = (bf16[64,3584]{1,0:T(8,128)(2,1)S(1)}, bf16[64,3584]{1,0:T(8,128)(2,1)S(1)}, u32[]{:S(2)}, u32[]{:S(2)}) collective-permute-start(bf16[64,3584]{1,0:T(8,128)(2,1)S(1)} %add_convert_fusion.4), channel_id=1, source_target_pairs={{0,2},{10,8},{2,4},{12,10},{4,6},{14,12},{6,7},{15,14},{7,5},{13,1... | collective-permute-start | bytes 1376264 | tf_op jit(solution)/shard_map/ppermute | solution.py:153
  60.0 1.7 %expert_half.15 = (bf16[64,3584]{1,0:T(8,128)(2,1)S(1)}, bf16[64,3584]{1,0:T(8,128)(2,1)S(1)}) custom-call(s32[1]{0:T(128)} %bitcast.expert_ref, bf16[64,3712]{1,0:T(8,128)(2,1)S(1)} %collective-permute-done.7.own_ref, bf16[64,3712]{1,0:T(8,128)(2,1)S(1)} %collective-permute-done.18.other_ref, bf16[3584,512]{1,0:T(8,128)(2,1)S(1)} %bitcast.9, ...), custom_call_target="tpu_custom_call" | custom-call | flops 1409286144 | bytes 11010048 | tf_op jit(solution)/shard_map/expert_half/pallas_call | solution.py:105
  61.7 0.1 collective-permute-start.19
  61.8 2.6 %attend.7 = (bf16[64,64,512]{2,1,0:T(8,128)(2,1)}, f32[8,128]{1,0:T(8,128)S(1)}) custom-call(s32[64]{0:T(128)S(1)} %copy-done.6, bf16[64,64,576]{2,1,0:T(8,128)(2,1)S(1)} %bitcast.29, bf16[64,64,576]{2,1,0:T(8,128)(2,1)S(1)} %bitcast.31, bf16[64,64,512]{2,1,0:T(8,128)(2,1)} %get-tuple-element.40.rest_0_, ...), custom_call_target="tpu_custom_call", output_to_operand_aliasing={{0}: (3, {})} | custom-call | flops 142606336 | bytes 3407872 | tf_op jit(solution)/shard_map/attend/pallas_call | solution.py:59
  64.4 0.5 collective-permute-start.12
  64.9 1.6 %collective-permute-start.9 = (bf16[64,3712]{1,0:T(8,128)(2,1)S(1)}, bf16[64,3712]{1,0:T(8,128)(2,1)S(1)}, u32[]{:S(2)}, u32[]{:S(2)}) collective-permute-start(bf16[64,3712]{1,0:T(8,128)(2,1)S(1)} %collective-permute-done.8.own_ref), channel_id=1, source_target_pairs={{0,2},{10,8},{2,4},{12,10},{4,6},{14,12},{6,7},{15,14},{7,5},{13,1... | collective-permute-start | bytes 1425416 | tf_op jit(solution)/shard_map/ppermute | solution.py:153
  66.4 1.9 %collective-permute-done.27 = bf16[64,3584]{1,0:T(8,128)(2,1)S(1)} collective-permute-done((bf16[64,3584]{1,0:T(8,128)(2,1)S(1)}, bf16[64,3584]{1,0:T(8,128)(2,1)S(1)}, u32[]{:S(2)}, u32[]{:S(2)}) %collective-permute-start.27) | collective-permute-done | bytes 458784 | tf_op jit(solution)/shard_map/ppermute | solution.py:153
  68.4 0.2 add_convert_fusion.3
  68.5 1.6 %collective-permute-start.28 = (bf16[64,3584]{1,0:T(8,128)(2,1)S(1)}, bf16[64,3584]{1,0:T(8,128)(2,1)S(1)}, u32[]{:S(2)}, u32[]{:S(2)}) collective-permute-start(bf16[64,3584]{1,0:T(8,128)(2,1)S(1)} %add_convert_fusion.3), channel_id=1, source_target_pairs={{0,2},{10,8},{2,4},{12,10},{4,6},{14,12},{6,7},{15,14},{7,5},{13,1... | collective-permute-start | bytes 1376264 | tf_op jit(solution)/shard_map/ppermute | solution.py:153
  70.2 1.7 %expert_half.14 = (bf16[64,3584]{1,0:T(8,128)(2,1)S(1)}, bf16[64,3584]{1,0:T(8,128)(2,1)S(1)}) custom-call(s32[1]{0:T(128)} %bitcast.expert_ref, bf16[64,3712]{1,0:T(8,128)(2,1)S(1)} %collective-permute-done.8.own_ref, bf16[64,3712]{1,0:T(8,128)(2,1)S(1)} %collective-permute-done.12.other_ref, bf16[3584,512]{1,0:T(8,128)(2,1)S(1)} %bitcast.10, ...), custom_call_target="tpu_custom_call" | custom-call | flops 1409286144 | bytes 11010048 | tf_op jit(solution)/shard_map/expert_half/pallas_call | solution.py:105
  72.0 1.6 %collective-permute-done.9.own_ref = bf16[64,3712]{1,0:T(8,128)(2,1)S(1)} collective-permute-done((bf16[64,3712]{1,0:T(8,128)(2,1)S(1)}, bf16[64,3712]{1,0:T(8,128)(2,1)S(1)}, u32[]{:S(2)}, u32[]{:S(2)}) %collective-permute-start.9) | collective-permute-done | bytes 475168 | tf_op jit(solution)/shard_map/ppermute | solution.py:153
  73.5 4.9 %collective-permute-done.28 = bf16[64,3584]{1,0:T(8,128)(2,1)S(1)} collective-permute-done((bf16[64,3584]{1,0:T(8,128)(2,1)S(1)}, bf16[64,3584]{1,0:T(8,128)(2,1)S(1)}, u32[]{:S(2)}, u32[]{:S(2)}) %collective-permute-start.28) | collective-permute-done | bytes 458784 | tf_op jit(solution)/shard_map/ppermute | solution.py:153
  78.4 0.2 add_convert_fusion.2
  78.6 1.6 %collective-permute-start.29 = (bf16[64,3584]{1,0:T(8,128)(2,1)S(1)}, bf16[64,3584]{1,0:T(8,128)(2,1)S(1)}, u32[]{:S(2)}, u32[]{:S(2)}) collective-permute-start(bf16[64,3584]{1,0:T(8,128)(2,1)S(1)} %add_convert_fusion.2), channel_id=1, source_target_pairs={{0,2},{10,8},{2,4},{12,10},{4,6},{14,12},{6,7},{15,14},{7,5},{13,1... | collective-permute-start | bytes 1376264 | tf_op jit(solution)/shard_map/ppermute | solution.py:153
  80.3 1.7 %expert_half.9 = (bf16[64,3584]{1,0:T(8,128)(2,1)S(1)}, bf16[64,3584]{1,0:T(8,128)(2,1)S(1)}) custom-call(s32[1]{0:T(128)} %bitcast.expert_ref, bf16[64,3712]{1,0:T(8,128)(2,1)S(1)} %collective-permute-done.9.own_ref, bf16[64,3712]{1,0:T(8,128)(2,1)S(1)} %collective-permute-done.10.other_ref, bf16[3584,512]{1,0:T(8,128)(2,1)S(1)} %bitcast.11, ...), custom_call_target="tpu_custom_call" | custom-call | flops 1409286144 | bytes 11010048 | tf_op jit(solution)/shard_map/expert_half/pallas_call | solution.py:105
  82.0 0.1 collective-permute-start.11
  82.1 0.5 collective-permute-start.2
  82.6 4.6 %collective-permute-done.29 = bf16[64,3584]{1,0:T(8,128)(2,1)S(1)} collective-permute-done((bf16[64,3584]{1,0:T(8,128)(2,1)S(1)}, bf16[64,3584]{1,0:T(8,128)(2,1)S(1)}, u32[]{:S(2)}, u32[]{:S(2)}) %collective-permute-start.29) | collective-permute-done | bytes 458784 | tf_op jit(solution)/shard_map/ppermute | solution.py:153
  87.2 0.2 add_convert_fusion.1
  87.5 1.6 %collective-permute-start.30 = (bf16[32,3584]{1,0:T(8,128)(2,1)S(1)}, bf16[32,3584]{1,0:T(8,128)(2,1)S(1)}, u32[]{:S(2)}, u32[]{:S(2)}) collective-permute-start(bf16[32,3584]{1,0:T(8,128)(2,1)S(1)} %get-tuple-element.54), channel_id=1, source_target_pairs={{0,2},{10,8},{2,4},{12,10},{4,6},{14,12},{6,7},{15,14},{7,5},{13,1... | collective-permute-start | bytes 688136 | tf_op jit(solution)/shard_map/ppermute | solution.py:153
  89.1 3.8 %collective-permute-done.31 = bf16[32,3584]{1,0:T(8,128)(2,1)S(1)} collective-permute-done((bf16[32,3584]{1,0:T(8,128)(2,1)S(1)}, bf16[32,3584]{1,0:T(8,128)(2,1)S(1)}, u32[]{:S(2)}, u32[]{:S(2)}) %collective-permute-start.31) | collective-permute-done | bytes 229408 | tf_op jit(solution)/shard_map/ppermute | solution.py:153
  92.9 2.0 %collective-permute-done.30 = bf16[32,3584]{1,0:T(8,128)(2,1)S(1)} collective-permute-done((bf16[32,3584]{1,0:T(8,128)(2,1)S(1)}, bf16[32,3584]{1,0:T(8,128)(2,1)S(1)}, u32[]{:S(2)}, u32[]{:S(2)}) %collective-permute-start.30) | collective-permute-done | bytes 229408 | tf_op jit(solution)/shard_map/ppermute | solution.py:153
  94.9 1.0 %add_convert_fusion = bf16[64,3584]{1,0:T(8,128)(2,1)} fusion(bf16[64,3584]{1,0:T(8,128)(2,1)S(1)} %collective-permute-done.2, bf16[64,3584]{1,0:T(8,128)(2,1)S(1)} %get-tuple-element.29.rest_0_, bf16[32,3584]{1,0:T(8,128)(2,1)S(1)} %collective-permute-done.31, bf16[32,3584]{1,0:T(8,128)(2,1)S(1)} %collective-permute-done.30, pred[]{:T(512)S(6)} %eq.19), kind=kLoop, calls=%fused_computation | loop fusion | flops 3440640 | bytes 1835009 | tf_op jit(solution)/shard_map/convert_element_type | solution.py:212
  (52 shorter events, 0.5 us)
Async XLA Ops:
  2.6 1.6 %collective-permute-start = (bf16[32,3712]{1,0:T(8,128)(2,1)S(1)}, bf16[32,3712]{1,0:T(8,128)(2,1)S(1)}, u32[]{:S(2)}, u32[]{:S(2)}) collective-permute-start(bf16[32,3712]{1,0:T(8,128)(2,1)S(1)} %pad_maximum_fusion.1), channel_id=1, source_target_pairs={{0,8},{8,0},{1,9},{9,1},{2,10},{10,2},{3,11},{11,3},{4,12},{12,4},... | collective-permute-start | bytes 712712 | tf_op jit(solution)/shard_map/ppermute | solution.py:156
  4.3 3.1 %collective-permute-start.1 = (bf16[64,3712]{1,0:T(8,128)(2,1)S(1)}, bf16[64,3712]{1,0:T(8,128)(2,1)S(1)}, u32[]{:S(2)}, u32[]{:S(2)}) collective-permute-start(bf16[64,3712]{1,0:T(8,128)(2,1)S(1)} %constant_dynamic-update-slice_fusion.own_ref), channel_id=1, source_target_pairs={{0,8},{8,0},{1,9},{9,1},{2,10},{10,2},{3,11},{11,3},{4,12},{12,4},... | collective-permute-start | bytes 1425416 | tf_op jit(solution)/shard_map/ppermute | solution.py:156
  4.7 10.6 %collective-permute-start.3 = (bf16[64,3712]{1,0:T(8,128)(2,1)S(1)}, bf16[64,3712]{1,0:T(8,128)(2,1)S(1)}, u32[]{:S(2)}, u32[]{:S(2)}) collective-permute-start(bf16[64,3712]{1,0:T(8,128)(2,1)S(1)} %pad_maximum_fusion), channel_id=1, source_target_pairs={{0,2},{10,8},{2,4},{12,10},{4,6},{14,12},{6,7},{15,14},{7,5},{13,1... | collective-permute-start | bytes 1425416 | tf_op jit(solution)/shard_map/ppermute | solution.py:153
  7.4 2.0 %copy-start = (bf16[1,3584,512]{2,1,0:T(8,128)(2,1)S(1)}, bf16[1,3584,512]{2,1,0:T(8,128)(2,1)}, u32[]{:S(2)}) copy-start(bf16[1,3584,512]{2,1,0:T(8,128)(2,1)} %param.12) | copy-start | bytes 11010052
  9.5 2.0 %copy-start.2 = (bf16[1,3584,512]{2,1,0:T(8,128)(2,1)S(1)}, bf16[1,3584,512]{2,1,0:T(8,128)(2,1)}, u32[]{:S(2)}) copy-start(bf16[1,3584,512]{2,1,0:T(8,128)(2,1)} %param.13) | copy-start | bytes 11010052
  11.5 2.0 %copy-start.4 = (bf16[1,512,3584]{2,1,0:T(8,128)(2,1)S(1)}, bf16[1,512,3584]{2,1,0:T(8,128)(2,1)}, u32[]{:S(2)}) copy-start(bf16[1,512,3584]{2,1,0:T(8,128)(2,1)} %param.14) | copy-start | bytes 11010052
  13.6 3.7 %copy-start.1 = (bf16[1,3584,512]{2,1,0:T(8,128)(2,1)S(1)}, bf16[1,3584,512]{2,1,0:T(8,128)(2,1)}, u32[]{:S(2)}) copy-start(bf16[1,3584,512]{2,1,0:T(8,128)(2,1)} %param.12) | copy-start | bytes 11010052
  13.6 3.7 %copy-start.3 = (bf16[1,3584,512]{2,1,0:T(8,128)(2,1)S(1)}, bf16[1,3584,512]{2,1,0:T(8,128)(2,1)}, u32[]{:S(2)}) copy-start(bf16[1,3584,512]{2,1,0:T(8,128)(2,1)} %param.13) | copy-start | bytes 11010052
  13.6 4.2 %copy-start.5 = (bf16[1,512,3584]{2,1,0:T(8,128)(2,1)S(1)}, bf16[1,512,3584]{2,1,0:T(8,128)(2,1)}, u32[]{:S(2)}) copy-start(bf16[1,512,3584]{2,1,0:T(8,128)(2,1)} %param.14) | copy-start | bytes 11010052
  15.3 1.9 %collective-permute-start.13 = (bf16[64,3712]{1,0:T(8,128)(2,1)S(1)}, bf16[64,3712]{1,0:T(8,128)(2,1)S(1)}, u32[]{:S(2)}, u32[]{:S(2)}) collective-permute-start(bf16[64,3712]{1,0:T(8,128)(2,1)S(1)} %collective-permute-done.3.own_ref), channel_id=1, source_target_pairs={{0,8},{8,0},{1,9},{9,1},{2,10},{10,2},{3,11},{11,3},{4,12},{12,4},... | collective-permute-start | bytes 1425416 | tf_op jit(solution)/shard_map/ppermute | solution.py:156
  15.4 8.7 %collective-permute-start.4 = (bf16[64,3712]{1,0:T(8,128)(2,1)S(1)}, bf16[64,3712]{1,0:T(8,128)(2,1)S(1)}, u32[]{:S(2)}, u32[]{:S(2)}) collective-permute-start(bf16[64,3712]{1,0:T(8,128)(2,1)S(1)} %collective-permute-done.3.own_ref), channel_id=1, source_target_pairs={{0,2},{10,8},{2,4},{12,10},{4,6},{14,12},{6,7},{15,14},{7,5},{13,1... | collective-permute-start | bytes 1425416 | tf_op jit(solution)/shard_map/ppermute | solution.py:153
  17.8 11.7 %slice-start.2 = ((s8[5242880]{0:T(1024)(128)(4,1)}), s8[4194304]{0:T(1024)(128)(4,1)S(1)}, s32[]{:S(2)}) async-start(s8[5242880]{0:T(1024)(128)(4,1)} %bitcast.30), calls=%async_computation.2 | async-start | bytes 8388608
  19.5 6.4 %collective-permute-start.23 = (bf16[64,3584]{1,0:T(8,128)(2,1)S(1)}, bf16[64,3584]{1,0:T(8,128)(2,1)S(1)}, u32[]{:S(2)}, u32[]{:S(2)}) collective-permute-start(bf16[64,3584]{1,0:T(8,128)(2,1)S(1)} %get-tuple-element.52), channel_id=1, source_target_pairs={{0,8},{8,0},{1,9},{9,1},{2,10},{10,2},{3,11},{11,3},{4,12},{12,4},... | collective-permute-start | bytes 1376264 | tf_op jit(solution)/shard_map/ppermute | solution.py:156
  24.1 3.6 %collective-permute-start.14 = (bf16[64,3712]{1,0:T(8,128)(2,1)S(1)}, bf16[64,3712]{1,0:T(8,128)(2,1)S(1)}, u32[]{:S(2)}, u32[]{:S(2)}) collective-permute-start(bf16[64,3712]{1,0:T(8,128)(2,1)S(1)} %collective-permute-done.4.own_ref), channel_id=1, source_target_pairs={{0,8},{8,0},{1,9},{9,1},{2,10},{10,2},{3,11},{11,3},{4,12},{12,4},... | collective-permute-start | bytes 1425416 | tf_op jit(solution)/shard_map/ppermute | solution.py:156
  24.1 8.7 %collective-permute-start.5 = (bf16[64,3712]{1,0:T(8,128)(2,1)S(1)}, bf16[64,3712]{1,0:T(8,128)(2,1)S(1)}, u32[]{:S(2)}, u32[]{:S(2)}) collective-permute-start(bf16[64,3712]{1,0:T(8,128)(2,1)S(1)} %collective-permute-done.4.own_ref), channel_id=1, source_target_pairs={{0,2},{10,8},{2,4},{12,10},{4,6},{14,12},{6,7},{15,14},{7,5},{13,1... | collective-permute-start | bytes 1425416 | tf_op jit(solution)/shard_map/ppermute | solution.py:153
  25.9 3.6 %slice-start = ((s8[5242880]{0:T(1024)(128)(4,1)}), s8[4194304]{0:T(1024)(128)(4,1)S(1)}, s32[]{:S(2)}) async-start(s8[5242880]{0:T(1024)(128)(4,1)} %bitcast.28), calls=%async_computation | async-start | bytes 8388608
  25.9 3.6 %slice-start.3 = ((s8[5242880]{0:T(1024)(128)(4,1)}), s8[1048576]{0:T(1024)(128)(4,1)S(1)}, s32[]{:S(2)}) async-start(s8[5242880]{0:T(1024)(128)(4,1)} %bitcast.30), calls=%async_computation.3 | async-start | bytes 2097152
  26.0 3.5 %slice-start.1 = ((s8[5242880]{0:T(1024)(128)(4,1)}), s8[1048576]{0:T(1024)(128)(4,1)S(1)}, s32[]{:S(2)}) async-start(s8[5242880]{0:T(1024)(128)(4,1)} %bitcast.28), calls=%async_computation.1 | async-start | bytes 2097152
  26.0 3.5 %copy-start.6 = (s32[64]{0:T(128)S(1)}, s32[64]{0:T(128)}, u32[]{:S(2)}) copy-start(s32[64]{0:T(128)} %len_ref.7) | copy-start | bytes 772
  26.0 11.7 %collective-permute-start.24 = (bf16[64,3584]{1,0:T(8,128)(2,1)S(1)}, bf16[64,3584]{1,0:T(8,128)(2,1)S(1)}, u32[]{:S(2)}, u32[]{:S(2)}) collective-permute-start(bf16[64,3584]{1,0:T(8,128)(2,1)S(1)} %add_convert_fusion.7), channel_id=1, source_target_pairs={{0,2},{10,8},{2,4},{12,10},{4,6},{14,12},{6,7},{15,14},{7,5},{13,1... | collective-permute-start | bytes 1376264 | tf_op jit(solution)/shard_map/ppermute | solution.py:153
  29.4 8.3 %collective-permute-start.22 = (bf16[64,3584]{1,0:T(8,128)(2,1)S(1)}, bf16[64,3584]{1,0:T(8,128)(2,1)S(1)}, u32[]{:S(2)}, u32[]{:S(2)}) collective-permute-start(bf16[64,3584]{1,0:T(8,128)(2,1)S(1)} %get-tuple-element.51), channel_id=1, source_target_pairs={{0,8},{8,0},{1,9},{9,1},{2,10},{10,2},{3,11},{11,3},{4,12},{12,4},... | collective-permute-start | bytes 1376264 | tf_op jit(solution)/shard_map/ppermute | solution.py:156
  32.8 6.9 %collective-permute-start.15 = (bf16[64,3712]{1,0:T(8,128)(2,1)S(1)}, bf16[64,3712]{1,0:T(8,128)(2,1)S(1)}, u32[]{:S(2)}, u32[]{:S(2)}) collective-permute-start(bf16[64,3712]{1,0:T(8,128)(2,1)S(1)} %collective-permute-done.5.own_ref), channel_id=1, source_target_pairs={{0,8},{8,0},{1,9},{9,1},{2,10},{10,2},{3,11},{11,3},{4,12},{12,4},... | collective-permute-start | bytes 1425416 | tf_op jit(solution)/shard_map/ppermute | solution.py:156
  32.8 11.3 %collective-permute-start.6 = (bf16[64,3712]{1,0:T(8,128)(2,1)S(1)}, bf16[64,3712]{1,0:T(8,128)(2,1)S(1)}, u32[]{:S(2)}, u32[]{:S(2)}) collective-permute-start(bf16[64,3712]{1,0:T(8,128)(2,1)S(1)} %collective-permute-done.5.own_ref), channel_id=1, source_target_pairs={{0,2},{10,8},{2,4},{12,10},{4,6},{14,12},{6,7},{15,14},{7,5},{13,1... | collective-permute-start | bytes 1425416 | tf_op jit(solution)/shard_map/ppermute | solution.py:153
  37.9 9.8 %collective-permute-start.25 = (bf16[64,3584]{1,0:T(8,128)(2,1)S(1)}, bf16[64,3584]{1,0:T(8,128)(2,1)S(1)}, u32[]{:S(2)}, u32[]{:S(2)}) collective-permute-start(bf16[64,3584]{1,0:T(8,128)(2,1)S(1)} %add_convert_fusion.6), channel_id=1, source_target_pairs={{0,2},{10,8},{2,4},{12,10},{4,6},{14,12},{6,7},{15,14},{7,5},{13,1... | collective-permute-start | bytes 1376264 | tf_op jit(solution)/shard_map/ppermute | solution.py:153
  41.4 6.3 %collective-permute-start.21 = (bf16[64,3584]{1,0:T(8,128)(2,1)S(1)}, bf16[64,3584]{1,0:T(8,128)(2,1)S(1)}, u32[]{:S(2)}, u32[]{:S(2)}) collective-permute-start(bf16[64,3584]{1,0:T(8,128)(2,1)S(1)} %get-tuple-element.50), channel_id=1, source_target_pairs={{0,8},{8,0},{1,9},{9,1},{2,10},{10,2},{3,11},{11,3},{4,12},{12,4},... | collective-permute-start | bytes 1376264 | tf_op jit(solution)/shard_map/ppermute | solution.py:156
  44.1 5.8 %collective-permute-start.16 = (bf16[64,3712]{1,0:T(8,128)(2,1)S(1)}, bf16[64,3712]{1,0:T(8,128)(2,1)S(1)}, u32[]{:S(2)}, u32[]{:S(2)}) collective-permute-start(bf16[64,3712]{1,0:T(8,128)(2,1)S(1)} %collective-permute-done.6.own_ref), channel_id=1, source_target_pairs={{0,8},{8,0},{1,9},{9,1},{2,10},{10,2},{3,11},{11,3},{4,12},{12,4},... | collective-permute-start | bytes 1425416 | tf_op jit(solution)/shard_map/ppermute | solution.py:156
  44.6 9.7 %collective-permute-start.7 = (bf16[64,3712]{1,0:T(8,128)(2,1)S(1)}, bf16[64,3712]{1,0:T(8,128)(2,1)S(1)}, u32[]{:S(2)}, u32[]{:S(2)}) collective-permute-start(bf16[64,3712]{1,0:T(8,128)(2,1)S(1)} %collective-permute-done.6.own_ref), channel_id=1, source_target_pairs={{0,2},{10,8},{2,4},{12,10},{4,6},{14,12},{6,7},{15,14},{7,5},{13,1... | collective-permute-start | bytes 1425416 | tf_op jit(solution)/shard_map/ppermute | solution.py:153
  47.9 10.3 %collective-permute-start.26 = (bf16[64,3584]{1,0:T(8,128)(2,1)S(1)}, bf16[64,3584]{1,0:T(8,128)(2,1)S(1)}, u32[]{:S(2)}, u32[]{:S(2)}) collective-permute-start(bf16[64,3584]{1,0:T(8,128)(2,1)S(1)} %add_convert_fusion.5), channel_id=1, source_target_pairs={{0,2},{10,8},{2,4},{12,10},{4,6},{14,12},{6,7},{15,14},{7,5},{13,1... | collective-permute-start | bytes 1376264 | tf_op jit(solution)/shard_map/ppermute | solution.py:153
  51.6 6.5 %collective-permute-start.20 = (bf16[64,3584]{1,0:T(8,128)(2,1)S(1)}, bf16[64,3584]{1,0:T(8,128)(2,1)S(1)}, u32[]{:S(2)}, u32[]{:S(2)}) collective-permute-start(bf16[64,3584]{1,0:T(8,128)(2,1)S(1)} %get-tuple-element.49), channel_id=1, source_target_pairs={{0,8},{8,0},{1,9},{9,1},{2,10},{10,2},{3,11},{11,3},{4,12},{12,4},... | collective-permute-start | bytes 1376264 | tf_op jit(solution)/shard_map/ppermute | solution.py:156
  54.3 5.7 %collective-permute-start.18 = (bf16[64,3712]{1,0:T(8,128)(2,1)S(1)}, bf16[64,3712]{1,0:T(8,128)(2,1)S(1)}, u32[]{:S(2)}, u32[]{:S(2)}) collective-permute-start(bf16[64,3712]{1,0:T(8,128)(2,1)S(1)} %collective-permute-done.7.own_ref), channel_id=1, source_target_pairs={{0,8},{8,0},{1,9},{9,1},{2,10},{10,2},{3,11},{11,3},{4,12},{12,4},... | collective-permute-start | bytes 1425416 | tf_op jit(solution)/shard_map/ppermute | solution.py:156
  54.8 9.6 %collective-permute-start.8 = (bf16[64,3712]{1,0:T(8,128)(2,1)S(1)}, bf16[64,3712]{1,0:T(8,128)(2,1)S(1)}, u32[]{:S(2)}, u32[]{:S(2)}) collective-permute-start(bf16[64,3712]{1,0:T(8,128)(2,1)S(1)} %collective-permute-done.7.own_ref), channel_id=1, source_target_pairs={{0,2},{10,8},{2,4},{12,10},{4,6},{14,12},{6,7},{15,14},{7,5},{13,1... | collective-permute-start | bytes 1425416 | tf_op jit(solution)/shard_map/ppermute | solution.py:153
  58.3 10.0 %collective-permute-start.27 = (bf16[64,3584]{1,0:T(8,128)(2,1)S(1)}, bf16[64,3584]{1,0:T(8,128)(2,1)S(1)}, u32[]{:S(2)}, u32[]{:S(2)}) collective-permute-start(bf16[64,3584]{1,0:T(8,128)(2,1)S(1)} %add_convert_fusion.4), channel_id=1, source_target_pairs={{0,2},{10,8},{2,4},{12,10},{4,6},{14,12},{6,7},{15,14},{7,5},{13,1... | collective-permute-start | bytes 1376264 | tf_op jit(solution)/shard_map/ppermute | solution.py:153
  61.7 6.6 %collective-permute-start.19 = (bf16[64,3584]{1,0:T(8,128)(2,1)S(1)}, bf16[64,3584]{1,0:T(8,128)(2,1)S(1)}, u32[]{:S(2)}, u32[]{:S(2)}) collective-permute-start(bf16[64,3584]{1,0:T(8,128)(2,1)S(1)} %get-tuple-element.48), channel_id=1, source_target_pairs={{0,8},{8,0},{1,9},{9,1},{2,10},{10,2},{3,11},{11,3},{4,12},{12,4},... | collective-permute-start | bytes 1376264 | tf_op jit(solution)/shard_map/ppermute | solution.py:156
  64.4 5.8 %collective-permute-start.12 = (bf16[64,3712]{1,0:T(8,128)(2,1)S(1)}, bf16[64,3712]{1,0:T(8,128)(2,1)S(1)}, u32[]{:S(2)}, u32[]{:S(2)}) collective-permute-start(bf16[64,3712]{1,0:T(8,128)(2,1)S(1)} %collective-permute-done.8.own_ref), channel_id=1, source_target_pairs={{0,8},{8,0},{1,9},{9,1},{2,10},{10,2},{3,11},{11,3},{4,12},{12,4},... | collective-permute-start | bytes 1425416 | tf_op jit(solution)/shard_map/ppermute | solution.py:156
  64.9 8.7 %collective-permute-start.9 = (bf16[64,3712]{1,0:T(8,128)(2,1)S(1)}, bf16[64,3712]{1,0:T(8,128)(2,1)S(1)}, u32[]{:S(2)}, u32[]{:S(2)}) collective-permute-start(bf16[64,3712]{1,0:T(8,128)(2,1)S(1)} %collective-permute-done.8.own_ref), channel_id=1, source_target_pairs={{0,2},{10,8},{2,4},{12,10},{4,6},{14,12},{6,7},{15,14},{7,5},{13,1... | collective-permute-start | bytes 1425416 | tf_op jit(solution)/shard_map/ppermute | solution.py:153
  68.5 9.9 %collective-permute-start.28 = (bf16[64,3584]{1,0:T(8,128)(2,1)S(1)}, bf16[64,3584]{1,0:T(8,128)(2,1)S(1)}, u32[]{:S(2)}, u32[]{:S(2)}) collective-permute-start(bf16[64,3584]{1,0:T(8,128)(2,1)S(1)} %add_convert_fusion.3), channel_id=1, source_target_pairs={{0,2},{10,8},{2,4},{12,10},{4,6},{14,12},{6,7},{15,14},{7,5},{13,1... | collective-permute-start | bytes 1376264 | tf_op jit(solution)/shard_map/ppermute | solution.py:153
  71.9 6.5 %collective-permute-start.17 = (bf16[64,3584]{1,0:T(8,128)(2,1)S(1)}, bf16[64,3584]{1,0:T(8,128)(2,1)S(1)}, u32[]{:S(2)}, u32[]{:S(2)}) collective-permute-start(bf16[64,3584]{1,0:T(8,128)(2,1)S(1)} %get-tuple-element.45), channel_id=1, source_target_pairs={{0,8},{8,0},{1,9},{9,1},{2,10},{10,2},{3,11},{11,3},{4,12},{12,4},... | collective-permute-start | bytes 1376264 | tf_op jit(solution)/shard_map/ppermute | solution.py:156
  73.5 6.7 %collective-permute-start.10 = (bf16[64,3712]{1,0:T(8,128)(2,1)S(1)}, bf16[64,3712]{1,0:T(8,128)(2,1)S(1)}, u32[]{:S(2)}, u32[]{:S(2)}) collective-permute-start(bf16[64,3712]{1,0:T(8,128)(2,1)S(1)} %collective-permute-done.9.own_ref), channel_id=1, source_target_pairs={{0,8},{8,0},{1,9},{9,1},{2,10},{10,2},{3,11},{11,3},{4,12},{12,4},... | collective-permute-start | bytes 1425416 | tf_op jit(solution)/shard_map/ppermute | solution.py:156
  78.6 8.5 %collective-permute-start.29 = (bf16[64,3584]{1,0:T(8,128)(2,1)S(1)}, bf16[64,3584]{1,0:T(8,128)(2,1)S(1)}, u32[]{:S(2)}, u32[]{:S(2)}) collective-permute-start(bf16[64,3584]{1,0:T(8,128)(2,1)S(1)} %add_convert_fusion.2), channel_id=1, source_target_pairs={{0,2},{10,8},{2,4},{12,10},{4,6},{14,12},{6,7},{15,14},{7,5},{13,1... | collective-permute-start | bytes 1376264 | tf_op jit(solution)/shard_map/ppermute | solution.py:153
  82.0 5.2 %collective-permute-start.11 = (bf16[64,3584]{1,0:T(8,128)(2,1)S(1)}, bf16[64,3584]{1,0:T(8,128)(2,1)S(1)}, u32[]{:S(2)}, u32[]{:S(2)}) collective-permute-start(bf16[64,3584]{1,0:T(8,128)(2,1)S(1)} %get-tuple-element.33), channel_id=1, source_target_pairs={{0,8},{8,0},{1,9},{9,1},{2,10},{10,2},{3,11},{11,3},{4,12},{12,4},... | collective-permute-start | bytes 1376264 | tf_op jit(solution)/shard_map/ppermute | solution.py:156
  82.1 7.0 %collective-permute-start.2 = (bf16[64,3584]{1,0:T(8,128)(2,1)S(1)}, bf16[64,3584]{1,0:T(8,128)(2,1)S(1)}, u32[]{:S(2)}, u32[]{:S(2)}) collective-permute-start(bf16[64,3584]{1,0:T(8,128)(2,1)S(1)} %get-tuple-element.30), channel_id=1, source_target_pairs={{0,8},{8,0},{1,9},{9,1},{2,10},{10,2},{3,11},{11,3},{4,12},{12,4},... | collective-permute-start | bytes 1376264 | tf_op jit(solution)/shard_map/ppermute | solution.py:156
  87.4 5.5 %collective-permute-start.31 = (bf16[32,3584]{1,0:T(8,128)(2,1)S(1)}, bf16[32,3584]{1,0:T(8,128)(2,1)S(1)}, u32[]{:S(2)}, u32[]{:S(2)}) collective-permute-start(bf16[32,3584]{1,0:T(8,128)(2,1)S(1)} %get-tuple-element.55), channel_id=1, source_target_pairs={{0,10},{10,0},{2,12},{12,2},{4,14},{14,4},{6,15},{15,6},{7,13},{13... | collective-permute-start | bytes 688136 | tf_op jit(solution)/shard_map/ppermute | solution.py:153
  87.5 7.4 %collective-permute-start.30 = (bf16[32,3584]{1,0:T(8,128)(2,1)S(1)}, bf16[32,3584]{1,0:T(8,128)(2,1)S(1)}, u32[]{:S(2)}, u32[]{:S(2)}) collective-permute-start(bf16[32,3584]{1,0:T(8,128)(2,1)S(1)} %get-tuple-element.54), channel_id=1, source_target_pairs={{0,2},{10,8},{2,4},{12,10},{4,6},{14,12},{6,7},{15,14},{7,5},{13,1... | collective-permute-start | bytes 688136 | tf_op jit(solution)/shard_map/ppermute | solution.py:153

commit v5 on v4

--- a/solution.py
+++ b/solution.py
@@ -80,52 +80,71 @@
     )(lengths, queries, latent_cache, *extra)
 
 
-def expert_kernel(expert_ref, own_ref, other_ref, gate_ref, up_ref, down_ref, *rest):
-    own_out, other_out = rest[-2:]
-    rows, width = own_out.shape
-    x = jnp.concatenate([own_ref[:, :width], other_ref[:, :width]], axis=0)
+def expert_kernel(expert_ref, *refs, own_parts, parts):
+    sources = refs[:parts]
+    gate_ref, up_ref, down_ref = refs[parts : parts + 3]
+    outs = refs[-2:]
+    width = outs[0].shape[1]
+    x = jnp.concatenate([source[:, :width] for source in sources], axis=0)
     gate = jnp.dot(x, gate_ref[...], preferred_element_type=jnp.float32)
     up = jnp.dot(x, up_ref[...], preferred_element_type=jnp.float32)
     hidden = (gate / (1.0 + jnp.exp(-gate)) * up).astype(jnp.bfloat16)
     down = jnp.dot(hidden, down_ref[...], preferred_element_type=jnp.float32)
-    lane = lax.broadcasted_iota(jnp.int32, (rows, LANES), 1)
-    for at, source, out in ((0, own_ref, own_out), (rows, other_ref, other_out)):
+    at = 0
+    for i, source in enumerate(sources):
+        rows = source.shape[0]
+        lane = lax.broadcasted_iota(jnp.int32, (rows, LANES), 1)
         route = source[:, width:].astype(jnp.float32)
         weight = jnp.sum(jnp.where(lane == expert_ref[0], route, 0.0), axis=1, keepdims=True)
-        out[...] = (weight * down[at : at + rows]).astype(jnp.bfloat16)
+        out = outs[0] if i < own_parts else outs[1]
+        to = at if i < own_parts else at - outs[0].shape[0]
+        out[to : to + rows] = (weight * down[at : at + rows]).astype(jnp.bfloat16)
+        at += rows
 
 
 def run_experts(expert, own, other, gate, up, down, after=()):
-    rows, wide = own.shape
+    counts = [sum(part.shape[0] for part in parts) for parts in (own, other)]
     width, hidden = gate.shape
-
-    def whole(shape):
-        return pl.BlockSpec(shape, lambda i, e: (0, 0))
-
+    inputs = (*own, *other, gate, up, down)
     return pl.pallas_call(
-        expert_kernel,
+        functools.partial(
+            expert_kernel, own_parts=len(own), parts=len(own) + len(other)
+        ),
         grid_spec=pltpu.PrefetchScalarGridSpec(
             num_scalar_prefetch=1,
             grid=(1,),
-            in_specs=[
-                whole((rows, wide)),
-                whole((rows, wide)),
-                whole((width, hidden)),
-                whole((width, hidden)),
-                whole((hidden, width)),
-            ]
+            in_specs=[pl.BlockSpec(a.shape, lambda i, e: (0, 0)) for a in inputs]
             + [pl.BlockSpec(memory_space=pl.ANY)] * len(after),
-            out_specs=[whole((rows, width)), whole((rows, width))],
-        ),
-        out_shape=[jax.ShapeDtypeStruct((rows, width), jnp.bfloat16)] * 2,
+            out_specs=[pl.BlockSpec((count, width), lambda i, e: (0, 0)) for count in counts],
+        ),
+        out_shape=[jax.ShapeDtypeStruct((count, width), jnp.bfloat16) for count in counts],
         compiler_params=pltpu.CompilerParams(vmem_limit_bytes=16 << 20),
         cost_estimate=pl.CostEstimate(
-            flops=12 * rows * width * hidden,
+            flops=6 * sum(counts) * width * hidden,
             bytes_accessed=6 * width * hidden,
-            transcendentals=2 * rows * hidden,
+            transcendentals=sum(counts) * hidden,
         ),
         name="expert_half",
-    )(expert, own, other, gate, up, down, *after)
+    )(expert, *inputs, *after)
+
+
+def join_kernel(first_ref, second_ref, out_ref):
+    rows = first_ref.shape[0]
+    out_ref[:rows] = first_ref[...]
+    out_ref[rows:] = second_ref[...]
+
+
+def join(first, second):
+    rows, width = first.shape
+    return pl.pallas_call(
+        join_kernel,
+        grid=(1,),
+        in_specs=[pl.BlockSpec((rows, width), lambda i: (0, 0))] * 2,
+        out_specs=pl.BlockSpec((2 * rows, width), lambda i: (0, 0)),
+        out_shape=jax.ShapeDtypeStruct((2 * rows, width), first.dtype),
+        compiler_params=pltpu.CompilerParams(vmem_limit_bytes=16 << 20),
+        name="join",
+    )(first, second)
 
 
 def ring_order(count):
@@ -155,6 +174,9 @@
     def across(a):
         return lax.ppermute(a, "node", [(0, 1), (1, 0)])
 
+    def chip_sum(a, b):
+        return a.astype(jnp.float32) + b.astype(jnp.float32)
+
     matches = expert_ids[:, :, None] == jnp.arange(LANES, dtype=jnp.int32)[None, None, :]
     route = jnp.sum(
         jnp.where(matches, combine_weights[:, :, None], jnp.zeros((), jnp.bfloat16)), axis=1
@@ -168,20 +190,23 @@
         jnp.concatenate(pair, axis=1) for pair in zip(halves(tokens), halves(route), strict=True)
     ]
     swapped = across(given)
-    block = jnp.concatenate([kept, swapped], axis=0)
-    mine = jnp.concatenate([tokens, lax.optimization_barrier((route, block))[0]], axis=1)
     gate, up, down = w_gate[0], w_up[0], w_down[0]
-    own, other = run_experts(expert, mine, across(mine), gate, up, down)
-    own_sums, other_sums = [own], [across(other)]
+    block = join(onward(kept), onward(swapped))
+    own, other = run_experts(
+        expert, (kept, given), (across(kept), swapped), gate, up, down
+    )
+    block = lax.optimization_barrier((block, own))[0]
+    mine_sum = chip_sum(own, across(other))
     after = (own,)
     attn_latent, done = None, None
     for k in range(1, local_count):
-        block = onward(block)
-        if k == 1:
-            block = lax.optimization_barrier((block, own))[0]
-        own, other = run_experts(expert, block, across(block), gate, up, down, after)
-        own_sums.append(own)
-        other_sums.append(across(other))
+        if k > 1:
+            block = onward(block)
+        own, other = run_experts(expert, (block,), (across(block),), gate, up, down, after)
+        total = chip_sum(own, across(other))
+        if k > 1:
+            total += onward(running).astype(jnp.float32)
+        running = total.astype(jnp.bfloat16)
         after = ()
         if done is not None:
             after, done = (done,), None
@@ -197,19 +222,14 @@
                 (own,),
             )
 
-    def chip_sum(k):
-        return own_sums[k].astype(jnp.float32) + other_sums[k].astype(jnp.float32)
-
-    running = chip_sum(1).astype(jnp.bfloat16)
-    for k in range(2, local_count - 1):
-        running = (chip_sum(k) + onward(running).astype(jnp.float32)).astype(jnp.bfloat16)
-    total = chip_sum(local_count - 1) + onward(running).astype(jnp.float32)
-    same = onward(total[:part].astype(jnp.bfloat16))
-    cross = onward(total[part:].astype(jnp.bfloat16), hops_out)
+    mine_sum = lax.optimization_barrier(
+        jnp.where(first, mine_sum, jnp.concatenate([mine_sum[part:], mine_sum[:part]], axis=0))
+    )
+    same, cross = onward(running[:part]), onward(running[part:], hops_out)
     arrived = jnp.where(
         first, jnp.concatenate([same, cross], axis=0), jnp.concatenate([cross, same], axis=0)
     )
-    moe_out = (chip_sum(0) + arrived.astype(jnp.float32)).astype(jnp.bfloat16)
+    moe_out = (mine_sum + arrived.astype(jnp.float32)).astype(jnp.bfloat16)
 
     return (moe_out, attn_latent)
 

time: 96.2 us -> 96.3 us (level)
  waiting for transfers between devices: 30.6 us -> 31.9 us
  local copies, waits for them, and re-layouts: 7.75 us -> 6.72 us
    ppermute x15 -> x16, waiting for transfers between devices: 30.5 us -> 31.7 us  [onward(): return lax.ppermute(a, ('node', 'local'), pairs)]
    unnamed x23 -> x22, local copies, waits for them, and re-layouts: 7.71 us -> 6.62 us
    convert_element_type x7 -> x8, other arithmetic: 1.94 us -> 2.1 us  [the longest x7 1.22 us: on_device(): running = total.astype(jnp.bfloat16)]
    ppermute x15 -> x16, starting transfers between devices: 24.8 us -> 24.7 us  [onward(): return lax.ppermute(a, ('node', 'local'), pairs)]
    pallas_call x8 -> x9, Pallas kernels: 13.8 us -> 13.8 us  [the longest x8 13.8 us: run_experts(): pl.pallas_call(functools.partial(expert_kernel, own_parts=len(own), parts...]
  transfers between devices with their start and end apart: 32 -> 33, of which waited for: 12 -> 12; matrix products, arithmetic and copies ran while one was open for 2% -> 1% of each run, Pallas kernels for 25% -> 25%
where the time goes in v5:
time: 96.3 us; the launch traced here: 95.7 us
  waiting for transfers between devices  31.9 us (33%)
  starting transfers between devices  27.5 us (29%)
  Pallas kernels  24.2 us (25%)
  local copies, waits for them, and re-layouts  6.72 us (7%)
  other arithmetic  4.35 us (5%)
  between operations  0.99 us (1%)
    ppermute x16, waiting for transfers between devices, onward(): return lax.ppermute(a, ('node', 'local'), pairs)  31.7 us
    ppermute x16, starting transfers between devices, onward(): return lax.ppermute(a, ('node', 'local'), pairs)  24.7 us
    pallas_call x8, Pallas kernels, run_experts(): pl.pallas_call(functools.partial(expert_kernel, own_parts=len(own), parts...  13.8 us
    pallas_call x4, Pallas kernels, attend_piece(): pl.pallas_call(functools.partial(attend_kernel, base=piece * count, pair=...  10.3 us
    unnamed x22, local copies, waits for them, and re-layouts  6.62 us
    ppermute x17, starting transfers between devices, across(): return lax.ppermute(a, 'node', [(0, 1), (1, 0)])  2.78 us
  transfers between devices with their start and end apart: 33, of which 12 were waited for; matrix products, arithmetic and copies ran while one was open for 1% of the time, Pallas kernels for 25%

profile of v5, /device:TPU:0, one launch (start us, length us, event | category | flops | bytes accessed | tf_op | source)
XLA Modules:
  0.0 95.7 jit_solution(706801617758874080)
XLA Ops:
  0.6 0.8 fusion.1
  1.5 1.1 %broadcast_select_fusion = (bf16[32,3584]{1,0:T(8,128)(2,1)S(1)}, bf16[32,3584]{1,0:T(8,128)(2,1)S(1)}) fusion(pred[]{:T(512)S(6)} %eq.16, bf16[64,3584]{1,0:T(8,128)(2,1)} %param.9), kind=kLoop, calls=%fused_computation.13 | loop fusion | flops 229376 | bytes 917505 | tf_op jit(solution)/shard_map/jit(_where)/select_n | solution.py:187
  2.6 0.5 collective-permute-start.1
  3.1 0.1 collective-permute-start
  3.3 3.0 %collective-permute-start.3 = (bf16[32,3712]{1,0:T(8,128)(2,1)S(1)}, bf16[32,3712]{1,0:T(8,128)(2,1)S(1)}, u32[]{:S(2)}, u32[]{:S(2)}) collective-permute-start(bf16[32,3712]{1,0:T(8,128)(2,1)S(1)} %pad_maximum_fusion.refs_0_), channel_id=1, source_target_pairs={{0,2},{10,8},{2,4},{12,10},{4,6},{14,12},{6,7},{15,14},{7,5},{13,1... | collective-permute-start | bytes 712712 | tf_op jit(solution)/shard_map/ppermute | solution.py:172
  6.3 1.6 %collective-permute-start.4 = (bf16[32,3712]{1,0:T(8,128)(2,1)S(1)}, bf16[32,3712]{1,0:T(8,128)(2,1)S(1)}, u32[]{:S(2)}, u32[]{:S(2)}) collective-permute-start(bf16[32,3712]{1,0:T(8,128)(2,1)S(1)} %collective-permute-done.1.refs_3_), channel_id=1, source_target_pairs={{0,2},{10,8},{2,4},{12,10},{4,6},{14,12},{6,7},{15,14},{7,5},{13,1... | collective-permute-start | bytes 712712 | tf_op jit(solution)/shard_map/ppermute | solution.py:172
  7.9 2.0 %copy-done = bf16[1,3584,512]{2,1,0:T(8,128)(2,1)S(1)} copy-done((bf16[1,3584,512]{2,1,0:T(8,128)(2,1)S(1)}, bf16[1,3584,512]{2,1,0:T(8,128)(2,1)}, u32[]{:S(2)}) %copy-start) | copy-done | bytes 3670040
  9.9 2.0 %copy-done.2 = bf16[1,3584,512]{2,1,0:T(8,128)(2,1)S(1)} copy-done((bf16[1,3584,512]{2,1,0:T(8,128)(2,1)S(1)}, bf16[1,3584,512]{2,1,0:T(8,128)(2,1)}, u32[]{:S(2)}) %copy-start.2) | copy-done | bytes 3670040
  11.9 2.0 %copy-done.4 = bf16[1,512,3584]{2,1,0:T(8,128)(2,1)S(1)} copy-done((bf16[1,512,3584]{2,1,0:T(8,128)(2,1)S(1)}, bf16[1,512,3584]{2,1,0:T(8,128)(2,1)}, u32[]{:S(2)}) %copy-start.4) | copy-done | bytes 3670040
  14.0 1.7 %expert_half.8 = (bf16[64,3584]{1,0:T(8,128)(2,1)S(1)}, bf16[64,3584]{1,0:T(8,128)(2,1)S(1)}) custom-call(s32[1]{0:T(128)} %bitcast.expert_ref, bf16[32,3712]{1,0:T(8,128)(2,1)S(1)} %pad_maximum_fusion.refs_0_, bf16[32,3712]{1,0:T(8,128)(2,1)S(1)} %pad_maximum_fusion.1.refs_1_, bf16[32,3712]{1,0:T(8,128)(2,1)S(1)} %collective-permute-done.refs_2_, ...), custom_call_target="tpu_custom_call" | custom-call | flops 1409286144 | bytes 11010048 | tf_op jit(solution)/shard_map/expert_half/pallas_call | solution.py:109
  15.8 0.1 collective-permute-start.14
  15.9 1.6 %collective-permute-start.5 = (bf16[64,3712]{1,0:T(8,128)(2,1)S(1)}, bf16[64,3712]{1,0:T(8,128)(2,1)S(1)}, u32[]{:S(2)}, u32[]{:S(2)}) collective-permute-start(bf16[64,3712]{1,0:T(8,128)(2,1)S(1)} %join.1.refs_0_), channel_id=1, source_target_pairs={{0,2},{10,8},{2,4},{12,10},{4,6},{14,12},{6,7},{15,14},{7,5},{13,1... | collective-permute-start | bytes 1425416 | tf_op jit(solution)/shard_map/ppermute | solution.py:172
  17.5 0.2 collective-permute-done.14.refs_1_
  17.7 0.5 copy-done.5
  18.2 1.7 %expert_half.10 = (bf16[64,3584]{1,0:T(8,128)(2,1)S(1)}, bf16[64,3584]{1,0:T(8,128)(2,1)S(1)}) custom-call(s32[1]{0:T(128)} %bitcast.expert_ref, bf16[64,3712]{1,0:T(8,128)(2,1)S(1)} %join.1.refs_0_, bf16[64,3712]{1,0:T(8,128)(2,1)S(1)} %collective-permute-done.14.refs_1_, bf16[3584,512]{1,0:T(8,128)(2,1)S(1)} %bitcast.5, bf16[3584,512]{1,0:T(8,128)(2,1)S(1)} %bitcast.13, ...), custom_call_target="tpu_custom_call" | custom-call | flops 1409286144 | bytes 11010048 | tf_op jit(solution)/shard_map/expert_half/pallas_call | solution.py:109
  19.9 0.1 collective-permute-start.24
  20.0 4.6 %collective-permute-done.5.refs_0_ = bf16[64,3712]{1,0:T(8,128)(2,1)S(1)} collective-permute-done((bf16[64,3712]{1,0:T(8,128)(2,1)S(1)}, bf16[64,3712]{1,0:T(8,128)(2,1)S(1)}, u32[]{:S(2)}, u32[]{:S(2)}) %collective-permute-start.5) | collective-permute-done | bytes 475168 | tf_op jit(solution)/shard_map/ppermute | solution.py:172
  24.6 1.6 %collective-permute-start.6 = (bf16[64,3712]{1,0:T(8,128)(2,1)S(1)}, bf16[64,3712]{1,0:T(8,128)(2,1)S(1)}, u32[]{:S(2)}, u32[]{:S(2)}) collective-permute-start(bf16[64,3712]{1,0:T(8,128)(2,1)S(1)} %collective-permute-done.5.refs_0_), channel_id=1, source_target_pairs={{0,2},{10,8},{2,4},{12,10},{4,6},{14,12},{6,7},{15,14},{7,5},{13,1... | collective-permute-start | bytes 1425416 | tf_op jit(solution)/shard_map/ppermute | solution.py:172
  26.2 0.1 add_convert_fusion.7
  26.3 1.6 %collective-permute-start.25 = (bf16[64,3584]{1,0:T(8,128)(2,1)S(1)}, bf16[64,3584]{1,0:T(8,128)(2,1)S(1)}, u32[]{:S(2)}, u32[]{:S(2)}) collective-permute-start(bf16[64,3584]{1,0:T(8,128)(2,1)S(1)} %add_convert_fusion.7), channel_id=1, source_target_pairs={{0,2},{10,8},{2,4},{12,10},{4,6},{14,12},{6,7},{15,14},{7,5},{13,1... | collective-permute-start | bytes 1376264 | tf_op jit(solution)/shard_map/ppermute | solution.py:172
  27.9 1.7 %expert_half.11 = (bf16[64,3584]{1,0:T(8,128)(2,1)S(1)}, bf16[64,3584]{1,0:T(8,128)(2,1)S(1)}) custom-call(s32[1]{0:T(128)} %bitcast.expert_ref, bf16[64,3712]{1,0:T(8,128)(2,1)S(1)} %collective-permute-done.5.refs_0_, bf16[64,3712]{1,0:T(8,128)(2,1)S(1)} %collective-permute-done.15.refs_1_, bf16[3584,512]{1,0:T(8,128)(2,1)S(1)} %bitcast.6, ...), custom_call_target="tpu_custom_call" | custom-call | flops 1409286144 | bytes 11010048 | tf_op jit(solution)/shard_map/expert_half/pallas_call | solution.py:109
  29.6 0.1 collective-permute-start.23
  29.8 2.6 %attend.4 = (bf16[64,64,512]{2,1,0:T(8,128)(2,1)}, f32[8,128]{1,0:T(8,128)S(1)}) custom-call(s32[64]{0:T(128)S(1)} %copy-done.6, bf16[64,64,576]{2,1,0:T(8,128)(2,1)S(1)} %bitcast.29, bf16[64,64,576]{2,1,0:T(8,128)(2,1)S(1)} %bitcast.31, bf16[64,3584]{1,0:T(8,128)(2,1)S(1)} %get-tuple-element.32.rest_0_), custom_call_target="tpu_custom_call" | custom-call | flops 142606336 | bytes 3407872 | tf_op jit(solution)/shard_map/attend/pallas_call | solution.py:59
  32.3 0.9 collective-permute-done.6.refs_0_
  33.3 1.6 %collective-permute-start.7 = (bf16[64,3712]{1,0:T(8,128)(2,1)S(1)}, bf16[64,3712]{1,0:T(8,128)(2,1)S(1)}, u32[]{:S(2)}, u32[]{:S(2)}) collective-permute-start(bf16[64,3712]{1,0:T(8,128)(2,1)S(1)} %collective-permute-done.6.refs_0_), channel_id=1, source_target_pairs={{0,2},{10,8},{2,4},{12,10},{4,6},{14,12},{6,7},{15,14},{7,5},{13,1... | collective-permute-start | bytes 1425416 | tf_op jit(solution)/shard_map/ppermute | solution.py:172
  34.8 3.3 %collective-permute-done.25 = bf16[64,3584]{1,0:T(8,128)(2,1)S(1)} collective-permute-done((bf16[64,3584]{1,0:T(8,128)(2,1)S(1)}, bf16[64,3584]{1,0:T(8,128)(2,1)S(1)}, u32[]{:S(2)}, u32[]{:S(2)}) %collective-permute-start.25) | collective-permute-done | bytes 458784 | tf_op jit(solution)/shard_map/ppermute | solution.py:172
  38.2 0.2 add_convert_fusion.6
  38.4 1.6 %collective-permute-start.26 = (bf16[64,3584]{1,0:T(8,128)(2,1)S(1)}, bf16[64,3584]{1,0:T(8,128)(2,1)S(1)}, u32[]{:S(2)}, u32[]{:S(2)}) collective-permute-start(bf16[64,3584]{1,0:T(8,128)(2,1)S(1)} %add_convert_fusion.6), channel_id=1, source_target_pairs={{0,2},{10,8},{2,4},{12,10},{4,6},{14,12},{6,7},{15,14},{7,5},{13,1... | collective-permute-start | bytes 1376264 | tf_op jit(solution)/shard_map/ppermute | solution.py:172
  40.0 1.7 %expert_half.12 = (bf16[64,3584]{1,0:T(8,128)(2,1)S(1)}, bf16[64,3584]{1,0:T(8,128)(2,1)S(1)}) custom-call(s32[1]{0:T(128)} %bitcast.expert_ref, bf16[64,3712]{1,0:T(8,128)(2,1)S(1)} %collective-permute-done.6.refs_0_, bf16[64,3712]{1,0:T(8,128)(2,1)S(1)} %collective-permute-done.16.refs_1_, bf16[3584,512]{1,0:T(8,128)(2,1)S(1)} %bitcast.7, ...), custom_call_target="tpu_custom_call" | custom-call | flops 1409286144 | bytes 11010048 | tf_op jit(solution)/shard_map/expert_half/pallas_call | solution.py:109
  41.8 2.6 %attend.5 = (bf16[64,64,512]{2,1,0:T(8,128)(2,1)}, f32[8,128]{1,0:T(8,128)S(1)}) custom-call(s32[64]{0:T(128)S(1)} %copy-done.6, bf16[64,64,576]{2,1,0:T(8,128)(2,1)S(1)} %bitcast.29, bf16[64,64,576]{2,1,0:T(8,128)(2,1)S(1)} %bitcast.31, bf16[64,64,512]{2,1,0:T(8,128)(2,1)} %get-tuple-element.33.rest_0_, ...), custom_call_target="tpu_custom_call", output_to_operand_aliasing={{0}: (3, {})} | custom-call | flops 142606336 | bytes 3407872 | tf_op jit(solution)/shard_map/attend/pallas_call | solution.py:59
  44.4 0.5 collective-permute-start.17
  44.9 1.5 %collective-permute-start.8 = (bf16[64,3712]{1,0:T(8,128)(2,1)S(1)}, bf16[64,3712]{1,0:T(8,128)(2,1)S(1)}, u32[]{:S(2)}, u32[]{:S(2)}) collective-permute-start(bf16[64,3712]{1,0:T(8,128)(2,1)S(1)} %collective-permute-done.7.refs_0_), channel_id=1, source_target_pairs={{0,2},{10,8},{2,4},{12,10},{4,6},{14,12},{6,7},{15,14},{7,5},{13,1... | collective-permute-start | bytes 1425416 | tf_op jit(solution)/shard_map/ppermute | solution.py:172
  46.4 1.7 %collective-permute-done.26 = bf16[64,3584]{1,0:T(8,128)(2,1)S(1)} collective-permute-done((bf16[64,3584]{1,0:T(8,128)(2,1)S(1)}, bf16[64,3584]{1,0:T(8,128)(2,1)S(1)}, u32[]{:S(2)}, u32[]{:S(2)}) %collective-permute-start.26) | collective-permute-done | bytes 458784 | tf_op jit(solution)/shard_map/ppermute | solution.py:172
  48.2 0.2 add_convert_fusion.5
  48.3 1.8 %collective-permute-start.27 = (bf16[64,3584]{1,0:T(8,128)(2,1)S(1)}, bf16[64,3584]{1,0:T(8,128)(2,1)S(1)}, u32[]{:S(2)}, u32[]{:S(2)}) collective-permute-start(bf16[64,3584]{1,0:T(8,128)(2,1)S(1)} %add_convert_fusion.5), channel_id=1, source_target_pairs={{0,2},{10,8},{2,4},{12,10},{4,6},{14,12},{6,7},{15,14},{7,5},{13,1... | collective-permute-start | bytes 1376264 | tf_op jit(solution)/shard_map/ppermute | solution.py:172
  50.2 1.7 %expert_half.13 = (bf16[64,3584]{1,0:T(8,128)(2,1)S(1)}, bf16[64,3584]{1,0:T(8,128)(2,1)S(1)}) custom-call(s32[1]{0:T(128)} %bitcast.expert_ref, bf16[64,3712]{1,0:T(8,128)(2,1)S(1)} %collective-permute-done.7.refs_0_, bf16[64,3712]{1,0:T(8,128)(2,1)S(1)} %collective-permute-done.17.refs_1_, bf16[3584,512]{1,0:T(8,128)(2,1)S(1)} %bitcast.8, ...), custom_call_target="tpu_custom_call" | custom-call | flops 1409286144 | bytes 11010048 | tf_op jit(solution)/shard_map/expert_half/pallas_call | solution.py:109
  52.0 2.6 %attend.6 = (bf16[64,64,512]{2,1,0:T(8,128)(2,1)}, f32[8,128]{1,0:T(8,128)S(1)}) custom-call(s32[64]{0:T(128)S(1)} %copy-done.6, bf16[64,64,576]{2,1,0:T(8,128)(2,1)S(1)} %bitcast.29, bf16[64,64,576]{2,1,0:T(8,128)(2,1)S(1)} %bitcast.31, bf16[64,64,512]{2,1,0:T(8,128)(2,1)} %get-tuple-element.35.rest_0_, ...), custom_call_target="tpu_custom_call", output_to_operand_aliasing={{0}: (3, {})} | custom-call | flops 142606336 | bytes 3407872 | tf_op jit(solution)/shard_map/attend/pallas_call | solution.py:59
  54.6 0.5 collective-permute-start.19
  55.1 1.5 %collective-permute-start.9 = (bf16[64,3712]{1,0:T(8,128)(2,1)S(1)}, bf16[64,3712]{1,0:T(8,128)(2,1)S(1)}, u32[]{:S(2)}, u32[]{:S(2)}) collective-permute-start(bf16[64,3712]{1,0:T(8,128)(2,1)S(1)} %collective-permute-done.8.refs_0_), channel_id=1, source_target_pairs={{0,2},{10,8},{2,4},{12,10},{4,6},{14,12},{6,7},{15,14},{7,5},{13,1... | collective-permute-start | bytes 1425416 | tf_op jit(solution)/shard_map/ppermute | solution.py:172
  56.6 1.9 %collective-permute-done.27 = bf16[64,3584]{1,0:T(8,128)(2,1)S(1)} collective-permute-done((bf16[64,3584]{1,0:T(8,128)(2,1)S(1)}, bf16[64,3584]{1,0:T(8,128)(2,1)S(1)}, u32[]{:S(2)}, u32[]{:S(2)}) %collective-permute-start.27) | collective-permute-done | bytes 458784 | tf_op jit(solution)/shard_map/ppermute | solution.py:172
  58.5 0.2 add_convert_fusion.4
  58.7 1.6 %collective-permute-start.28 = (bf16[64,3584]{1,0:T(8,128)(2,1)S(1)}, bf16[64,3584]{1,0:T(8,128)(2,1)S(1)}, u32[]{:S(2)}, u32[]{:S(2)}) collective-permute-start(bf16[64,3584]{1,0:T(8,128)(2,1)S(1)} %add_convert_fusion.4), channel_id=1, source_target_pairs={{0,2},{10,8},{2,4},{12,10},{4,6},{14,12},{6,7},{15,14},{7,5},{13,1... | collective-permute-start | bytes 1376264 | tf_op jit(solution)/shard_map/ppermute | solution.py:172
  60.3 1.7 %expert_half.15 = (bf16[64,3584]{1,0:T(8,128)(2,1)S(1)}, bf16[64,3584]{1,0:T(8,128)(2,1)S(1)}) custom-call(s32[1]{0:T(128)} %bitcast.expert_ref, bf16[64,3712]{1,0:T(8,128)(2,1)S(1)} %collective-permute-done.8.refs_0_, bf16[64,3712]{1,0:T(8,128)(2,1)S(1)} %collective-permute-done.19.refs_1_, bf16[3584,512]{1,0:T(8,128)(2,1)S(1)} %bitcast.9, ...), custom_call_target="tpu_custom_call" | custom-call | flops 1409286144 | bytes 11010048 | tf_op jit(solution)/shard_map/expert_half/pallas_call | solution.py:109
  62.1 0.5 collective-permute-start.2
  62.6 2.6 %attend.7 = (bf16[64,64,512]{2,1,0:T(8,128)(2,1)}, f32[8,128]{1,0:T(8,128)S(1)}) custom-call(s32[64]{0:T(128)S(1)} %copy-done.6, bf16[64,64,576]{2,1,0:T(8,128)(2,1)S(1)} %bitcast.29, bf16[64,64,576]{2,1,0:T(8,128)(2,1)S(1)} %bitcast.31, bf16[64,64,512]{2,1,0:T(8,128)(2,1)} %get-tuple-element.38.rest_0_, ...), custom_call_target="tpu_custom_call", output_to_operand_aliasing={{0}: (3, {})} | custom-call | flops 142606336 | bytes 3407872 | tf_op jit(solution)/shard_map/attend/pallas_call | solution.py:59
  65.2 0.1 collective-permute-start.13
  65.2 1.3 %collective-permute-start.10 = (bf16[64,3712]{1,0:T(8,128)(2,1)S(1)}, bf16[64,3712]{1,0:T(8,128)(2,1)S(1)}, u32[]{:S(2)}, u32[]{:S(2)}) collective-permute-start(bf16[64,3712]{1,0:T(8,128)(2,1)S(1)} %collective-permute-done.9.refs_0_), channel_id=1, source_target_pairs={{0,2},{10,8},{2,4},{12,10},{4,6},{14,12},{6,7},{15,14},{7,5},{13,1... | collective-permute-start | bytes 1425416 | tf_op jit(solution)/shard_map/ppermute | solution.py:172
  66.5 2.1 %collective-permute-done.28 = bf16[64,3584]{1,0:T(8,128)(2,1)S(1)} collective-permute-done((bf16[64,3584]{1,0:T(8,128)(2,1)S(1)}, bf16[64,3584]{1,0:T(8,128)(2,1)S(1)}, u32[]{:S(2)}, u32[]{:S(2)}) %collective-permute-start.28) | collective-permute-done | bytes 458784 | tf_op jit(solution)/shard_map/ppermute | solution.py:172
  68.6 0.2 add_convert_fusion.3
  68.8 1.6 %collective-permute-start.29 = (bf16[64,3584]{1,0:T(8,128)(2,1)S(1)}, bf16[64,3584]{1,0:T(8,128)(2,1)S(1)}, u32[]{:S(2)}, u32[]{:S(2)}) collective-permute-start(bf16[64,3584]{1,0:T(8,128)(2,1)S(1)} %add_convert_fusion.3), channel_id=1, source_target_pairs={{0,2},{10,8},{2,4},{12,10},{4,6},{14,12},{6,7},{15,14},{7,5},{13,1... | collective-permute-start | bytes 1376264 | tf_op jit(solution)/shard_map/ppermute | solution.py:172
  70.4 1.7 %expert_half.14 = (bf16[64,3584]{1,0:T(8,128)(2,1)S(1)}, bf16[64,3584]{1,0:T(8,128)(2,1)S(1)}) custom-call(s32[1]{0:T(128)} %bitcast.expert_ref, bf16[64,3712]{1,0:T(8,128)(2,1)S(1)} %collective-permute-done.9.refs_0_, bf16[64,3712]{1,0:T(8,128)(2,1)S(1)} %collective-permute-done.13.refs_1_, bf16[3584,512]{1,0:T(8,128)(2,1)S(1)} %bitcast.10, ...), custom_call_target="tpu_custom_call" | custom-call | flops 1409286144 | bytes 11010048 | tf_op jit(solution)/shard_map/expert_half/pallas_call | solution.py:109
  72.2 0.1 convert_add_fusion
  72.4 1.5 %collective-permute-done.10.refs_0_ = bf16[64,3712]{1,0:T(8,128)(2,1)S(1)} collective-permute-done((bf16[64,3712]{1,0:T(8,128)(2,1)S(1)}, bf16[64,3712]{1,0:T(8,128)(2,1)S(1)}, u32[]{:S(2)}, u32[]{:S(2)}) %collective-permute-start.10) | collective-permute-done | bytes 475168 | tf_op jit(solution)/shard_map/ppermute | solution.py:172
  73.9 4.9 %collective-permute-done.29 = bf16[64,3584]{1,0:T(8,128)(2,1)S(1)} collective-permute-done((bf16[64,3584]{1,0:T(8,128)(2,1)S(1)}, bf16[64,3584]{1,0:T(8,128)(2,1)S(1)}, u32[]{:S(2)}, u32[]{:S(2)}) %collective-permute-start.29) | collective-permute-done | bytes 458784 | tf_op jit(solution)/shard_map/ppermute | solution.py:172
  78.8 0.2 add_convert_fusion.2
  79.0 1.4 %collective-permute-start.30 = (bf16[64,3584]{1,0:T(8,128)(2,1)S(1)}, bf16[64,3584]{1,0:T(8,128)(2,1)S(1)}, u32[]{:S(2)}, u32[]{:S(2)}) collective-permute-start(bf16[64,3584]{1,0:T(8,128)(2,1)S(1)} %add_convert_fusion.2), channel_id=1, source_target_pairs={{0,2},{10,8},{2,4},{12,10},{4,6},{14,12},{6,7},{15,14},{7,5},{13,1... | collective-permute-start | bytes 1376264 | tf_op jit(solution)/shard_map/ppermute | solution.py:172
  80.4 1.7 %expert_half.9 = (bf16[64,3584]{1,0:T(8,128)(2,1)S(1)}, bf16[64,3584]{1,0:T(8,128)(2,1)S(1)}) custom-call(s32[1]{0:T(128)} %bitcast.expert_ref, bf16[64,3712]{1,0:T(8,128)(2,1)S(1)} %collective-permute-done.10.refs_0_, bf16[64,3712]{1,0:T(8,128)(2,1)S(1)} %collective-permute-done.11.refs_1_, bf16[3584,512]{1,0:T(8,128)(2,1)S(1)} %bitcast.11, ...), custom_call_target="tpu_custom_call" | custom-call | flops 1409286144 | bytes 11010048 | tf_op jit(solution)/shard_map/expert_half/pallas_call | solution.py:109
  82.3 5.3 %collective-permute-done.30 = bf16[64,3584]{1,0:T(8,128)(2,1)S(1)} collective-permute-done((bf16[64,3584]{1,0:T(8,128)(2,1)S(1)}, bf16[64,3584]{1,0:T(8,128)(2,1)S(1)}, u32[]{:S(2)}, u32[]{:S(2)}) %collective-permute-start.30) | collective-permute-done | bytes 458784 | tf_op jit(solution)/shard_map/ppermute | solution.py:172
  87.6 0.2 add_convert_fusion.1
  87.8 1.4 %collective-permute-start.31 = (bf16[32,3584]{1,0:T(8,128)(2,1)S(1)}, bf16[32,3584]{1,0:T(8,128)(2,1)S(1)}, u32[]{:S(2)}, u32[]{:S(2)}) collective-permute-start(bf16[32,3584]{1,0:T(8,128)(2,1)S(1)} %get-tuple-element.54), channel_id=1, source_target_pairs={{0,2},{10,8},{2,4},{12,10},{4,6},{14,12},{6,7},{15,14},{7,5},{13,1... | collective-permute-start | bytes 688136 | tf_op jit(solution)/shard_map/ppermute | solution.py:172
  89.2 0.2 maximum_select_fusion
  89.4 3.9 %collective-permute-done.32 = bf16[32,3584]{1,0:T(8,128)(2,1)S(1)} collective-permute-done((bf16[32,3584]{1,0:T(8,128)(2,1)S(1)}, bf16[32,3584]{1,0:T(8,128)(2,1)S(1)}, u32[]{:S(2)}, u32[]{:S(2)}) %collective-permute-start.32) | collective-permute-done | bytes 229408 | tf_op jit(solution)/shard_map/ppermute | solution.py:172
  93.3 1.5 %collective-permute-done.31 = bf16[32,3584]{1,0:T(8,128)(2,1)S(1)} collective-permute-done((bf16[32,3584]{1,0:T(8,128)(2,1)S(1)}, bf16[32,3584]{1,0:T(8,128)(2,1)S(1)}, u32[]{:S(2)}, u32[]{:S(2)}) %collective-permute-start.31) | collective-permute-done | bytes 229408 | tf_op jit(solution)/shard_map/ppermute | solution.py:172
  94.8 0.9 add_convert_fusion
  (56 shorter events, 0.7 us)
Async XLA Ops:
  2.6 3.7 %collective-permute-start.1 = (bf16[32,3712]{1,0:T(8,128)(2,1)S(1)}, bf16[32,3712]{1,0:T(8,128)(2,1)S(1)}, u32[]{:S(2)}, u32[]{:S(2)}) collective-permute-start(bf16[32,3712]{1,0:T(8,128)(2,1)S(1)} %pad_maximum_fusion.1.refs_1_), channel_id=1, source_target_pairs={{0,8},{8,0},{1,9},{9,1},{2,10},{10,2},{3,11},{11,3},{4,12},{12,4},... | collective-permute-start | bytes 712712 | tf_op jit(solution)/shard_map/ppermute | solution.py:175
  3.1 4.7 %collective-permute-start = (bf16[32,3712]{1,0:T(8,128)(2,1)S(1)}, bf16[32,3712]{1,0:T(8,128)(2,1)S(1)}, u32[]{:S(2)}, u32[]{:S(2)}) collective-permute-start(bf16[32,3712]{1,0:T(8,128)(2,1)S(1)} %pad_maximum_fusion.refs_0_), channel_id=1, source_target_pairs={{0,8},{8,0},{1,9},{9,1},{2,10},{10,2},{3,11},{11,3},{4,12},{12,4},... | collective-permute-start | bytes 712712 | tf_op jit(solution)/shard_map/ppermute | solution.py:175
  3.3 12.5 %collective-permute-start.3 = (bf16[32,3712]{1,0:T(8,128)(2,1)S(1)}, bf16[32,3712]{1,0:T(8,128)(2,1)S(1)}, u32[]{:S(2)}, u32[]{:S(2)}) collective-permute-start(bf16[32,3712]{1,0:T(8,128)(2,1)S(1)} %pad_maximum_fusion.refs_0_), channel_id=1, source_target_pairs={{0,2},{10,8},{2,4},{12,10},{4,6},{14,12},{6,7},{15,14},{7,5},{13,1... | collective-permute-start | bytes 712712 | tf_op jit(solution)/shard_map/ppermute | solution.py:172
  6.3 9.5 %collective-permute-start.4 = (bf16[32,3712]{1,0:T(8,128)(2,1)S(1)}, bf16[32,3712]{1,0:T(8,128)(2,1)S(1)}, u32[]{:S(2)}, u32[]{:S(2)}) collective-permute-start(bf16[32,3712]{1,0:T(8,128)(2,1)S(1)} %collective-permute-done.1.refs_3_), channel_id=1, source_target_pairs={{0,2},{10,8},{2,4},{12,10},{4,6},{14,12},{6,7},{15,14},{7,5},{13,1... | collective-permute-start | bytes 712712 | tf_op jit(solution)/shard_map/ppermute | solution.py:172
  7.9 2.0 %copy-start = (bf16[1,3584,512]{2,1,0:T(8,128)(2,1)S(1)}, bf16[1,3584,512]{2,1,0:T(8,128)(2,1)}, u32[]{:S(2)}) copy-start(bf16[1,3584,512]{2,1,0:T(8,128)(2,1)} %param.12) | copy-start | bytes 11010052
  9.9 2.0 %copy-start.2 = (bf16[1,3584,512]{2,1,0:T(8,128)(2,1)S(1)}, bf16[1,3584,512]{2,1,0:T(8,128)(2,1)}, u32[]{:S(2)}) copy-start(bf16[1,3584,512]{2,1,0:T(8,128)(2,1)} %param.13) | copy-start | bytes 11010052
  11.9 2.0 %copy-start.4 = (bf16[1,512,3584]{2,1,0:T(8,128)(2,1)S(1)}, bf16[1,512,3584]{2,1,0:T(8,128)(2,1)}, u32[]{:S(2)}) copy-start(bf16[1,512,3584]{2,1,0:T(8,128)(2,1)} %param.14) | copy-start | bytes 11010052
  14.0 3.7 %copy-start.1 = (bf16[1,3584,512]{2,1,0:T(8,128)(2,1)S(1)}, bf16[1,3584,512]{2,1,0:T(8,128)(2,1)}, u32[]{:S(2)}) copy-start(bf16[1,3584,512]{2,1,0:T(8,128)(2,1)} %param.12) | copy-start | bytes 11010052
  14.0 3.7 %copy-start.3 = (bf16[1,3584,512]{2,1,0:T(8,128)(2,1)S(1)}, bf16[1,3584,512]{2,1,0:T(8,128)(2,1)}, u32[]{:S(2)}) copy-start(bf16[1,3584,512]{2,1,0:T(8,128)(2,1)} %param.13) | copy-start | bytes 11010052
  14.0 4.2 %copy-start.5 = (bf16[1,512,3584]{2,1,0:T(8,128)(2,1)S(1)}, bf16[1,512,3584]{2,1,0:T(8,128)(2,1)}, u32[]{:S(2)}) copy-start(bf16[1,512,3584]{2,1,0:T(8,128)(2,1)} %param.14) | copy-start | bytes 11010052
  15.8 1.9 %collective-permute-start.14 = (bf16[64,3712]{1,0:T(8,128)(2,1)S(1)}, bf16[64,3712]{1,0:T(8,128)(2,1)S(1)}, u32[]{:S(2)}, u32[]{:S(2)}) collective-permute-start(bf16[64,3712]{1,0:T(8,128)(2,1)S(1)} %join.1.refs_0_), channel_id=1, source_target_pairs={{0,8},{8,0},{1,9},{9,1},{2,10},{10,2},{3,11},{11,3},{4,12},{12,4},... | collective-permute-start | bytes 1425416 | tf_op jit(solution)/shard_map/ppermute | solution.py:175
  15.9 8.7 %collective-permute-start.5 = (bf16[64,3712]{1,0:T(8,128)(2,1)S(1)}, bf16[64,3712]{1,0:T(8,128)(2,1)S(1)}, u32[]{:S(2)}, u32[]{:S(2)}) collective-permute-start(bf16[64,3712]{1,0:T(8,128)(2,1)S(1)} %join.1.refs_0_), channel_id=1, source_target_pairs={{0,2},{10,8},{2,4},{12,10},{4,6},{14,12},{6,7},{15,14},{7,5},{13,1... | collective-permute-start | bytes 1425416 | tf_op jit(solution)/shard_map/ppermute | solution.py:172
  18.2 11.5 %slice-start.2 = ((s8[5242880]{0:T(1024)(128)(4,1)}), s8[4194304]{0:T(1024)(128)(4,1)S(1)}, s32[]{:S(2)}) async-start(s8[5242880]{0:T(1024)(128)(4,1)} %bitcast.30), calls=%async_computation.2 | async-start | bytes 8388608
  19.9 6.3 %collective-permute-start.24 = (bf16[64,3584]{1,0:T(8,128)(2,1)S(1)}, bf16[64,3584]{1,0:T(8,128)(2,1)S(1)}, u32[]{:S(2)}, u32[]{:S(2)}) collective-permute-start(bf16[64,3584]{1,0:T(8,128)(2,1)S(1)} %get-tuple-element.50), channel_id=1, source_target_pairs={{0,8},{8,0},{1,9},{9,1},{2,10},{10,2},{3,11},{11,3},{4,12},{12,4},... | collective-permute-start | bytes 1376264 | tf_op jit(solution)/shard_map/ppermute | solution.py:175
  24.6 3.3 %collective-permute-start.15 = (bf16[64,3712]{1,0:T(8,128)(2,1)S(1)}, bf16[64,3712]{1,0:T(8,128)(2,1)S(1)}, u32[]{:S(2)}, u32[]{:S(2)}) collective-permute-start(bf16[64,3712]{1,0:T(8,128)(2,1)S(1)} %collective-permute-done.5.refs_0_), channel_id=1, source_target_pairs={{0,8},{8,0},{1,9},{9,1},{2,10},{10,2},{3,11},{11,3},{4,12},{12,4},... | collective-permute-start | bytes 1425416 | tf_op jit(solution)/shard_map/ppermute | solution.py:175
  24.6 8.7 %collective-permute-start.6 = (bf16[64,3712]{1,0:T(8,128)(2,1)S(1)}, bf16[64,3712]{1,0:T(8,128)(2,1)S(1)}, u32[]{:S(2)}, u32[]{:S(2)}) collective-permute-start(bf16[64,3712]{1,0:T(8,128)(2,1)S(1)} %collective-permute-done.5.refs_0_), channel_id=1, source_target_pairs={{0,2},{10,8},{2,4},{12,10},{4,6},{14,12},{6,7},{15,14},{7,5},{13,1... | collective-permute-start | bytes 1425416 | tf_op jit(solution)/shard_map/ppermute | solution.py:172
  26.2 3.5 %slice-start = ((s8[5242880]{0:T(1024)(128)(4,1)}), s8[4194304]{0:T(1024)(128)(4,1)S(1)}, s32[]{:S(2)}) async-start(s8[5242880]{0:T(1024)(128)(4,1)} %bitcast.28), calls=%async_computation | async-start | bytes 8388608
  26.2 3.5 %slice-start.3 = ((s8[5242880]{0:T(1024)(128)(4,1)}), s8[1048576]{0:T(1024)(128)(4,1)S(1)}, s32[]{:S(2)}) async-start(s8[5242880]{0:T(1024)(128)(4,1)} %bitcast.30), calls=%async_computation.3 | async-start | bytes 2097152
  26.3 3.4 %slice-start.1 = ((s8[5242880]{0:T(1024)(128)(4,1)}), s8[1048576]{0:T(1024)(128)(4,1)S(1)}, s32[]{:S(2)}) async-start(s8[5242880]{0:T(1024)(128)(4,1)} %bitcast.28), calls=%async_computation.1 | async-start | bytes 2097152
  26.3 3.4 %copy-start.6 = (s32[64]{0:T(128)S(1)}, s32[64]{0:T(128)}, u32[]{:S(2)}) copy-start(s32[64]{0:T(128)} %len_ref.7) | copy-start | bytes 772
  26.3 11.8 %collective-permute-start.25 = (bf16[64,3584]{1,0:T(8,128)(2,1)S(1)}, bf16[64,3584]{1,0:T(8,128)(2,1)S(1)}, u32[]{:S(2)}, u32[]{:S(2)}) collective-permute-start(bf16[64,3584]{1,0:T(8,128)(2,1)S(1)} %add_convert_fusion.7), channel_id=1, source_target_pairs={{0,2},{10,8},{2,4},{12,10},{4,6},{14,12},{6,7},{15,14},{7,5},{13,1... | collective-permute-start | bytes 1376264 | tf_op jit(solution)/shard_map/ppermute | solution.py:172
  29.6 8.6 %collective-permute-start.23 = (bf16[64,3584]{1,0:T(8,128)(2,1)S(1)}, bf16[64,3584]{1,0:T(8,128)(2,1)S(1)}, u32[]{:S(2)}, u32[]{:S(2)}) collective-permute-start(bf16[64,3584]{1,0:T(8,128)(2,1)S(1)} %get-tuple-element.49), channel_id=1, source_target_pairs={{0,8},{8,0},{1,9},{9,1},{2,10},{10,2},{3,11},{11,3},{4,12},{12,4},... | collective-permute-start | bytes 1376264 | tf_op jit(solution)/shard_map/ppermute | solution.py:175
  33.2 6.8 %collective-permute-start.16 = (bf16[64,3712]{1,0:T(8,128)(2,1)S(1)}, bf16[64,3712]{1,0:T(8,128)(2,1)S(1)}, u32[]{:S(2)}, u32[]{:S(2)}) collective-permute-start(bf16[64,3712]{1,0:T(8,128)(2,1)S(1)} %collective-permute-done.6.refs_0_), channel_id=1, source_target_pairs={{0,8},{8,0},{1,9},{9,1},{2,10},{10,2},{3,11},{11,3},{4,12},{12,4},... | collective-permute-start | bytes 1425416 | tf_op jit(solution)/shard_map/ppermute | solution.py:175
  33.3 11.1 %collective-permute-start.7 = (bf16[64,3712]{1,0:T(8,128)(2,1)S(1)}, bf16[64,3712]{1,0:T(8,128)(2,1)S(1)}, u32[]{:S(2)}, u32[]{:S(2)}) collective-permute-start(bf16[64,3712]{1,0:T(8,128)(2,1)S(1)} %collective-permute-done.6.refs_0_), channel_id=1, source_target_pairs={{0,2},{10,8},{2,4},{12,10},{4,6},{14,12},{6,7},{15,14},{7,5},{13,1... | collective-permute-start | bytes 1425416 | tf_op jit(solution)/shard_map/ppermute | solution.py:172
  38.4 9.8 %collective-permute-start.26 = (bf16[64,3584]{1,0:T(8,128)(2,1)S(1)}, bf16[64,3584]{1,0:T(8,128)(2,1)S(1)}, u32[]{:S(2)}, u32[]{:S(2)}) collective-permute-start(bf16[64,3584]{1,0:T(8,128)(2,1)S(1)} %add_convert_fusion.6), channel_id=1, source_target_pairs={{0,2},{10,8},{2,4},{12,10},{4,6},{14,12},{6,7},{15,14},{7,5},{13,1... | collective-permute-start | bytes 1376264 | tf_op jit(solution)/shard_map/ppermute | solution.py:172
  41.7 6.4 %collective-permute-start.22 = (bf16[64,3584]{1,0:T(8,128)(2,1)S(1)}, bf16[64,3584]{1,0:T(8,128)(2,1)S(1)}, u32[]{:S(2)}, u32[]{:S(2)}) collective-permute-start(bf16[64,3584]{1,0:T(8,128)(2,1)S(1)} %get-tuple-element.48), channel_id=1, source_target_pairs={{0,8},{8,0},{1,9},{9,1},{2,10},{10,2},{3,11},{11,3},{4,12},{12,4},... | collective-permute-start | bytes 1376264 | tf_op jit(solution)/shard_map/ppermute | solution.py:175
  44.4 5.8 %collective-permute-start.17 = (bf16[64,3712]{1,0:T(8,128)(2,1)S(1)}, bf16[64,3712]{1,0:T(8,128)(2,1)S(1)}, u32[]{:S(2)}, u32[]{:S(2)}) collective-permute-start(bf16[64,3712]{1,0:T(8,128)(2,1)S(1)} %collective-permute-done.7.refs_0_), channel_id=1, source_target_pairs={{0,8},{8,0},{1,9},{9,1},{2,10},{10,2},{3,11},{11,3},{4,12},{12,4},... | collective-permute-start | bytes 1425416 | tf_op jit(solution)/shard_map/ppermute | solution.py:175
  44.9 9.7 %collective-permute-start.8 = (bf16[64,3712]{1,0:T(8,128)(2,1)S(1)}, bf16[64,3712]{1,0:T(8,128)(2,1)S(1)}, u32[]{:S(2)}, u32[]{:S(2)}) collective-permute-start(bf16[64,3712]{1,0:T(8,128)(2,1)S(1)} %collective-permute-done.7.refs_0_), channel_id=1, source_target_pairs={{0,2},{10,8},{2,4},{12,10},{4,6},{14,12},{6,7},{15,14},{7,5},{13,1... | collective-permute-start | bytes 1425416 | tf_op jit(solution)/shard_map/ppermute | solution.py:172
  48.3 10.1 %collective-permute-start.27 = (bf16[64,3584]{1,0:T(8,128)(2,1)S(1)}, bf16[64,3584]{1,0:T(8,128)(2,1)S(1)}, u32[]{:S(2)}, u32[]{:S(2)}) collective-permute-start(bf16[64,3584]{1,0:T(8,128)(2,1)S(1)} %add_convert_fusion.5), channel_id=1, source_target_pairs={{0,2},{10,8},{2,4},{12,10},{4,6},{14,12},{6,7},{15,14},{7,5},{13,1... | collective-permute-start | bytes 1376264 | tf_op jit(solution)/shard_map/ppermute | solution.py:172
  51.9 6.6 %collective-permute-start.21 = (bf16[64,3584]{1,0:T(8,128)(2,1)S(1)}, bf16[64,3584]{1,0:T(8,128)(2,1)S(1)}, u32[]{:S(2)}, u32[]{:S(2)}) collective-permute-start(bf16[64,3584]{1,0:T(8,128)(2,1)S(1)} %get-tuple-element.47), channel_id=1, source_target_pairs={{0,8},{8,0},{1,9},{9,1},{2,10},{10,2},{3,11},{11,3},{4,12},{12,4},... | collective-permute-start | bytes 1376264 | tf_op jit(solution)/shard_map/ppermute | solution.py:175
  54.6 5.7 %collective-permute-start.19 = (bf16[64,3712]{1,0:T(8,128)(2,1)S(1)}, bf16[64,3712]{1,0:T(8,128)(2,1)S(1)}, u32[]{:S(2)}, u32[]{:S(2)}) collective-permute-start(bf16[64,3712]{1,0:T(8,128)(2,1)S(1)} %collective-permute-done.8.refs_0_), channel_id=1, source_target_pairs={{0,8},{8,0},{1,9},{9,1},{2,10},{10,2},{3,11},{11,3},{4,12},{12,4},... | collective-permute-start | bytes 1425416 | tf_op jit(solution)/shard_map/ppermute | solution.py:175
  55.1 10.1 %collective-permute-start.9 = (bf16[64,3712]{1,0:T(8,128)(2,1)S(1)}, bf16[64,3712]{1,0:T(8,128)(2,1)S(1)}, u32[]{:S(2)}, u32[]{:S(2)}) collective-permute-start(bf16[64,3712]{1,0:T(8,128)(2,1)S(1)} %collective-permute-done.8.refs_0_), channel_id=1, source_target_pairs={{0,2},{10,8},{2,4},{12,10},{4,6},{14,12},{6,7},{15,14},{7,5},{13,1... | collective-permute-start | bytes 1425416 | tf_op jit(solution)/shard_map/ppermute | solution.py:172
  58.7 9.9 %collective-permute-start.28 = (bf16[64,3584]{1,0:T(8,128)(2,1)S(1)}, bf16[64,3584]{1,0:T(8,128)(2,1)S(1)}, u32[]{:S(2)}, u32[]{:S(2)}) collective-permute-start(bf16[64,3584]{1,0:T(8,128)(2,1)S(1)} %add_convert_fusion.4), channel_id=1, source_target_pairs={{0,2},{10,8},{2,4},{12,10},{4,6},{14,12},{6,7},{15,14},{7,5},{13,1... | collective-permute-start | bytes 1376264 | tf_op jit(solution)/shard_map/ppermute | solution.py:172
  62.0 6.6 %collective-permute-start.20 = (bf16[64,3584]{1,0:T(8,128)(2,1)S(1)}, bf16[64,3584]{1,0:T(8,128)(2,1)S(1)}, u32[]{:S(2)}, u32[]{:S(2)}) collective-permute-start(bf16[64,3584]{1,0:T(8,128)(2,1)S(1)} %get-tuple-element.46), channel_id=1, source_target_pairs={{0,8},{8,0},{1,9},{9,1},{2,10},{10,2},{3,11},{11,3},{4,12},{12,4},... | collective-permute-start | bytes 1376264 | tf_op jit(solution)/shard_map/ppermute | solution.py:175
  62.1 10.1 %collective-permute-start.2 = (bf16[64,3584]{1,0:T(8,128)(2,1)S(1)}, bf16[64,3584]{1,0:T(8,128)(2,1)S(1)}, u32[]{:S(2)}, u32[]{:S(2)}) collective-permute-start(bf16[64,3584]{1,0:T(8,128)(2,1)S(1)} %get-tuple-element.28), channel_id=1, source_target_pairs={{0,8},{8,0},{1,9},{9,1},{2,10},{10,2},{3,11},{11,3},{4,12},{12,4},... | collective-permute-start | bytes 1376264 | tf_op jit(solution)/shard_map/ppermute | solution.py:175
  65.2 5.2 %collective-permute-start.13 = (bf16[64,3712]{1,0:T(8,128)(2,1)S(1)}, bf16[64,3712]{1,0:T(8,128)(2,1)S(1)}, u32[]{:S(2)}, u32[]{:S(2)}) collective-permute-start(bf16[64,3712]{1,0:T(8,128)(2,1)S(1)} %collective-permute-done.9.refs_0_), channel_id=1, source_target_pairs={{0,8},{8,0},{1,9},{9,1},{2,10},{10,2},{3,11},{11,3},{4,12},{12,4},... | collective-permute-start | bytes 1425416 | tf_op jit(solution)/shard_map/ppermute | solution.py:175
  65.2 8.7 %collective-permute-start.10 = (bf16[64,3712]{1,0:T(8,128)(2,1)S(1)}, bf16[64,3712]{1,0:T(8,128)(2,1)S(1)}, u32[]{:S(2)}, u32[]{:S(2)}) collective-permute-start(bf16[64,3712]{1,0:T(8,128)(2,1)S(1)} %collective-permute-done.9.refs_0_), channel_id=1, source_target_pairs={{0,2},{10,8},{2,4},{12,10},{4,6},{14,12},{6,7},{15,14},{7,5},{13,1... | collective-permute-start | bytes 1425416 | tf_op jit(solution)/shard_map/ppermute | solution.py:172
  68.8 10.0 %collective-permute-start.29 = (bf16[64,3584]{1,0:T(8,128)(2,1)S(1)}, bf16[64,3584]{1,0:T(8,128)(2,1)S(1)}, u32[]{:S(2)}, u32[]{:S(2)}) collective-permute-start(bf16[64,3584]{1,0:T(8,128)(2,1)S(1)} %add_convert_fusion.3), channel_id=1, source_target_pairs={{0,2},{10,8},{2,4},{12,10},{4,6},{14,12},{6,7},{15,14},{7,5},{13,1... | collective-permute-start | bytes 1376264 | tf_op jit(solution)/shard_map/ppermute | solution.py:172
  72.1 6.7 %collective-permute-start.18 = (bf16[64,3584]{1,0:T(8,128)(2,1)S(1)}, bf16[64,3584]{1,0:T(8,128)(2,1)S(1)}, u32[]{:S(2)}, u32[]{:S(2)}) collective-permute-start(bf16[64,3584]{1,0:T(8,128)(2,1)S(1)} %get-tuple-element.43), channel_id=1, source_target_pairs={{0,8},{8,0},{1,9},{9,1},{2,10},{10,2},{3,11},{11,3},{4,12},{12,4},... | collective-permute-start | bytes 1376264 | tf_op jit(solution)/shard_map/ppermute | solution.py:175
  73.9 6.5 %collective-permute-start.11 = (bf16[64,3712]{1,0:T(8,128)(2,1)S(1)}, bf16[64,3712]{1,0:T(8,128)(2,1)S(1)}, u32[]{:S(2)}, u32[]{:S(2)}) collective-permute-start(bf16[64,3712]{1,0:T(8,128)(2,1)S(1)} %collective-permute-done.10.refs_0_), channel_id=1, source_target_pairs={{0,8},{8,0},{1,9},{9,1},{2,10},{10,2},{3,11},{11,3},{4,12},{12,4},... | collective-permute-start | bytes 1425416 | tf_op jit(solution)/shard_map/ppermute | solution.py:175
  79.0 8.5 %collective-permute-start.30 = (bf16[64,3584]{1,0:T(8,128)(2,1)S(1)}, bf16[64,3584]{1,0:T(8,128)(2,1)S(1)}, u32[]{:S(2)}, u32[]{:S(2)}) collective-permute-start(bf16[64,3584]{1,0:T(8,128)(2,1)S(1)} %add_convert_fusion.2), channel_id=1, source_target_pairs={{0,2},{10,8},{2,4},{12,10},{4,6},{14,12},{6,7},{15,14},{7,5},{13,1... | collective-permute-start | bytes 1376264 | tf_op jit(solution)/shard_map/ppermute | solution.py:172
  82.1 5.4 %collective-permute-start.12 = (bf16[64,3584]{1,0:T(8,128)(2,1)S(1)}, bf16[64,3584]{1,0:T(8,128)(2,1)S(1)}, u32[]{:S(2)}, u32[]{:S(2)}) collective-permute-start(bf16[64,3584]{1,0:T(8,128)(2,1)S(1)} %get-tuple-element.31), channel_id=1, source_target_pairs={{0,8},{8,0},{1,9},{9,1},{2,10},{10,2},{3,11},{11,3},{4,12},{12,4},... | collective-permute-start | bytes 1376264 | tf_op jit(solution)/shard_map/ppermute | solution.py:175
  87.8 5.5 %collective-permute-start.32 = (bf16[32,3584]{1,0:T(8,128)(2,1)S(1)}, bf16[32,3584]{1,0:T(8,128)(2,1)S(1)}, u32[]{:S(2)}, u32[]{:S(2)}) collective-permute-start(bf16[32,3584]{1,0:T(8,128)(2,1)S(1)} %get-tuple-element.55), channel_id=1, source_target_pairs={{0,10},{10,0},{2,12},{12,2},{4,14},{14,4},{6,15},{15,6},{7,13},{13... | collective-permute-start | bytes 688136 | tf_op jit(solution)/shard_map/ppermute | solution.py:172
  87.8 6.9 %collective-permute-start.31 = (bf16[32,3584]{1,0:T(8,128)(2,1)S(1)}, bf16[32,3584]{1,0:T(8,128)(2,1)S(1)}, u32[]{:S(2)}, u32[]{:S(2)}) collective-permute-start(bf16[32,3584]{1,0:T(8,128)(2,1)S(1)} %get-tuple-element.54), channel_id=1, source_target_pairs={{0,2},{10,8},{2,4},{12,10},{4,6},{14,12},{6,7},{15,14},{7,5},{13,1... | collective-permute-start | bytes 688136 | tf_op jit(solution)/shard_map/ppermute | solution.py:172

commit v6 on v5

--- a/solution.py
+++ b/solution.py
@@ -128,6 +128,34 @@
     )(expert, *inputs, *after)
 
 
+def load_kernel(*refs, count):
+    sources, targets, sems = refs[:count], refs[-count - 1 : -1], refs[-1]
+    copies = [
+        pltpu.make_async_copy(sources[i].at[0], targets[i], sems.at[i]) for i in range(count)
+    ]
+    for copy in copies:
+        copy.start()
+    for copy in copies:
+        copy.wait()
+
+
+def load_weights(weights, after):
+    count = len(weights)
+    anywhere = pl.BlockSpec(memory_space=pl.ANY)
+    return pl.pallas_call(
+        functools.partial(load_kernel, count=count),
+        in_specs=[anywhere] * (count + len(after)),
+        out_specs=[anywhere] * count,
+        out_shape=[jax.ShapeDtypeStruct(w.shape[1:], w.dtype) for w in weights],
+        scratch_shapes=[pltpu.SemaphoreType.DMA((count,))],
+        compiler_params=pltpu.CompilerParams(vmem_limit_bytes=41 << 20),
+        cost_estimate=pl.CostEstimate(
+            flops=0, bytes_accessed=2 * sum(w.size for w in weights), transcendentals=0
+        ),
+        name="load_weights",
+    )(*weights, *after)
+
+
 def join_kernel(first_ref, second_ref, out_ref):
     rows = first_ref.shape[0]
     out_ref[:rows] = first_ref[...]
@@ -190,7 +218,7 @@
         jnp.concatenate(pair, axis=1) for pair in zip(halves(tokens), halves(route), strict=True)
     ]
     swapped = across(given)
-    gate, up, down = w_gate[0], w_up[0], w_down[0]
+    gate, up, down = load_weights((w_gate, w_up, w_down), (kept,))
     block = join(onward(kept), onward(swapped))
     own, other = run_experts(
         expert, (kept, given), (across(kept), swapped), gate, up, down

time: 96.3 us -> 94.1 us (0.977)
  local copies, waits for them, and re-layouts: 6.72 us -> 0.12 us
  Pallas kernels: 24.2 us -> 28.2 us
    unnamed x22 -> x10, local copies, waits for them, and re-layouts: 6.62 us -> 0.03 us
    pallas_call x0 -> x1, Pallas kernels: none -> 4.23 us  [load_weights(): pl.pallas_call(functools.partial(load_kernel, count=count), in_specs=[any...]
  transfers between devices with their start and end apart: 33 -> 33, of which waited for: 12 -> 12; matrix products, arithmetic and copies ran while one was open for 1% -> 2% of each run, Pallas kernels for 25% -> 30%
where the time goes in v6:
time: 94.1 us; the launch traced here: 93.7 us
  waiting for transfers between devices  32 us (34%)
  Pallas kernels  28.2 us (30%)
  starting transfers between devices  27.9 us (30%)
  other arithmetic  4.35 us (5%)
  between operations  1 us (1%)
    ppermute x16, waiting for transfers between devices, onward(): return lax.ppermute(a, ('node', 'local'), pairs)  31.8 us
    ppermute x16, starting transfers between devices, onward(): return lax.ppermute(a, ('node', 'local'), pairs)  25.1 us
    pallas_call x8, Pallas kernels, run_experts(): pl.pallas_call(functools.partial(expert_kernel, own_parts=len(own), parts...  13.7 us
    pallas_call x4, Pallas kernels, attend_piece(): pl.pallas_call(functools.partial(attend_kernel, base=piece * count, pair=...  10.3 us
    pallas_call x1, Pallas kernels, load_weights(): pl.pallas_call(functools.partial(load_kernel, count=count), in_specs=[any...  4.23 us
    ppermute x17, starting transfers between devices, across(): return lax.ppermute(a, 'node', [(0, 1), (1, 0)])  2.89 us
  transfers between devices with their start and end apart: 33, of which 12 were waited for; matrix products, arithmetic and copies ran while one was open for 2% of the time, Pallas kernels for 30%

profile of v6, /device:TPU:0, one launch (start us, length us, event | category | flops | bytes accessed | tf_op | source)
XLA Modules:
  0.0 93.7 jit_solution(8081249676380815950)
XLA Ops:
  0.6 0.8 fusion.1
  1.5 1.1 %broadcast_select_fusion = (bf16[32,3584]{1,0:T(8,128)(2,1)S(1)}, bf16[32,3584]{1,0:T(8,128)(2,1)S(1)}) fusion(pred[]{:T(512)S(6)} %eq.16, bf16[64,3584]{1,0:T(8,128)(2,1)} %param.9), kind=kLoop, calls=%fused_computation.13 | loop fusion | flops 229376 | bytes 917505 | tf_op jit(solution)/shard_map/jit(_where)/select_n | solution.py:215
  2.6 0.5 collective-permute-start.1
  3.1 0.1 collective-permute-start
  3.3 3.0 %collective-permute-start.3 = (bf16[32,3712]{1,0:T(8,128)(2,1)S(1)}, bf16[32,3712]{1,0:T(8,128)(2,1)S(1)}, u32[]{:S(2)}, u32[]{:S(2)}) collective-permute-start(bf16[32,3712]{1,0:T(8,128)(2,1)S(1)} %pad_maximum_fusion.refs_3_.refs_0_), channel_id=1, source_target_pairs={{0,2},{10,8},{2,4},{12,10},{4,6},{14,12},{6,7},{15,14},{7,5},{13,1... | collective-permute-start | bytes 712712 | tf_op jit(solution)/shard_map/ppermute | solution.py:200
  6.3 1.6 %collective-permute-start.4 = (bf16[32,3712]{1,0:T(8,128)(2,1)S(1)}, bf16[32,3712]{1,0:T(8,128)(2,1)S(1)}, u32[]{:S(2)}, u32[]{:S(2)}) collective-permute-start(bf16[32,3712]{1,0:T(8,128)(2,1)S(1)} %collective-permute-done.1.refs_3_), channel_id=1, source_target_pairs={{0,2},{10,8},{2,4},{12,10},{4,6},{14,12},{6,7},{15,14},{7,5},{13,1... | collective-permute-start | bytes 712712 | tf_op jit(solution)/shard_map/ppermute | solution.py:200
  7.9 4.2 %load_weights.1 = (bf16[3584,512]{1,0:T(8,128)(2,1)S(1)}, bf16[3584,512]{1,0:T(8,128)(2,1)S(1)}, bf16[512,3584]{1,0:T(8,128)(2,1)S(1)}) custom-call(bf16[1,3584,512]{2,1,0:T(8,128)(2,1)} %refs_0_.1, bf16[1,3584,512]{2,1,0:T(8,128)(2,1)} %refs_1_.1, bf16[1,512,3584]{2,1,0:T(8,128)(2,1)} %refs_2_.1, bf16[32,3712]{1,0:T(8,128)(2,1)S(1)} %pad_maximum_fusion.refs_3_.refs_0_), custom_call_target="tpu_custom_call" | custom-call | bytes 11010048 | tf_op jit(solution)/shard_map/load_weights/pallas_call | solution.py:145
  12.1 1.7 %expert_half.8 = (bf16[64,3584]{1,0:T(8,128)(2,1)S(1)}, bf16[64,3584]{1,0:T(8,128)(2,1)S(1)}) custom-call(s32[1]{0:T(128)} %bitcast.expert_ref, bf16[32,3712]{1,0:T(8,128)(2,1)S(1)} %pad_maximum_fusion.refs_3_.refs_0_, bf16[32,3712]{1,0:T(8,128)(2,1)S(1)} %pad_maximum_fusion.1.refs_1_, bf16[32,3712]{1,0:T(8,128)(2,1)S(1)} %collective-permute-done.refs_2_, ...), custom_call_target="tpu_custom_call" | custom-call | flops 1409286144 | bytes 11010048 | tf_op jit(solution)/shard_map/expert_half/pallas_call | solution.py:109
  13.9 0.1 collective-permute-start.14
  14.0 1.6 %collective-permute-start.5 = (bf16[64,3712]{1,0:T(8,128)(2,1)S(1)}, bf16[64,3712]{1,0:T(8,128)(2,1)S(1)}, u32[]{:S(2)}, u32[]{:S(2)}) collective-permute-start(bf16[64,3712]{1,0:T(8,128)(2,1)S(1)} %join.1.refs_0_), channel_id=1, source_target_pairs={{0,2},{10,8},{2,4},{12,10},{4,6},{14,12},{6,7},{15,14},{7,5},{13,1... | collective-permute-start | bytes 1425416 | tf_op jit(solution)/shard_map/ppermute | solution.py:200
  15.6 0.2 collective-permute-done.14.refs_1_
  15.8 1.7 %expert_half.10 = (bf16[64,3584]{1,0:T(8,128)(2,1)S(1)}, bf16[64,3584]{1,0:T(8,128)(2,1)S(1)}) custom-call(s32[1]{0:T(128)} %bitcast.expert_ref, bf16[64,3712]{1,0:T(8,128)(2,1)S(1)} %join.1.refs_0_, bf16[64,3712]{1,0:T(8,128)(2,1)S(1)} %collective-permute-done.14.refs_1_, bf16[3584,512]{1,0:T(8,128)(2,1)S(1)} %get-tuple-element.30.refs_4_.refs_2_, ...), custom_call_target="tpu_custom_call" | custom-call | flops 1409286144 | bytes 11010048 | tf_op jit(solution)/shard_map/expert_half/pallas_call | solution.py:109
  17.5 0.2 collective-permute-start.24
  17.7 5.0 %collective-permute-done.5.refs_0_ = bf16[64,3712]{1,0:T(8,128)(2,1)S(1)} collective-permute-done((bf16[64,3712]{1,0:T(8,128)(2,1)S(1)}, bf16[64,3712]{1,0:T(8,128)(2,1)S(1)}, u32[]{:S(2)}, u32[]{:S(2)}) %collective-permute-start.5) | collective-permute-done | bytes 475168 | tf_op jit(solution)/shard_map/ppermute | solution.py:200
  22.7 1.6 %collective-permute-start.6 = (bf16[64,3712]{1,0:T(8,128)(2,1)S(1)}, bf16[64,3712]{1,0:T(8,128)(2,1)S(1)}, u32[]{:S(2)}, u32[]{:S(2)}) collective-permute-start(bf16[64,3712]{1,0:T(8,128)(2,1)S(1)} %collective-permute-done.5.refs_0_), channel_id=1, source_target_pairs={{0,2},{10,8},{2,4},{12,10},{4,6},{14,12},{6,7},{15,14},{7,5},{13,1... | collective-permute-start | bytes 1425416 | tf_op jit(solution)/shard_map/ppermute | solution.py:200
  24.3 0.1 add_convert_fusion.7
  24.4 1.6 %collective-permute-start.25 = (bf16[64,3584]{1,0:T(8,128)(2,1)S(1)}, bf16[64,3584]{1,0:T(8,128)(2,1)S(1)}, u32[]{:S(2)}, u32[]{:S(2)}) collective-permute-start(bf16[64,3584]{1,0:T(8,128)(2,1)S(1)} %add_convert_fusion.7), channel_id=1, source_target_pairs={{0,2},{10,8},{2,4},{12,10},{4,6},{14,12},{6,7},{15,14},{7,5},{13,1... | collective-permute-start | bytes 1376264 | tf_op jit(solution)/shard_map/ppermute | solution.py:200
  26.0 1.7 %expert_half.11 = (bf16[64,3584]{1,0:T(8,128)(2,1)S(1)}, bf16[64,3584]{1,0:T(8,128)(2,1)S(1)}) custom-call(s32[1]{0:T(128)} %bitcast.expert_ref, bf16[64,3712]{1,0:T(8,128)(2,1)S(1)} %collective-permute-done.5.refs_0_, bf16[64,3712]{1,0:T(8,128)(2,1)S(1)} %collective-permute-done.15.refs_1_, bf16[3584,512]{1,0:T(8,128)(2,1)S(1)} %get-tuple-element.30.refs_4_.refs_2_, ...), custom_call_target="tpu_custom_call" | custom-call | flops 1409286144 | bytes 11010048 | tf_op jit(solution)/shard_map/expert_half/pallas_call | solution.py:109
  27.7 0.1 collective-permute-start.23
  27.9 2.6 %attend.4 = (bf16[64,64,512]{2,1,0:T(8,128)(2,1)}, f32[8,128]{1,0:T(8,128)S(1)}) custom-call(s32[64]{0:T(128)S(1)} %copy-done, bf16[64,64,576]{2,1,0:T(8,128)(2,1)S(1)} %bitcast.2, bf16[64,64,576]{2,1,0:T(8,128)(2,1)S(1)} %bitcast.4, bf16[64,3584]{1,0:T(8,128)(2,1)S(1)} %get-tuple-element.38.rest_0_), custom_call_target="tpu_custom_call" | custom-call | flops 142606336 | bytes 3407872 | tf_op jit(solution)/shard_map/attend/pallas_call | solution.py:59
  30.4 0.9 collective-permute-done.6.refs_0_
  31.3 1.6 %collective-permute-start.7 = (bf16[64,3712]{1,0:T(8,128)(2,1)S(1)}, bf16[64,3712]{1,0:T(8,128)(2,1)S(1)}, u32[]{:S(2)}, u32[]{:S(2)}) collective-permute-start(bf16[64,3712]{1,0:T(8,128)(2,1)S(1)} %collective-permute-done.6.refs_0_), channel_id=1, source_target_pairs={{0,2},{10,8},{2,4},{12,10},{4,6},{14,12},{6,7},{15,14},{7,5},{13,1... | collective-permute-start | bytes 1425416 | tf_op jit(solution)/shard_map/ppermute | solution.py:200
  32.9 3.3 %collective-permute-done.25 = bf16[64,3584]{1,0:T(8,128)(2,1)S(1)} collective-permute-done((bf16[64,3584]{1,0:T(8,128)(2,1)S(1)}, bf16[64,3584]{1,0:T(8,128)(2,1)S(1)}, u32[]{:S(2)}, u32[]{:S(2)}) %collective-permute-start.25) | collective-permute-done | bytes 458784 | tf_op jit(solution)/shard_map/ppermute | solution.py:200
  36.3 0.2 add_convert_fusion.6
  36.4 1.6 %collective-permute-start.26 = (bf16[64,3584]{1,0:T(8,128)(2,1)S(1)}, bf16[64,3584]{1,0:T(8,128)(2,1)S(1)}, u32[]{:S(2)}, u32[]{:S(2)}) collective-permute-start(bf16[64,3584]{1,0:T(8,128)(2,1)S(1)} %add_convert_fusion.6), channel_id=1, source_target_pairs={{0,2},{10,8},{2,4},{12,10},{4,6},{14,12},{6,7},{15,14},{7,5},{13,1... | collective-permute-start | bytes 1376264 | tf_op jit(solution)/shard_map/ppermute | solution.py:200
  38.1 1.7 %expert_half.12 = (bf16[64,3584]{1,0:T(8,128)(2,1)S(1)}, bf16[64,3584]{1,0:T(8,128)(2,1)S(1)}) custom-call(s32[1]{0:T(128)} %bitcast.expert_ref, bf16[64,3712]{1,0:T(8,128)(2,1)S(1)} %collective-permute-done.6.refs_0_, bf16[64,3712]{1,0:T(8,128)(2,1)S(1)} %collective-permute-done.16.refs_1_, bf16[3584,512]{1,0:T(8,128)(2,1)S(1)} %get-tuple-element.30.refs_4_.refs_2_, ...), custom_call_target="tpu_custom_call" | custom-call | flops 1409286144 | bytes 11010048 | tf_op jit(solution)/shard_map/expert_half/pallas_call | solution.py:109
  39.8 0.1 collective-permute-start.22
  39.9 2.6 %attend.5 = (bf16[64,64,512]{2,1,0:T(8,128)(2,1)}, f32[8,128]{1,0:T(8,128)S(1)}) custom-call(s32[64]{0:T(128)S(1)} %copy-done, bf16[64,64,576]{2,1,0:T(8,128)(2,1)S(1)} %bitcast.2, bf16[64,64,576]{2,1,0:T(8,128)(2,1)S(1)} %bitcast.4, bf16[64,64,512]{2,1,0:T(8,128)(2,1)} %get-tuple-element.39.rest_0_, ...), custom_call_target="tpu_custom_call", output_to_operand_aliasing={{0}: (3, {})} | custom-call | flops 142606336 | bytes 3407872 | tf_op jit(solution)/shard_map/attend/pallas_call | solution.py:59
  42.4 0.5 collective-permute-start.17
  42.9 1.5 %collective-permute-start.8 = (bf16[64,3712]{1,0:T(8,128)(2,1)S(1)}, bf16[64,3712]{1,0:T(8,128)(2,1)S(1)}, u32[]{:S(2)}, u32[]{:S(2)}) collective-permute-start(bf16[64,3712]{1,0:T(8,128)(2,1)S(1)} %collective-permute-done.7.refs_0_), channel_id=1, source_target_pairs={{0,2},{10,8},{2,4},{12,10},{4,6},{14,12},{6,7},{15,14},{7,5},{13,1... | collective-permute-start | bytes 1425416 | tf_op jit(solution)/shard_map/ppermute | solution.py:200
  44.4 1.8 %collective-permute-done.26 = bf16[64,3584]{1,0:T(8,128)(2,1)S(1)} collective-permute-done((bf16[64,3584]{1,0:T(8,128)(2,1)S(1)}, bf16[64,3584]{1,0:T(8,128)(2,1)S(1)}, u32[]{:S(2)}, u32[]{:S(2)}) %collective-permute-start.26) | collective-permute-done | bytes 458784 | tf_op jit(solution)/shard_map/ppermute | solution.py:200
  46.3 0.2 add_convert_fusion.5
  46.5 1.8 %collective-permute-start.27 = (bf16[64,3584]{1,0:T(8,128)(2,1)S(1)}, bf16[64,3584]{1,0:T(8,128)(2,1)S(1)}, u32[]{:S(2)}, u32[]{:S(2)}) collective-permute-start(bf16[64,3584]{1,0:T(8,128)(2,1)S(1)} %add_convert_fusion.5), channel_id=1, source_target_pairs={{0,2},{10,8},{2,4},{12,10},{4,6},{14,12},{6,7},{15,14},{7,5},{13,1... | collective-permute-start | bytes 1376264 | tf_op jit(solution)/shard_map/ppermute | solution.py:200
  48.3 1.7 %expert_half.13 = (bf16[64,3584]{1,0:T(8,128)(2,1)S(1)}, bf16[64,3584]{1,0:T(8,128)(2,1)S(1)}) custom-call(s32[1]{0:T(128)} %bitcast.expert_ref, bf16[64,3712]{1,0:T(8,128)(2,1)S(1)} %collective-permute-done.7.refs_0_, bf16[64,3712]{1,0:T(8,128)(2,1)S(1)} %collective-permute-done.17.refs_1_, bf16[3584,512]{1,0:T(8,128)(2,1)S(1)} %get-tuple-element.30.refs_4_.refs_2_, ...), custom_call_target="tpu_custom_call" | custom-call | flops 1409286144 | bytes 11010048 | tf_op jit(solution)/shard_map/expert_half/pallas_call | solution.py:109
  50.0 0.1 collective-permute-start.21
  50.1 2.6 %attend.6 = (bf16[64,64,512]{2,1,0:T(8,128)(2,1)}, f32[8,128]{1,0:T(8,128)S(1)}) custom-call(s32[64]{0:T(128)S(1)} %copy-done, bf16[64,64,576]{2,1,0:T(8,128)(2,1)S(1)} %bitcast.2, bf16[64,64,576]{2,1,0:T(8,128)(2,1)S(1)} %bitcast.4, bf16[64,64,512]{2,1,0:T(8,128)(2,1)} %get-tuple-element.41.rest_0_, ...), custom_call_target="tpu_custom_call", output_to_operand_aliasing={{0}: (3, {})} | custom-call | flops 142606336 | bytes 3407872 | tf_op jit(solution)/shard_map/attend/pallas_call | solution.py:59
  52.7 0.5 collective-permute-start.19
  53.2 1.5 %collective-permute-start.9 = (bf16[64,3712]{1,0:T(8,128)(2,1)S(1)}, bf16[64,3712]{1,0:T(8,128)(2,1)S(1)}, u32[]{:S(2)}, u32[]{:S(2)}) collective-permute-start(bf16[64,3712]{1,0:T(8,128)(2,1)S(1)} %collective-permute-done.8.refs_0_), channel_id=1, source_target_pairs={{0,2},{10,8},{2,4},{12,10},{4,6},{14,12},{6,7},{15,14},{7,5},{13,1... | collective-permute-start | bytes 1425416 | tf_op jit(solution)/shard_map/ppermute | solution.py:200
  54.7 1.8 %collective-permute-done.27 = bf16[64,3584]{1,0:T(8,128)(2,1)S(1)} collective-permute-done((bf16[64,3584]{1,0:T(8,128)(2,1)S(1)}, bf16[64,3584]{1,0:T(8,128)(2,1)S(1)}, u32[]{:S(2)}, u32[]{:S(2)}) %collective-permute-start.27) | collective-permute-done | bytes 458784 | tf_op jit(solution)/shard_map/ppermute | solution.py:200
  56.5 0.2 add_convert_fusion.4
  56.7 1.6 %collective-permute-start.28 = (bf16[64,3584]{1,0:T(8,128)(2,1)S(1)}, bf16[64,3584]{1,0:T(8,128)(2,1)S(1)}, u32[]{:S(2)}, u32[]{:S(2)}) collective-permute-start(bf16[64,3584]{1,0:T(8,128)(2,1)S(1)} %add_convert_fusion.4), channel_id=1, source_target_pairs={{0,2},{10,8},{2,4},{12,10},{4,6},{14,12},{6,7},{15,14},{7,5},{13,1... | collective-permute-start | bytes 1376264 | tf_op jit(solution)/shard_map/ppermute | solution.py:200
  58.3 1.7 %expert_half.15 = (bf16[64,3584]{1,0:T(8,128)(2,1)S(1)}, bf16[64,3584]{1,0:T(8,128)(2,1)S(1)}) custom-call(s32[1]{0:T(128)} %bitcast.expert_ref, bf16[64,3712]{1,0:T(8,128)(2,1)S(1)} %collective-permute-done.8.refs_0_, bf16[64,3712]{1,0:T(8,128)(2,1)S(1)} %collective-permute-done.19.refs_1_, bf16[3584,512]{1,0:T(8,128)(2,1)S(1)} %get-tuple-element.30.refs_4_.refs_2_, ...), custom_call_target="tpu_custom_call" | custom-call | flops 1409286144 | bytes 11010048 | tf_op jit(solution)/shard_map/expert_half/pallas_call | solution.py:109
  60.0 0.1 collective-permute-start.20
  60.1 0.5 collective-permute-start.2
  60.6 2.6 %attend.7 = (bf16[64,64,512]{2,1,0:T(8,128)(2,1)}, f32[8,128]{1,0:T(8,128)S(1)}) custom-call(s32[64]{0:T(128)S(1)} %copy-done, bf16[64,64,576]{2,1,0:T(8,128)(2,1)S(1)} %bitcast.2, bf16[64,64,576]{2,1,0:T(8,128)(2,1)S(1)} %bitcast.4, bf16[64,64,512]{2,1,0:T(8,128)(2,1)} %get-tuple-element.44.rest_0_, ...), custom_call_target="tpu_custom_call", output_to_operand_aliasing={{0}: (3, {})} | custom-call | flops 142606336 | bytes 3407872 | tf_op jit(solution)/shard_map/attend/pallas_call | solution.py:59
  63.1 0.1 collective-permute-start.13
  63.2 1.4 %collective-permute-start.10 = (bf16[64,3712]{1,0:T(8,128)(2,1)S(1)}, bf16[64,3712]{1,0:T(8,128)(2,1)S(1)}, u32[]{:S(2)}, u32[]{:S(2)}) collective-permute-start(bf16[64,3712]{1,0:T(8,128)(2,1)S(1)} %collective-permute-done.9.refs_0_), channel_id=1, source_target_pairs={{0,2},{10,8},{2,4},{12,10},{4,6},{14,12},{6,7},{15,14},{7,5},{13,1... | collective-permute-start | bytes 1425416 | tf_op jit(solution)/shard_map/ppermute | solution.py:200
  64.6 2.2 %collective-permute-done.28 = bf16[64,3584]{1,0:T(8,128)(2,1)S(1)} collective-permute-done((bf16[64,3584]{1,0:T(8,128)(2,1)S(1)}, bf16[64,3584]{1,0:T(8,128)(2,1)S(1)}, u32[]{:S(2)}, u32[]{:S(2)}) %collective-permute-start.28) | collective-permute-done | bytes 458784 | tf_op jit(solution)/shard_map/ppermute | solution.py:200
  66.7 0.2 add_convert_fusion.3
  66.9 1.6 %collective-permute-start.29 = (bf16[64,3584]{1,0:T(8,128)(2,1)S(1)}, bf16[64,3584]{1,0:T(8,128)(2,1)S(1)}, u32[]{:S(2)}, u32[]{:S(2)}) collective-permute-start(bf16[64,3584]{1,0:T(8,128)(2,1)S(1)} %add_convert_fusion.3), channel_id=1, source_target_pairs={{0,2},{10,8},{2,4},{12,10},{4,6},{14,12},{6,7},{15,14},{7,5},{13,1... | collective-permute-start | bytes 1376264 | tf_op jit(solution)/shard_map/ppermute | solution.py:200
  68.5 1.7 %expert_half.14 = (bf16[64,3584]{1,0:T(8,128)(2,1)S(1)}, bf16[64,3584]{1,0:T(8,128)(2,1)S(1)}) custom-call(s32[1]{0:T(128)} %bitcast.expert_ref, bf16[64,3712]{1,0:T(8,128)(2,1)S(1)} %collective-permute-done.9.refs_0_, bf16[64,3712]{1,0:T(8,128)(2,1)S(1)} %collective-permute-done.13.refs_1_, bf16[3584,512]{1,0:T(8,128)(2,1)S(1)} %get-tuple-element.30.refs_4_.refs_2_, ...), custom_call_target="tpu_custom_call" | custom-call | flops 1409286144 | bytes 11010048 | tf_op jit(solution)/shard_map/expert_half/pallas_call | solution.py:109
  70.3 0.1 convert_add_fusion
  70.4 1.4 %collective-permute-done.10.refs_0_ = bf16[64,3712]{1,0:T(8,128)(2,1)S(1)} collective-permute-done((bf16[64,3712]{1,0:T(8,128)(2,1)S(1)}, bf16[64,3712]{1,0:T(8,128)(2,1)S(1)}, u32[]{:S(2)}, u32[]{:S(2)}) %collective-permute-start.10) | collective-permute-done | bytes 475168 | tf_op jit(solution)/shard_map/ppermute | solution.py:200
  71.9 4.9 %collective-permute-done.29 = bf16[64,3584]{1,0:T(8,128)(2,1)S(1)} collective-permute-done((bf16[64,3584]{1,0:T(8,128)(2,1)S(1)}, bf16[64,3584]{1,0:T(8,128)(2,1)S(1)}, u32[]{:S(2)}, u32[]{:S(2)}) %collective-permute-start.29) | collective-permute-done | bytes 458784 | tf_op jit(solution)/shard_map/ppermute | solution.py:200
  76.8 0.2 add_convert_fusion.2
  77.0 1.5 %collective-permute-start.30 = (bf16[64,3584]{1,0:T(8,128)(2,1)S(1)}, bf16[64,3584]{1,0:T(8,128)(2,1)S(1)}, u32[]{:S(2)}, u32[]{:S(2)}) collective-permute-start(bf16[64,3584]{1,0:T(8,128)(2,1)S(1)} %add_convert_fusion.2), channel_id=1, source_target_pairs={{0,2},{10,8},{2,4},{12,10},{4,6},{14,12},{6,7},{15,14},{7,5},{13,1... | collective-permute-start | bytes 1376264 | tf_op jit(solution)/shard_map/ppermute | solution.py:200
  78.5 1.7 %expert_half.9 = (bf16[64,3584]{1,0:T(8,128)(2,1)S(1)}, bf16[64,3584]{1,0:T(8,128)(2,1)S(1)}) custom-call(s32[1]{0:T(128)} %bitcast.expert_ref, bf16[64,3712]{1,0:T(8,128)(2,1)S(1)} %collective-permute-done.10.refs_0_, bf16[64,3712]{1,0:T(8,128)(2,1)S(1)} %collective-permute-done.11.refs_1_, bf16[3584,512]{1,0:T(8,128)(2,1)S(1)} %get-tuple-element.30.refs_4_.refs_2_, ...), custom_call_target="tpu_custom_call" | custom-call | flops 1409286144 | bytes 11010048 | tf_op jit(solution)/shard_map/expert_half/pallas_call | solution.py:109
  80.4 5.1 %collective-permute-done.30 = bf16[64,3584]{1,0:T(8,128)(2,1)S(1)} collective-permute-done((bf16[64,3584]{1,0:T(8,128)(2,1)S(1)}, bf16[64,3584]{1,0:T(8,128)(2,1)S(1)}, u32[]{:S(2)}, u32[]{:S(2)}) %collective-permute-start.30) | collective-permute-done | bytes 458784 | tf_op jit(solution)/shard_map/ppermute | solution.py:200
  85.5 0.2 add_convert_fusion.1
  85.8 1.5 %collective-permute-start.31 = (bf16[32,3584]{1,0:T(8,128)(2,1)S(1)}, bf16[32,3584]{1,0:T(8,128)(2,1)S(1)}, u32[]{:S(2)}, u32[]{:S(2)}) collective-permute-start(bf16[32,3584]{1,0:T(8,128)(2,1)S(1)} %get-tuple-element.60), channel_id=1, source_target_pairs={{0,2},{10,8},{2,4},{12,10},{4,6},{14,12},{6,7},{15,14},{7,5},{13,1... | collective-permute-start | bytes 688136 | tf_op jit(solution)/shard_map/ppermute | solution.py:200
  87.4 0.2 maximum_select_fusion
  87.5 3.7 %collective-permute-done.32 = bf16[32,3584]{1,0:T(8,128)(2,1)S(1)} collective-permute-done((bf16[32,3584]{1,0:T(8,128)(2,1)S(1)}, bf16[32,3584]{1,0:T(8,128)(2,1)S(1)}, u32[]{:S(2)}, u32[]{:S(2)}) %collective-permute-start.32) | collective-permute-done | bytes 229408 | tf_op jit(solution)/shard_map/ppermute | solution.py:200
  91.3 1.5 %collective-permute-done.31 = bf16[32,3584]{1,0:T(8,128)(2,1)S(1)} collective-permute-done((bf16[32,3584]{1,0:T(8,128)(2,1)S(1)}, bf16[32,3584]{1,0:T(8,128)(2,1)S(1)}, u32[]{:S(2)}, u32[]{:S(2)}) %collective-permute-start.31) | collective-permute-done | bytes 229408 | tf_op jit(solution)/shard_map/ppermute | solution.py:200
  92.8 0.9 add_convert_fusion
  (45 shorter events, 0.5 us)
Async XLA Ops:
  2.6 3.7 %collective-permute-start.1 = (bf16[32,3712]{1,0:T(8,128)(2,1)S(1)}, bf16[32,3712]{1,0:T(8,128)(2,1)S(1)}, u32[]{:S(2)}, u32[]{:S(2)}) collective-permute-start(bf16[32,3712]{1,0:T(8,128)(2,1)S(1)} %pad_maximum_fusion.1.refs_1_), channel_id=1, source_target_pairs={{0,8},{8,0},{1,9},{9,1},{2,10},{10,2},{3,11},{11,3},{4,12},{12,4},... | collective-permute-start | bytes 712712 | tf_op jit(solution)/shard_map/ppermute | solution.py:203
  3.1 9.0 %collective-permute-start = (bf16[32,3712]{1,0:T(8,128)(2,1)S(1)}, bf16[32,3712]{1,0:T(8,128)(2,1)S(1)}, u32[]{:S(2)}, u32[]{:S(2)}) collective-permute-start(bf16[32,3712]{1,0:T(8,128)(2,1)S(1)} %pad_maximum_fusion.refs_3_.refs_0_), channel_id=1, source_target_pairs={{0,8},{8,0},{1,9},{9,1},{2,10},{10,2},{3,11},{11,3},{4,12},{12,4},... | collective-permute-start | bytes 712712 | tf_op jit(solution)/shard_map/ppermute | solution.py:203
  3.3 10.6 %collective-permute-start.3 = (bf16[32,3712]{1,0:T(8,128)(2,1)S(1)}, bf16[32,3712]{1,0:T(8,128)(2,1)S(1)}, u32[]{:S(2)}, u32[]{:S(2)}) collective-permute-start(bf16[32,3712]{1,0:T(8,128)(2,1)S(1)} %pad_maximum_fusion.refs_3_.refs_0_), channel_id=1, source_target_pairs={{0,2},{10,8},{2,4},{12,10},{4,6},{14,12},{6,7},{15,14},{7,5},{13,1... | collective-permute-start | bytes 712712 | tf_op jit(solution)/shard_map/ppermute | solution.py:200
  6.3 7.6 %collective-permute-start.4 = (bf16[32,3712]{1,0:T(8,128)(2,1)S(1)}, bf16[32,3712]{1,0:T(8,128)(2,1)S(1)}, u32[]{:S(2)}, u32[]{:S(2)}) collective-permute-start(bf16[32,3712]{1,0:T(8,128)(2,1)S(1)} %collective-permute-done.1.refs_3_), channel_id=1, source_target_pairs={{0,2},{10,8},{2,4},{12,10},{4,6},{14,12},{6,7},{15,14},{7,5},{13,1... | collective-permute-start | bytes 712712 | tf_op jit(solution)/shard_map/ppermute | solution.py:200
  13.9 1.9 %collective-permute-start.14 = (bf16[64,3712]{1,0:T(8,128)(2,1)S(1)}, bf16[64,3712]{1,0:T(8,128)(2,1)S(1)}, u32[]{:S(2)}, u32[]{:S(2)}) collective-permute-start(bf16[64,3712]{1,0:T(8,128)(2,1)S(1)} %join.1.refs_0_), channel_id=1, source_target_pairs={{0,8},{8,0},{1,9},{9,1},{2,10},{10,2},{3,11},{11,3},{4,12},{12,4},... | collective-permute-start | bytes 1425416 | tf_op jit(solution)/shard_map/ppermute | solution.py:203
  14.0 8.7 %collective-permute-start.5 = (bf16[64,3712]{1,0:T(8,128)(2,1)S(1)}, bf16[64,3712]{1,0:T(8,128)(2,1)S(1)}, u32[]{:S(2)}, u32[]{:S(2)}) collective-permute-start(bf16[64,3712]{1,0:T(8,128)(2,1)S(1)} %join.1.refs_0_), channel_id=1, source_target_pairs={{0,2},{10,8},{2,4},{12,10},{4,6},{14,12},{6,7},{15,14},{7,5},{13,1... | collective-permute-start | bytes 1425416 | tf_op jit(solution)/shard_map/ppermute | solution.py:200
  15.8 12.0 %slice-start.2 = ((s8[5242880]{0:T(1024)(128)(4,1)}), s8[4194304]{0:T(1024)(128)(4,1)S(1)}, s32[]{:S(2)}) async-start(s8[5242880]{0:T(1024)(128)(4,1)} %bitcast.3), calls=%async_computation.2 | async-start | bytes 8388608
  17.5 6.7 %collective-permute-start.24 = (bf16[64,3584]{1,0:T(8,128)(2,1)S(1)}, bf16[64,3584]{1,0:T(8,128)(2,1)S(1)}, u32[]{:S(2)}, u32[]{:S(2)}) collective-permute-start(bf16[64,3584]{1,0:T(8,128)(2,1)S(1)} %get-tuple-element.56), channel_id=1, source_target_pairs={{0,8},{8,0},{1,9},{9,1},{2,10},{10,2},{3,11},{11,3},{4,12},{12,4},... | collective-permute-start | bytes 1376264 | tf_op jit(solution)/shard_map/ppermute | solution.py:203
  22.7 3.3 %collective-permute-start.15 = (bf16[64,3712]{1,0:T(8,128)(2,1)S(1)}, bf16[64,3712]{1,0:T(8,128)(2,1)S(1)}, u32[]{:S(2)}, u32[]{:S(2)}) collective-permute-start(bf16[64,3712]{1,0:T(8,128)(2,1)S(1)} %collective-permute-done.5.refs_0_), channel_id=1, source_target_pairs={{0,8},{8,0},{1,9},{9,1},{2,10},{10,2},{3,11},{11,3},{4,12},{12,4},... | collective-permute-start | bytes 1425416 | tf_op jit(solution)/shard_map/ppermute | solution.py:203
  22.7 8.7 %collective-permute-start.6 = (bf16[64,3712]{1,0:T(8,128)(2,1)S(1)}, bf16[64,3712]{1,0:T(8,128)(2,1)S(1)}, u32[]{:S(2)}, u32[]{:S(2)}) collective-permute-start(bf16[64,3712]{1,0:T(8,128)(2,1)S(1)} %collective-permute-done.5.refs_0_), channel_id=1, source_target_pairs={{0,2},{10,8},{2,4},{12,10},{4,6},{14,12},{6,7},{15,14},{7,5},{13,1... | collective-permute-start | bytes 1425416 | tf_op jit(solution)/shard_map/ppermute | solution.py:200
  24.3 3.5 %slice-start = ((s8[5242880]{0:T(1024)(128)(4,1)}), s8[4194304]{0:T(1024)(128)(4,1)S(1)}, s32[]{:S(2)}) async-start(s8[5242880]{0:T(1024)(128)(4,1)} %bitcast.1), calls=%async_computation | async-start | bytes 8388608
  24.3 3.5 %slice-start.3 = ((s8[5242880]{0:T(1024)(128)(4,1)}), s8[1048576]{0:T(1024)(128)(4,1)S(1)}, s32[]{:S(2)}) async-start(s8[5242880]{0:T(1024)(128)(4,1)} %bitcast.3), calls=%async_computation.3 | async-start | bytes 2097152
  24.4 3.4 %slice-start.1 = ((s8[5242880]{0:T(1024)(128)(4,1)}), s8[1048576]{0:T(1024)(128)(4,1)S(1)}, s32[]{:S(2)}) async-start(s8[5242880]{0:T(1024)(128)(4,1)} %bitcast.1), calls=%async_computation.1 | async-start | bytes 2097152
  24.4 3.4 %copy-start = (s32[64]{0:T(128)S(1)}, s32[64]{0:T(128)}, u32[]{:S(2)}) copy-start(s32[64]{0:T(128)} %len_ref.7) | copy-start | bytes 772
  24.4 11.8 %collective-permute-start.25 = (bf16[64,3584]{1,0:T(8,128)(2,1)S(1)}, bf16[64,3584]{1,0:T(8,128)(2,1)S(1)}, u32[]{:S(2)}, u32[]{:S(2)}) collective-permute-start(bf16[64,3584]{1,0:T(8,128)(2,1)S(1)} %add_convert_fusion.7), channel_id=1, source_target_pairs={{0,2},{10,8},{2,4},{12,10},{4,6},{14,12},{6,7},{15,14},{7,5},{13,1... | collective-permute-start | bytes 1376264 | tf_op jit(solution)/shard_map/ppermute | solution.py:200
  27.7 8.6 %collective-permute-start.23 = (bf16[64,3584]{1,0:T(8,128)(2,1)S(1)}, bf16[64,3584]{1,0:T(8,128)(2,1)S(1)}, u32[]{:S(2)}, u32[]{:S(2)}) collective-permute-start(bf16[64,3584]{1,0:T(8,128)(2,1)S(1)} %get-tuple-element.55), channel_id=1, source_target_pairs={{0,8},{8,0},{1,9},{9,1},{2,10},{10,2},{3,11},{11,3},{4,12},{12,4},... | collective-permute-start | bytes 1376264 | tf_op jit(solution)/shard_map/ppermute | solution.py:203
  31.3 6.7 %collective-permute-start.16 = (bf16[64,3712]{1,0:T(8,128)(2,1)S(1)}, bf16[64,3712]{1,0:T(8,128)(2,1)S(1)}, u32[]{:S(2)}, u32[]{:S(2)}) collective-permute-start(bf16[64,3712]{1,0:T(8,128)(2,1)S(1)} %collective-permute-done.6.refs_0_), channel_id=1, source_target_pairs={{0,8},{8,0},{1,9},{9,1},{2,10},{10,2},{3,11},{11,3},{4,12},{12,4},... | collective-permute-start | bytes 1425416 | tf_op jit(solution)/shard_map/ppermute | solution.py:203
  31.3 11.1 %collective-permute-start.7 = (bf16[64,3712]{1,0:T(8,128)(2,1)S(1)}, bf16[64,3712]{1,0:T(8,128)(2,1)S(1)}, u32[]{:S(2)}, u32[]{:S(2)}) collective-permute-start(bf16[64,3712]{1,0:T(8,128)(2,1)S(1)} %collective-permute-done.6.refs_0_), channel_id=1, source_target_pairs={{0,2},{10,8},{2,4},{12,10},{4,6},{14,12},{6,7},{15,14},{7,5},{13,1... | collective-permute-start | bytes 1425416 | tf_op jit(solution)/shard_map/ppermute | solution.py:200
  36.4 9.8 %collective-permute-start.26 = (bf16[64,3584]{1,0:T(8,128)(2,1)S(1)}, bf16[64,3584]{1,0:T(8,128)(2,1)S(1)}, u32[]{:S(2)}, u32[]{:S(2)}) collective-permute-start(bf16[64,3584]{1,0:T(8,128)(2,1)S(1)} %add_convert_fusion.6), channel_id=1, source_target_pairs={{0,2},{10,8},{2,4},{12,10},{4,6},{14,12},{6,7},{15,14},{7,5},{13,1... | collective-permute-start | bytes 1376264 | tf_op jit(solution)/shard_map/ppermute | solution.py:200
  39.8 6.5 %collective-permute-start.22 = (bf16[64,3584]{1,0:T(8,128)(2,1)S(1)}, bf16[64,3584]{1,0:T(8,128)(2,1)S(1)}, u32[]{:S(2)}, u32[]{:S(2)}) collective-permute-start(bf16[64,3584]{1,0:T(8,128)(2,1)S(1)} %get-tuple-element.54), channel_id=1, source_target_pairs={{0,8},{8,0},{1,9},{9,1},{2,10},{10,2},{3,11},{11,3},{4,12},{12,4},... | collective-permute-start | bytes 1376264 | tf_op jit(solution)/shard_map/ppermute | solution.py:203
  42.4 5.9 %collective-permute-start.17 = (bf16[64,3712]{1,0:T(8,128)(2,1)S(1)}, bf16[64,3712]{1,0:T(8,128)(2,1)S(1)}, u32[]{:S(2)}, u32[]{:S(2)}) collective-permute-start(bf16[64,3712]{1,0:T(8,128)(2,1)S(1)} %collective-permute-done.7.refs_0_), channel_id=1, source_target_pairs={{0,8},{8,0},{1,9},{9,1},{2,10},{10,2},{3,11},{11,3},{4,12},{12,4},... | collective-permute-start | bytes 1425416 | tf_op jit(solution)/shard_map/ppermute | solution.py:203
  42.9 9.8 %collective-permute-start.8 = (bf16[64,3712]{1,0:T(8,128)(2,1)S(1)}, bf16[64,3712]{1,0:T(8,128)(2,1)S(1)}, u32[]{:S(2)}, u32[]{:S(2)}) collective-permute-start(bf16[64,3712]{1,0:T(8,128)(2,1)S(1)} %collective-permute-done.7.refs_0_), channel_id=1, source_target_pairs={{0,2},{10,8},{2,4},{12,10},{4,6},{14,12},{6,7},{15,14},{7,5},{13,1... | collective-permute-start | bytes 1425416 | tf_op jit(solution)/shard_map/ppermute | solution.py:200
  46.5 10.0 %collective-permute-start.27 = (bf16[64,3584]{1,0:T(8,128)(2,1)S(1)}, bf16[64,3584]{1,0:T(8,128)(2,1)S(1)}, u32[]{:S(2)}, u32[]{:S(2)}) collective-permute-start(bf16[64,3584]{1,0:T(8,128)(2,1)S(1)} %add_convert_fusion.5), channel_id=1, source_target_pairs={{0,2},{10,8},{2,4},{12,10},{4,6},{14,12},{6,7},{15,14},{7,5},{13,1... | collective-permute-start | bytes 1376264 | tf_op jit(solution)/shard_map/ppermute | solution.py:200
  50.0 6.5 %collective-permute-start.21 = (bf16[64,3584]{1,0:T(8,128)(2,1)S(1)}, bf16[64,3584]{1,0:T(8,128)(2,1)S(1)}, u32[]{:S(2)}, u32[]{:S(2)}) collective-permute-start(bf16[64,3584]{1,0:T(8,128)(2,1)S(1)} %get-tuple-element.53), channel_id=1, source_target_pairs={{0,8},{8,0},{1,9},{9,1},{2,10},{10,2},{3,11},{11,3},{4,12},{12,4},... | collective-permute-start | bytes 1376264 | tf_op jit(solution)/shard_map/ppermute | solution.py:203
  52.7 5.6 %collective-permute-start.19 = (bf16[64,3712]{1,0:T(8,128)(2,1)S(1)}, bf16[64,3712]{1,0:T(8,128)(2,1)S(1)}, u32[]{:S(2)}, u32[]{:S(2)}) collective-permute-start(bf16[64,3712]{1,0:T(8,128)(2,1)S(1)} %collective-permute-done.8.refs_0_), channel_id=1, source_target_pairs={{0,8},{8,0},{1,9},{9,1},{2,10},{10,2},{3,11},{11,3},{4,12},{12,4},... | collective-permute-start | bytes 1425416 | tf_op jit(solution)/shard_map/ppermute | solution.py:203
  53.2 10.0 %collective-permute-start.9 = (bf16[64,3712]{1,0:T(8,128)(2,1)S(1)}, bf16[64,3712]{1,0:T(8,128)(2,1)S(1)}, u32[]{:S(2)}, u32[]{:S(2)}) collective-permute-start(bf16[64,3712]{1,0:T(8,128)(2,1)S(1)} %collective-permute-done.8.refs_0_), channel_id=1, source_target_pairs={{0,2},{10,8},{2,4},{12,10},{4,6},{14,12},{6,7},{15,14},{7,5},{13,1... | collective-permute-start | bytes 1425416 | tf_op jit(solution)/shard_map/ppermute | solution.py:200
  56.7 10.0 %collective-permute-start.28 = (bf16[64,3584]{1,0:T(8,128)(2,1)S(1)}, bf16[64,3584]{1,0:T(8,128)(2,1)S(1)}, u32[]{:S(2)}, u32[]{:S(2)}) collective-permute-start(bf16[64,3584]{1,0:T(8,128)(2,1)S(1)} %add_convert_fusion.4), channel_id=1, source_target_pairs={{0,2},{10,8},{2,4},{12,10},{4,6},{14,12},{6,7},{15,14},{7,5},{13,1... | collective-permute-start | bytes 1376264 | tf_op jit(solution)/shard_map/ppermute | solution.py:200
  60.0 6.7 %collective-permute-start.20 = (bf16[64,3584]{1,0:T(8,128)(2,1)S(1)}, bf16[64,3584]{1,0:T(8,128)(2,1)S(1)}, u32[]{:S(2)}, u32[]{:S(2)}) collective-permute-start(bf16[64,3584]{1,0:T(8,128)(2,1)S(1)} %get-tuple-element.52), channel_id=1, source_target_pairs={{0,8},{8,0},{1,9},{9,1},{2,10},{10,2},{3,11},{11,3},{4,12},{12,4},... | collective-permute-start | bytes 1376264 | tf_op jit(solution)/shard_map/ppermute | solution.py:203
  60.1 10.2 %collective-permute-start.2 = (bf16[64,3584]{1,0:T(8,128)(2,1)S(1)}, bf16[64,3584]{1,0:T(8,128)(2,1)S(1)}, u32[]{:S(2)}, u32[]{:S(2)}) collective-permute-start(bf16[64,3584]{1,0:T(8,128)(2,1)S(1)} %get-tuple-element.34), channel_id=1, source_target_pairs={{0,8},{8,0},{1,9},{9,1},{2,10},{10,2},{3,11},{11,3},{4,12},{12,4},... | collective-permute-start | bytes 1376264 | tf_op jit(solution)/shard_map/ppermute | solution.py:203
  63.1 5.4 %collective-permute-start.13 = (bf16[64,3712]{1,0:T(8,128)(2,1)S(1)}, bf16[64,3712]{1,0:T(8,128)(2,1)S(1)}, u32[]{:S(2)}, u32[]{:S(2)}) collective-permute-start(bf16[64,3712]{1,0:T(8,128)(2,1)S(1)} %collective-permute-done.9.refs_0_), channel_id=1, source_target_pairs={{0,8},{8,0},{1,9},{9,1},{2,10},{10,2},{3,11},{11,3},{4,12},{12,4},... | collective-permute-start | bytes 1425416 | tf_op jit(solution)/shard_map/ppermute | solution.py:203
  63.2 8.7 %collective-permute-start.10 = (bf16[64,3712]{1,0:T(8,128)(2,1)S(1)}, bf16[64,3712]{1,0:T(8,128)(2,1)S(1)}, u32[]{:S(2)}, u32[]{:S(2)}) collective-permute-start(bf16[64,3712]{1,0:T(8,128)(2,1)S(1)} %collective-permute-done.9.refs_0_), channel_id=1, source_target_pairs={{0,2},{10,8},{2,4},{12,10},{4,6},{14,12},{6,7},{15,14},{7,5},{13,1... | collective-permute-start | bytes 1425416 | tf_op jit(solution)/shard_map/ppermute | solution.py:200
  66.9 9.9 %collective-permute-start.29 = (bf16[64,3584]{1,0:T(8,128)(2,1)S(1)}, bf16[64,3584]{1,0:T(8,128)(2,1)S(1)}, u32[]{:S(2)}, u32[]{:S(2)}) collective-permute-start(bf16[64,3584]{1,0:T(8,128)(2,1)S(1)} %add_convert_fusion.3), channel_id=1, source_target_pairs={{0,2},{10,8},{2,4},{12,10},{4,6},{14,12},{6,7},{15,14},{7,5},{13,1... | collective-permute-start | bytes 1376264 | tf_op jit(solution)/shard_map/ppermute | solution.py:200
  70.2 6.6 %collective-permute-start.18 = (bf16[64,3584]{1,0:T(8,128)(2,1)S(1)}, bf16[64,3584]{1,0:T(8,128)(2,1)S(1)}, u32[]{:S(2)}, u32[]{:S(2)}) collective-permute-start(bf16[64,3584]{1,0:T(8,128)(2,1)S(1)} %get-tuple-element.49), channel_id=1, source_target_pairs={{0,8},{8,0},{1,9},{9,1},{2,10},{10,2},{3,11},{11,3},{4,12},{12,4},... | collective-permute-start | bytes 1376264 | tf_op jit(solution)/shard_map/ppermute | solution.py:203
  71.9 6.7 %collective-permute-start.11 = (bf16[64,3712]{1,0:T(8,128)(2,1)S(1)}, bf16[64,3712]{1,0:T(8,128)(2,1)S(1)}, u32[]{:S(2)}, u32[]{:S(2)}) collective-permute-start(bf16[64,3712]{1,0:T(8,128)(2,1)S(1)} %collective-permute-done.10.refs_0_), channel_id=1, source_target_pairs={{0,8},{8,0},{1,9},{9,1},{2,10},{10,2},{3,11},{11,3},{4,12},{12,4},... | collective-permute-start | bytes 1425416 | tf_op jit(solution)/shard_map/ppermute | solution.py:203
  77.0 8.5 %collective-permute-start.30 = (bf16[64,3584]{1,0:T(8,128)(2,1)S(1)}, bf16[64,3584]{1,0:T(8,128)(2,1)S(1)}, u32[]{:S(2)}, u32[]{:S(2)}) collective-permute-start(bf16[64,3584]{1,0:T(8,128)(2,1)S(1)} %add_convert_fusion.2), channel_id=1, source_target_pairs={{0,2},{10,8},{2,4},{12,10},{4,6},{14,12},{6,7},{15,14},{7,5},{13,1... | collective-permute-start | bytes 1376264 | tf_op jit(solution)/shard_map/ppermute | solution.py:200
  80.3 5.3 %collective-permute-start.12 = (bf16[64,3584]{1,0:T(8,128)(2,1)S(1)}, bf16[64,3584]{1,0:T(8,128)(2,1)S(1)}, u32[]{:S(2)}, u32[]{:S(2)}) collective-permute-start(bf16[64,3584]{1,0:T(8,128)(2,1)S(1)} %get-tuple-element.37), channel_id=1, source_target_pairs={{0,8},{8,0},{1,9},{9,1},{2,10},{10,2},{3,11},{11,3},{4,12},{12,4},... | collective-permute-start | bytes 1376264 | tf_op jit(solution)/shard_map/ppermute | solution.py:203
  85.7 5.5 %collective-permute-start.32 = (bf16[32,3584]{1,0:T(8,128)(2,1)S(1)}, bf16[32,3584]{1,0:T(8,128)(2,1)S(1)}, u32[]{:S(2)}, u32[]{:S(2)}) collective-permute-start(bf16[32,3584]{1,0:T(8,128)(2,1)S(1)} %get-tuple-element.61), channel_id=1, source_target_pairs={{0,10},{10,0},{2,12},{12,2},{4,14},{14,4},{6,15},{15,6},{7,13},{13... | collective-permute-start | bytes 688136 | tf_op jit(solution)/shard_map/ppermute | solution.py:200
  85.8 7.0 %collective-permute-start.31 = (bf16[32,3584]{1,0:T(8,128)(2,1)S(1)}, bf16[32,3584]{1,0:T(8,128)(2,1)S(1)}, u32[]{:S(2)}, u32[]{:S(2)}) collective-permute-start(bf16[32,3584]{1,0:T(8,128)(2,1)S(1)} %get-tuple-element.60), channel_id=1, source_target_pairs={{0,2},{10,8},{2,4},{12,10},{4,6},{14,12},{6,7},{15,14},{7,5},{13,1... | collective-permute-start | bytes 688136 | tf_op jit(solution)/shard_map/ppermute | solution.py:200

commit v7 on v6

--- a/solution.py
+++ b/solution.py
@@ -226,7 +226,9 @@
     block = lax.optimization_barrier((block, own))[0]
     mine_sum = chip_sum(own, across(other))
     after = (own,)
-    attn_latent, done = None, None
+    attn_latent, done = attend_piece(
+        cache_lengths, queries, latent_cache, LAT, 0, queries.shape[0] // PIECES, None, (block,)
+    )
     for k in range(1, local_count):
         if k > 1:
             block = onward(block)
@@ -238,13 +240,13 @@
         after = ()
         if done is not None:
             after, done = (done,), None
-        if k <= PIECES:
+        if k < PIECES:
             attn_latent, done = attend_piece(
                 cache_lengths,
                 queries,
                 latent_cache,
                 LAT,
-                k - 1,
+                k,
                 queries.shape[0] // PIECES,
                 attn_latent,
                 (own,),

time: 94.1 us -> 94.1 us (level)
  transfers between devices with their start and end apart: 33 -> 33, of which waited for: 12 -> 13; matrix products, arithmetic and copies ran while one was open for 2% -> 2% of each run, Pallas kernels for 30% -> 30%
where the time goes in v7:
time: 94.1 us; the launch traced here: 93.7 us
  waiting for transfers between devices  31.6 us (34%)
  Pallas kernels  28.4 us (30%)
  starting transfers between devices  28.2 us (30%)
  other arithmetic  4.34 us (5%)
  between operations  0.99 us (1%)
    ppermute x16, waiting for transfers between devices, onward(): return lax.ppermute(a, ('node', 'local'), pairs)  31.3 us
    ppermute x16, starting transfers between devices, onward(): return lax.ppermute(a, ('node', 'local'), pairs)  25.3 us
    pallas_call x8, Pallas kernels, run_experts(): pl.pallas_call(functools.partial(expert_kernel, own_parts=len(own), parts...  13.9 us
    pallas_call x4, Pallas kernels, attend_piece(): pl.pallas_call(functools.partial(attend_kernel, base=piece * count, pair=...  10.3 us
    pallas_call x1, Pallas kernels, load_weights(): pl.pallas_call(functools.partial(load_kernel, count=count), in_specs=[any...  4.23 us
    ppermute x17, starting transfers between devices, across(): return lax.ppermute(a, 'node', [(0, 1), (1, 0)])  2.84 us
  transfers between devices with their start and end apart: 33, of which 13 were waited for; matrix products, arithmetic and copies ran while one was open for 2% of the time, Pallas kernels for 30%

profile of v7, /device:TPU:0, one launch (start us, length us, event | category | flops | bytes accessed | tf_op | source)
XLA Modules:
  0.0 93.7 jit_solution(8943467151719298732)
XLA Ops:
  0.6 0.8 fusion.1
  1.5 1.1 %broadcast_select_fusion = (bf16[32,3584]{1,0:T(8,128)(2,1)S(1)}, bf16[32,3584]{1,0:T(8,128)(2,1)S(1)}) fusion(pred[]{:T(512)S(6)} %eq.16, bf16[64,3584]{1,0:T(8,128)(2,1)} %param.9), kind=kLoop, calls=%fused_computation.13 | loop fusion | flops 229376 | bytes 917505 | tf_op jit(solution)/shard_map/jit(_where)/select_n | solution.py:215
  2.6 0.5 collective-permute-start.1
  3.1 0.1 collective-permute-start
  3.3 3.0 %collective-permute-start.3 = (bf16[32,3712]{1,0:T(8,128)(2,1)S(1)}, bf16[32,3712]{1,0:T(8,128)(2,1)S(1)}, u32[]{:S(2)}, u32[]{:S(2)}) collective-permute-start(bf16[32,3712]{1,0:T(8,128)(2,1)S(1)} %pad_maximum_fusion.refs_3_.refs_0_), channel_id=1, source_target_pairs={{0,2},{10,8},{2,4},{12,10},{4,6},{14,12},{6,7},{15,14},{7,5},{13,1... | collective-permute-start | bytes 712712 | tf_op jit(solution)/shard_map/ppermute | solution.py:200
  6.3 1.6 %collective-permute-start.4 = (bf16[32,3712]{1,0:T(8,128)(2,1)S(1)}, bf16[32,3712]{1,0:T(8,128)(2,1)S(1)}, u32[]{:S(2)}, u32[]{:S(2)}) collective-permute-start(bf16[32,3712]{1,0:T(8,128)(2,1)S(1)} %collective-permute-done.1.refs_3_), channel_id=1, source_target_pairs={{0,2},{10,8},{2,4},{12,10},{4,6},{14,12},{6,7},{15,14},{7,5},{13,1... | collective-permute-start | bytes 712712 | tf_op jit(solution)/shard_map/ppermute | solution.py:200
  7.9 4.2 %load_weights.1 = (bf16[3584,512]{1,0:T(8,128)(2,1)S(1)}, bf16[3584,512]{1,0:T(8,128)(2,1)S(1)}, bf16[512,3584]{1,0:T(8,128)(2,1)S(1)}) custom-call(bf16[1,3584,512]{2,1,0:T(8,128)(2,1)} %refs_0_.1, bf16[1,3584,512]{2,1,0:T(8,128)(2,1)} %refs_1_.1, bf16[1,512,3584]{2,1,0:T(8,128)(2,1)} %refs_2_.1, bf16[32,3712]{1,0:T(8,128)(2,1)S(1)} %pad_maximum_fusion.refs_3_.refs_0_), custom_call_target="tpu_custom_call" | custom-call | bytes 11010048 | tf_op jit(solution)/shard_map/load_weights/pallas_call | solution.py:145
  12.1 1.7 %expert_half.8 = (bf16[64,3584]{1,0:T(8,128)(2,1)S(1)}, bf16[64,3584]{1,0:T(8,128)(2,1)S(1)}) custom-call(s32[1]{0:T(128)} %bitcast.expert_ref, bf16[32,3712]{1,0:T(8,128)(2,1)S(1)} %pad_maximum_fusion.refs_3_.refs_0_, bf16[32,3712]{1,0:T(8,128)(2,1)S(1)} %pad_maximum_fusion.1.refs_1_, bf16[32,3712]{1,0:T(8,128)(2,1)S(1)} %collective-permute-done.refs_2_, ...), custom_call_target="tpu_custom_call" | custom-call | flops 1409286144 | bytes 11010048 | tf_op jit(solution)/shard_map/expert_half/pallas_call | solution.py:109
  14.0 1.6 %collective-permute-start.5 = (bf16[64,3712]{1,0:T(8,128)(2,1)S(1)}, bf16[64,3712]{1,0:T(8,128)(2,1)S(1)}, u32[]{:S(2)}, u32[]{:S(2)}) collective-permute-start(bf16[64,3712]{1,0:T(8,128)(2,1)S(1)} %join.1.rest_0_.refs_0_), channel_id=1, source_target_pairs={{0,2},{10,8},{2,4},{12,10},{4,6},{14,12},{6,7},{15,14},{7,5},{13,1... | collective-permute-start | bytes 1425416 | tf_op jit(solution)/shard_map/ppermute | solution.py:200
  15.7 0.2 collective-permute-done.16.refs_1_
  15.9 1.7 %expert_half.11 = (bf16[64,3584]{1,0:T(8,128)(2,1)S(1)}, bf16[64,3584]{1,0:T(8,128)(2,1)S(1)}) custom-call(s32[1]{0:T(128)} %bitcast.expert_ref, bf16[64,3712]{1,0:T(8,128)(2,1)S(1)} %join.1.rest_0_.refs_0_, bf16[64,3712]{1,0:T(8,128)(2,1)S(1)} %collective-permute-done.16.refs_1_, bf16[3584,512]{1,0:T(8,128)(2,1)S(1)} %get-tuple-element.30.refs_4_.refs_2_, ...), custom_call_target="tpu_custom_call" | custom-call | flops 1409286144 | bytes 11010048 | tf_op jit(solution)/shard_map/expert_half/pallas_call | solution.py:109
  17.6 0.2 collective-permute-start.24
  17.9 2.6 %attend.4 = (bf16[64,64,512]{2,1,0:T(8,128)(2,1)}, f32[8,128]{1,0:T(8,128)S(1)}) custom-call(s32[64]{0:T(128)S(1)} %copy-done, bf16[64,64,576]{2,1,0:T(8,128)(2,1)S(1)} %bitcast.2, bf16[64,64,576]{2,1,0:T(8,128)(2,1)S(1)} %bitcast.4, bf16[64,3712]{1,0:T(8,128)(2,1)S(1)} %join.1.rest_0_.refs_0_), custom_call_target="tpu_custom_call" | custom-call | flops 142606336 | bytes 3407872 | tf_op jit(solution)/shard_map/attend/pallas_call | solution.py:59
  20.4 2.3 %collective-permute-done.5.refs_0_ = bf16[64,3712]{1,0:T(8,128)(2,1)S(1)} collective-permute-done((bf16[64,3712]{1,0:T(8,128)(2,1)S(1)}, bf16[64,3712]{1,0:T(8,128)(2,1)S(1)}, u32[]{:S(2)}, u32[]{:S(2)}) %collective-permute-start.5) | collective-permute-done | bytes 475168 | tf_op jit(solution)/shard_map/ppermute | solution.py:200
  22.8 1.6 %collective-permute-start.6 = (bf16[64,3712]{1,0:T(8,128)(2,1)S(1)}, bf16[64,3712]{1,0:T(8,128)(2,1)S(1)}, u32[]{:S(2)}, u32[]{:S(2)}) collective-permute-start(bf16[64,3712]{1,0:T(8,128)(2,1)S(1)} %collective-permute-done.5.refs_0_), channel_id=1, source_target_pairs={{0,2},{10,8},{2,4},{12,10},{4,6},{14,12},{6,7},{15,14},{7,5},{13,1... | collective-permute-start | bytes 1425416 | tf_op jit(solution)/shard_map/ppermute | solution.py:200
  24.3 0.1 add_convert_fusion.7
  24.4 1.6 %collective-permute-start.25 = (bf16[64,3584]{1,0:T(8,128)(2,1)S(1)}, bf16[64,3584]{1,0:T(8,128)(2,1)S(1)}, u32[]{:S(2)}, u32[]{:S(2)}) collective-permute-start(bf16[64,3584]{1,0:T(8,128)(2,1)S(1)} %add_convert_fusion.7), channel_id=1, source_target_pairs={{0,2},{10,8},{2,4},{12,10},{4,6},{14,12},{6,7},{15,14},{7,5},{13,1... | collective-permute-start | bytes 1376264 | tf_op jit(solution)/shard_map/ppermute | solution.py:200
  26.0 1.7 %expert_half.12 = (bf16[64,3584]{1,0:T(8,128)(2,1)S(1)}, bf16[64,3584]{1,0:T(8,128)(2,1)S(1)}) custom-call(s32[1]{0:T(128)} %bitcast.expert_ref, bf16[64,3712]{1,0:T(8,128)(2,1)S(1)} %collective-permute-done.5.refs_0_, bf16[64,3712]{1,0:T(8,128)(2,1)S(1)} %collective-permute-done.17.refs_1_, bf16[3584,512]{1,0:T(8,128)(2,1)S(1)} %get-tuple-element.30.refs_4_.refs_2_, ...), custom_call_target="tpu_custom_call" | custom-call | flops 1409286144 | bytes 11010048 | tf_op jit(solution)/shard_map/expert_half/pallas_call | solution.py:109
  27.8 2.6 %attend.5 = (bf16[64,64,512]{2,1,0:T(8,128)(2,1)}, f32[8,128]{1,0:T(8,128)S(1)}) custom-call(s32[64]{0:T(128)S(1)} %copy-done, bf16[64,64,576]{2,1,0:T(8,128)(2,1)S(1)} %bitcast.2, bf16[64,64,576]{2,1,0:T(8,128)(2,1)S(1)} %bitcast.4, bf16[64,64,512]{2,1,0:T(8,128)(2,1)} %get-tuple-element.40.rest_0_, ...), custom_call_target="tpu_custom_call", output_to_operand_aliasing={{0}: (3, {})} | custom-call | flops 142606336 | bytes 3407872 | tf_op jit(solution)/shard_map/attend/pallas_call | solution.py:59
  30.4 1.0 %collective-permute-done.6.refs_0_ = bf16[64,3712]{1,0:T(8,128)(2,1)S(1)} collective-permute-done((bf16[64,3712]{1,0:T(8,128)(2,1)S(1)}, bf16[64,3712]{1,0:T(8,128)(2,1)S(1)}, u32[]{:S(2)}, u32[]{:S(2)}) %collective-permute-start.6) | collective-permute-done | bytes 475168 | tf_op jit(solution)/shard_map/ppermute | solution.py:200
  31.4 1.6 %collective-permute-start.7 = (bf16[64,3712]{1,0:T(8,128)(2,1)S(1)}, bf16[64,3712]{1,0:T(8,128)(2,1)S(1)}, u32[]{:S(2)}, u32[]{:S(2)}) collective-permute-start(bf16[64,3712]{1,0:T(8,128)(2,1)S(1)} %collective-permute-done.6.refs_0_), channel_id=1, source_target_pairs={{0,2},{10,8},{2,4},{12,10},{4,6},{14,12},{6,7},{15,14},{7,5},{13,1... | collective-permute-start | bytes 1425416 | tf_op jit(solution)/shard_map/ppermute | solution.py:200
  33.0 3.3 %collective-permute-done.25 = bf16[64,3584]{1,0:T(8,128)(2,1)S(1)} collective-permute-done((bf16[64,3584]{1,0:T(8,128)(2,1)S(1)}, bf16[64,3584]{1,0:T(8,128)(2,1)S(1)}, u32[]{:S(2)}, u32[]{:S(2)}) %collective-permute-start.25) | collective-permute-done | bytes 458784 | tf_op jit(solution)/shard_map/ppermute | solution.py:200
  36.3 0.2 add_convert_fusion.6
  36.5 1.6 %collective-permute-start.26 = (bf16[64,3584]{1,0:T(8,128)(2,1)S(1)}, bf16[64,3584]{1,0:T(8,128)(2,1)S(1)}, u32[]{:S(2)}, u32[]{:S(2)}) collective-permute-start(bf16[64,3584]{1,0:T(8,128)(2,1)S(1)} %add_convert_fusion.6), channel_id=1, source_target_pairs={{0,2},{10,8},{2,4},{12,10},{4,6},{14,12},{6,7},{15,14},{7,5},{13,1... | collective-permute-start | bytes 1376264 | tf_op jit(solution)/shard_map/ppermute | solution.py:200
  38.2 1.7 %expert_half.13 = (bf16[64,3584]{1,0:T(8,128)(2,1)S(1)}, bf16[64,3584]{1,0:T(8,128)(2,1)S(1)}) custom-call(s32[1]{0:T(128)} %bitcast.expert_ref, bf16[64,3712]{1,0:T(8,128)(2,1)S(1)} %collective-permute-done.6.refs_0_, bf16[64,3712]{1,0:T(8,128)(2,1)S(1)} %collective-permute-done.18.refs_1_, bf16[3584,512]{1,0:T(8,128)(2,1)S(1)} %get-tuple-element.30.refs_4_.refs_2_, ...), custom_call_target="tpu_custom_call" | custom-call | flops 1409286144 | bytes 11010048 | tf_op jit(solution)/shard_map/expert_half/pallas_call | solution.py:109
  39.9 0.1 collective-permute-start.22
  40.0 2.6 %attend.6 = (bf16[64,64,512]{2,1,0:T(8,128)(2,1)}, f32[8,128]{1,0:T(8,128)S(1)}) custom-call(s32[64]{0:T(128)S(1)} %copy-done, bf16[64,64,576]{2,1,0:T(8,128)(2,1)S(1)} %bitcast.2, bf16[64,64,576]{2,1,0:T(8,128)(2,1)S(1)} %bitcast.4, bf16[64,64,512]{2,1,0:T(8,128)(2,1)} %get-tuple-element.42.rest_0_, ...), custom_call_target="tpu_custom_call", output_to_operand_aliasing={{0}: (3, {})} | custom-call | flops 142606336 | bytes 3407872 | tf_op jit(solution)/shard_map/attend/pallas_call | solution.py:59
  42.6 0.5 collective-permute-start.20
  43.0 1.5 %collective-permute-start.8 = (bf16[64,3712]{1,0:T(8,128)(2,1)S(1)}, bf16[64,3712]{1,0:T(8,128)(2,1)S(1)}, u32[]{:S(2)}, u32[]{:S(2)}) collective-permute-start(bf16[64,3712]{1,0:T(8,128)(2,1)S(1)} %collective-permute-done.7.refs_0_), channel_id=1, source_target_pairs={{0,2},{10,8},{2,4},{12,10},{4,6},{14,12},{6,7},{15,14},{7,5},{13,1... | collective-permute-start | bytes 1425416 | tf_op jit(solution)/shard_map/ppermute | solution.py:200
  44.6 1.8 %collective-permute-done.26 = bf16[64,3584]{1,0:T(8,128)(2,1)S(1)} collective-permute-done((bf16[64,3584]{1,0:T(8,128)(2,1)S(1)}, bf16[64,3584]{1,0:T(8,128)(2,1)S(1)}, u32[]{:S(2)}, u32[]{:S(2)}) %collective-permute-start.26) | collective-permute-done | bytes 458784 | tf_op jit(solution)/shard_map/ppermute | solution.py:200
  46.3 0.2 add_convert_fusion.5
  46.5 1.8 %collective-permute-start.27 = (bf16[64,3584]{1,0:T(8,128)(2,1)S(1)}, bf16[64,3584]{1,0:T(8,128)(2,1)S(1)}, u32[]{:S(2)}, u32[]{:S(2)}) collective-permute-start(bf16[64,3584]{1,0:T(8,128)(2,1)S(1)} %add_convert_fusion.5), channel_id=1, source_target_pairs={{0,2},{10,8},{2,4},{12,10},{4,6},{14,12},{6,7},{15,14},{7,5},{13,1... | collective-permute-start | bytes 1376264 | tf_op jit(solution)/shard_map/ppermute | solution.py:200
  48.3 1.7 %expert_half.15 = (bf16[64,3584]{1,0:T(8,128)(2,1)S(1)}, bf16[64,3584]{1,0:T(8,128)(2,1)S(1)}) custom-call(s32[1]{0:T(128)} %bitcast.expert_ref, bf16[64,3712]{1,0:T(8,128)(2,1)S(1)} %collective-permute-done.7.refs_0_, bf16[64,3712]{1,0:T(8,128)(2,1)S(1)} %collective-permute-done.20.refs_1_, bf16[3584,512]{1,0:T(8,128)(2,1)S(1)} %get-tuple-element.30.refs_4_.refs_2_, ...), custom_call_target="tpu_custom_call" | custom-call | flops 1409286144 | bytes 11010048 | tf_op jit(solution)/shard_map/expert_half/pallas_call | solution.py:109
  50.1 0.1 collective-permute-start.21
  50.2 2.6 %attend.7 = (bf16[64,64,512]{2,1,0:T(8,128)(2,1)}, f32[8,128]{1,0:T(8,128)S(1)}) custom-call(s32[64]{0:T(128)S(1)} %copy-done, bf16[64,64,576]{2,1,0:T(8,128)(2,1)S(1)} %bitcast.2, bf16[64,64,576]{2,1,0:T(8,128)(2,1)S(1)} %bitcast.4, bf16[64,64,512]{2,1,0:T(8,128)(2,1)} %get-tuple-element.45.rest_0_, ...), custom_call_target="tpu_custom_call", output_to_operand_aliasing={{0}: (3, {})} | custom-call | flops 142606336 | bytes 3407872 | tf_op jit(solution)/shard_map/attend/pallas_call | solution.py:59
  52.7 0.5 collective-permute-start.15
  53.2 1.5 %collective-permute-start.9 = (bf16[64,3712]{1,0:T(8,128)(2,1)S(1)}, bf16[64,3712]{1,0:T(8,128)(2,1)S(1)}, u32[]{:S(2)}, u32[]{:S(2)}) collective-permute-start(bf16[64,3712]{1,0:T(8,128)(2,1)S(1)} %collective-permute-done.8.refs_0_), channel_id=1, source_target_pairs={{0,2},{10,8},{2,4},{12,10},{4,6},{14,12},{6,7},{15,14},{7,5},{13,1... | collective-permute-start | bytes 1425416 | tf_op jit(solution)/shard_map/ppermute | solution.py:200
  54.8 1.9 %collective-permute-done.27 = bf16[64,3584]{1,0:T(8,128)(2,1)S(1)} collective-permute-done((bf16[64,3584]{1,0:T(8,128)(2,1)S(1)}, bf16[64,3584]{1,0:T(8,128)(2,1)S(1)}, u32[]{:S(2)}, u32[]{:S(2)}) %collective-permute-start.27) | collective-permute-done | bytes 458784 | tf_op jit(solution)/shard_map/ppermute | solution.py:200
  56.6 0.2 add_convert_fusion.4
  56.8 1.6 %collective-permute-start.28 = (bf16[64,3584]{1,0:T(8,128)(2,1)S(1)}, bf16[64,3584]{1,0:T(8,128)(2,1)S(1)}, u32[]{:S(2)}, u32[]{:S(2)}) collective-permute-start(bf16[64,3584]{1,0:T(8,128)(2,1)S(1)} %add_convert_fusion.4), channel_id=1, source_target_pairs={{0,2},{10,8},{2,4},{12,10},{4,6},{14,12},{6,7},{15,14},{7,5},{13,1... | collective-permute-start | bytes 1376264 | tf_op jit(solution)/shard_map/ppermute | solution.py:200
  58.4 1.7 %expert_half.14 = (bf16[64,3584]{1,0:T(8,128)(2,1)S(1)}, bf16[64,3584]{1,0:T(8,128)(2,1)S(1)}) custom-call(s32[1]{0:T(128)} %bitcast.expert_ref, bf16[64,3712]{1,0:T(8,128)(2,1)S(1)} %collective-permute-done.8.refs_0_, bf16[64,3712]{1,0:T(8,128)(2,1)S(1)} %collective-permute-done.15.refs_1_, bf16[3584,512]{1,0:T(8,128)(2,1)S(1)} %get-tuple-element.30.refs_4_.refs_2_, ...), custom_call_target="tpu_custom_call" | custom-call | flops 1409286144 | bytes 11010048 | tf_op jit(solution)/shard_map/expert_half/pallas_call | solution.py:109
  60.1 0.1 collective-permute-start.19
  60.2 0.5 collective-permute-start.2
  60.7 1.2 %collective-permute-done.9.refs_0_ = bf16[64,3712]{1,0:T(8,128)(2,1)S(1)} collective-permute-done((bf16[64,3712]{1,0:T(8,128)(2,1)S(1)}, bf16[64,3712]{1,0:T(8,128)(2,1)S(1)}, u32[]{:S(2)}, u32[]{:S(2)}) %collective-permute-start.9) | collective-permute-done | bytes 475168 | tf_op jit(solution)/shard_map/ppermute | solution.py:200
  61.9 1.5 %collective-permute-start.10 = (bf16[64,3712]{1,0:T(8,128)(2,1)S(1)}, bf16[64,3712]{1,0:T(8,128)(2,1)S(1)}, u32[]{:S(2)}, u32[]{:S(2)}) collective-permute-start(bf16[64,3712]{1,0:T(8,128)(2,1)S(1)} %collective-permute-done.9.refs_0_), channel_id=1, source_target_pairs={{0,2},{10,8},{2,4},{12,10},{4,6},{14,12},{6,7},{15,14},{7,5},{13,1... | collective-permute-start | bytes 1425416 | tf_op jit(solution)/shard_map/ppermute | solution.py:200
  63.4 3.4 %collective-permute-done.28 = bf16[64,3584]{1,0:T(8,128)(2,1)S(1)} collective-permute-done((bf16[64,3584]{1,0:T(8,128)(2,1)S(1)}, bf16[64,3584]{1,0:T(8,128)(2,1)S(1)}, u32[]{:S(2)}, u32[]{:S(2)}) %collective-permute-start.28) | collective-permute-done | bytes 458784 | tf_op jit(solution)/shard_map/ppermute | solution.py:200
  66.8 0.2 add_convert_fusion.3
  67.0 1.6 %collective-permute-start.29 = (bf16[64,3584]{1,0:T(8,128)(2,1)S(1)}, bf16[64,3584]{1,0:T(8,128)(2,1)S(1)}, u32[]{:S(2)}, u32[]{:S(2)}) collective-permute-start(bf16[64,3584]{1,0:T(8,128)(2,1)S(1)} %add_convert_fusion.3), channel_id=1, source_target_pairs={{0,2},{10,8},{2,4},{12,10},{4,6},{14,12},{6,7},{15,14},{7,5},{13,1... | collective-permute-start | bytes 1376264 | tf_op jit(solution)/shard_map/ppermute | solution.py:200
  68.6 1.7 %expert_half.10 = (bf16[64,3584]{1,0:T(8,128)(2,1)S(1)}, bf16[64,3584]{1,0:T(8,128)(2,1)S(1)}) custom-call(s32[1]{0:T(128)} %bitcast.expert_ref, bf16[64,3712]{1,0:T(8,128)(2,1)S(1)} %collective-permute-done.9.refs_0_, bf16[64,3712]{1,0:T(8,128)(2,1)S(1)} %collective-permute-done.13.refs_1_, bf16[3584,512]{1,0:T(8,128)(2,1)S(1)} %get-tuple-element.30.refs_4_.refs_2_, ...), custom_call_target="tpu_custom_call" | custom-call | flops 1409286144 | bytes 11010048 | tf_op jit(solution)/shard_map/expert_half/pallas_call | solution.py:109
  70.3 0.1 collective-permute-start.14
  70.4 0.1 convert_add_fusion
  70.6 1.3 %collective-permute-done.10.refs_0_ = bf16[64,3712]{1,0:T(8,128)(2,1)S(1)} collective-permute-done((bf16[64,3712]{1,0:T(8,128)(2,1)S(1)}, bf16[64,3712]{1,0:T(8,128)(2,1)S(1)}, u32[]{:S(2)}, u32[]{:S(2)}) %collective-permute-start.10) | collective-permute-done | bytes 475168 | tf_op jit(solution)/shard_map/ppermute | solution.py:200
  71.9 4.9 %collective-permute-done.29 = bf16[64,3584]{1,0:T(8,128)(2,1)S(1)} collective-permute-done((bf16[64,3584]{1,0:T(8,128)(2,1)S(1)}, bf16[64,3584]{1,0:T(8,128)(2,1)S(1)}, u32[]{:S(2)}, u32[]{:S(2)}) %collective-permute-start.29) | collective-permute-done | bytes 458784 | tf_op jit(solution)/shard_map/ppermute | solution.py:200
  76.8 0.2 add_convert_fusion.2
  77.0 1.6 %collective-permute-start.30 = (bf16[64,3584]{1,0:T(8,128)(2,1)S(1)}, bf16[64,3584]{1,0:T(8,128)(2,1)S(1)}, u32[]{:S(2)}, u32[]{:S(2)}) collective-permute-start(bf16[64,3584]{1,0:T(8,128)(2,1)S(1)} %add_convert_fusion.2), channel_id=1, source_target_pairs={{0,2},{10,8},{2,4},{12,10},{4,6},{14,12},{6,7},{15,14},{7,5},{13,1... | collective-permute-start | bytes 1376264 | tf_op jit(solution)/shard_map/ppermute | solution.py:200
  78.6 1.7 %expert_half.9 = (bf16[64,3584]{1,0:T(8,128)(2,1)S(1)}, bf16[64,3584]{1,0:T(8,128)(2,1)S(1)}) custom-call(s32[1]{0:T(128)} %bitcast.expert_ref, bf16[64,3712]{1,0:T(8,128)(2,1)S(1)} %collective-permute-done.10.refs_0_, bf16[64,3712]{1,0:T(8,128)(2,1)S(1)} %collective-permute-done.11.refs_1_, bf16[3584,512]{1,0:T(8,128)(2,1)S(1)} %get-tuple-element.30.refs_4_.refs_2_, ...), custom_call_target="tpu_custom_call" | custom-call | flops 1409286144 | bytes 11010048 | tf_op jit(solution)/shard_map/expert_half/pallas_call | solution.py:109
  80.5 5.1 %collective-permute-done.30 = bf16[64,3584]{1,0:T(8,128)(2,1)S(1)} collective-permute-done((bf16[64,3584]{1,0:T(8,128)(2,1)S(1)}, bf16[64,3584]{1,0:T(8,128)(2,1)S(1)}, u32[]{:S(2)}, u32[]{:S(2)}) %collective-permute-start.30) | collective-permute-done | bytes 458784 | tf_op jit(solution)/shard_map/ppermute | solution.py:200
  85.5 0.2 add_convert_fusion.1
  85.7 0.1 collective-permute-start.32
  85.8 1.6 %collective-permute-start.31 = (bf16[32,3584]{1,0:T(8,128)(2,1)S(1)}, bf16[32,3584]{1,0:T(8,128)(2,1)S(1)}, u32[]{:S(2)}, u32[]{:S(2)}) collective-permute-start(bf16[32,3584]{1,0:T(8,128)(2,1)S(1)} %get-tuple-element.60), channel_id=1, source_target_pairs={{0,2},{10,8},{2,4},{12,10},{4,6},{14,12},{6,7},{15,14},{7,5},{13,1... | collective-permute-start | bytes 688136 | tf_op jit(solution)/shard_map/ppermute | solution.py:200
  87.4 0.2 maximum_select_fusion
  87.6 3.7 %collective-permute-done.32 = bf16[32,3584]{1,0:T(8,128)(2,1)S(1)} collective-permute-done((bf16[32,3584]{1,0:T(8,128)(2,1)S(1)}, bf16[32,3584]{1,0:T(8,128)(2,1)S(1)}, u32[]{:S(2)}, u32[]{:S(2)}) %collective-permute-start.32) | collective-permute-done | bytes 229408 | tf_op jit(solution)/shard_map/ppermute | solution.py:200
  91.3 1.5 %collective-permute-done.31 = bf16[32,3584]{1,0:T(8,128)(2,1)S(1)} collective-permute-done((bf16[32,3584]{1,0:T(8,128)(2,1)S(1)}, bf16[32,3584]{1,0:T(8,128)(2,1)S(1)}, u32[]{:S(2)}, u32[]{:S(2)}) %collective-permute-start.31) | collective-permute-done | bytes 229408 | tf_op jit(solution)/shard_map/ppermute | solution.py:200
  92.8 0.9 add_convert_fusion
  (45 shorter events, 0.5 us)
Async XLA Ops:
  2.6 3.7 %collective-permute-start.1 = (bf16[32,3712]{1,0:T(8,128)(2,1)S(1)}, bf16[32,3712]{1,0:T(8,128)(2,1)S(1)}, u32[]{:S(2)}, u32[]{:S(2)}) collective-permute-start(bf16[32,3712]{1,0:T(8,128)(2,1)S(1)} %pad_maximum_fusion.1.refs_1_), channel_id=1, source_target_pairs={{0,8},{8,0},{1,9},{9,1},{2,10},{10,2},{3,11},{11,3},{4,12},{12,4},... | collective-permute-start | bytes 712712 | tf_op jit(solution)/shard_map/ppermute | solution.py:203
  3.1 9.0 %collective-permute-start = (bf16[32,3712]{1,0:T(8,128)(2,1)S(1)}, bf16[32,3712]{1,0:T(8,128)(2,1)S(1)}, u32[]{:S(2)}, u32[]{:S(2)}) collective-permute-start(bf16[32,3712]{1,0:T(8,128)(2,1)S(1)} %pad_maximum_fusion.refs_3_.refs_0_), channel_id=1, source_target_pairs={{0,8},{8,0},{1,9},{9,1},{2,10},{10,2},{3,11},{11,3},{4,12},{12,4},... | collective-permute-start | bytes 712712 | tf_op jit(solution)/shard_map/ppermute | solution.py:203
  3.3 10.6 %collective-permute-start.3 = (bf16[32,3712]{1,0:T(8,128)(2,1)S(1)}, bf16[32,3712]{1,0:T(8,128)(2,1)S(1)}, u32[]{:S(2)}, u32[]{:S(2)}) collective-permute-start(bf16[32,3712]{1,0:T(8,128)(2,1)S(1)} %pad_maximum_fusion.refs_3_.refs_0_), channel_id=1, source_target_pairs={{0,2},{10,8},{2,4},{12,10},{4,6},{14,12},{6,7},{15,14},{7,5},{13,1... | collective-permute-start | bytes 712712 | tf_op jit(solution)/shard_map/ppermute | solution.py:200
  6.3 7.6 %collective-permute-start.4 = (bf16[32,3712]{1,0:T(8,128)(2,1)S(1)}, bf16[32,3712]{1,0:T(8,128)(2,1)S(1)}, u32[]{:S(2)}, u32[]{:S(2)}) collective-permute-start(bf16[32,3712]{1,0:T(8,128)(2,1)S(1)} %collective-permute-done.1.refs_3_), channel_id=1, source_target_pairs={{0,2},{10,8},{2,4},{12,10},{4,6},{14,12},{6,7},{15,14},{7,5},{13,1... | collective-permute-start | bytes 712712 | tf_op jit(solution)/shard_map/ppermute | solution.py:200
  12.1 5.7 %slice-start.2 = ((s8[5242880]{0:T(1024)(128)(4,1)}), s8[4194304]{0:T(1024)(128)(4,1)S(1)}, s32[]{:S(2)}) async-start(s8[5242880]{0:T(1024)(128)(4,1)} %bitcast.3), calls=%async_computation.2 | async-start | bytes 8388608
  13.9 4.0 %slice-start.3 = ((s8[5242880]{0:T(1024)(128)(4,1)}), s8[1048576]{0:T(1024)(128)(4,1)S(1)}, s32[]{:S(2)}) async-start(s8[5242880]{0:T(1024)(128)(4,1)} %bitcast.3), calls=%async_computation.3 | async-start | bytes 2097152
  13.9 3.9 %slice-start = ((s8[5242880]{0:T(1024)(128)(4,1)}), s8[4194304]{0:T(1024)(128)(4,1)S(1)}, s32[]{:S(2)}) async-start(s8[5242880]{0:T(1024)(128)(4,1)} %bitcast.1), calls=%async_computation | async-start | bytes 8388608
  13.9 3.9 %slice-start.1 = ((s8[5242880]{0:T(1024)(128)(4,1)}), s8[1048576]{0:T(1024)(128)(4,1)S(1)}, s32[]{:S(2)}) async-start(s8[5242880]{0:T(1024)(128)(4,1)} %bitcast.1), calls=%async_computation.1 | async-start | bytes 2097152
  14.0 3.9 %copy-start = (s32[64]{0:T(128)S(1)}, s32[64]{0:T(128)}, u32[]{:S(2)}) copy-start(s32[64]{0:T(128)} %len_ref.7) | copy-start | bytes 772
  14.0 1.9 %collective-permute-start.16 = (bf16[64,3712]{1,0:T(8,128)(2,1)S(1)}, bf16[64,3712]{1,0:T(8,128)(2,1)S(1)}, u32[]{:S(2)}, u32[]{:S(2)}) collective-permute-start(bf16[64,3712]{1,0:T(8,128)(2,1)S(1)} %join.1.rest_0_.refs_0_), channel_id=1, source_target_pairs={{0,8},{8,0},{1,9},{9,1},{2,10},{10,2},{3,11},{11,3},{4,12},{12,4},... | collective-permute-start | bytes 1425416 | tf_op jit(solution)/shard_map/ppermute | solution.py:203
  14.0 8.7 %collective-permute-start.5 = (bf16[64,3712]{1,0:T(8,128)(2,1)S(1)}, bf16[64,3712]{1,0:T(8,128)(2,1)S(1)}, u32[]{:S(2)}, u32[]{:S(2)}) collective-permute-start(bf16[64,3712]{1,0:T(8,128)(2,1)S(1)} %join.1.rest_0_.refs_0_), channel_id=1, source_target_pairs={{0,2},{10,8},{2,4},{12,10},{4,6},{14,12},{6,7},{15,14},{7,5},{13,1... | collective-permute-start | bytes 1425416 | tf_op jit(solution)/shard_map/ppermute | solution.py:200
  17.6 6.7 %collective-permute-start.24 = (bf16[64,3584]{1,0:T(8,128)(2,1)S(1)}, bf16[64,3584]{1,0:T(8,128)(2,1)S(1)}, u32[]{:S(2)}, u32[]{:S(2)}) collective-permute-start(bf16[64,3584]{1,0:T(8,128)(2,1)S(1)} %get-tuple-element.56), channel_id=1, source_target_pairs={{0,8},{8,0},{1,9},{9,1},{2,10},{10,2},{3,11},{11,3},{4,12},{12,4},... | collective-permute-start | bytes 1376264 | tf_op jit(solution)/shard_map/ppermute | solution.py:203
  22.8 3.3 %collective-permute-start.17 = (bf16[64,3712]{1,0:T(8,128)(2,1)S(1)}, bf16[64,3712]{1,0:T(8,128)(2,1)S(1)}, u32[]{:S(2)}, u32[]{:S(2)}) collective-permute-start(bf16[64,3712]{1,0:T(8,128)(2,1)S(1)} %collective-permute-done.5.refs_0_), channel_id=1, source_target_pairs={{0,8},{8,0},{1,9},{9,1},{2,10},{10,2},{3,11},{11,3},{4,12},{12,4},... | collective-permute-start | bytes 1425416 | tf_op jit(solution)/shard_map/ppermute | solution.py:203
  22.8 8.7 %collective-permute-start.6 = (bf16[64,3712]{1,0:T(8,128)(2,1)S(1)}, bf16[64,3712]{1,0:T(8,128)(2,1)S(1)}, u32[]{:S(2)}, u32[]{:S(2)}) collective-permute-start(bf16[64,3712]{1,0:T(8,128)(2,1)S(1)} %collective-permute-done.5.refs_0_), channel_id=1, source_target_pairs={{0,2},{10,8},{2,4},{12,10},{4,6},{14,12},{6,7},{15,14},{7,5},{13,1... | collective-permute-start | bytes 1425416 | tf_op jit(solution)/shard_map/ppermute | solution.py:200
  24.4 11.9 %collective-permute-start.25 = (bf16[64,3584]{1,0:T(8,128)(2,1)S(1)}, bf16[64,3584]{1,0:T(8,128)(2,1)S(1)}, u32[]{:S(2)}, u32[]{:S(2)}) collective-permute-start(bf16[64,3584]{1,0:T(8,128)(2,1)S(1)} %add_convert_fusion.7), channel_id=1, source_target_pairs={{0,2},{10,8},{2,4},{12,10},{4,6},{14,12},{6,7},{15,14},{7,5},{13,1... | collective-permute-start | bytes 1376264 | tf_op jit(solution)/shard_map/ppermute | solution.py:200
  27.8 8.6 %collective-permute-start.23 = (bf16[64,3584]{1,0:T(8,128)(2,1)S(1)}, bf16[64,3584]{1,0:T(8,128)(2,1)S(1)}, u32[]{:S(2)}, u32[]{:S(2)}) collective-permute-start(bf16[64,3584]{1,0:T(8,128)(2,1)S(1)} %get-tuple-element.55), channel_id=1, source_target_pairs={{0,8},{8,0},{1,9},{9,1},{2,10},{10,2},{3,11},{11,3},{4,12},{12,4},... | collective-permute-start | bytes 1376264 | tf_op jit(solution)/shard_map/ppermute | solution.py:203
  31.4 6.7 %collective-permute-start.18 = (bf16[64,3712]{1,0:T(8,128)(2,1)S(1)}, bf16[64,3712]{1,0:T(8,128)(2,1)S(1)}, u32[]{:S(2)}, u32[]{:S(2)}) collective-permute-start(bf16[64,3712]{1,0:T(8,128)(2,1)S(1)} %collective-permute-done.6.refs_0_), channel_id=1, source_target_pairs={{0,8},{8,0},{1,9},{9,1},{2,10},{10,2},{3,11},{11,3},{4,12},{12,4},... | collective-permute-start | bytes 1425416 | tf_op jit(solution)/shard_map/ppermute | solution.py:203
  31.4 11.2 %collective-permute-start.7 = (bf16[64,3712]{1,0:T(8,128)(2,1)S(1)}, bf16[64,3712]{1,0:T(8,128)(2,1)S(1)}, u32[]{:S(2)}, u32[]{:S(2)}) collective-permute-start(bf16[64,3712]{1,0:T(8,128)(2,1)S(1)} %collective-permute-done.6.refs_0_), channel_id=1, source_target_pairs={{0,2},{10,8},{2,4},{12,10},{4,6},{14,12},{6,7},{15,14},{7,5},{13,1... | collective-permute-start | bytes 1425416 | tf_op jit(solution)/shard_map/ppermute | solution.py:200
  36.5 9.8 %collective-permute-start.26 = (bf16[64,3584]{1,0:T(8,128)(2,1)S(1)}, bf16[64,3584]{1,0:T(8,128)(2,1)S(1)}, u32[]{:S(2)}, u32[]{:S(2)}) collective-permute-start(bf16[64,3584]{1,0:T(8,128)(2,1)S(1)} %add_convert_fusion.6), channel_id=1, source_target_pairs={{0,2},{10,8},{2,4},{12,10},{4,6},{14,12},{6,7},{15,14},{7,5},{13,1... | collective-permute-start | bytes 1376264 | tf_op jit(solution)/shard_map/ppermute | solution.py:200
  39.9 6.4 %collective-permute-start.22 = (bf16[64,3584]{1,0:T(8,128)(2,1)S(1)}, bf16[64,3584]{1,0:T(8,128)(2,1)S(1)}, u32[]{:S(2)}, u32[]{:S(2)}) collective-permute-start(bf16[64,3584]{1,0:T(8,128)(2,1)S(1)} %get-tuple-element.54), channel_id=1, source_target_pairs={{0,8},{8,0},{1,9},{9,1},{2,10},{10,2},{3,11},{11,3},{4,12},{12,4},... | collective-permute-start | bytes 1376264 | tf_op jit(solution)/shard_map/ppermute | solution.py:203
  42.6 5.8 %collective-permute-start.20 = (bf16[64,3712]{1,0:T(8,128)(2,1)S(1)}, bf16[64,3712]{1,0:T(8,128)(2,1)S(1)}, u32[]{:S(2)}, u32[]{:S(2)}) collective-permute-start(bf16[64,3712]{1,0:T(8,128)(2,1)S(1)} %collective-permute-done.7.refs_0_), channel_id=1, source_target_pairs={{0,8},{8,0},{1,9},{9,1},{2,10},{10,2},{3,11},{11,3},{4,12},{12,4},... | collective-permute-start | bytes 1425416 | tf_op jit(solution)/shard_map/ppermute | solution.py:203
  43.0 9.7 %collective-permute-start.8 = (bf16[64,3712]{1,0:T(8,128)(2,1)S(1)}, bf16[64,3712]{1,0:T(8,128)(2,1)S(1)}, u32[]{:S(2)}, u32[]{:S(2)}) collective-permute-start(bf16[64,3712]{1,0:T(8,128)(2,1)S(1)} %collective-permute-done.7.refs_0_), channel_id=1, source_target_pairs={{0,2},{10,8},{2,4},{12,10},{4,6},{14,12},{6,7},{15,14},{7,5},{13,1... | collective-permute-start | bytes 1425416 | tf_op jit(solution)/shard_map/ppermute | solution.py:200
  46.5 10.1 %collective-permute-start.27 = (bf16[64,3584]{1,0:T(8,128)(2,1)S(1)}, bf16[64,3584]{1,0:T(8,128)(2,1)S(1)}, u32[]{:S(2)}, u32[]{:S(2)}) collective-permute-start(bf16[64,3584]{1,0:T(8,128)(2,1)S(1)} %add_convert_fusion.5), channel_id=1, source_target_pairs={{0,2},{10,8},{2,4},{12,10},{4,6},{14,12},{6,7},{15,14},{7,5},{13,1... | collective-permute-start | bytes 1376264 | tf_op jit(solution)/shard_map/ppermute | solution.py:200
  50.1 6.5 %collective-permute-start.21 = (bf16[64,3584]{1,0:T(8,128)(2,1)S(1)}, bf16[64,3584]{1,0:T(8,128)(2,1)S(1)}, u32[]{:S(2)}, u32[]{:S(2)}) collective-permute-start(bf16[64,3584]{1,0:T(8,128)(2,1)S(1)} %get-tuple-element.53), channel_id=1, source_target_pairs={{0,8},{8,0},{1,9},{9,1},{2,10},{10,2},{3,11},{11,3},{4,12},{12,4},... | collective-permute-start | bytes 1376264 | tf_op jit(solution)/shard_map/ppermute | solution.py:203
  52.7 5.7 %collective-permute-start.15 = (bf16[64,3712]{1,0:T(8,128)(2,1)S(1)}, bf16[64,3712]{1,0:T(8,128)(2,1)S(1)}, u32[]{:S(2)}, u32[]{:S(2)}) collective-permute-start(bf16[64,3712]{1,0:T(8,128)(2,1)S(1)} %collective-permute-done.8.refs_0_), channel_id=1, source_target_pairs={{0,8},{8,0},{1,9},{9,1},{2,10},{10,2},{3,11},{11,3},{4,12},{12,4},... | collective-permute-start | bytes 1425416 | tf_op jit(solution)/shard_map/ppermute | solution.py:203
  53.2 8.7 %collective-permute-start.9 = (bf16[64,3712]{1,0:T(8,128)(2,1)S(1)}, bf16[64,3712]{1,0:T(8,128)(2,1)S(1)}, u32[]{:S(2)}, u32[]{:S(2)}) collective-permute-start(bf16[64,3712]{1,0:T(8,128)(2,1)S(1)} %collective-permute-done.8.refs_0_), channel_id=1, source_target_pairs={{0,2},{10,8},{2,4},{12,10},{4,6},{14,12},{6,7},{15,14},{7,5},{13,1... | collective-permute-start | bytes 1425416 | tf_op jit(solution)/shard_map/ppermute | solution.py:200
  56.8 10.0 %collective-permute-start.28 = (bf16[64,3584]{1,0:T(8,128)(2,1)S(1)}, bf16[64,3584]{1,0:T(8,128)(2,1)S(1)}, u32[]{:S(2)}, u32[]{:S(2)}) collective-permute-start(bf16[64,3584]{1,0:T(8,128)(2,1)S(1)} %add_convert_fusion.4), channel_id=1, source_target_pairs={{0,2},{10,8},{2,4},{12,10},{4,6},{14,12},{6,7},{15,14},{7,5},{13,1... | collective-permute-start | bytes 1376264 | tf_op jit(solution)/shard_map/ppermute | solution.py:200
  60.1 6.7 %collective-permute-start.19 = (bf16[64,3584]{1,0:T(8,128)(2,1)S(1)}, bf16[64,3584]{1,0:T(8,128)(2,1)S(1)}, u32[]{:S(2)}, u32[]{:S(2)}) collective-permute-start(bf16[64,3584]{1,0:T(8,128)(2,1)S(1)} %get-tuple-element.50), channel_id=1, source_target_pairs={{0,8},{8,0},{1,9},{9,1},{2,10},{10,2},{3,11},{11,3},{4,12},{12,4},... | collective-permute-start | bytes 1376264 | tf_op jit(solution)/shard_map/ppermute | solution.py:203
  60.2 10.2 %collective-permute-start.2 = (bf16[64,3584]{1,0:T(8,128)(2,1)S(1)}, bf16[64,3584]{1,0:T(8,128)(2,1)S(1)}, u32[]{:S(2)}, u32[]{:S(2)}) collective-permute-start(bf16[64,3584]{1,0:T(8,128)(2,1)S(1)} %get-tuple-element.34), channel_id=1, source_target_pairs={{0,8},{8,0},{1,9},{9,1},{2,10},{10,2},{3,11},{11,3},{4,12},{12,4},... | collective-permute-start | bytes 1376264 | tf_op jit(solution)/shard_map/ppermute | solution.py:203
  61.9 6.7 %collective-permute-start.13 = (bf16[64,3712]{1,0:T(8,128)(2,1)S(1)}, bf16[64,3712]{1,0:T(8,128)(2,1)S(1)}, u32[]{:S(2)}, u32[]{:S(2)}) collective-permute-start(bf16[64,3712]{1,0:T(8,128)(2,1)S(1)} %collective-permute-done.9.refs_0_), channel_id=1, source_target_pairs={{0,8},{8,0},{1,9},{9,1},{2,10},{10,2},{3,11},{11,3},{4,12},{12,4},... | collective-permute-start | bytes 1425416 | tf_op jit(solution)/shard_map/ppermute | solution.py:203
  61.9 10.0 %collective-permute-start.10 = (bf16[64,3712]{1,0:T(8,128)(2,1)S(1)}, bf16[64,3712]{1,0:T(8,128)(2,1)S(1)}, u32[]{:S(2)}, u32[]{:S(2)}) collective-permute-start(bf16[64,3712]{1,0:T(8,128)(2,1)S(1)} %collective-permute-done.9.refs_0_), channel_id=1, source_target_pairs={{0,2},{10,8},{2,4},{12,10},{4,6},{14,12},{6,7},{15,14},{7,5},{13,1... | collective-permute-start | bytes 1425416 | tf_op jit(solution)/shard_map/ppermute | solution.py:200
  67.0 9.8 %collective-permute-start.29 = (bf16[64,3584]{1,0:T(8,128)(2,1)S(1)}, bf16[64,3584]{1,0:T(8,128)(2,1)S(1)}, u32[]{:S(2)}, u32[]{:S(2)}) collective-permute-start(bf16[64,3584]{1,0:T(8,128)(2,1)S(1)} %add_convert_fusion.3), channel_id=1, source_target_pairs={{0,2},{10,8},{2,4},{12,10},{4,6},{14,12},{6,7},{15,14},{7,5},{13,1... | collective-permute-start | bytes 1376264 | tf_op jit(solution)/shard_map/ppermute | solution.py:200
  70.3 6.5 %collective-permute-start.14 = (bf16[64,3584]{1,0:T(8,128)(2,1)S(1)}, bf16[64,3584]{1,0:T(8,128)(2,1)S(1)}, u32[]{:S(2)}, u32[]{:S(2)}) collective-permute-start(bf16[64,3584]{1,0:T(8,128)(2,1)S(1)} %get-tuple-element.39), channel_id=1, source_target_pairs={{0,8},{8,0},{1,9},{9,1},{2,10},{10,2},{3,11},{11,3},{4,12},{12,4},... | collective-permute-start | bytes 1376264 | tf_op jit(solution)/shard_map/ppermute | solution.py:203
  71.9 6.7 %collective-permute-start.11 = (bf16[64,3712]{1,0:T(8,128)(2,1)S(1)}, bf16[64,3712]{1,0:T(8,128)(2,1)S(1)}, u32[]{:S(2)}, u32[]{:S(2)}) collective-permute-start(bf16[64,3712]{1,0:T(8,128)(2,1)S(1)} %collective-permute-done.10.refs_0_), channel_id=1, source_target_pairs={{0,8},{8,0},{1,9},{9,1},{2,10},{10,2},{3,11},{11,3},{4,12},{12,4},... | collective-permute-start | bytes 1425416 | tf_op jit(solution)/shard_map/ppermute | solution.py:203
  77.0 8.5 %collective-permute-start.30 = (bf16[64,3584]{1,0:T(8,128)(2,1)S(1)}, bf16[64,3584]{1,0:T(8,128)(2,1)S(1)}, u32[]{:S(2)}, u32[]{:S(2)}) collective-permute-start(bf16[64,3584]{1,0:T(8,128)(2,1)S(1)} %add_convert_fusion.2), channel_id=1, source_target_pairs={{0,2},{10,8},{2,4},{12,10},{4,6},{14,12},{6,7},{15,14},{7,5},{13,1... | collective-permute-start | bytes 1376264 | tf_op jit(solution)/shard_map/ppermute | solution.py:200
  80.3 5.2 %collective-permute-start.12 = (bf16[64,3584]{1,0:T(8,128)(2,1)S(1)}, bf16[64,3584]{1,0:T(8,128)(2,1)S(1)}, u32[]{:S(2)}, u32[]{:S(2)}) collective-permute-start(bf16[64,3584]{1,0:T(8,128)(2,1)S(1)} %get-tuple-element.37), channel_id=1, source_target_pairs={{0,8},{8,0},{1,9},{9,1},{2,10},{10,2},{3,11},{11,3},{4,12},{12,4},... | collective-permute-start | bytes 1376264 | tf_op jit(solution)/shard_map/ppermute | solution.py:203
  85.7 5.5 %collective-permute-start.32 = (bf16[32,3584]{1,0:T(8,128)(2,1)S(1)}, bf16[32,3584]{1,0:T(8,128)(2,1)S(1)}, u32[]{:S(2)}, u32[]{:S(2)}) collective-permute-start(bf16[32,3584]{1,0:T(8,128)(2,1)S(1)} %get-tuple-element.61), channel_id=1, source_target_pairs={{0,10},{10,0},{2,12},{12,2},{4,14},{14,4},{6,15},{15,6},{7,13},{13... | collective-permute-start | bytes 688136 | tf_op jit(solution)/shard_map/ppermute | solution.py:200
  85.8 7.0 %collective-permute-start.31 = (bf16[32,3584]{1,0:T(8,128)(2,1)S(1)}, bf16[32,3584]{1,0:T(8,128)(2,1)S(1)}, u32[]{:S(2)}, u32[]{:S(2)}) collective-permute-start(bf16[32,3584]{1,0:T(8,128)(2,1)S(1)} %get-tuple-element.60), channel_id=1, source_target_pairs={{0,2},{10,8},{2,4},{12,10},{4,6},{14,12},{6,7},{15,14},{7,5},{13,1... | collective-permute-start | bytes 688136 | tf_op jit(solution)/shard_map/ppermute | solution.py:200

commit v8 on v7

--- a/solution.py
+++ b/solution.py
@@ -10,7 +10,7 @@
 LAT = 512
 SOFTMAX_SCALE = 192.0 ** (-0.5)
 LANES = 128
-PIECES = 4
+PIECES = 8
 
 
 def attend_kernel(len_ref, q_ref, c_ref, *rest, base, pair):

time: 94.1 us -> 93.9 us (level)
  waiting for transfers between devices: 31.6 us -> 24.5 us
  Pallas kernels: 28.4 us -> 34.8 us
    ppermute x16, waiting for transfers between devices: 31.3 us -> 24.2 us  [onward(): return lax.ppermute(a, ('node', 'local'), pairs)]
    pallas_call x4 -> x8, Pallas kernels: 10.3 us -> 16.7 us  [attend_piece(): pl.pallas_call(functools.partial(attend_kernel, base=piece * count, pair=...]
  transfers between devices with their start and end apart: 33 -> 33, of which waited for: 13 -> 10; matrix products, arithmetic and copies ran while one was open for 2% -> 1% of each run, Pallas kernels for 30% -> 37%
where the time goes in v8:
time: 93.9 us; the launch traced here: 93.7 us
  Pallas kernels  34.8 us (37%)
  starting transfers between devices  28.9 us (31%)
  waiting for transfers between devices  24.5 us (26%)
  other arithmetic  4.34 us (5%)
  between operations  1 us (1%)
    ppermute x16, starting transfers between devices, onward(): return lax.ppermute(a, ('node', 'local'), pairs)  25.5 us
    ppermute x16, waiting for transfers between devices, onward(): return lax.ppermute(a, ('node', 'local'), pairs)  24.2 us
    pallas_call x8, Pallas kernels, attend_piece(): pl.pallas_call(functools.partial(attend_kernel, base=piece * count, pair=...  16.7 us
    pallas_call x8, Pallas kernels, run_experts(): pl.pallas_call(functools.partial(expert_kernel, own_parts=len(own), parts...  13.8 us
    pallas_call x1, Pallas kernels, load_weights(): pl.pallas_call(functools.partial(load_kernel, count=count), in_specs=[any...  4.23 us
    ppermute x17, starting transfers between devices, across(): return lax.ppermute(a, 'node', [(0, 1), (1, 0)])  3.41 us
  transfers between devices with their start and end apart: 33, of which 10 were waited for; matrix products, arithmetic and copies ran while one was open for 1% of the time, Pallas kernels for 37%

profile of v8, /device:TPU:0, one launch (start us, length us, event | category | flops | bytes accessed | tf_op | source)
XLA Modules:
  0.0 93.7 jit_solution(16043025408891409752)
XLA Ops:
  0.6 0.8 fusion.1
  1.5 1.1 %broadcast_select_fusion = (bf16[32,3584]{1,0:T(8,128)(2,1)S(1)}, bf16[32,3584]{1,0:T(8,128)(2,1)S(1)}) fusion(pred[]{:T(512)S(6)} %eq.16, bf16[64,3584]{1,0:T(8,128)(2,1)} %param.9), kind=kLoop, calls=%fused_computation.13 | loop fusion | flops 229376 | bytes 917505 | tf_op jit(solution)/shard_map/jit(_where)/select_n | solution.py:215
  2.6 0.5 collective-permute-start.1
  3.1 0.1 collective-permute-start
  3.3 3.0 %collective-permute-start.3 = (bf16[32,3712]{1,0:T(8,128)(2,1)S(1)}, bf16[32,3712]{1,0:T(8,128)(2,1)S(1)}, u32[]{:S(2)}, u32[]{:S(2)}) collective-permute-start(bf16[32,3712]{1,0:T(8,128)(2,1)S(1)} %pad_maximum_fusion.refs_3_.refs_0_), channel_id=1, source_target_pairs={{0,2},{10,8},{2,4},{12,10},{4,6},{14,12},{6,7},{15,14},{7,5},{13,1... | collective-permute-start | bytes 712712 | tf_op jit(solution)/shard_map/ppermute | solution.py:200
  6.3 1.6 %collective-permute-start.4 = (bf16[32,3712]{1,0:T(8,128)(2,1)S(1)}, bf16[32,3712]{1,0:T(8,128)(2,1)S(1)}, u32[]{:S(2)}, u32[]{:S(2)}) collective-permute-start(bf16[32,3712]{1,0:T(8,128)(2,1)S(1)} %collective-permute-done.1.refs_3_), channel_id=1, source_target_pairs={{0,2},{10,8},{2,4},{12,10},{4,6},{14,12},{6,7},{15,14},{7,5},{13,1... | collective-permute-start | bytes 712712 | tf_op jit(solution)/shard_map/ppermute | solution.py:200
  7.9 4.2 %load_weights.1 = (bf16[3584,512]{1,0:T(8,128)(2,1)S(1)}, bf16[3584,512]{1,0:T(8,128)(2,1)S(1)}, bf16[512,3584]{1,0:T(8,128)(2,1)S(1)}) custom-call(bf16[1,3584,512]{2,1,0:T(8,128)(2,1)} %refs_0_.1, bf16[1,3584,512]{2,1,0:T(8,128)(2,1)} %refs_1_.1, bf16[1,512,3584]{2,1,0:T(8,128)(2,1)} %refs_2_.1, bf16[32,3712]{1,0:T(8,128)(2,1)S(1)} %pad_maximum_fusion.refs_3_.refs_0_), custom_call_target="tpu_custom_call" | custom-call | bytes 11010048 | tf_op jit(solution)/shard_map/load_weights/pallas_call | solution.py:145
  12.1 1.7 %expert_half.8 = (bf16[64,3584]{1,0:T(8,128)(2,1)S(1)}, bf16[64,3584]{1,0:T(8,128)(2,1)S(1)}) custom-call(s32[1]{0:T(128)} %bitcast.expert_ref, bf16[32,3712]{1,0:T(8,128)(2,1)S(1)} %pad_maximum_fusion.refs_3_.refs_0_, bf16[32,3712]{1,0:T(8,128)(2,1)S(1)} %pad_maximum_fusion.1.refs_1_, bf16[32,3712]{1,0:T(8,128)(2,1)S(1)} %collective-permute-done.refs_2_, ...), custom_call_target="tpu_custom_call" | custom-call | flops 1409286144 | bytes 11010048 | tf_op jit(solution)/shard_map/expert_half/pallas_call | solution.py:109
  14.0 1.6 %collective-permute-start.5 = (bf16[64,3712]{1,0:T(8,128)(2,1)S(1)}, bf16[64,3712]{1,0:T(8,128)(2,1)S(1)}, u32[]{:S(2)}, u32[]{:S(2)}) collective-permute-start(bf16[64,3712]{1,0:T(8,128)(2,1)S(1)} %join.1.rest_0_.refs_0_), channel_id=1, source_target_pairs={{0,2},{10,8},{2,4},{12,10},{4,6},{14,12},{6,7},{15,14},{7,5},{13,1... | collective-permute-start | bytes 1425416 | tf_op jit(solution)/shard_map/ppermute | solution.py:200
  15.7 0.2 collective-permute-done.12.refs_1_
  15.9 1.7 %expert_half.9 = (bf16[64,3584]{1,0:T(8,128)(2,1)S(1)}, bf16[64,3584]{1,0:T(8,128)(2,1)S(1)}) custom-call(s32[1]{0:T(128)} %bitcast.expert_ref, bf16[64,3712]{1,0:T(8,128)(2,1)S(1)} %join.1.rest_0_.refs_0_, bf16[64,3712]{1,0:T(8,128)(2,1)S(1)} %collective-permute-done.12.refs_1_, bf16[3584,512]{1,0:T(8,128)(2,1)S(1)} %get-tuple-element.36.refs_4_.refs_2_, ...), custom_call_target="tpu_custom_call" | custom-call | flops 1409286144 | bytes 11010048 | tf_op jit(solution)/shard_map/expert_half/pallas_call | solution.py:109
  17.6 0.2 collective-permute-start.24
  17.9 2.1 %attend.8 = (bf16[64,64,512]{2,1,0:T(8,128)(2,1)}, f32[8,128]{1,0:T(8,128)S(1)}) custom-call(s32[64]{0:T(128)S(1)} %copy-done, bf16[64,64,576]{2,1,0:T(8,128)(2,1)S(1)} %bitcast.2, bf16[64,64,576]{2,1,0:T(8,128)(2,1)S(1)} %bitcast.4, bf16[64,3712]{1,0:T(8,128)(2,1)S(1)} %join.1.rest_0_.refs_0_), custom_call_target="tpu_custom_call" | custom-call | flops 71303168 | bytes 1703936 | tf_op jit(solution)/shard_map/attend/pallas_call | solution.py:59
  20.0 2.8 %collective-permute-done.5.refs_0_ = bf16[64,3712]{1,0:T(8,128)(2,1)S(1)} collective-permute-done((bf16[64,3712]{1,0:T(8,128)(2,1)S(1)}, bf16[64,3712]{1,0:T(8,128)(2,1)S(1)}, u32[]{:S(2)}, u32[]{:S(2)}) %collective-permute-start.5) | collective-permute-done | bytes 475168 | tf_op jit(solution)/shard_map/ppermute | solution.py:200
  22.8 1.6 %collective-permute-start.6 = (bf16[64,3712]{1,0:T(8,128)(2,1)S(1)}, bf16[64,3712]{1,0:T(8,128)(2,1)S(1)}, u32[]{:S(2)}, u32[]{:S(2)}) collective-permute-start(bf16[64,3712]{1,0:T(8,128)(2,1)S(1)} %collective-permute-done.5.refs_0_), channel_id=1, source_target_pairs={{0,2},{10,8},{2,4},{12,10},{4,6},{14,12},{6,7},{15,14},{7,5},{13,1... | collective-permute-start | bytes 1425416 | tf_op jit(solution)/shard_map/ppermute | solution.py:200
  24.3 0.1 add_convert_fusion.7
  24.4 1.6 %collective-permute-start.25 = (bf16[64,3584]{1,0:T(8,128)(2,1)S(1)}, bf16[64,3584]{1,0:T(8,128)(2,1)S(1)}, u32[]{:S(2)}, u32[]{:S(2)}) collective-permute-start(bf16[64,3584]{1,0:T(8,128)(2,1)S(1)} %add_convert_fusion.7), channel_id=1, source_target_pairs={{0,2},{10,8},{2,4},{12,10},{4,6},{14,12},{6,7},{15,14},{7,5},{13,1... | collective-permute-start | bytes 1376264 | tf_op jit(solution)/shard_map/ppermute | solution.py:200
  26.0 1.7 %expert_half.10 = (bf16[64,3584]{1,0:T(8,128)(2,1)S(1)}, bf16[64,3584]{1,0:T(8,128)(2,1)S(1)}) custom-call(s32[1]{0:T(128)} %bitcast.expert_ref, bf16[64,3712]{1,0:T(8,128)(2,1)S(1)} %collective-permute-done.5.refs_0_, bf16[64,3712]{1,0:T(8,128)(2,1)S(1)} %collective-permute-done.13.refs_1_, bf16[3584,512]{1,0:T(8,128)(2,1)S(1)} %get-tuple-element.36.refs_4_.refs_2_, ...), custom_call_target="tpu_custom_call" | custom-call | flops 1409286144 | bytes 11010048 | tf_op jit(solution)/shard_map/expert_half/pallas_call | solution.py:109
  27.8 2.1 %attend.9 = (bf16[64,64,512]{2,1,0:T(8,128)(2,1)}, f32[8,128]{1,0:T(8,128)S(1)}) custom-call(s32[64]{0:T(128)S(1)} %copy-done, bf16[64,64,576]{2,1,0:T(8,128)(2,1)S(1)} %bitcast.2, bf16[64,64,576]{2,1,0:T(8,128)(2,1)S(1)} %bitcast.4, bf16[64,64,512]{2,1,0:T(8,128)(2,1)} %get-tuple-element.42.rest_0_, ...), custom_call_target="tpu_custom_call", output_to_operand_aliasing={{0}: (3, {})} | custom-call | flops 71303168 | bytes 1703936 | tf_op jit(solution)/shard_map/attend/pallas_call | solution.py:59
  29.9 1.5 %collective-permute-done.6.refs_0_ = bf16[64,3712]{1,0:T(8,128)(2,1)S(1)} collective-permute-done((bf16[64,3712]{1,0:T(8,128)(2,1)S(1)}, bf16[64,3712]{1,0:T(8,128)(2,1)S(1)}, u32[]{:S(2)}, u32[]{:S(2)}) %collective-permute-start.6) | collective-permute-done | bytes 475168 | tf_op jit(solution)/shard_map/ppermute | solution.py:200
  31.4 1.6 %collective-permute-start.7 = (bf16[64,3712]{1,0:T(8,128)(2,1)S(1)}, bf16[64,3712]{1,0:T(8,128)(2,1)S(1)}, u32[]{:S(2)}, u32[]{:S(2)}) collective-permute-start(bf16[64,3712]{1,0:T(8,128)(2,1)S(1)} %collective-permute-done.6.refs_0_), channel_id=1, source_target_pairs={{0,2},{10,8},{2,4},{12,10},{4,6},{14,12},{6,7},{15,14},{7,5},{13,1... | collective-permute-start | bytes 1425416 | tf_op jit(solution)/shard_map/ppermute | solution.py:200
  33.0 3.3 %collective-permute-done.25 = bf16[64,3584]{1,0:T(8,128)(2,1)S(1)} collective-permute-done((bf16[64,3584]{1,0:T(8,128)(2,1)S(1)}, bf16[64,3584]{1,0:T(8,128)(2,1)S(1)}, u32[]{:S(2)}, u32[]{:S(2)}) %collective-permute-start.25) | collective-permute-done | bytes 458784 | tf_op jit(solution)/shard_map/ppermute | solution.py:200
  36.3 0.2 add_convert_fusion.6
  36.5 1.6 %collective-permute-start.26 = (bf16[64,3584]{1,0:T(8,128)(2,1)S(1)}, bf16[64,3584]{1,0:T(8,128)(2,1)S(1)}, u32[]{:S(2)}, u32[]{:S(2)}) collective-permute-start(bf16[64,3584]{1,0:T(8,128)(2,1)S(1)} %add_convert_fusion.6), channel_id=1, source_target_pairs={{0,2},{10,8},{2,4},{12,10},{4,6},{14,12},{6,7},{15,14},{7,5},{13,1... | collective-permute-start | bytes 1376264 | tf_op jit(solution)/shard_map/ppermute | solution.py:200
  38.1 1.7 %expert_half.11 = (bf16[64,3584]{1,0:T(8,128)(2,1)S(1)}, bf16[64,3584]{1,0:T(8,128)(2,1)S(1)}) custom-call(s32[1]{0:T(128)} %bitcast.expert_ref, bf16[64,3712]{1,0:T(8,128)(2,1)S(1)} %collective-permute-done.6.refs_0_, bf16[64,3712]{1,0:T(8,128)(2,1)S(1)} %collective-permute-done.14.refs_1_, bf16[3584,512]{1,0:T(8,128)(2,1)S(1)} %get-tuple-element.36.refs_4_.refs_2_, ...), custom_call_target="tpu_custom_call" | custom-call | flops 1409286144 | bytes 11010048 | tf_op jit(solution)/shard_map/expert_half/pallas_call | solution.py:109
  39.9 0.1 collective-permute-start.22
  39.9 2.1 %attend.10 = (bf16[64,64,512]{2,1,0:T(8,128)(2,1)}, f32[8,128]{1,0:T(8,128)S(1)}) custom-call(s32[64]{0:T(128)S(1)} %copy-done, bf16[64,64,576]{2,1,0:T(8,128)(2,1)S(1)} %bitcast.2, bf16[64,64,576]{2,1,0:T(8,128)(2,1)S(1)} %bitcast.4, bf16[64,64,512]{2,1,0:T(8,128)(2,1)} %get-tuple-element.44.rest_0_, ...), custom_call_target="tpu_custom_call", output_to_operand_aliasing={{0}: (3, {})} | custom-call | flops 71303168 | bytes 1703936 | tf_op jit(solution)/shard_map/attend/pallas_call | solution.py:59
  42.0 0.5 collective-permute-start.15
  42.5 1.5 %collective-permute-start.8 = (bf16[64,3712]{1,0:T(8,128)(2,1)S(1)}, bf16[64,3712]{1,0:T(8,128)(2,1)S(1)}, u32[]{:S(2)}, u32[]{:S(2)}) collective-permute-start(bf16[64,3712]{1,0:T(8,128)(2,1)S(1)} %collective-permute-done.7.refs_0_), channel_id=1, source_target_pairs={{0,2},{10,8},{2,4},{12,10},{4,6},{14,12},{6,7},{15,14},{7,5},{13,1... | collective-permute-start | bytes 1425416 | tf_op jit(solution)/shard_map/ppermute | solution.py:200
  44.1 2.3 %collective-permute-done.26 = bf16[64,3584]{1,0:T(8,128)(2,1)S(1)} collective-permute-done((bf16[64,3584]{1,0:T(8,128)(2,1)S(1)}, bf16[64,3584]{1,0:T(8,128)(2,1)S(1)}, u32[]{:S(2)}, u32[]{:S(2)}) %collective-permute-start.26) | collective-permute-done | bytes 458784 | tf_op jit(solution)/shard_map/ppermute | solution.py:200
  46.3 0.2 add_convert_fusion.5
  46.6 1.8 %collective-permute-start.27 = (bf16[64,3584]{1,0:T(8,128)(2,1)S(1)}, bf16[64,3584]{1,0:T(8,128)(2,1)S(1)}, u32[]{:S(2)}, u32[]{:S(2)}) collective-permute-start(bf16[64,3584]{1,0:T(8,128)(2,1)S(1)} %add_convert_fusion.5), channel_id=1, source_target_pairs={{0,2},{10,8},{2,4},{12,10},{4,6},{14,12},{6,7},{15,14},{7,5},{13,1... | collective-permute-start | bytes 1376264 | tf_op jit(solution)/shard_map/ppermute | solution.py:200
  48.4 1.7 %expert_half.12 = (bf16[64,3584]{1,0:T(8,128)(2,1)S(1)}, bf16[64,3584]{1,0:T(8,128)(2,1)S(1)}) custom-call(s32[1]{0:T(128)} %bitcast.expert_ref, bf16[64,3712]{1,0:T(8,128)(2,1)S(1)} %collective-permute-done.7.refs_0_, bf16[64,3712]{1,0:T(8,128)(2,1)S(1)} %collective-permute-done.15.refs_1_, bf16[3584,512]{1,0:T(8,128)(2,1)S(1)} %get-tuple-element.36.refs_4_.refs_2_, ...), custom_call_target="tpu_custom_call" | custom-call | flops 1409286144 | bytes 11010048 | tf_op jit(solution)/shard_map/expert_half/pallas_call | solution.py:109
  50.2 2.1 %attend.11 = (bf16[64,64,512]{2,1,0:T(8,128)(2,1)}, f32[8,128]{1,0:T(8,128)S(1)}) custom-call(s32[64]{0:T(128)S(1)} %copy-done, bf16[64,64,576]{2,1,0:T(8,128)(2,1)S(1)} %bitcast.2, bf16[64,64,576]{2,1,0:T(8,128)(2,1)S(1)} %bitcast.4, bf16[64,64,512]{2,1,0:T(8,128)(2,1)} %get-tuple-element.47.rest_0_, ...), custom_call_target="tpu_custom_call", output_to_operand_aliasing={{0}: (3, {})} | custom-call | flops 71303168 | bytes 1703936 | tf_op jit(solution)/shard_map/attend/pallas_call | solution.py:59
  52.3 0.5 collective-permute-start.16
  52.8 1.5 %collective-permute-start.9 = (bf16[64,3712]{1,0:T(8,128)(2,1)S(1)}, bf16[64,3712]{1,0:T(8,128)(2,1)S(1)}, u32[]{:S(2)}, u32[]{:S(2)}) collective-permute-start(bf16[64,3712]{1,0:T(8,128)(2,1)S(1)} %collective-permute-done.8.refs_0_), channel_id=1, source_target_pairs={{0,2},{10,8},{2,4},{12,10},{4,6},{14,12},{6,7},{15,14},{7,5},{13,1... | collective-permute-start | bytes 1425416 | tf_op jit(solution)/shard_map/ppermute | solution.py:200
  54.3 2.0 %collective-permute-done.27 = bf16[64,3584]{1,0:T(8,128)(2,1)S(1)} collective-permute-done((bf16[64,3584]{1,0:T(8,128)(2,1)S(1)}, bf16[64,3584]{1,0:T(8,128)(2,1)S(1)}, u32[]{:S(2)}, u32[]{:S(2)}) %collective-permute-start.27) | collective-permute-done | bytes 458784 | tf_op jit(solution)/shard_map/ppermute | solution.py:200
  56.3 0.2 add_convert_fusion.4
  56.5 1.6 %collective-permute-start.28 = (bf16[64,3584]{1,0:T(8,128)(2,1)S(1)}, bf16[64,3584]{1,0:T(8,128)(2,1)S(1)}, u32[]{:S(2)}, u32[]{:S(2)}) collective-permute-start(bf16[64,3584]{1,0:T(8,128)(2,1)S(1)} %add_convert_fusion.4), channel_id=1, source_target_pairs={{0,2},{10,8},{2,4},{12,10},{4,6},{14,12},{6,7},{15,14},{7,5},{13,1... | collective-permute-start | bytes 1376264 | tf_op jit(solution)/shard_map/ppermute | solution.py:200
  58.2 1.7 %expert_half.13 = (bf16[64,3584]{1,0:T(8,128)(2,1)S(1)}, bf16[64,3584]{1,0:T(8,128)(2,1)S(1)}) custom-call(s32[1]{0:T(128)} %bitcast.expert_ref, bf16[64,3712]{1,0:T(8,128)(2,1)S(1)} %collective-permute-done.8.refs_0_, bf16[64,3712]{1,0:T(8,128)(2,1)S(1)} %collective-permute-done.16.refs_1_, bf16[3584,512]{1,0:T(8,128)(2,1)S(1)} %get-tuple-element.36.refs_4_.refs_2_, ...), custom_call_target="tpu_custom_call" | custom-call | flops 1409286144 | bytes 11010048 | tf_op jit(solution)/shard_map/expert_half/pallas_call | solution.py:109
  59.9 0.1 collective-permute-start.20
  60.0 0.5 collective-permute-start.2
  60.5 2.1 %attend.12 = (bf16[64,64,512]{2,1,0:T(8,128)(2,1)}, f32[8,128]{1,0:T(8,128)S(1)}) custom-call(s32[64]{0:T(128)S(1)} %copy-done, bf16[64,64,576]{2,1,0:T(8,128)(2,1)S(1)} %bitcast.2, bf16[64,64,576]{2,1,0:T(8,128)(2,1)S(1)} %bitcast.4, bf16[64,64,512]{2,1,0:T(8,128)(2,1)} %get-tuple-element.50.rest_0_, ...), custom_call_target="tpu_custom_call", output_to_operand_aliasing={{0}: (3, {})} | custom-call | flops 71303168 | bytes 1703936 | tf_op jit(solution)/shard_map/attend/pallas_call | solution.py:59
  62.6 0.1 collective-permute-start.18
  62.6 1.5 %collective-permute-start.10 = (bf16[64,3712]{1,0:T(8,128)(2,1)S(1)}, bf16[64,3712]{1,0:T(8,128)(2,1)S(1)}, u32[]{:S(2)}, u32[]{:S(2)}) collective-permute-start(bf16[64,3712]{1,0:T(8,128)(2,1)S(1)} %collective-permute-done.9.refs_0_), channel_id=1, source_target_pairs={{0,2},{10,8},{2,4},{12,10},{4,6},{14,12},{6,7},{15,14},{7,5},{13,1... | collective-permute-start | bytes 1425416 | tf_op jit(solution)/shard_map/ppermute | solution.py:200
  64.2 2.2 %collective-permute-done.28 = bf16[64,3584]{1,0:T(8,128)(2,1)S(1)} collective-permute-done((bf16[64,3584]{1,0:T(8,128)(2,1)S(1)}, bf16[64,3584]{1,0:T(8,128)(2,1)S(1)}, u32[]{:S(2)}, u32[]{:S(2)}) %collective-permute-start.28) | collective-permute-done | bytes 458784 | tf_op jit(solution)/shard_map/ppermute | solution.py:200
  66.3 0.2 add_convert_fusion.3
  66.6 1.6 %collective-permute-start.29 = (bf16[64,3584]{1,0:T(8,128)(2,1)S(1)}, bf16[64,3584]{1,0:T(8,128)(2,1)S(1)}, u32[]{:S(2)}, u32[]{:S(2)}) collective-permute-start(bf16[64,3584]{1,0:T(8,128)(2,1)S(1)} %add_convert_fusion.3), channel_id=1, source_target_pairs={{0,2},{10,8},{2,4},{12,10},{4,6},{14,12},{6,7},{15,14},{7,5},{13,1... | collective-permute-start | bytes 1376264 | tf_op jit(solution)/shard_map/ppermute | solution.py:200
  68.2 1.7 %expert_half.15 = (bf16[64,3584]{1,0:T(8,128)(2,1)S(1)}, bf16[64,3584]{1,0:T(8,128)(2,1)S(1)}) custom-call(s32[1]{0:T(128)} %bitcast.expert_ref, bf16[64,3712]{1,0:T(8,128)(2,1)S(1)} %collective-permute-done.9.refs_0_, bf16[64,3712]{1,0:T(8,128)(2,1)S(1)} %collective-permute-done.18.refs_1_, bf16[3584,512]{1,0:T(8,128)(2,1)S(1)} %get-tuple-element.36.refs_4_.refs_2_, ...), custom_call_target="tpu_custom_call" | custom-call | flops 1409286144 | bytes 11010048 | tf_op jit(solution)/shard_map/expert_half/pallas_call | solution.py:109
  70.0 0.1 convert_add_fusion
  70.1 2.1 %attend.13 = (bf16[64,64,512]{2,1,0:T(8,128)(2,1)}, f32[8,128]{1,0:T(8,128)S(1)}) custom-call(s32[64]{0:T(128)S(1)} %copy-done, bf16[64,64,576]{2,1,0:T(8,128)(2,1)S(1)} %bitcast.2, bf16[64,64,576]{2,1,0:T(8,128)(2,1)S(1)} %bitcast.4, bf16[64,64,512]{2,1,0:T(8,128)(2,1)} %get-tuple-element.53.rest_0_, ...), custom_call_target="tpu_custom_call", output_to_operand_aliasing={{0}: (3, {})} | custom-call | flops 71303168 | bytes 1703936 | tf_op jit(solution)/shard_map/attend/pallas_call | solution.py:59
  72.2 0.5 collective-permute-start.11
  72.7 3.6 %collective-permute-done.29 = bf16[64,3584]{1,0:T(8,128)(2,1)S(1)} collective-permute-done((bf16[64,3584]{1,0:T(8,128)(2,1)S(1)}, bf16[64,3584]{1,0:T(8,128)(2,1)S(1)}, u32[]{:S(2)}, u32[]{:S(2)}) %collective-permute-start.29) | collective-permute-done | bytes 458784 | tf_op jit(solution)/shard_map/ppermute | solution.py:200
  76.4 0.2 add_convert_fusion.2
  76.6 1.6 %collective-permute-start.30 = (bf16[64,3584]{1,0:T(8,128)(2,1)S(1)}, bf16[64,3584]{1,0:T(8,128)(2,1)S(1)}, u32[]{:S(2)}, u32[]{:S(2)}) collective-permute-start(bf16[64,3584]{1,0:T(8,128)(2,1)S(1)} %add_convert_fusion.2), channel_id=1, source_target_pairs={{0,2},{10,8},{2,4},{12,10},{4,6},{14,12},{6,7},{15,14},{7,5},{13,1... | collective-permute-start | bytes 1376264 | tf_op jit(solution)/shard_map/ppermute | solution.py:200
  78.2 1.7 %expert_half.14 = (bf16[64,3584]{1,0:T(8,128)(2,1)S(1)}, bf16[64,3584]{1,0:T(8,128)(2,1)S(1)}) custom-call(s32[1]{0:T(128)} %bitcast.expert_ref, bf16[64,3712]{1,0:T(8,128)(2,1)S(1)} %collective-permute-done.10.refs_0_, bf16[64,3712]{1,0:T(8,128)(2,1)S(1)} %collective-permute-done.11.refs_1_, bf16[3584,512]{1,0:T(8,128)(2,1)S(1)} %get-tuple-element.36.refs_4_.refs_2_, ...), custom_call_target="tpu_custom_call" | custom-call | flops 1409286144 | bytes 11010048 | tf_op jit(solution)/shard_map/expert_half/pallas_call | solution.py:109
  80.1 5.0 %collective-permute-done.30 = bf16[64,3584]{1,0:T(8,128)(2,1)S(1)} collective-permute-done((bf16[64,3584]{1,0:T(8,128)(2,1)S(1)}, bf16[64,3584]{1,0:T(8,128)(2,1)S(1)}, u32[]{:S(2)}, u32[]{:S(2)}) %collective-permute-start.30) | collective-permute-done | bytes 458784 | tf_op jit(solution)/shard_map/ppermute | solution.py:200
  85.1 0.2 add_convert_fusion.1
  85.4 1.6 %collective-permute-start.31 = (bf16[32,3584]{1,0:T(8,128)(2,1)S(1)}, bf16[32,3584]{1,0:T(8,128)(2,1)S(1)}, u32[]{:S(2)}, u32[]{:S(2)}) collective-permute-start(bf16[32,3584]{1,0:T(8,128)(2,1)S(1)} %get-tuple-element.72), channel_id=1, source_target_pairs={{0,2},{10,8},{2,4},{12,10},{4,6},{14,12},{6,7},{15,14},{7,5},{13,1... | collective-permute-start | bytes 688136 | tf_op jit(solution)/shard_map/ppermute | solution.py:200
  87.0 0.1 maximum_select_fusion
  87.1 2.1 %attend.14 = (bf16[64,64,512]{2,1,0:T(8,128)(2,1)}, f32[8,128]{1,0:T(8,128)}) custom-call(s32[64]{0:T(128)S(1)} %copy-done, bf16[64,64,576]{2,1,0:T(8,128)(2,1)S(1)} %bitcast.2, bf16[64,64,576]{2,1,0:T(8,128)(2,1)S(1)} %bitcast.4, bf16[64,64,512]{2,1,0:T(8,128)(2,1)} %get-tuple-element.67.rest_0_, ...), custom_call_target="tpu_custom_call", output_to_operand_aliasing={{0}: (3, {})} | custom-call | flops 71303168 | bytes 1703936 | tf_op jit(solution)/shard_map/attend/pallas_call | solution.py:59
  89.2 2.1 %attend.15 = (bf16[64,64,512]{2,1,0:T(8,128)(2,1)}, f32[8,128]{1,0:T(8,128)}) custom-call(s32[64]{0:T(128)S(1)} %copy-done, bf16[64,64,576]{2,1,0:T(8,128)(2,1)S(1)} %bitcast.2, bf16[64,64,576]{2,1,0:T(8,128)(2,1)S(1)} %bitcast.4, bf16[64,64,512]{2,1,0:T(8,128)(2,1)} %get-tuple-element.68.rest_0_, ...), custom_call_target="tpu_custom_call", output_to_operand_aliasing={{0}: (3, {})} | custom-call | flops 71303168 | bytes 1703936 | tf_op jit(solution)/shard_map/attend/pallas_call | solution.py:59
  91.3 1.5 %collective-permute-done.31 = bf16[32,3584]{1,0:T(8,128)(2,1)S(1)} collective-permute-done((bf16[32,3584]{1,0:T(8,128)(2,1)S(1)}, bf16[32,3584]{1,0:T(8,128)(2,1)S(1)}, u32[]{:S(2)}, u32[]{:S(2)}) %collective-permute-start.31) | collective-permute-done | bytes 229408 | tf_op jit(solution)/shard_map/ppermute | solution.py:200
  92.8 0.9 add_convert_fusion
  (49 shorter events, 0.7 us)
Async XLA Ops:
  2.6 3.7 %collective-permute-start.1 = (bf16[32,3712]{1,0:T(8,128)(2,1)S(1)}, bf16[32,3712]{1,0:T(8,128)(2,1)S(1)}, u32[]{:S(2)}, u32[]{:S(2)}) collective-permute-start(bf16[32,3712]{1,0:T(8,128)(2,1)S(1)} %pad_maximum_fusion.1.refs_1_), channel_id=1, source_target_pairs={{0,8},{8,0},{1,9},{9,1},{2,10},{10,2},{3,11},{11,3},{4,12},{12,4},... | collective-permute-start | bytes 712712 | tf_op jit(solution)/shard_map/ppermute | solution.py:203
  3.1 9.0 %collective-permute-start = (bf16[32,3712]{1,0:T(8,128)(2,1)S(1)}, bf16[32,3712]{1,0:T(8,128)(2,1)S(1)}, u32[]{:S(2)}, u32[]{:S(2)}) collective-permute-start(bf16[32,3712]{1,0:T(8,128)(2,1)S(1)} %pad_maximum_fusion.refs_3_.refs_0_), channel_id=1, source_target_pairs={{0,8},{8,0},{1,9},{9,1},{2,10},{10,2},{3,11},{11,3},{4,12},{12,4},... | collective-permute-start | bytes 712712 | tf_op jit(solution)/shard_map/ppermute | solution.py:203
  3.3 10.6 %collective-permute-start.3 = (bf16[32,3712]{1,0:T(8,128)(2,1)S(1)}, bf16[32,3712]{1,0:T(8,128)(2,1)S(1)}, u32[]{:S(2)}, u32[]{:S(2)}) collective-permute-start(bf16[32,3712]{1,0:T(8,128)(2,1)S(1)} %pad_maximum_fusion.refs_3_.refs_0_), channel_id=1, source_target_pairs={{0,2},{10,8},{2,4},{12,10},{4,6},{14,12},{6,7},{15,14},{7,5},{13,1... | collective-permute-start | bytes 712712 | tf_op jit(solution)/shard_map/ppermute | solution.py:200
  6.3 7.6 %collective-permute-start.4 = (bf16[32,3712]{1,0:T(8,128)(2,1)S(1)}, bf16[32,3712]{1,0:T(8,128)(2,1)S(1)}, u32[]{:S(2)}, u32[]{:S(2)}) collective-permute-start(bf16[32,3712]{1,0:T(8,128)(2,1)S(1)} %collective-permute-done.1.refs_3_), channel_id=1, source_target_pairs={{0,2},{10,8},{2,4},{12,10},{4,6},{14,12},{6,7},{15,14},{7,5},{13,1... | collective-permute-start | bytes 712712 | tf_op jit(solution)/shard_map/ppermute | solution.py:200
  12.1 5.7 %slice-start.2 = ((s8[5242880]{0:T(1024)(128)(4,1)}), s8[4194304]{0:T(1024)(128)(4,1)S(1)}, s32[]{:S(2)}) async-start(s8[5242880]{0:T(1024)(128)(4,1)} %bitcast.3), calls=%async_computation.2 | async-start | bytes 8388608
  13.9 4.0 %slice-start.3 = ((s8[5242880]{0:T(1024)(128)(4,1)}), s8[1048576]{0:T(1024)(128)(4,1)S(1)}, s32[]{:S(2)}) async-start(s8[5242880]{0:T(1024)(128)(4,1)} %bitcast.3), calls=%async_computation.3 | async-start | bytes 2097152
  13.9 3.9 %slice-start = ((s8[5242880]{0:T(1024)(128)(4,1)}), s8[4194304]{0:T(1024)(128)(4,1)S(1)}, s32[]{:S(2)}) async-start(s8[5242880]{0:T(1024)(128)(4,1)} %bitcast.1), calls=%async_computation | async-start | bytes 8388608
  13.9 3.9 %slice-start.1 = ((s8[5242880]{0:T(1024)(128)(4,1)}), s8[1048576]{0:T(1024)(128)(4,1)S(1)}, s32[]{:S(2)}) async-start(s8[5242880]{0:T(1024)(128)(4,1)} %bitcast.1), calls=%async_computation.1 | async-start | bytes 2097152
  14.0 3.9 %copy-start = (s32[64]{0:T(128)S(1)}, s32[64]{0:T(128)}, u32[]{:S(2)}) copy-start(s32[64]{0:T(128)} %len_ref.15) | copy-start | bytes 772
  14.0 1.9 %collective-permute-start.12 = (bf16[64,3712]{1,0:T(8,128)(2,1)S(1)}, bf16[64,3712]{1,0:T(8,128)(2,1)S(1)}, u32[]{:S(2)}, u32[]{:S(2)}) collective-permute-start(bf16[64,3712]{1,0:T(8,128)(2,1)S(1)} %join.1.rest_0_.refs_0_), channel_id=1, source_target_pairs={{0,8},{8,0},{1,9},{9,1},{2,10},{10,2},{3,11},{11,3},{4,12},{12,4},... | collective-permute-start | bytes 1425416 | tf_op jit(solution)/shard_map/ppermute | solution.py:203
  14.0 8.7 %collective-permute-start.5 = (bf16[64,3712]{1,0:T(8,128)(2,1)S(1)}, bf16[64,3712]{1,0:T(8,128)(2,1)S(1)}, u32[]{:S(2)}, u32[]{:S(2)}) collective-permute-start(bf16[64,3712]{1,0:T(8,128)(2,1)S(1)} %join.1.rest_0_.refs_0_), channel_id=1, source_target_pairs={{0,2},{10,8},{2,4},{12,10},{4,6},{14,12},{6,7},{15,14},{7,5},{13,1... | collective-permute-start | bytes 1425416 | tf_op jit(solution)/shard_map/ppermute | solution.py:200
  17.6 6.7 %collective-permute-start.24 = (bf16[64,3584]{1,0:T(8,128)(2,1)S(1)}, bf16[64,3584]{1,0:T(8,128)(2,1)S(1)}, u32[]{:S(2)}, u32[]{:S(2)}) collective-permute-start(bf16[64,3584]{1,0:T(8,128)(2,1)S(1)} %get-tuple-element.66), channel_id=1, source_target_pairs={{0,8},{8,0},{1,9},{9,1},{2,10},{10,2},{3,11},{11,3},{4,12},{12,4},... | collective-permute-start | bytes 1376264 | tf_op jit(solution)/shard_map/ppermute | solution.py:203
  22.8 3.3 %collective-permute-start.13 = (bf16[64,3712]{1,0:T(8,128)(2,1)S(1)}, bf16[64,3712]{1,0:T(8,128)(2,1)S(1)}, u32[]{:S(2)}, u32[]{:S(2)}) collective-permute-start(bf16[64,3712]{1,0:T(8,128)(2,1)S(1)} %collective-permute-done.5.refs_0_), channel_id=1, source_target_pairs={{0,8},{8,0},{1,9},{9,1},{2,10},{10,2},{3,11},{11,3},{4,12},{12,4},... | collective-permute-start | bytes 1425416 | tf_op jit(solution)/shard_map/ppermute | solution.py:203
  22.8 8.7 %collective-permute-start.6 = (bf16[64,3712]{1,0:T(8,128)(2,1)S(1)}, bf16[64,3712]{1,0:T(8,128)(2,1)S(1)}, u32[]{:S(2)}, u32[]{:S(2)}) collective-permute-start(bf16[64,3712]{1,0:T(8,128)(2,1)S(1)} %collective-permute-done.5.refs_0_), channel_id=1, source_target_pairs={{0,2},{10,8},{2,4},{12,10},{4,6},{14,12},{6,7},{15,14},{7,5},{13,1... | collective-permute-start | bytes 1425416 | tf_op jit(solution)/shard_map/ppermute | solution.py:200
  24.4 11.9 %collective-permute-start.25 = (bf16[64,3584]{1,0:T(8,128)(2,1)S(1)}, bf16[64,3584]{1,0:T(8,128)(2,1)S(1)}, u32[]{:S(2)}, u32[]{:S(2)}) collective-permute-start(bf16[64,3584]{1,0:T(8,128)(2,1)S(1)} %add_convert_fusion.7), channel_id=1, source_target_pairs={{0,2},{10,8},{2,4},{12,10},{4,6},{14,12},{6,7},{15,14},{7,5},{13,1... | collective-permute-start | bytes 1376264 | tf_op jit(solution)/shard_map/ppermute | solution.py:200
  27.8 8.6 %collective-permute-start.23 = (bf16[64,3584]{1,0:T(8,128)(2,1)S(1)}, bf16[64,3584]{1,0:T(8,128)(2,1)S(1)}, u32[]{:S(2)}, u32[]{:S(2)}) collective-permute-start(bf16[64,3584]{1,0:T(8,128)(2,1)S(1)} %get-tuple-element.65), channel_id=1, source_target_pairs={{0,8},{8,0},{1,9},{9,1},{2,10},{10,2},{3,11},{11,3},{4,12},{12,4},... | collective-permute-start | bytes 1376264 | tf_op jit(solution)/shard_map/ppermute | solution.py:203
  31.4 6.7 %collective-permute-start.14 = (bf16[64,3712]{1,0:T(8,128)(2,1)S(1)}, bf16[64,3712]{1,0:T(8,128)(2,1)S(1)}, u32[]{:S(2)}, u32[]{:S(2)}) collective-permute-start(bf16[64,3712]{1,0:T(8,128)(2,1)S(1)} %collective-permute-done.6.refs_0_), channel_id=1, source_target_pairs={{0,8},{8,0},{1,9},{9,1},{2,10},{10,2},{3,11},{11,3},{4,12},{12,4},... | collective-permute-start | bytes 1425416 | tf_op jit(solution)/shard_map/ppermute | solution.py:203
  31.4 10.6 %collective-permute-start.7 = (bf16[64,3712]{1,0:T(8,128)(2,1)S(1)}, bf16[64,3712]{1,0:T(8,128)(2,1)S(1)}, u32[]{:S(2)}, u32[]{:S(2)}) collective-permute-start(bf16[64,3712]{1,0:T(8,128)(2,1)S(1)} %collective-permute-done.6.refs_0_), channel_id=1, source_target_pairs={{0,2},{10,8},{2,4},{12,10},{4,6},{14,12},{6,7},{15,14},{7,5},{13,1... | collective-permute-start | bytes 1425416 | tf_op jit(solution)/shard_map/ppermute | solution.py:200
  36.5 9.8 %collective-permute-start.26 = (bf16[64,3584]{1,0:T(8,128)(2,1)S(1)}, bf16[64,3584]{1,0:T(8,128)(2,1)S(1)}, u32[]{:S(2)}, u32[]{:S(2)}) collective-permute-start(bf16[64,3584]{1,0:T(8,128)(2,1)S(1)} %add_convert_fusion.6), channel_id=1, source_target_pairs={{0,2},{10,8},{2,4},{12,10},{4,6},{14,12},{6,7},{15,14},{7,5},{13,1... | collective-permute-start | bytes 1376264 | tf_op jit(solution)/shard_map/ppermute | solution.py:200
  39.9 6.5 %collective-permute-start.22 = (bf16[64,3584]{1,0:T(8,128)(2,1)S(1)}, bf16[64,3584]{1,0:T(8,128)(2,1)S(1)}, u32[]{:S(2)}, u32[]{:S(2)}) collective-permute-start(bf16[64,3584]{1,0:T(8,128)(2,1)S(1)} %get-tuple-element.64), channel_id=1, source_target_pairs={{0,8},{8,0},{1,9},{9,1},{2,10},{10,2},{3,11},{11,3},{4,12},{12,4},... | collective-permute-start | bytes 1376264 | tf_op jit(solution)/shard_map/ppermute | solution.py:203
  42.0 6.3 %collective-permute-start.15 = (bf16[64,3712]{1,0:T(8,128)(2,1)S(1)}, bf16[64,3712]{1,0:T(8,128)(2,1)S(1)}, u32[]{:S(2)}, u32[]{:S(2)}) collective-permute-start(bf16[64,3712]{1,0:T(8,128)(2,1)S(1)} %collective-permute-done.7.refs_0_), channel_id=1, source_target_pairs={{0,8},{8,0},{1,9},{9,1},{2,10},{10,2},{3,11},{11,3},{4,12},{12,4},... | collective-permute-start | bytes 1425416 | tf_op jit(solution)/shard_map/ppermute | solution.py:203
  42.5 9.7 %collective-permute-start.8 = (bf16[64,3712]{1,0:T(8,128)(2,1)S(1)}, bf16[64,3712]{1,0:T(8,128)(2,1)S(1)}, u32[]{:S(2)}, u32[]{:S(2)}) collective-permute-start(bf16[64,3712]{1,0:T(8,128)(2,1)S(1)} %collective-permute-done.7.refs_0_), channel_id=1, source_target_pairs={{0,2},{10,8},{2,4},{12,10},{4,6},{14,12},{6,7},{15,14},{7,5},{13,1... | collective-permute-start | bytes 1425416 | tf_op jit(solution)/shard_map/ppermute | solution.py:200
  46.6 9.8 %collective-permute-start.27 = (bf16[64,3584]{1,0:T(8,128)(2,1)S(1)}, bf16[64,3584]{1,0:T(8,128)(2,1)S(1)}, u32[]{:S(2)}, u32[]{:S(2)}) collective-permute-start(bf16[64,3584]{1,0:T(8,128)(2,1)S(1)} %add_convert_fusion.5), channel_id=1, source_target_pairs={{0,2},{10,8},{2,4},{12,10},{4,6},{14,12},{6,7},{15,14},{7,5},{13,1... | collective-permute-start | bytes 1376264 | tf_op jit(solution)/shard_map/ppermute | solution.py:200
  50.1 6.2 %collective-permute-start.21 = (bf16[64,3584]{1,0:T(8,128)(2,1)S(1)}, bf16[64,3584]{1,0:T(8,128)(2,1)S(1)}, u32[]{:S(2)}, u32[]{:S(2)}) collective-permute-start(bf16[64,3584]{1,0:T(8,128)(2,1)S(1)} %get-tuple-element.63), channel_id=1, source_target_pairs={{0,8},{8,0},{1,9},{9,1},{2,10},{10,2},{3,11},{11,3},{4,12},{12,4},... | collective-permute-start | bytes 1376264 | tf_op jit(solution)/shard_map/ppermute | solution.py:203
  52.3 5.9 %collective-permute-start.16 = (bf16[64,3712]{1,0:T(8,128)(2,1)S(1)}, bf16[64,3712]{1,0:T(8,128)(2,1)S(1)}, u32[]{:S(2)}, u32[]{:S(2)}) collective-permute-start(bf16[64,3712]{1,0:T(8,128)(2,1)S(1)} %collective-permute-done.8.refs_0_), channel_id=1, source_target_pairs={{0,8},{8,0},{1,9},{9,1},{2,10},{10,2},{3,11},{11,3},{4,12},{12,4},... | collective-permute-start | bytes 1425416 | tf_op jit(solution)/shard_map/ppermute | solution.py:203
  52.8 9.8 %collective-permute-start.9 = (bf16[64,3712]{1,0:T(8,128)(2,1)S(1)}, bf16[64,3712]{1,0:T(8,128)(2,1)S(1)}, u32[]{:S(2)}, u32[]{:S(2)}) collective-permute-start(bf16[64,3712]{1,0:T(8,128)(2,1)S(1)} %collective-permute-done.8.refs_0_), channel_id=1, source_target_pairs={{0,2},{10,8},{2,4},{12,10},{4,6},{14,12},{6,7},{15,14},{7,5},{13,1... | collective-permute-start | bytes 1425416 | tf_op jit(solution)/shard_map/ppermute | solution.py:200
  56.5 9.8 %collective-permute-start.28 = (bf16[64,3584]{1,0:T(8,128)(2,1)S(1)}, bf16[64,3584]{1,0:T(8,128)(2,1)S(1)}, u32[]{:S(2)}, u32[]{:S(2)}) collective-permute-start(bf16[64,3584]{1,0:T(8,128)(2,1)S(1)} %add_convert_fusion.4), channel_id=1, source_target_pairs={{0,2},{10,8},{2,4},{12,10},{4,6},{14,12},{6,7},{15,14},{7,5},{13,1... | collective-permute-start | bytes 1376264 | tf_op jit(solution)/shard_map/ppermute | solution.py:200
  59.9 6.4 %collective-permute-start.20 = (bf16[64,3584]{1,0:T(8,128)(2,1)S(1)}, bf16[64,3584]{1,0:T(8,128)(2,1)S(1)}, u32[]{:S(2)}, u32[]{:S(2)}) collective-permute-start(bf16[64,3584]{1,0:T(8,128)(2,1)S(1)} %get-tuple-element.62), channel_id=1, source_target_pairs={{0,8},{8,0},{1,9},{9,1},{2,10},{10,2},{3,11},{11,3},{4,12},{12,4},... | collective-permute-start | bytes 1376264 | tf_op jit(solution)/shard_map/ppermute | solution.py:203
  60.0 10.0 %collective-permute-start.2 = (bf16[64,3584]{1,0:T(8,128)(2,1)S(1)}, bf16[64,3584]{1,0:T(8,128)(2,1)S(1)}, u32[]{:S(2)}, u32[]{:S(2)}) collective-permute-start(bf16[64,3584]{1,0:T(8,128)(2,1)S(1)} %get-tuple-element.40), channel_id=1, source_target_pairs={{0,8},{8,0},{1,9},{9,1},{2,10},{10,2},{3,11},{11,3},{4,12},{12,4},... | collective-permute-start | bytes 1376264 | tf_op jit(solution)/shard_map/ppermute | solution.py:203
  62.6 5.6 %collective-permute-start.18 = (bf16[64,3712]{1,0:T(8,128)(2,1)S(1)}, bf16[64,3712]{1,0:T(8,128)(2,1)S(1)}, u32[]{:S(2)}, u32[]{:S(2)}) collective-permute-start(bf16[64,3712]{1,0:T(8,128)(2,1)S(1)} %collective-permute-done.9.refs_0_), channel_id=1, source_target_pairs={{0,8},{8,0},{1,9},{9,1},{2,10},{10,2},{3,11},{11,3},{4,12},{12,4},... | collective-permute-start | bytes 1425416 | tf_op jit(solution)/shard_map/ppermute | solution.py:203
  62.6 9.6 %collective-permute-start.10 = (bf16[64,3712]{1,0:T(8,128)(2,1)S(1)}, bf16[64,3712]{1,0:T(8,128)(2,1)S(1)}, u32[]{:S(2)}, u32[]{:S(2)}) collective-permute-start(bf16[64,3712]{1,0:T(8,128)(2,1)S(1)} %collective-permute-done.9.refs_0_), channel_id=1, source_target_pairs={{0,2},{10,8},{2,4},{12,10},{4,6},{14,12},{6,7},{15,14},{7,5},{13,1... | collective-permute-start | bytes 1425416 | tf_op jit(solution)/shard_map/ppermute | solution.py:200
  66.6 9.8 %collective-permute-start.29 = (bf16[64,3584]{1,0:T(8,128)(2,1)S(1)}, bf16[64,3584]{1,0:T(8,128)(2,1)S(1)}, u32[]{:S(2)}, u32[]{:S(2)}) collective-permute-start(bf16[64,3584]{1,0:T(8,128)(2,1)S(1)} %add_convert_fusion.3), channel_id=1, source_target_pairs={{0,2},{10,8},{2,4},{12,10},{4,6},{14,12},{6,7},{15,14},{7,5},{13,1... | collective-permute-start | bytes 1376264 | tf_op jit(solution)/shard_map/ppermute | solution.py:200
  69.9 6.4 %collective-permute-start.19 = (bf16[64,3584]{1,0:T(8,128)(2,1)S(1)}, bf16[64,3584]{1,0:T(8,128)(2,1)S(1)}, u32[]{:S(2)}, u32[]{:S(2)}) collective-permute-start(bf16[64,3584]{1,0:T(8,128)(2,1)S(1)} %get-tuple-element.61), channel_id=1, source_target_pairs={{0,8},{8,0},{1,9},{9,1},{2,10},{10,2},{3,11},{11,3},{4,12},{12,4},... | collective-permute-start | bytes 1376264 | tf_op jit(solution)/shard_map/ppermute | solution.py:203
  72.2 6.0 %collective-permute-start.11 = (bf16[64,3712]{1,0:T(8,128)(2,1)S(1)}, bf16[64,3712]{1,0:T(8,128)(2,1)S(1)}, u32[]{:S(2)}, u32[]{:S(2)}) collective-permute-start(bf16[64,3712]{1,0:T(8,128)(2,1)S(1)} %collective-permute-done.10.refs_0_), channel_id=1, source_target_pairs={{0,8},{8,0},{1,9},{9,1},{2,10},{10,2},{3,11},{11,3},{4,12},{12,4},... | collective-permute-start | bytes 1425416 | tf_op jit(solution)/shard_map/ppermute | solution.py:203
  76.6 8.5 %collective-permute-start.30 = (bf16[64,3584]{1,0:T(8,128)(2,1)S(1)}, bf16[64,3584]{1,0:T(8,128)(2,1)S(1)}, u32[]{:S(2)}, u32[]{:S(2)}) collective-permute-start(bf16[64,3584]{1,0:T(8,128)(2,1)S(1)} %add_convert_fusion.2), channel_id=1, source_target_pairs={{0,2},{10,8},{2,4},{12,10},{4,6},{14,12},{6,7},{15,14},{7,5},{13,1... | collective-permute-start | bytes 1376264 | tf_op jit(solution)/shard_map/ppermute | solution.py:200
  79.9 5.2 %collective-permute-start.17 = (bf16[64,3584]{1,0:T(8,128)(2,1)S(1)}, bf16[64,3584]{1,0:T(8,128)(2,1)S(1)}, u32[]{:S(2)}, u32[]{:S(2)}) collective-permute-start(bf16[64,3584]{1,0:T(8,128)(2,1)S(1)} %get-tuple-element.58), channel_id=1, source_target_pairs={{0,8},{8,0},{1,9},{9,1},{2,10},{10,2},{3,11},{11,3},{4,12},{12,4},... | collective-permute-start | bytes 1376264 | tf_op jit(solution)/shard_map/ppermute | solution.py:203
  85.3 6.0 %collective-permute-start.32 = (bf16[32,3584]{1,0:T(8,128)(2,1)S(1)}, bf16[32,3584]{1,0:T(8,128)(2,1)S(1)}, u32[]{:S(2)}, u32[]{:S(2)}) collective-permute-start(bf16[32,3584]{1,0:T(8,128)(2,1)S(1)} %get-tuple-element.73), channel_id=1, source_target_pairs={{0,10},{10,0},{2,12},{12,2},{4,14},{14,4},{6,15},{15,6},{7,13},{13... | collective-permute-start | bytes 688136 | tf_op jit(solution)/shard_map/ppermute | solution.py:200
  85.4 7.4 %collective-permute-start.31 = (bf16[32,3584]{1,0:T(8,128)(2,1)S(1)}, bf16[32,3584]{1,0:T(8,128)(2,1)S(1)}, u32[]{:S(2)}, u32[]{:S(2)}) collective-permute-start(bf16[32,3584]{1,0:T(8,128)(2,1)S(1)} %get-tuple-element.72), channel_id=1, source_target_pairs={{0,2},{10,8},{2,4},{12,10},{4,6},{14,12},{6,7},{15,14},{7,5},{13,1... | collective-permute-start | bytes 688136 | tf_op jit(solution)/shard_map/ppermute | solution.py:200
